TPU v7x, 32 devices: a whole 2x2x4 slice. The times are simulated.
32 devices in a mesh: ctx: 8 (over y, x, core), fsdp: 4 (over z).
Axes of the slice: x: 2, y: 2, z: 4, core: 2. Of those that a mesh axis runs over, the one named last changes fastest.
Arguments:
- layer_input: bfloat16 [4, 1024, 2048], P('fsdp', 'ctx'), may hold values from -6 to 6
- pairing: int32 [4, 8], P('fsdp'), may hold values from 0 to 7, each once within a row
- query_weight: bfloat16 [2048, 2048], P(('ctx', 'fsdp')), may hold values from -0.125 to 0.125
- key_weight: bfloat16 [2048, 2048], P(('ctx', 'fsdp')), may hold values from -0.125 to 0.125
- value_weight: bfloat16 [2048, 2048], P(('ctx', 'fsdp')), may hold values from -0.125 to 0.125
- merge_weight: bfloat16 [2048, 2048], P(('ctx', 'fsdp')), may hold values from -3 to 3
- gate_weight: bfloat16 [2048, 8192], P(('ctx', 'fsdp')), may hold values from -0.125 to 0.125
- up_weight: bfloat16 [2048, 8192], P(('ctx', 'fsdp')), may hold values from -0.125 to 0.125
- down_weight: bfloat16 [8192, 2048], P(('ctx', 'fsdp')), may hold values from -0.0625 to 0.0625
- norm_first: bfloat16 [2048], P(('ctx', 'fsdp')), may hold values from 0.5 to 1.5
- norm_second: bfloat16 [2048], P(('ctx', 'fsdp')), may hold values from 0.5 to 1.5
- output_cotangent: bfloat16 [4, 1024, 2048], P('fsdp', 'ctx'), may hold values from -6 to 6
Outputs:
- layer_output: bfloat16 [4, 1024, 2048], P('fsdp', 'ctx')
- input_grad: bfloat16 [4, 1024, 2048], P('fsdp', 'ctx')
- query_grad: float32 [2048, 2048], P(('ctx', 'fsdp'))
- key_grad: float32 [2048, 2048], P(('ctx', 'fsdp'))
- value_grad: float32 [2048, 2048], P(('ctx', 'fsdp'))
- merge_grad: float32 [2048, 2048], P(('ctx', 'fsdp'))
- gate_grad: float32 [2048, 8192], P(('ctx', 'fsdp'))
- up_grad: float32 [2048, 8192], P(('ctx', 'fsdp'))
- down_grad: float32 [8192, 2048], P(('ctx', 'fsdp'))
- first_grad: float32 [2048], P(('ctx', 'fsdp'))
- second_grad: float32 [2048], P(('ctx', 'fsdp'))
Inputs may be any that keep to these rules, and one draw needn't show every extreme that they name: Each row is a permutation of the ctx indices: index c holds causal blocks pairing[s, c] and 15 - pairing[s, c] of sequence s, each of 64 tokens.
All inputs are finite; a program needn't handle non-finite values.
Results may differ from a plain program's by a relative error of at most 0.018.
Values may be sent and summed in bfloat16 or wider, within the bound.
No kernel may reach another device: no remote copies, remote signals or barrier semaphores. Data moves between devices by JAX's collectives and lax.ppermute only.
A program may use at most 320 MiB of HBM per device.

v0:
```python
import jax
import jax.numpy as jnp
from jax import lax
from jax.sharding import PartitionSpec as P

HEAD_DIM = 64


THETA = 130000.0
EPS = 1e-05


def block_positions(pair_cols, length_block, n_ctx):
    lower = pair_cols * length_block
    upper = (2 * n_ctx - 1 - pair_cols) * length_block
    starts = jnp.stack([lower, upper], axis=-1)
    offsets = jnp.arange(length_block, dtype=jnp.int32)
    return (starts[..., None] + offsets).reshape(pair_cols.shape[0], -1)


def rotary(values, position, sign):
    shape = values.shape
    heads_view = values.reshape(shape[:-1] + (shape[-1] // HEAD_DIM, HEAD_DIM))
    half = HEAD_DIM // 2
    freq = THETA ** (-2.0 * jnp.arange(half, dtype=jnp.float32) / HEAD_DIM)
    angle = position[..., None].astype(jnp.float32) * freq
    cosine = jnp.cos(angle)[..., None, :]
    sine = sign * jnp.sin(angle)[..., None, :]
    first = heads_view[..., :half]
    second = heads_view[..., half:]
    turned = jnp.concatenate(
        [first * cosine - second * sine, second * cosine + first * sine], axis=-1
    )
    return turned.reshape(shape)


def contract(left, right):
    return lax.dot_general(
        left, right, (((1,), (1,)), ((), ())), preferred_element_type=jnp.float32
    )


def weight_term(left, right):
    return jnp.einsum("nc,nd->cd", left, right, preferred_element_type=jnp.float32)


def rounded(values):
    return lax.optimization_barrier(values.astype(jnp.bfloat16)).astype(jnp.float32)


def on_device(
    layer_input,
    pairing,
    query_weight,
    key_weight,
    value_weight,
    merge_weight,
    gate_weight,
    up_weight,
    down_weight,
    norm_first,
    norm_second,
    output_cotangent,
):
    n_ctx = lax.axis_size("ctx")
    n_fsdp = lax.axis_size("fsdp")
    seqs, rows, width = layer_input.shape
    length_block = rows // 2
    count = seqs * rows
    scale = HEAD_DIM ** (-0.5)
    group_width = 4 * HEAD_DIM
    groups = width // group_width
    own_pair = lax.dynamic_slice_in_dim(pairing, lax.axis_index("ctx"), 1, 1)
    own_position = block_positions(own_pair, length_block, n_ctx)
    key_position = block_positions(pairing, length_block, n_ctx)
    visible = key_position[:, None, None, :] <= own_position[:, None, :, None]
    query_full, key_full, value_full, merge_full, gain_first, gain_second = (
        lax.all_gather(query_weight, ("ctx", "fsdp"), axis=0, tiled=True),
        lax.all_gather(key_weight, ("ctx", "fsdp"), axis=0, tiled=True),
        lax.all_gather(value_weight, ("ctx", "fsdp"), axis=0, tiled=True),
        lax.all_gather(merge_weight, ("ctx", "fsdp"), axis=0, tiled=True),
        lax.all_gather(norm_first, ("ctx", "fsdp"), axis=0, tiled=True),
        lax.all_gather(norm_second, ("ctx", "fsdp"), axis=0, tiled=True),
    )
    gain_first = gain_first.astype(jnp.float32)
    gain_second = gain_second.astype(jnp.float32)
    tokens = layer_input.astype(jnp.float32)
    scale_first = lax.rsqrt(jnp.mean(tokens * tokens, axis=-1, keepdims=True) + EPS)
    unit_first = tokens * scale_first
    normed = (unit_first * gain_first).astype(jnp.bfloat16).reshape(count, width)
    queries = rotary(
        jnp.dot(normed, query_full, preferred_element_type=jnp.float32).reshape(seqs, rows, width),
        own_position,
        1.0,
    ).astype(jnp.bfloat16)
    keys_own = rotary(
        jnp.dot(normed, key_full, preferred_element_type=jnp.float32).reshape(seqs, rows, width),
        own_position,
        1.0,
    ).astype(jnp.bfloat16)
    values_own = (
        jnp.dot(normed, value_full, preferred_element_type=jnp.float32)
        .reshape(seqs, rows, width)
        .astype(jnp.bfloat16)
    )
    keys_all, values_all = (
        lax.all_gather(keys_own, "ctx", axis=1, tiled=True),
        lax.all_gather(values_own, "ctx", axis=1, tiled=True),
    )

    def slice_heads(values, index):
        piece = lax.dynamic_slice_in_dim(values, index * group_width, group_width, 2)
        return piece.reshape(piece.shape[0], piece.shape[1], 4, HEAD_DIM)

    def group_scores(index):
        query_part = slice_heads(queries, index)
        key_part = slice_heads(keys_all, index)
        scores = (
            jnp.einsum("srhd,skhd->shrk", query_part, key_part, preferred_element_type=jnp.float32)
            * scale
        )
        return (jnp.where(visible, scores, -1e30), query_part, key_part)

    def forward_group(index):
        scores, query_part, key_part = group_scores(index)
        peak = jnp.max(scores, axis=-1, keepdims=True)
        weights = jnp.exp(scores - peak)
        total = jnp.sum(weights, axis=-1, keepdims=True)
        probs = (weights / total).astype(jnp.bfloat16)
        value_part = slice_heads(values_all, index)
        result = jnp.einsum(
            "shrk,skhd->srhd", probs, value_part, preferred_element_type=jnp.float32
        )
        return (
            result.reshape(seqs, rows, group_width).astype(jnp.bfloat16),
            (peak + jnp.log(total))[..., 0],
        )

    attended, log_total = lax.map(forward_group, jnp.arange(groups, dtype=jnp.int32))
    attended = attended.transpose(1, 2, 0, 3).reshape(count, width)
    mixed = tokens + jnp.dot(attended, merge_full, preferred_element_type=jnp.float32).reshape(
        seqs, rows, width
    )
    scale_second = lax.rsqrt(jnp.mean(mixed * mixed, axis=-1, keepdims=True) + EPS)
    unit_second = mixed * scale_second
    normed_two = (unit_second * gain_second).astype(jnp.bfloat16).reshape(count, width)
    cotangent = output_cotangent.reshape(count, width)
    dev_rows = gate_weight.shape[0]
    hidden_total = gate_weight.shape[1]
    piece_cols = hidden_total // (n_ctx * n_fsdp)

    def regroup(matrix):
        return (
            matrix.reshape(dev_rows, n_ctx, n_fsdp, piece_cols)
            .transpose(2, 0, 1, 3)
            .reshape(n_fsdp, dev_rows, n_ctx * piece_cols)
        )

    gate_moved, up_moved = (
        lax.all_to_all(regroup(gate_weight), "fsdp", split_axis=0, concat_axis=1, tiled=True),
        lax.all_to_all(regroup(up_weight), "fsdp", split_axis=0, concat_axis=1, tiled=True),
    )
    gate_cols, up_cols, down_rows = (
        lax.all_gather(gate_moved[0], "ctx", axis=0, tiled=True),
        lax.all_gather(up_moved[0], "ctx", axis=0, tiled=True),
        lax.all_gather(down_weight, "ctx", axis=0, tiled=True),
    )
    normed_all, cotangent_all = (
        lax.all_gather(normed_two, "fsdp", axis=0, tiled=True),
        lax.all_gather(cotangent, "fsdp", axis=0, tiled=True),
    )
    gate = jnp.dot(normed_all, gate_cols, preferred_element_type=jnp.float32)
    up = jnp.dot(normed_all, up_cols, preferred_element_type=jnp.float32)
    gate_sigmoid = jax.nn.sigmoid(gate)
    active = gate * gate_sigmoid
    hidden = (active * up).astype(jnp.bfloat16)
    branch_out = lax.psum_scatter(
        jnp.dot(hidden, down_rows, preferred_element_type=jnp.float32).astype(jnp.bfloat16),
        "fsdp",
        scatter_dimension=0,
        tiled=True,
    ).astype(jnp.float32)
    layer_output = (mixed + branch_out.reshape(seqs, rows, width)).astype(jnp.bfloat16)
    grad_hidden = contract(cotangent_all, down_rows)
    grad_gate = (grad_hidden * up * gate_sigmoid * (1.0 + gate * (1.0 - gate_sigmoid))).astype(
        jnp.bfloat16
    )
    grad_up = (grad_hidden * active).astype(jnp.bfloat16)
    partial_two = contract(grad_gate, gate_cols) + contract(grad_up, up_cols)
    grad_normed_two = (
        lax.psum_scatter(partial_two.astype(jnp.bfloat16), "fsdp", scatter_dimension=0, tiled=True)
        .astype(jnp.float32)
        .reshape(seqs, rows, width)
    )
    paired = jnp.stack([grad_gate, grad_up], axis=1)
    columns = normed_all
    slice_sum = lax.psum_scatter(
        jnp.einsum("nc,nkf->ckf", columns, paired, preferred_element_type=jnp.float32).astype(
            jnp.bfloat16
        ),
        "ctx",
        scatter_dimension=0,
        tiled=True,
    ).astype(jnp.float32)
    slice_sum = slice_sum.reshape(n_fsdp, dev_rows, 2, n_ctx, piece_cols)
    returned = lax.all_to_all(
        slice_sum.astype(jnp.bfloat16), "fsdp", split_axis=0, concat_axis=0, tiled=True
    ).astype(slice_sum.dtype)
    returned = returned.transpose(1, 2, 3, 0, 4).reshape(dev_rows, 2, hidden_total)
    gate_grad = returned[:, 0]
    up_grad = returned[:, 1]
    columns = hidden
    down_grad = lax.psum_scatter(
        jnp.einsum("nc,nd->cd", columns, cotangent_all, preferred_element_type=jnp.float32).astype(
            jnp.bfloat16
        ),
        "ctx",
        scatter_dimension=0,
        tiled=True,
    ).astype(jnp.float32)
    second_term = jnp.sum(grad_normed_two * unit_second, axis=(0, 1))
    scaled_two = grad_normed_two * gain_second
    grad_mixed = output_cotangent.astype(jnp.float32) + scale_second * (
        scaled_two - unit_second * jnp.mean(scaled_two * unit_second, axis=-1, keepdims=True)
    )
    grad_branch = grad_mixed.reshape(count, width).astype(jnp.bfloat16)
    query_full, key_full, value_full, merge_full = (
        lax.all_gather(query_weight, ("ctx", "fsdp"), axis=0, tiled=True),
        lax.all_gather(key_weight, ("ctx", "fsdp"), axis=0, tiled=True),
        lax.all_gather(value_weight, ("ctx", "fsdp"), axis=0, tiled=True),
        lax.all_gather(merge_weight, ("ctx", "fsdp"), axis=0, tiled=True),
    )
    grad_attended = (
        contract(grad_branch, merge_full).astype(jnp.bfloat16).reshape(seqs, rows, width)
    )

    def backward_group(index):
        scores, query_part, key_part = group_scores(index)
        probs = jnp.exp(scores - log_total[index][..., None])
        value_part = slice_heads(values_all, index)
        grad_part = slice_heads(grad_attended, index)
        grad_probs = jnp.einsum(
            "srhd,skhd->shrk", grad_part, value_part, preferred_element_type=jnp.float32
        )
        centre = jnp.sum(probs * grad_probs, axis=-1, keepdims=True)
        grad_scores = (probs * (grad_probs - centre)).astype(jnp.bfloat16)
        grad_values = jnp.einsum(
            "shrk,srhd->skhd",
            probs.astype(jnp.bfloat16),
            grad_part,
            preferred_element_type=jnp.float32,
        )
        grad_queries = (
            jnp.einsum("shrk,skhd->srhd", grad_scores, key_part, preferred_element_type=jnp.float32)
            * scale
        )
        grad_keys = (
            jnp.einsum(
                "shrk,srhd->skhd", grad_scores, query_part, preferred_element_type=jnp.float32
            )
            * scale
        )
        keys_rows = key_part.shape[1]
        return (
            grad_queries.reshape(seqs, rows, group_width),
            grad_keys.reshape(seqs, keys_rows, group_width),
            grad_values.reshape(seqs, keys_rows, group_width),
        )

    grad_queries, grad_keys, grad_values = lax.map(
        backward_group, jnp.arange(groups, dtype=jnp.int32)
    )

    def join_heads(stacked):
        return stacked.transpose(1, 2, 0, 3).reshape(stacked.shape[1], stacked.shape[2], width)

    keys_grad_own, values_grad_own = (
        lax.psum_scatter(
            join_heads(grad_keys).astype(jnp.bfloat16), "ctx", scatter_dimension=1, tiled=True
        ).astype(jnp.float32),
        lax.psum_scatter(
            join_heads(grad_values).astype(jnp.bfloat16), "ctx", scatter_dimension=1, tiled=True
        ).astype(jnp.float32),
    )
    grad_query_raw = (
        rotary(rounded(join_heads(grad_queries)), own_position, -1.0)
        .astype(jnp.bfloat16)
        .reshape(count, width)
    )
    grad_key_raw = (
        rotary(rounded(keys_grad_own), own_position, -1.0)
        .astype(jnp.bfloat16)
        .reshape(count, width)
    )
    grad_value_raw = values_grad_own.astype(jnp.bfloat16).reshape(count, width)
    grad_normed = (
        contract(grad_query_raw, query_full)
        + contract(grad_key_raw, key_full)
        + contract(grad_value_raw, value_full)
    )
    grad_normed = grad_normed.reshape(seqs, rows, width)
    first_term = jnp.sum(grad_normed * unit_first, axis=(0, 1))
    scaled_one = grad_normed * gain_first
    input_grad = (
        grad_mixed
        + scale_first
        * (scaled_one - unit_first * jnp.mean(scaled_one * unit_first, axis=-1, keepdims=True))
    ).astype(jnp.bfloat16)
    sums = (
        lax.psum_scatter(
            weight_term(normed, grad_query_raw), ("ctx", "fsdp"), scatter_dimension=0, tiled=True
        ),
        lax.psum_scatter(
            weight_term(normed, grad_key_raw), ("ctx", "fsdp"), scatter_dimension=0, tiled=True
        ),
        lax.psum_scatter(
            weight_term(normed, grad_value_raw), ("ctx", "fsdp"), scatter_dimension=0, tiled=True
        ),
        lax.psum_scatter(
            weight_term(attended, grad_branch), ("ctx", "fsdp"), scatter_dimension=0, tiled=True
        ),
        lax.psum_scatter(first_term, ("ctx", "fsdp"), scatter_dimension=0, tiled=True),
        lax.psum_scatter(second_term, ("ctx", "fsdp"), scatter_dimension=0, tiled=True),
    )
    return (
        layer_output,
        input_grad,
        sums[0],
        sums[1],
        sums[2],
        sums[3],
        gate_grad,
        up_grad,
        down_grad,
        sums[4],
        sums[5],
    )


def solution(mesh):
    placed = (
        P("fsdp", "ctx", None),
        P("fsdp", None),
        P(("ctx", "fsdp"), None),
        P(("ctx", "fsdp"), None),
        P(("ctx", "fsdp"), None),
        P(("ctx", "fsdp"), None),
        P(("ctx", "fsdp"), None),
        P(("ctx", "fsdp"), None),
        P(("ctx", "fsdp"), None),
        P(("ctx", "fsdp")),
        P(("ctx", "fsdp")),
        P("fsdp", "ctx", None),
    )
    return jax.shard_map(
        on_device,
        mesh=mesh,
        in_specs=placed,
        out_specs=(
            P("fsdp", "ctx", None),
            P("fsdp", "ctx", None),
            P(("ctx", "fsdp"), None),
            P(("ctx", "fsdp"), None),
            P(("ctx", "fsdp"), None),
            P(("ctx", "fsdp"), None),
            P(("ctx", "fsdp"), None),
            P(("ctx", "fsdp"), None),
            P(("ctx", "fsdp"), None),
            P(("ctx", "fsdp")),
            P(("ctx", "fsdp")),
        ),
        check_vma=False,
    )
```

profile of v0, /device:TPU:18, one launch (start us, length us, event | category | flops | bytes accessed | tf_op | source)
XLA Modules:
  0.0 2696.1 jit_solution(15465540661539308992)
XLA Ops:
  11.2 41.6 %all-reduce.5 = (bf16[2048]{0:T(1024)(128)(2,1)S(1)}, bf16[2048]{0:T(1024)(128)(2,1)S(1)}) all-reduce(bf16[2048]{0:T(1024)(128)(2,1)S(1)} %dynamic-update-slice, bf16[2048]{0:T(1024)(128)(2,1)S(1)} %dynamic-update-slice.1), channel_id=1, replica_groups=mesh['ctx'=8,'fsdp'=4] {'ctx','fsdp'}, use_global_device_ids=true, to_apply=%add | all-reduce | flops 4096 | bytes 16384
  54.0 35.1 %all-gather.15.cloned.1.call-done = bf16[2048,2048]{1,0:T(8,128)(2,1)} async-done(((bf16[64,2048]{1,0:T(8,128)(2,1)}), bf16[2048,2048]{1,0:T(8,128)(2,1)}) %all-gather.15.cloned.1.call-update) | async-done | bytes 8388624 | tf_op jit(solution)/shard_map/all_gather | solution.py:80
  97.8 70.2 %all-gather.19.cloned.1.call-done = bf16[2048,2048]{1,0:T(8,128)(2,1)} async-done(((bf16[64,2048]{1,0:T(8,128)(2,1)}), bf16[2048,2048]{1,0:T(8,128)(2,1)}) %all-gather.19.cloned.1.call-update) | async-done | bytes 8388624 | tf_op jit(solution)/shard_map/all_gather | solution.py:79
  168.0 12.3 copy.52
  180.4 66.6 %all-gather.17.cloned.1.call-done = bf16[2048,2048]{1,0:T(8,128)(2,1)} async-done(((bf16[64,2048]{1,0:T(8,128)(2,1)}), bf16[2048,2048]{1,0:T(8,128)(2,1)}) %all-gather.17.cloned.1.call-update) | async-done | bytes 8388624 | tf_op jit(solution)/shard_map/all_gather | solution.py:78
  247.0 12.4 copy.51
  259.4 6.0 convolution_bitcast_fusion.1
  277.4 22.9 all-to-all-done.1
  302.6 6.4 copy.54
  309.1 15.9 all-gather.21.cloned.1.call-done
  325.0 42.6 %while.28 = (s32[]{:T(128)}, bf16[8,1,128,256]{2,3,1,0:T(8,128)(2,1)S(1)}, f32[8,1,4,128]{3,2,1,0:T(4,128)}, s32[8]{0:T(128)S(1)}, bf16[1,1024,2048]{1,2,0:T(8,1...) while((s32[]{:T(128)}, ...), condition=%wide.region_4.5_spmd.clone, body=%wide.region_1.4_spmd.clone.sunk | while | flops 140672512 | bytes 10376387 | solution.py:139
  367.6 37.2 %all-gather.23.cloned.1.call-done = bf16[2048,2048]{1,0:T(8,128)(2,1)} async-done(((bf16[64,2048]{1,0:T(8,128)(2,1)}), bf16[2048,2048]{1,0:T(8,128)(2,1)}) %all-gather.23.cloned.1.call-update) | async-done | bytes 8388624 | tf_op jit(solution)/shard_map/all_gather | solution.py:81
  415.0 29.0 %all_to_all.23 = bf16[4,64,2048]{2,1,0:T(8,128)(2,1)} all-to-all(bf16[4,64,2048]{2,1,0:T(8,128)(2,1)} %reshape.655), channel_id=1, replica_groups=mesh['ctx'=8,'fsdp'=4] {'fsdp'}, dimensions={0} | all-to-all | bytes 2097152 | tf_op jit(solution)/shard_map/all_to_all | solution.py:160
  445.4 15.3 all-gather.27.cloned.1.call-done
  460.7 46.8 %all-gather.33.cloned.1.call-done = bf16[1,512,2048]{2,1,0:T(8,128)(2,1)} async-done(((bf16[1,128,2048]{2,1,0:T(8,128)(2,1)}), bf16[1,512,2048]{2,1,0:T(8,128)(2,1)}) %all-gather.33.cloned.1.call-update) | async-done | bytes 2097168 | tf_op jit(solution)/shard_map/all_gather | solution.py:169
  507.5 10.5 fusion.21
  518.0 45.9 %all-gather.25.cloned.1.call-done = bf16[2048,2048]{1,0:T(8,128)(2,1)} async-done(((bf16[256,2048]{1,0:T(8,128)(2,1)}), bf16[2048,2048]{1,0:T(8,128)(2,1)}) %all-gather.25.cloned.1.call-update) | async-done | bytes 8388624 | tf_op jit(solution)/shard_map/all_gather | solution.py:164
  563.9 10.5 fusion.23
  574.4 35.5 %all-gather.35.cloned.1.call-done = bf16[1,512,2048]{2,1,0:T(8,128)(2,1)} async-done(((bf16[1,128,2048]{2,1,0:T(8,128)(2,1)}), bf16[1,512,2048]{2,1,0:T(8,128)(2,1)}) %all-gather.35.cloned.1.call-update) | async-done | bytes 2097168 | tf_op jit(solution)/shard_map/all_gather | solution.py:170
  609.9 56.4 %all-gather.29.cloned.1.call-done = bf16[2048,2048]{1,0:T(8,128)(2,1)} async-done(((bf16[256,2048]{1,0:T(8,128)(2,1)}), bf16[2048,2048]{1,0:T(8,128)(2,1)}) %all-gather.29.cloned.1.call-update) | async-done | bytes 8388624 | tf_op jit(solution)/shard_map/all_gather | solution.py:166
  666.3 13.6 multiply_convert_fusion.1
  679.9 8.4 fusion.72
  688.4 9.2 add_convert_fusion
  697.6 9.9 convolution_convert_fusion.3
  707.6 33.3 %reduce-scatter.17.cloned.1.call-done = bf16[128,2048]{1,0:T(8,128)(2,1)} async-done(((bf16[512,2048]{1,0:T(8,128)(2,1)}), bf16[128,2048]{1,0:T(8,128)(2,1)}) %reduce-scatter.17.cloned.1.call-update) | async-done | bytes 524304 | tf_op jit(solution)/shard_map/reduce_scatter | solution.py:191
  742.4 44.7 %reduce-scatter.15.cloned.1.call-done = bf16[128,2048]{1,0:T(8,128)(2,1)} async-done(((bf16[512,2048]{1,0:T(8,128)(2,1)}), bf16[128,2048]{1,0:T(8,128)(2,1)}) %reduce-scatter.15.cloned.1.call-update) | async-done | bytes 524304 | tf_op jit(solution)/shard_map/reduce_scatter | solution.py:177
  789.5 7.4 fusion.16
  797.0 101.4 %while.29 = (s32[]{:T(128)}, bf16[8,1,128,256]{2,3,1,0:T(8,128)(2,1)}, bf16[8,1,1024,256]{2,3,1,0:T(8,128)(2,1)}, bf16[8,1,1024,256]{2,3,1,0:T(8,128)(2,1)}, s32...) while((s32[]{:T(128)}, ...), condition=%wide.region_11.12_spmd.clone, body=%wide.region_9.11_spmd.clone.sunk | while | flops 340983296 | bytes 23674636 | solution.py:270
  898.4 20.6 copy.64
  919.0 8.0 copy.77
  927.1 20.8 copy.66
  947.9 8.7 copy.76
  958.2 14.9 convolution_convert_fusion.1
  974.7 8.4 convolution_convert_fusion.2
  984.3 9.6 fusion.49
  1001.2 8.7 fusion.54
  1010.0 8.2 fusion.57
  1018.3 15.2 reduce-scatter.33.cloned.1.call-done
  1038.5 10.9 fusion.46
  1049.4 103.4 %reduce-scatter.27.cloned.1.call-done = bf16[256,2,2048]{2,0,1:T(8,128)(2,1)} async-done(((bf16[2048,2,2048]{2,0,1:T(8,128)(2,1)}), bf16[256,2,2048]{2,0,1:T(8,128)(2,1)}) %reduce-scatter.27.cloned.1.call-update) | async-done | bytes 2097168 | tf_op jit(solution)/shard_map/reduce_scatter | solution.py:197
  1161.8 7.4 fusion.73
  1169.2 7.4 convolution_add_fusion.1
  1179.8 48.8 %all-reduce.4 = (f32[2048]{0:T(1024)S(1)}, f32[2048]{0:T(1024)S(1)}) all-reduce(f32[2048]{0:T(1024)S(1)} %get-tuple-element.254, f32[2048]{0:T(1024)S(1)} %get-tuple-element.252), channel_id=15, replica_groups=mesh['ctx'=8,'fsdp'=4] {'ctx','fsdp'}, use_global_device_ids=true, to_apply=%region_22.23.clone | all-reduce | flops 4096 | bytes 32768
  1240.4 5.8 reshape.678
  1250.9 342.9 %reduce-scatter.25.cloned.1.call-done = f32[64,2048]{1,0:T(8,128)} async-done(((f32[2048,2048]{1,0:T(8,128)}), f32[64,2048]{1,0:T(8,128)}) %reduce-scatter.25.cloned.1.call-update) | async-done | bytes 524304 | tf_op jit(solution)/shard_map/reduce_scatter | solution.py:319
  1593.7 365.1 %reduce-scatter.19.cloned.1.call-done = f32[64,2048]{1,0:T(8,128)} async-done(((f32[2048,2048]{1,0:T(8,128)}), f32[64,2048]{1,0:T(8,128)}) %reduce-scatter.19.cloned.1.call-update) | async-done | bytes 524304 | tf_op jit(solution)/shard_map/reduce_scatter | solution.py:310
  1958.9 365.0 %reduce-scatter.21.cloned.1.call-done = f32[64,2048]{1,0:T(8,128)} async-done(((f32[2048,2048]{1,0:T(8,128)}), f32[64,2048]{1,0:T(8,128)}) %reduce-scatter.21.cloned.1.call-update) | async-done | bytes 524304 | tf_op jit(solution)/shard_map/reduce_scatter | solution.py:313
  2323.9 365.2 %reduce-scatter.23.cloned.1.call-done = f32[64,2048]{1,0:T(8,128)} async-done(((f32[2048,2048]{1,0:T(8,128)}), f32[64,2048]{1,0:T(8,128)}) %reduce-scatter.23.cloned.1.call-update) | async-done | bytes 524304 | tf_op jit(solution)/shard_map/reduce_scatter | solution.py:316
  (364 shorter events, 204.7 us)
Async XLA Ops:
  7.2 81.9 %all-gather.15.cloned.1.call-start = ((), (), s32[]{:S(2)}) async-start(), calls=%async_computation.13 | async-start | bytes 8650752 | tf_op jit(solution)/shard_map/all_gather | solution.py:80
  7.9 160.1 %all-gather.19.cloned.1.call-start = ((), (), s32[]{:S(2)}) async-start(), calls=%async_computation.15 | async-start | bytes 8650752 | tf_op jit(solution)/shard_map/all_gather | solution.py:79
  8.7 238.3 %all-gather.17.cloned.1.call-start = ((), (), s32[]{:S(2)}) async-start(), calls=%async_computation.14 | async-start | bytes 8650752 | tf_op jit(solution)/shard_map/all_gather | solution.py:78
  9.4 293.2 %all-gather.31.cloned.1.call-start = ((), (), s32[]{:S(2)}) async-start(), calls=%async_computation.29 | async-start | bytes 4718592 | tf_op jit(solution)/shard_map/all_gather | solution.py:108
  52.7 212.7 %copy-start.8 = (f32[2048]{0:T(1024)}, f32[2048]{0:T(1024)S(1)}, u32[]{:S(2)}) copy-start(f32[2048]{0:T(1024)S(1)} %convert_element_type.244) | copy-start | bytes 24580
  54.0 211.4 %copy-start.15 = (f32[128]{0:T(128)}, f32[128]{0:T(128)S(1)}, u32[]{:S(2)}) copy-start(f32[128]{0:T(128)S(1)} %add_rsqrt_fusion.1) | copy-start | bytes 1540
  54.0 40.9 %copy-start.18 = (s32[1,8]{1,0:T(1,128)S(1)}, s32[1,8]{1,0:T(1,128)}, u32[]{:S(2)}) copy-start(s32[1,8]{1,0:T(1,128)} %param.17) | copy-start | bytes 100
  94.8 230.2 %all-gather.21.cloned.1.call-start = ((), (), s32[]{:S(2)}) async-start(), calls=%async_computation.16 | async-start | bytes 4718592 | tf_op jit(solution)/shard_map/all_gather | solution.py:107
  97.8 170.1 %copy-start.13 = (f32[128,32]{0,1:T(8,128)}, f32[128,32]{0,1:T(8,128)S(1)}, u32[]{:S(2)}) copy-start(f32[128,32]{0,1:T(8,128)S(1)} %get-tuple-element.333) | copy-start | bytes 49156
  247.0 12.4 copy-start
  259.4 6.0 copy-start.2
  267.9 2.5 copy-start.10
  269.8 134.9 %all-gather.23.cloned.1.call-start = ((), (), s32[]{:S(2)}) async-start(), calls=%async_computation.17 | async-start | bytes 8650752 | tf_op jit(solution)/shard_map/all_gather | solution.py:81
  272.7 27.7 %all-to-all-start.1 = ((bf16[4,64,2048]{2,1,0:T(8,128)(2,1)}), bf16[4,64,2048]{2,1,0:T(8,128)(2,1)S(1)}, u32[]{:S(2)}, u32[]{:S(2)}) async-start(bf16[4,64,2048]{2,1,0:T(8,128)(2,1)} %reshape.657), calls=%async_computation.1 | async-start | bytes 2097152 | tf_op jit(solution)/shard_map/all_to_all | solution.py:161
  277.2 183.6 %all-gather.27.cloned.1.call-start = ((), (), s32[]{:S(2)}) async-start(), calls=%async_computation.19 | async-start | bytes 9437184 | tf_op jit(solution)/shard_map/all_gather | solution.py:165
  300.3 1.0 copy-start.5
  301.3 206.1 %all-gather.33.cloned.1.call-start = ((), (), s32[]{:S(2)}) async-start(), calls=%async_computation.30 | async-start | bytes 2621440 | tf_op jit(solution)/shard_map/all_gather | solution.py:169
  367.6 37.2 %copy-start.6 = (bf16[1,128,2048]{1,2,0:T(8,128)(2,1)}, bf16[1,128,2048]{1,2,0:T(8,128)(2,1)S(1)}, u32[]{:S(2)}) copy-start(bf16[1,128,2048]{1,2,0:T(8,128)(2,1)S(1)} %get-tuple-element.629) | copy-start | bytes 1572868
  404.7 5.9 copy-start.11
  410.6 153.3 %all-gather.25.cloned.1.call-start = ((), (), s32[]{:S(2)}) async-start(), calls=%async_computation.18 | async-start | bytes 9437184 | tf_op jit(solution)/shard_map/all_gather | solution.py:164
  444.0 165.9 %all-gather.35.cloned.1.call-start = ((), (), s32[]{:S(2)}) async-start(), calls=%async_computation.31 | async-start | bytes 2621440 | tf_op jit(solution)/shard_map/all_gather | solution.py:170
  444.6 221.7 %all-gather.29.cloned.1.call-start = ((), (), s32[]{:S(2)}) async-start(), calls=%async_computation.20 | async-start | bytes 9437184 | tf_op jit(solution)/shard_map/all_gather | solution.py:166
  445.4 295.6 %reduce-scatter.17.cloned.1.call-start = ((), (), s32[]{:S(2)}) async-start(), calls=%async_computation.22 | async-start | bytes 2621440 | tf_op jit(solution)/shard_map/reduce_scatter | solution.py:191
  679.9 8.5 copy-start.22
  679.9 8.5 copy-start.21
  697.6 89.5 %reduce-scatter.15.cloned.1.call-start = ((), (), s32[]{:S(2)}) async-start(), calls=%async_computation.21 | async-start | bytes 2621440 | tf_op jit(solution)/shard_map/reduce_scatter | solution.py:177
  697.6 89.5 %copy-start.7 = (bf16[1,128,2048]{2,1,0:T(8,128)(2,1)S(1)}, bf16[1,128,2048]{2,1,0:T(8,128)(2,1)}, u32[]{:S(2)}) copy-start(bf16[1,128,2048]{2,1,0:T(8,128)(2,1)} %param.27) | copy-start | bytes 1572868
  707.5 287.6 %reduce-scatter.31.cloned.1.call-start = ((), (), s32[]{:S(2)}) async-start(), calls=%async_computation.32 | async-start | bytes 4718592
  789.5 7.5 copy-start.3
  927.0 106.4 %reduce-scatter.33.cloned.1.call-start = ((), (), s32[]{:S(2)}) async-start(), calls=%async_computation.33 | async-start | bytes 4718592
  956.6 1.6 copy-start.19
  956.6 196.1 %reduce-scatter.27.cloned.1.call-start = ((), (), s32[]{:S(2)}) async-start(), calls=%async_computation.27 | async-start | bytes 18874368 | tf_op jit(solution)/shard_map/reduce_scatter | solution.py:197
  973.1 1.6 copy-start.20
  973.1 257.8 %reduce-scatter.29.cloned.1.call-start = ((), (), s32[]{:S(2)}) async-start(), calls=%async_computation.28 | async-start | bytes 9437184 | tf_op jit(solution)/shard_map/reduce_scatter | solution.py:213
  983.1 1.2 copy-start.4
  983.1 610.6 %reduce-scatter.25.cloned.1.call-start = ((), (), s32[]{:S(2)}) async-start(), calls=%async_computation.26 | async-start | bytes 17301504 | tf_op jit(solution)/shard_map/reduce_scatter | solution.py:319
  993.9 1.1 copy-start.12
  993.9 6.8 copy-start.14
  993.9 6.8 copy-start.17
  994.0 964.9 %reduce-scatter.19.cloned.1.call-start = ((), (), s32[]{:S(2)}) async-start(), calls=%async_computation.23 | async-start | bytes 17301504 | tf_op jit(solution)/shard_map/reduce_scatter | solution.py:310
  997.8 3.4 copy-start.1
  997.8 3.4 copy-start.9
  997.8 3.4 copy-start.16
  1009.9 1314.0 %reduce-scatter.21.cloned.1.call-start = ((), (), s32[]{:S(2)}) async-start(), calls=%async_computation.24 | async-start | bytes 17301504 | tf_op jit(solution)/shard_map/reduce_scatter | solution.py:313
  1018.2 1670.9 %reduce-scatter.23.cloned.1.call-start = ((), (), s32[]{:S(2)}) async-start(), calls=%async_computation.25 | async-start | bytes 17301504 | tf_op jit(solution)/shard_map/reduce_scatter | solution.py:316
  1156.5 77.1 %all-to-all-start.2 = ((bf16[4,64,2,8,256]{4,3,1,2,0:T(8,128)(2,1)}), bf16[4,64,2,8,256]{4,3,1,2,0:T(8,128)(2,1)}, u32[]{:S(2)}, u32[]{:S(2)}) async-start(bf16[4,64,2,8,256]{4,3,1,2,0:T(8,128)(2,1)} %copy.60), calls=%async_computation.9 | async-start | bytes 4194304 | tf_op jit(solution)/shard_map/all_to_all | solution.py:206
  1161.8 14.8 slice-start
  1169.2 7.4 slice-start.1
Sparse Core Ops, SparseCore 0:
  10.9 78.1 all-gather.14
  92.0 75.9 all-gather.18
  171.0 75.9 all-gather.16
  249.3 35.8 all-gather.30
  287.5 37.4 all-gather.20
  327.7 76.9 all-gather.22
  407.2 53.5 all-gather.26
  462.9 44.5 all-gather.32
  509.4 54.4 all-gather.24
  565.3 44.5 all-gather.34
  611.8 54.4 all-gather.28
  697.7 43.1 reduce-scatter.16
  743.9 43.1 reduce-scatter.14
  927.2 51.2 reduce-scatter.30
  982.0 51.3 reduce-scatter.32
  1036.8 115.8 reduce-scatter.26
  1156.1 72.6 reduce-scatter.28
  1231.6 362.0 reduce-scatter.24
  1596.7 362.1 reduce-scatter.18
  1961.7 362.1 reduce-scatter.20
  2326.9 362.1 reduce-scatter.22
where the time goes:
time: 2710 us; the launch traced here: 2700 us
  waiting for transfers between devices  2090 us (77%)
  local copies, waits for them, and re-layouts  206 us (8%)
  matrix products  198 us (7%)
  blocking collectives  119 us (4%)
  other arithmetic  32 us (1%)
    reduce_scatter x1, waiting for transfers between devices, on_device(): lax.psum_scatter(weight_term(normed, grad_value_raw), ('ctx', 'fsdp'), sc...  365 us
    reduce_scatter x1, waiting for transfers between devices, on_device(): lax.psum_scatter(weight_term(normed, grad_query_raw), ('ctx', 'fsdp'), sc...  365 us
    reduce_scatter x1, waiting for transfers between devices, on_device(): lax.psum_scatter(weight_term(normed, grad_key_raw), ('ctx', 'fsdp'), scat...  365 us
    reduce_scatter x1, waiting for transfers between devices, on_device(): lax.psum_scatter(weight_term(attended, grad_branch), ('ctx', 'fsdp'), sca...  343 us
    reduce_scatter x1, waiting for transfers between devices, on_device(): lax.psum_scatter(jnp.einsum('nc,nkf->ckf', columns, paired, preferred_ele...  103 us
    unnamed x2, blocking collectives  90.3 us
    unnamed x66, local copies, waits for them, and re-layouts  86.5 us
    all_gather x1, waiting for transfers between devices, on_device(): lax.all_gather(key_weight, ('ctx', 'fsdp'), axis=0, tiled=True)  70.2 us
  transfers between devices with their start and end apart: 23, of which 19 were waited for; matrix products, arithmetic and copies ran while one was open for 10% of the time, Pallas kernels for 0%

commit v1 on v0

v1 whole, which is shorter than its diff:
```python
import functools

import jax
import jax.numpy as jnp
from jax import lax
from jax.experimental import pallas as pl
from jax.experimental.pallas import tpu as pltpu
from jax.sharding import Mesh, PartitionSpec as P

HEAD_DIM = 64
THETA = 130000.0
EPS = 1e-05
SCALE = HEAD_DIM**-0.5
NEG = -1e30
BF = jnp.bfloat16
F32 = jnp.float32
CTX = ("plane", "core")
TOK = ("core", "fsdp")
VMEM_LIMIT = 56 * 1024 * 1024


def mm(left, right):
    return jnp.dot(left, right, preferred_element_type=F32)


def mm_t(left, right):
    return lax.dot_general(left, right, (((1,), (1,)), ((), ())), preferred_element_type=F32)


def t_mm(left, right):
    return lax.dot_general(left, right, (((0,), (0,)), ((), ())), preferred_element_type=F32)


def rope_tables(length, cols):
    half = HEAD_DIM // 2
    freq = THETA ** (-2.0 * jnp.arange(half, dtype=F32) / HEAD_DIM)
    angle = jnp.arange(length, dtype=jnp.int32).astype(F32)[:, None] * freq
    cosine, sine = jnp.cos(angle), jnp.sin(angle)
    heads = cols // HEAD_DIM
    return (
        jnp.tile(jnp.concatenate([cosine, cosine], axis=1), (1, heads)),
        jnp.tile(jnp.concatenate([-sine, sine], axis=1), (1, heads)),
    )


def swap_halves(values):
    cols = values.shape[1]
    half = HEAD_DIM // 2
    lane = lax.broadcasted_iota(jnp.int32, values.shape, 1)
    up = pltpu.roll(values, half, 1)
    down = pltpu.roll(values, cols - half, 1)
    return jnp.where(lane % HEAD_DIM < half, down, up)


def slot_block(pair_ref, slot, n_ctx):
    low = pair_ref[0, slot // 2]
    return low if slot % 2 == 0 else 2 * n_ctx - 1 - low


def head_mask(shape, head):
    lane = lax.broadcasted_iota(jnp.int32, shape, 1)
    return lane // HEAD_DIM == head


def forward_kernel(n_ctx, qblk, pair_ref, qkv_ref, cos_ref, sin_ref, q_ref, k_ref, v_ref, o_ref, acc_ref):
    length, cols = q_ref.shape
    blk = length // (2 * n_ctx)
    heads = cols // HEAD_DIM
    for slot in range(2 * n_ctx):
        at = pl.multiple_of(slot_block(pair_ref, slot, n_ctx) * blk, blk)
        rows = pl.ds(slot * blk, blk)
        to = pl.ds(at, blk)
        cosine, sine = cos_ref[to, :], sin_ref[to, :]
        query = qkv_ref[rows, :cols]
        key = qkv_ref[rows, cols : 2 * cols]
        q_ref[to, :] = (query * cosine + swap_halves(query) * sine).astype(BF)
        k_ref[to, :] = (key * cosine + swap_halves(key) * sine).astype(BF)
        v_ref[to, :] = qkv_ref[rows, 2 * cols :].astype(BF)
    acc_ref[...] = jnp.zeros_like(acc_ref)

    def one_head(head, carry):
        for i in range(length // qblk):
            have = (i + 1) * qblk
            rows = pl.ds(i * qblk, qblk)
            mask = head_mask((qblk, cols), head)
            query = jnp.where(mask, q_ref[rows, :], jnp.zeros((), BF))
            scores = mm_t(query, k_ref[:have, :]) * SCALE
            row = lax.broadcasted_iota(jnp.int32, scores.shape, 0) + i * qblk
            col = lax.broadcasted_iota(jnp.int32, scores.shape, 1)
            scores = jnp.where(col <= row, scores, NEG)
            peak = jnp.max(scores, axis=1, keepdims=True)
            weights = jnp.exp(scores - peak)
            total = jnp.sum(weights, axis=1, keepdims=True)
            probs = (weights * (1.0 / total)).astype(BF)
            out = mm(probs, v_ref[:have, :])
            acc_ref[rows, :] = jnp.where(mask, out, acc_ref[rows, :])
        return carry

    lax.fori_loop(0, heads, one_head, 0)
    for slot in range(2 * n_ctx):
        at = pl.multiple_of(slot_block(pair_ref, slot, n_ctx) * blk, blk)
        o_ref[pl.ds(slot * blk, blk), :] = acc_ref[pl.ds(at, blk), :].astype(BF)


def attention_forward(pair, qkv, cosine, sine, n_ctx):
    length, cols = cosine.shape
    vm = pl.BlockSpec(memory_space=pltpu.VMEM)
    return pl.pallas_call(
        functools.partial(forward_kernel, n_ctx, 256),
        out_shape=[jax.ShapeDtypeStruct((length, cols), BF)] * 4,
        in_specs=[pl.BlockSpec(memory_space=pltpu.SMEM), vm, vm, vm],
        out_specs=[vm] * 4,
        scratch_shapes=[pltpu.VMEM((length, cols), F32)],
        compiler_params=pltpu.CompilerParams(vmem_limit_bytes=VMEM_LIMIT),
        name="attention_forward",
    )(pair, qkv, cosine, sine)


def backward_kernel(
    n_ctx, qblk, pair_ref, q_ref, k_ref, v_ref, do_ref, r_ref, cos_ref, sin_ref,
    g_ref, gr_ref, go_ref, dq_ref, dk_ref, dv_ref,
):
    length, cols = q_ref.shape
    blk = length // (2 * n_ctx)
    heads = cols // HEAD_DIM
    for slot in range(2 * n_ctx):
        at = pl.multiple_of(slot_block(pair_ref, slot, n_ctx) * blk, blk)
        go_ref[pl.ds(at, blk), :] = do_ref[pl.ds(slot * blk, blk), :]
    dq_ref[...] = jnp.zeros_like(dq_ref)
    dk_ref[...] = jnp.zeros_like(dk_ref)
    dv_ref[...] = jnp.zeros_like(dv_ref)

    def one_head(head, carry):
        for i in range(length // qblk):
            have = (i + 1) * qblk
            rows = pl.ds(i * qblk, qblk)
            mask = head_mask((qblk, cols), head)
            query = jnp.where(mask, q_ref[rows, :], jnp.zeros((), BF))
            grad = jnp.where(mask, go_ref[rows, :], jnp.zeros((), BF))
            scores = mm_t(k_ref[:have, :], query) * SCALE
            key_at = lax.broadcasted_iota(jnp.int32, scores.shape, 0)
            query_at = lax.broadcasted_iota(jnp.int32, scores.shape, 1) + i * qblk
            scores = jnp.where(key_at <= query_at, scores, NEG)
            peak = jnp.max(scores, axis=0, keepdims=True)
            weights = jnp.exp(scores - peak)
            total = jnp.sum(weights, axis=0, keepdims=True)
            probs = weights * (1.0 / total)
            grad_probs = mm_t(v_ref[:have, :], grad)
            centre = jnp.sum(probs * grad_probs, axis=0, keepdims=True)
            grad_scores = (probs * (grad_probs - centre)).astype(BF)
            dk_ref[:have, :] += mm(grad_scores, query)
            dv_ref[:have, :] += mm(probs.astype(BF), grad)
            out = t_mm(grad_scores, k_ref[:have, :])
            dq_ref[rows, :] = jnp.where(mask, out, dq_ref[rows, :])
        return carry

    lax.fori_loop(0, heads, one_head, 0)
    for slot in range(2 * n_ctx):
        at = pl.multiple_of(slot_block(pair_ref, slot, n_ctx) * blk, blk)
        rows = pl.ds(slot * blk, blk)
        to = pl.ds(at, blk)
        cosine, sine = cos_ref[to, :], sin_ref[to, :]
        scale = r_ref[rows, :]
        query = (dq_ref[to, :] * SCALE).astype(BF).astype(F32)
        key = (dk_ref[to, :] * SCALE).astype(BF).astype(F32)
        value = dv_ref[to, :].astype(BF).astype(F32)
        query = query * cosine - swap_halves(query) * sine
        key = key * cosine - swap_halves(key) * sine
        for at_col, part in enumerate((query, key, value)):
            span = pl.ds(at_col * cols, cols)
            g_ref[rows, span] = part.astype(BF)
            gr_ref[rows, span] = (part * scale).astype(BF)


def attention_backward(pair, q, k, v, grad, scale, cosine, sine, n_ctx):
    length, cols = cosine.shape
    vm = pl.BlockSpec(memory_space=pltpu.VMEM)
    return pl.pallas_call(
        functools.partial(backward_kernel, n_ctx, 256),
        out_shape=[jax.ShapeDtypeStruct((length, 3 * cols), BF)] * 2,
        in_specs=[pl.BlockSpec(memory_space=pltpu.SMEM)] + [vm] * 7,
        out_specs=[vm] * 2,
        scratch_shapes=[pltpu.VMEM((length, cols), BF)] + [pltpu.VMEM((length, cols), F32)] * 3,
        compiler_params=pltpu.CompilerParams(vmem_limit_bytes=VMEM_LIMIT),
        name="attention_backward",
    )(pair, q, k, v, grad, scale, cosine, sine)


def gather(value, axes, axis=0):
    return lax.all_gather(value, axes, axis=axis, tiled=True)


def scatter(value, axes):
    return lax.psum_scatter(value, axes, scatter_dimension=0, tiled=True)


def exchange(value, axes):
    return lax.all_to_all(value, axes, split_axis=0, concat_axis=0, tiled=True)


def on_device(
    layer_input, pairing, query_weight, key_weight, value_weight, merge_weight,
    gate_weight, up_weight, down_weight, norm_first, norm_second, output_cotangent,
):
    n_plane = lax.axis_size("plane")
    n_core = lax.axis_size("core")
    n_fsdp = lax.axis_size("fsdp")
    n_ctx = n_plane * n_core
    n_tok = n_core * n_fsdp
    _, rows, width = layer_input.shape
    length = rows * n_ctx
    cols = width // n_ctx
    dev_rows = gate_weight.shape[0]
    hidden_total = gate_weight.shape[1]
    piece = hidden_total // (n_ctx * n_fsdp)
    hid = piece * n_plane
    tokens = layer_input.reshape(rows, width)
    cotangent = output_cotangent.reshape(rows, width)
    gain_first = norm_first.astype(F32)[:, None]
    gain_second = norm_second.astype(F32)[:, None]

    own = jnp.stack(
        [(w.astype(F32) * gain_first).astype(BF).reshape(dev_rows, n_ctx, cols) for w in (query_weight, key_weight, value_weight)],
        axis=2,
    )
    own = own.transpose(1, 0, 2, 3).reshape(n_ctx, dev_rows, 3 * cols)
    own = exchange(own, CTX)
    qkv_weight = gather(own[:, None], "fsdp", axis=1).reshape(width, 3 * cols)
    merge_rows = gather(merge_weight, "fsdp")
    x_all = gather(tokens, CTX)

    both = jnp.stack(
        [(w.astype(F32) * gain_second).astype(BF).reshape(dev_rows, n_plane, n_tok, piece) for w in (gate_weight, up_weight)],
        axis=1,
    )
    both = both.transpose(3, 0, 1, 2, 4).reshape(n_tok, dev_rows, 2 * hid)
    both = exchange(both, TOK).reshape(n_tok * dev_rows, 2 * hid)
    gate_up = gather(both, "plane")
    down_rows = gather(down_weight, "plane")
    cot_all = gather(cotangent, TOK)

    x_f = x_all.astype(F32)
    scale_all = lax.rsqrt(jnp.mean(x_f * x_f, axis=-1, keepdims=True) + EPS)
    qkv = mm(x_all, qkv_weight) * scale_all
    cosine, sine = rope_tables(length, cols)
    q, k, v, attended = attention_forward(pairing, qkv, cosine, sine, n_ctx)
    own_f = tokens.astype(F32)
    mixed = own_f + scatter(mm(attended, merge_rows).astype(BF), CTX).astype(F32)

    scale_second = lax.rsqrt(jnp.mean(mixed * mixed, axis=-1, keepdims=True) + EPS)
    unit_second = mixed * scale_second
    normed_all = gather(unit_second.astype(BF), TOK)
    gu = mm(normed_all, gate_up)
    gate, up = gu[:, :hid], gu[:, hid:]
    sig = jax.nn.sigmoid(gate)
    active = gate * sig
    hidden = (active * up).astype(BF)
    branch = scatter(mm(hidden, down_rows).astype(BF), TOK).astype(F32)
    layer_output = (mixed + branch).astype(BF)
    grad_hidden = mm_t(cot_all, down_rows)
    grad_gate = (grad_hidden * up * sig * (1.0 + gate * (1.0 - sig))).astype(BF)
    grad_up = (grad_hidden * active).astype(BF)
    grad_gu = jnp.concatenate([grad_gate, grad_up], axis=1)
    e_two = scatter(mm_t(grad_gu, gate_up).astype(BF), TOK).astype(F32)
    grad_mixed = cotangent.astype(F32) + scale_second * (
        e_two - unit_second * jnp.mean(e_two * unit_second, axis=-1, keepdims=True)
    )
    branch_all = gather(grad_mixed.astype(BF), CTX)

    gu_sum = scatter(t_mm(normed_all, grad_gu).astype(BF), "plane")
    gu_sum = exchange(gu_sum.reshape(n_tok, dev_rows, 2 * hid), TOK)
    gu_sum = gu_sum.reshape(n_tok, dev_rows, 2, n_plane, piece).transpose(1, 2, 3, 0, 4)
    gu_sum = gu_sum.reshape(dev_rows, 2, hidden_total).astype(F32)
    gate_grad = gu_sum[:, 0] * gain_second
    up_grad = gu_sum[:, 1] * gain_second
    second_grad = jnp.sum(
        gu_sum[:, 0] * gate_weight.astype(F32) + gu_sum[:, 1] * up_weight.astype(F32), axis=1
    )
    down_grad = scatter(t_mm(hidden, cot_all).astype(BF), "plane").astype(F32)

    merge_grad = scatter(t_mm(attended, branch_all).astype(BF), "fsdp").astype(F32)
    grad_attended = mm_t(branch_all, merge_rows).astype(BF)
    grad_qkv, grad_scaled = attention_backward(
        pairing, q, k, v, grad_attended, scale_all, cosine, sine, n_ctx
    )
    e_one = scatter(mm_t(grad_qkv, qkv_weight).astype(BF), CTX).astype(F32)
    scale_first = lax.rsqrt(jnp.mean(own_f * own_f, axis=-1, keepdims=True) + EPS)
    unit_first = own_f * scale_first
    input_grad = (
        grad_mixed
        + scale_first * (e_one - unit_first * jnp.mean(e_one * unit_first, axis=-1, keepdims=True))
    ).astype(BF)
    sums = t_mm(x_all, grad_scaled).astype(BF).reshape(n_ctx, n_fsdp, dev_rows, 3 * cols)
    sums = scatter(sums.transpose(1, 0, 2, 3).reshape(width, 3 * cols), "fsdp")
    sums = exchange(sums.reshape(n_ctx, dev_rows, 3 * cols), CTX)
    sums = sums.reshape(n_ctx, dev_rows, 3, cols).transpose(1, 2, 0, 3)
    sums = sums.reshape(dev_rows, 3, width).astype(F32)
    first_grad = jnp.sum(
        sums[:, 0] * query_weight.astype(F32)
        + sums[:, 1] * key_weight.astype(F32)
        + sums[:, 2] * value_weight.astype(F32),
        axis=1,
    )
    return (
        layer_output.reshape(1, rows, width),
        input_grad.reshape(1, rows, width),
        sums[:, 0] * gain_first,
        sums[:, 1] * gain_first,
        sums[:, 2] * gain_first,
        merge_grad,
        gate_grad,
        up_grad,
        down_grad,
        first_grad,
        second_grad,
    )


def solution(mesh):
    n_ctx, n_fsdp = mesh.shape["ctx"], mesh.shape["fsdp"]
    inner = Mesh(mesh.devices.reshape(n_ctx // 2, 2, n_fsdp), ("plane", "core", "fsdp"))
    token = P("fsdp", CTX, None)
    weight = P(("plane", "core", "fsdp"), None)
    gain = P(("plane", "core", "fsdp"))
    return jax.shard_map(
        on_device,
        mesh=inner,
        in_specs=(token, P("fsdp", None)) + (weight,) * 7 + (gain, gain, token),
        out_specs=(token, token) + (weight,) * 7 + (gain, gain),
        check_vma=False,
    )
```

time: 2710 us -> 995 us (0.37)
  waiting for transfers between devices: 2090 us -> 672 us
  local copies, waits for them, and re-layouts: 206 us -> 43.4 us
  matrix products: 198 us -> 107 us
  blocking collectives: 119 us -> 72.6 us
  Pallas kernels: 0 us -> 31.6 us
    reduce_scatter x8, waiting for transfers between devices: 1620 us -> 344 us  [scatter(): return lax.psum_scatter(value, axes, scatter_dimension=0, tiled=True)]
    all_gather x11 -> x8, waiting for transfers between devices: 425 us -> 325 us  [gather(): return lax.all_gather(value, axes, axis=axis, tiled=True)]
    dot_general x76 -> x12, matrix products: 198 us -> 107 us  [the longest x4 37 us: mm_t(): lax.dot_general(left, right, (((1,), (1,)), ((), ())), preferred_element_...]
    unnamed x2 -> x0, blocking collectives: 90.3 us -> none
    unnamed x66 -> x47, local copies, waits for them, and re-layouts: 86.5 us -> 4.32 us
    dynamic_slice x72 -> x0, local copies, waits for them, and re-layouts: 51.6 us -> none  [the longest x56 42.2 us: slice_heads(): lax.dynamic_slice_in_dim(values, index * group_width, group_width, 2)]
    all_to_all x1 -> x2, blocking collectives: 29 us -> 72.6 us  [exchange(): return lax.all_to_all(value, axes, split_axis=0, concat_axis=0, tiled=True)]
    pallas_call x0 -> x2, Pallas kernels: none -> 31.6 us  [the longest x1 18.3 us: attention_backward(): pl.pallas_call(functools.partial(backward_kernel, n_ctx, 256), out_shape=...]
  transfers between devices with their start and end apart: 23 -> 18, of which waited for: 19 -> 15; matrix products, arithmetic and copies ran while one was open for 10% -> 14% of each run, Pallas kernels for 0% -> 3%
where the time goes in v1:
time: 995 us; the launch traced here: 988 us
  waiting for transfers between devices  672 us (68%)
  matrix products  107 us (11%)
  blocking collectives  72.6 us (7%)
  local copies, waits for them, and re-layouts  43.4 us (4%)
  other arithmetic  32.9 us (3%)
  Pallas kernels  31.6 us (3%)
  between operations  16.2 us (2%)
  starting transfers between devices  11.5 us (1%)
    reduce_scatter x8, waiting for transfers between devices, scatter(): return lax.psum_scatter(value, axes, scatter_dimension=0, tiled=True)  344 us
    all_gather x8, waiting for transfers between devices, gather(): return lax.all_gather(value, axes, axis=axis, tiled=True)  325 us
    all_to_all x2, blocking collectives, exchange(): return lax.all_to_all(value, axes, split_axis=0, concat_axis=0, tiled=True)  72.6 us
    dot_general x4, matrix products, mm_t(): lax.dot_general(left, right, (((1,), (1,)), ((), ())), preferred_element_...  37 us
    dot_general x4, matrix products, mm(): return jnp.dot(left, right, preferred_element_type=F32)  36 us
    dot_general x4, matrix products, t_mm(): lax.dot_general(left, right, (((0,), (0,)), ((), ())), preferred_element_...  34.3 us
  transfers between devices with their start and end apart: 18, of which 15 were waited for; matrix products, arithmetic and copies ran while one was open for 14% of the time, Pallas kernels for 3%

profile of v1, /device:TPU:18, one launch (start us, length us, event | category | flops | bytes accessed | tf_op | source)
XLA Modules:
  0.0 987.8 jit_solution(9325462389702877621)
XLA Ops:
  12.2 1.8 maximum_bitcast_fusion.1
  15.0 20.5 %all_to_all.20 = bf16[8,64,768]{2,1,0:T(8,128)(2,1)} all-to-all(bf16[8,64,768]{2,1,0:T(8,128)(2,1)S(1)} %reshape.135), channel_id=1, replica_groups=mesh['plane'=4,'core'=2,'fsdp'=4] {'plane','core'}, dimensions={0} | all-to-all | bytes 1572864 | tf_op jit(solution)/shard_map/all_to_all | solution.py:198
  40.4 16.1 %all-gather.24.cloned.1.call-done = bf16[1,1024,2048]{2,1,0:T(8,128)(2,1)} async-done(((bf16[1,128,2048]{2,1,0:T(8,128)(2,1)}), bf16[1,1024,2048]{2,1,0:T(8,128)(2,1)}) %all-gather.24.cloned.1.call-update) | async-done | bytes 4194320 | tf_op jit(solution)/shard_map/all_gather | solution.py:190
  56.4 3.1 multiply_reduce_fusion
  59.5 60.7 %all-gather.22.cloned.1.call-done = bf16[8,256,768]{2,1,0:T(8,128)(2,1)} async-done(((bf16[8,64,768]{2,1,0:T(8,128)(2,1)}), bf16[8,256,768]{2,1,0:T(8,128)(2,1)}) %all-gather.22.cloned.1.call-update) | async-done | bytes 3145744 | tf_op jit(solution)/shard_map/all_gather | solution.py:190
  120.2 8.3 multiply_bitcast_fusion.qkv_ref
  128.5 13.3 %attention_forward.1 = (bf16[1024,256]{1,0:T(8,128)(2,1)}, bf16[1024,256]{1,0:T(8,128)(2,1)}, bf16[1024,256]{1,0:T(8,128)(2,1)}, bf16[1024,256]{1,0:T(8,128)(2,1)}) custom-call(s32[1,8]{1,0:T(1,128)} %pair_ref.3, f32[1024,768]{1,0:T(8,128)} %multiply_bitcast_fusion.qkv_ref, f32[1024,256]{1,0:T(8,128)} %copy.47.cos_ref, f32[1024,256]{1,0:T(8,128)} %copy.48.sin_ref), custom_call_target="tpu_custom_call" | custom-call | tf_op jit(solution)/shard_map/attention_forward/pallas_call | solution.py:108
  141.8 7.4 all-gather.12.cloned.1.call-done
  149.2 4.8 convolution_convert_fusion.2
  157.5 2.8 reshape.137
  160.3 52.1 %all_to_all.21 = bf16[8,64,2048]{2,1,0:T(8,128)(2,1)} all-to-all(bf16[8,64,2048]{2,1,0:T(8,128)(2,1)} %reshape.137), channel_id=1, replica_groups=mesh['plane'=4,'core'=2,'fsdp'=4] {'core','fsdp'}, dimensions={0} | all-to-all | bytes 4194304 | tf_op jit(solution)/shard_map/all_to_all | solution.py:198
  213.8 2.0 fusion.36
  217.2 82.7 %all-gather.16.cloned.1.call-done = bf16[2048,2048]{1,0:T(8,128)(2,1)} async-done(((bf16[512,2048]{1,0:T(8,128)(2,1)}), bf16[2048,2048]{1,0:T(8,128)(2,1)}) %all-gather.16.cloned.1.call-update) | async-done | bytes 8388624 | tf_op jit(solution)/shard_map/all_gather | solution.py:190
  299.9 47.7 %all-gather.14.cloned.1.call-done = bf16[1024,2048]{1,0:T(8,128)(2,1)} async-done(((bf16[128,2048]{1,0:T(8,128)(2,1)}), bf16[1024,2048]{1,0:T(8,128)(2,1)}) %all-gather.14.cloned.1.call-update) | async-done | bytes 4194320 | tf_op jit(solution)/shard_map/all_gather | solution.py:190
  347.7 14.5 %fusion.52 = f32[1024,2048]{1,0:T(8,128)} fusion(bf16[1024,2048]{1,0:T(8,128)(2,1)} %all-gather.14.cloned.1.call-done, bf16[2048,2048]{1,0:T(8,128)(2,1)} %all-gather.16.cloned.1.call-done), kind=kOutput, calls=%fused_computation.96 | convolution fusion | flops 8589934592 | bytes 20971520 | tf_op jit(solution)/shard_map/dot_general | solution.py:23
  362.2 40.0 %all-gather.18.cloned.1.call-done = bf16[1024,2048]{1,0:T(8,128)(2,1)} async-done(((bf16[256,2048]{1,0:T(8,128)(2,1)}), bf16[1024,2048]{1,0:T(8,128)(2,1)}) %all-gather.18.cloned.1.call-update) | async-done | bytes 4194320 | tf_op jit(solution)/shard_map/all_gather | solution.py:190
  402.1 47.3 %all-gather.26.cloned.1.call-done = bf16[1,1024,2048]{2,1,0:T(8,128)(2,1)} async-done(((bf16[1,128,2048]{2,1,0:T(8,128)(2,1)}), bf16[1,1024,2048]{2,1,0:T(8,128)(2,1)}) %all-gather.26.cloned.1.call-update) | async-done | bytes 4194320 | tf_op jit(solution)/shard_map/all_gather | solution.py:190
  449.4 13.1 %multiply_convert_fusion.1 = (bf16[1024,1024]{1,0:T(8,128)(2,1)S(1)}, bf16[1024,1024]{1,0:T(8,128)(2,1)S(1)}, bf16[1024,1024]{1,0:T(8,128)(2,1)}) fusion(f32[1024,2048]{1,0:T(8,128)} %fusion.52, bf16[1024,2048]{1,0:T(8,128)(2,1)} %all-gather.18.cloned.1.call-done, bf16[1,1024,2048]{2,1,0:T(8,128)(2,1)} %all-gather.26.cloned.1.call-done), kind=kOutput, calls=%fused_computation.13 | convolution fusion | flops 4310695936 | bytes 23068672 | tf_op jit(solution)/shard_map/dot_general | solution.py:27
  464.6 12.6 %convolution_convert_fusion.1 = bf16[1024,2048]{1,0:T(8,128)(2,1)} fusion(bf16[2048,2048]{1,0:T(8,128)(2,1)} %all-gather.16.cloned.1.call-done, bf16[1024,1024]{1,0:T(8,128)(2,1)S(1)} %get-tuple-element.26, bf16[1024,1024]{1,0:T(8,128)(2,1)S(1)} %get-tuple-element.25), kind=kOutput, calls=%fused_computation.17 | convolution fusion | flops 8600420352 | bytes 16777216 | tf_op jit(solution)/shard_map/dot_general | solution.py:27
  477.7 87.3 %reduce-scatter.13.cloned.1.call-done = bf16[128,2048]{1,0:T(8,128)(2,1)} async-done(((bf16[1024,2048]{1,0:T(8,128)(2,1)}), bf16[128,2048]{1,0:T(8,128)(2,1)}) %reduce-scatter.13.cloned.1.call-update) | async-done | bytes 524304 | tf_op jit(solution)/shard_map/reduce_scatter | solution.py:194
  566.4 2.3 fusion.51
  568.8 14.1 %convolution_convert_fusion = bf16[2048,2048]{1,0:T(8,128)(2,1)} fusion(bf16[1024,2048]{1,0:T(8,128)(2,1)} %all-gather.14.cloned.1.call-done, bf16[1024,1024]{1,0:T(8,128)(2,1)} %copy-done.20, bf16[1024,1024]{1,0:T(8,128)(2,1)} %copy-done.19), kind=kOutput, calls=%fused_computation.1 | convolution fusion | flops 8602517504 | bytes 16777216 | tf_op jit(solution)/shard_map/dot_general | solution.py:31
  582.9 9.5 fusion.9
  592.5 23.6 %all-gather.20.cloned.1.call-done = bf16[1024,2048]{1,0:T(8,128)(2,1)} async-done(((bf16[128,2048]{1,0:T(8,128)(2,1)}), bf16[1024,2048]{1,0:T(8,128)(2,1)}) %all-gather.20.cloned.1.call-update) | async-done | bytes 4194320 | tf_op jit(solution)/shard_map/all_gather | solution.py:190
  616.1 4.4 convolution_convert_fusion.5
  621.8 4.3 convolution_convert_fusion.6.do_ref
  626.1 18.3 %attention_backward.1 = (bf16[1024,768]{1,0:T(8,128)(2,1)}, bf16[1024,768]{1,0:T(8,128)(2,1)}) custom-call(s32[1,8]{1,0:T(1,128)} %pair_ref.3, bf16[1024,256]{1,0:T(8,128)(2,1)} %get-tuple-element.18.q_ref, bf16[1024,256]{1,0:T(8,128)(2,1)} %get-tuple-element.19.k_ref, bf16[1024,256]{1,0:T(8,128)(2,1)} %get-tuple-element.20.v_ref, ...), custom_call_target="tpu_custom_call" | custom-call | tf_op jit(solution)/shard_map/attention_backward/pallas_call | solution.py:178
  644.4 6.3 fusion.15
  650.7 4.7 copy.56
  655.4 4.0 copy.57
  659.5 7.0 convolution_convert_fusion.3
  668.1 8.4 convolution_convert_fusion.4
  676.6 3.8 reduce-scatter.21.cloned.1.call-done
  680.4 5.4 all-to-all-start.3
  685.7 50.0 %reduce-scatter.23.cloned.1.call-done = bf16[256,2048]{1,0:T(8,128)(2,1)} async-done(((bf16[1024,2048]{1,0:T(8,128)(2,1)}), bf16[256,2048]{1,0:T(8,128)(2,1)}) %reduce-scatter.23.cloned.1.call-update) | async-done | bytes 1048592 | tf_op jit(solution)/shard_map/reduce_scatter | solution.py:194
  735.8 2.8 convert_element_type.202
  738.6 25.3 %reduce-scatter.19.cloned.1.call-done = bf16[64,2048]{1,0:T(8,128)(2,1)} async-done(((bf16[256,2048]{1,0:T(8,128)(2,1)}), bf16[64,2048]{1,0:T(8,128)(2,1)}) %reduce-scatter.19.cloned.1.call-update) | async-done | bytes 262160 | tf_op jit(solution)/shard_map/reduce_scatter | solution.py:194
  765.6 4.5 reshape.149
  770.1 6.6 copy.68
  776.8 5.1 reshape.147
  781.9 5.8 fusion.23
  787.7 38.6 %reduce-scatter.17.cloned.1.call-done = bf16[512,768]{1,0:T(8,128)(2,1)} async-done(((bf16[2048,768]{1,0:T(8,128)(2,1)}), bf16[512,768]{1,0:T(8,128)(2,1)}) %reduce-scatter.17.cloned.1.call-update) | async-done | bytes 786448 | tf_op jit(solution)/shard_map/reduce_scatter | solution.py:194
  826.3 4.2 all-to-all-start.2
  830.5 50.4 %reduce-scatter.15.cloned.1.call-done = bf16[128,2048]{1,0:T(8,128)(2,1)} async-done(((bf16[1024,2048]{1,0:T(8,128)(2,1)}), bf16[128,2048]{1,0:T(8,128)(2,1)}) %reduce-scatter.15.cloned.1.call-update) | async-done | bytes 524304 | tf_op jit(solution)/shard_map/reduce_scatter | solution.py:194
  882.2 88.6 %reduce-scatter.11.cloned.1.call-done = bf16[128,2048]{1,0:T(8,128)(2,1)} async-done(((bf16[1024,2048]{1,0:T(8,128)(2,1)}), bf16[128,2048]{1,0:T(8,128)(2,1)}) %reduce-scatter.11.cloned.1.call-update) | async-done | bytes 524304 | tf_op jit(solution)/shard_map/reduce_scatter | solution.py:194
  970.9 3.0 fusion.44
  974.7 2.1 copy.58
  978.4 1.9 fusion.47
  (113 shorter events, 28.7 us)
Async XLA Ops:
  8.0 48.4 %all-gather.24.cloned.1.call-start = ((), (), s32[]{:S(2)}) async-start(), calls=%async_computation.26 | async-start | bytes 4718592 | tf_op jit(solution)/shard_map/all_gather | solution.py:190
  8.7 111.5 %all-gather.22.cloned.1.call-start = ((), (), s32[]{:S(2)}) async-start(), calls=%async_computation.25 | async-start | bytes 3932160 | tf_op jit(solution)/shard_map/all_gather | solution.py:190
  9.4 1.4 copy-start.14
  35.5 113.8 %all-gather.12.cloned.1.call-start = ((), (), s32[]{:S(2)}) async-start(), calls=%async_computation.12 | async-start | bytes 1310720 | tf_op jit(solution)/shard_map/all_gather | solution.py:190
  36.2 176.2 %reduce-scatter.9.cloned.1.call-start = ((), (), s32[]{:S(2)}) async-start(), calls=%async_computation.13 | async-start | bytes 4718592 | tf_op jit(solution)/shard_map/reduce_scatter | solution.py:194
  149.2 5.0 copy-start.17
  149.2 5.0 copy-start.6
  149.2 5.0 copy-start.8
  154.0 145.9 %all-gather.16.cloned.1.call-start = ((), (), s32[]{:S(2)}) async-start(), calls=%async_computation.15 | async-start | bytes 10485760 | tf_op jit(solution)/shard_map/all_gather | solution.py:190
  160.3 52.2 %copy-start = (bf16[1,128,2048]{2,1,0:T(8,128)(2,1)S(1)}, bf16[1,128,2048]{2,1,0:T(8,128)(2,1)}, u32[]{:S(2)}) copy-start(bf16[1,128,2048]{2,1,0:T(8,128)(2,1)} %param.12) | copy-start | bytes 1572868
  212.4 135.3 %all-gather.14.cloned.1.call-start = ((), (), s32[]{:S(2)}) async-start(), calls=%async_computation.14 | async-start | bytes 4718592 | tf_op jit(solution)/shard_map/all_gather | solution.py:190
  215.8 186.3 %all-gather.18.cloned.1.call-start = ((), (), s32[]{:S(2)}) async-start(), calls=%async_computation.16 | async-start | bytes 5242880 | tf_op jit(solution)/shard_map/all_gather | solution.py:190
  216.4 233.0 %all-gather.26.cloned.1.call-start = ((), (), s32[]{:S(2)}) async-start(), calls=%async_computation.27 | async-start | bytes 4718592 | tf_op jit(solution)/shard_map/all_gather | solution.py:190
  217.1 347.8 %reduce-scatter.13.cloned.1.call-start = ((), (), s32[]{:S(2)}) async-start(), calls=%async_computation.18 | async-start | bytes 4718592 | tf_op jit(solution)/shard_map/reduce_scatter | solution.py:194
  462.6 1.3 copy-start.19
  462.6 2.0 copy-start.20
  477.2 87.8 %copy-start.1 = (bf16[128,2048]{1,0:T(8,128)(2,1)S(1)}, bf16[128,2048]{1,0:T(8,128)(2,1)}, u32[]{:S(2)}) copy-start(bf16[128,2048]{1,0:T(8,128)(2,1)} %reduce-scatter.9.cloned.1.call-done) | copy-start | bytes 1572868
  477.2 89.2 %copy-start.3 = (bf16[1,128,2048]{2,1,0:T(8,128)(2,1)S(1)}, bf16[1,128,2048]{2,1,0:T(8,128)(2,1)}, u32[]{:S(2)}) copy-start(bf16[1,128,2048]{2,1,0:T(8,128)(2,1)} %param.23) | copy-start | bytes 1572868
  477.2 138.8 %all-gather.20.cloned.1.call-start = ((), (), s32[]{:S(2)}) async-start(), calls=%async_computation.19 | async-start | bytes 4718592 | tf_op jit(solution)/shard_map/all_gather | solution.py:190
  568.7 111.6 %reduce-scatter.21.cloned.1.call-start = ((), (), s32[]{:S(2)}) async-start(), calls=%async_computation.23 | async-start | bytes 10485760 | tf_op jit(solution)/shard_map/reduce_scatter | solution.py:194
  582.9 152.9 %reduce-scatter.23.cloned.1.call-start = ((), (), s32[]{:S(2)}) async-start(), calls=%async_computation.24 | async-start | bytes 5242880 | tf_op jit(solution)/shard_map/reduce_scatter | solution.py:194
  592.4 23.7 %copy-start.9 = (bf16[1024,256]{1,0:T(8,128)(2,1)S(1)}, bf16[1024,256]{1,0:T(8,128)(2,1)}, u32[]{:S(2)}) copy-start(bf16[1024,256]{1,0:T(8,128)(2,1)} %get-tuple-element.17) | copy-start | bytes 1572868
  592.4 29.4 %copy-start.13 = (bf16[256,2048]{1,0:T(8,128)(2,1)S(1)}, bf16[256,2048]{1,0:T(8,128)(2,1)}, u32[]{:S(2)}) copy-start(bf16[256,2048]{1,0:T(8,128)(2,1)} %all-gather.12.cloned.1.call-done) | copy-start | bytes 3145732
  592.4 171.4 %reduce-scatter.19.cloned.1.call-start = ((), (), s32[]{:S(2)}) async-start(), calls=%async_computation.22 | async-start | bytes 1310720 | tf_op jit(solution)/shard_map/reduce_scatter | solution.py:194
  620.5 205.8 %reduce-scatter.17.cloned.1.call-start = ((), (), s32[]{:S(2)}) async-start(), calls=%async_computation.21 | async-start | bytes 3932160 | tf_op jit(solution)/shard_map/reduce_scatter | solution.py:194
  626.1 18.3 %copy-start.5 = (bf16[1,1024,2048]{2,1,0:T(8,128)(2,1)S(1)}, bf16[1,1024,2048]{2,1,0:T(8,128)(2,1)}, u32[]{:S(2)}) copy-start(bf16[1,1024,2048]{2,1,0:T(8,128)(2,1)} %all-gather.24.cloned.1.call-done) | copy-start | bytes 12582916
  655.4 4.1 copy-start.16
  659.4 221.4 %reduce-scatter.15.cloned.1.call-start = ((), (), s32[]{:S(2)}) async-start(), calls=%async_computation.20 | async-start | bytes 4718592 | tf_op jit(solution)/shard_map/reduce_scatter | solution.py:194
  666.5 1.6 copy-start.18
  666.5 304.3 %reduce-scatter.11.cloned.1.call-start = ((), (), s32[]{:S(2)}) async-start(), calls=%async_computation.17 | async-start | bytes 4718592 | tf_op jit(solution)/shard_map/reduce_scatter | solution.py:194
  680.4 85.3 %all-to-all-start.3 = ((bf16[8,64,2048]{2,1,0:T(8,128)(2,1)}), bf16[8,64,2048]{2,1,0:T(8,128)(2,1)S(1)}, u32[]{:S(2)}, u32[]{:S(2)}) async-start(bf16[8,64,2048]{2,1,0:T(8,128)(2,1)} %bitcast.156), calls=%async_computation.10 | async-start | bytes 4194304 | tf_op jit(solution)/shard_map/all_to_all | solution.py:198
  776.8 5.1 copy-start.7
  781.9 189.0 %copy-start.2 = (bf16[128,2048]{1,0:T(8,128)(2,1)S(1)}, bf16[128,2048]{1,0:T(8,128)(2,1)}, u32[]{:S(2)}) copy-start(bf16[128,2048]{1,0:T(8,128)(2,1)} %reduce-scatter.13.cloned.1.call-done) | copy-start | bytes 1572868
  781.9 189.0 %copy-start.4 = (bf16[1,128,2048]{2,1,0:T(8,128)(2,1)S(1)}, bf16[1,128,2048]{2,1,0:T(8,128)(2,1)}, u32[]{:S(2)}) copy-start(bf16[1,128,2048]{2,1,0:T(8,128)(2,1)} %param.23) | copy-start | bytes 1572868
  826.3 147.5 %all-to-all-start.2 = ((bf16[8,64,768]{2,1,0:T(8,128)(2,1)}), bf16[8,64,768]{2,1,0:T(8,128)(2,1)S(1)}, u32[]{:S(2)}, u32[]{:S(2)}) async-start(bf16[8,64,768]{2,1,0:T(8,128)(2,1)} %bitcast.163), calls=%async_computation.7 | async-start | bytes 1572864 | tf_op jit(solution)/shard_map/all_to_all | solution.py:198
  973.8 4.5 copy-start.10
  973.8 4.5 copy-start.11
  973.8 4.6 copy-start.15
  974.7 3.7 copy-start.12
Sparse Core Ops, SparseCore 0:
  10.7 45.6 all-gather.23
  58.0 62.1 all-gather.21
  121.8 27.4 all-gather.11
  154.1 51.2 reduce-scatter.8
  568.9 47.1 all-gather.19
Sparse Core Ops, SparseCore 1:
  212.5 87.4 all-gather.15
  302.1 45.6 all-gather.13
  349.6 52.5 all-gather.17
  403.8 45.6 all-gather.25
  477.3 87.6 reduce-scatter.12
  583.0 97.4 reduce-scatter.20
  683.2 52.5 reduce-scatter.22
  738.1 25.7 reduce-scatter.18
  766.0 60.2 reduce-scatter.16
  829.7 51.1 reduce-scatter.14
  883.1 87.7 reduce-scatter.10

commit v2 on v1

v2 whole, which is shorter than its diff:
```python
import functools

import jax
import jax.numpy as jnp
from jax import lax
from jax.experimental import pallas as pl
from jax.experimental.pallas import tpu as pltpu
from jax.sharding import Mesh, PartitionSpec as P

HEAD_DIM = 64
THETA = 130000.0
EPS = 1e-05
SCALE = HEAD_DIM**-0.5
NEG = -1e30
BF = jnp.bfloat16
F32 = jnp.float32
CTX = ("plane", "core")
TOK = ("core", "fsdp")
VMEM_LIMIT = 56 * 1024 * 1024


def mm(left, right):
    return jnp.dot(left, right, preferred_element_type=F32)


def mm_t(left, right):
    return lax.dot_general(left, right, (((1,), (1,)), ((), ())), preferred_element_type=F32)


def t_mm(left, right):
    return lax.dot_general(left, right, (((0,), (0,)), ((), ())), preferred_element_type=F32)


def rope_tables(length, cols):
    half = HEAD_DIM // 2
    freq = THETA ** (-2.0 * jnp.arange(half, dtype=F32) / HEAD_DIM)
    angle = jnp.arange(length, dtype=jnp.int32).astype(F32)[:, None] * freq
    cosine, sine = jnp.cos(angle), jnp.sin(angle)
    heads = cols // HEAD_DIM
    return (
        jnp.tile(jnp.concatenate([cosine, cosine], axis=1), (1, heads)),
        jnp.tile(jnp.concatenate([-sine, sine], axis=1), (1, heads)),
    )


def swap_halves(values):
    cols = values.shape[1]
    half = HEAD_DIM // 2
    lane = lax.broadcasted_iota(jnp.int32, values.shape, 1)
    up = pltpu.roll(values, half, 1)
    down = pltpu.roll(values, cols - half, 1)
    return jnp.where(lane % HEAD_DIM < half, down, up)


def relative(n_plane):
    bits = n_plane.bit_length() - 1
    steps = [[1 << ((s + c) % bits) for s in range(bits)] for c in range(2)]
    order = []
    for masks in steps:
        found = [0]
        for mask in masks:
            found += [m ^ mask for m in found]
        order.append(found)
    return steps, order


def slot_block(pair_ref, me_ref, slot, n_ctx):
    _, order = relative(n_ctx // 2)
    at, half = slot // 2, n_ctx // 2
    plane, core = me_ref[0], me_ref[1]
    if at < half:
        holder = jnp.bitwise_xor(plane, jnp.where(core == 0, order[0][at], order[1][at])) * 2 + core
    else:
        at -= half
        holder = jnp.bitwise_xor(plane, jnp.where(core == 0, order[1][at], order[0][at])) * 2 + 1 - core
    low = pair_ref[0, holder]
    return low if slot % 2 == 0 else 2 * n_ctx - 1 - low


def head_mask(shape, head):
    lane = lax.broadcasted_iota(jnp.int32, shape, 1)
    return lane // HEAD_DIM == head


def params():
    return pltpu.CompilerParams(vmem_limit_bytes=VMEM_LIMIT)


def cost(flops, moved):
    return pl.CostEstimate(flops=int(flops), bytes_accessed=int(moved), transcendentals=0)


def in_vmem(n):
    return [pl.BlockSpec(memory_space=pltpu.VMEM)] * n


def in_smem(n):
    return [pl.BlockSpec(memory_space=pltpu.SMEM)] * n


def forward_kernel(n_ctx, qblk, pair_ref, me_ref, *refs):
    x_refs = refs[:n_ctx]
    w_ref, cos_ref, sin_ref, q_ref, k_ref, v_ref, r_ref, o_ref, acc_ref = refs[n_ctx:]
    length, cols = q_ref.shape
    blk = length // (2 * n_ctx)
    heads = cols // HEAD_DIM
    for at, x_ref in enumerate(x_refs):
        x = x_ref[...]
        x_f = x.astype(F32)
        scale = lax.rsqrt(jnp.mean(x_f * x_f, axis=1, keepdims=True) + EPS)
        r_ref[pl.ds(at * 2 * blk, 2 * blk), :] = scale
        qkv = mm(x, w_ref[...]) * scale
        for second in range(2):
            to = pl.ds(pl.multiple_of(slot_block(pair_ref, me_ref, 2 * at + second, n_ctx) * blk, blk), blk)
            cosine, sine = cos_ref[to, :], sin_ref[to, :]
            query = qkv[second * blk : (second + 1) * blk, :cols]
            key = qkv[second * blk : (second + 1) * blk, cols : 2 * cols]
            q_ref[to, :] = (query * cosine + swap_halves(query) * sine).astype(BF)
            k_ref[to, :] = (key * cosine + swap_halves(key) * sine).astype(BF)
            v_ref[to, :] = qkv[second * blk : (second + 1) * blk, 2 * cols :].astype(BF)
    acc_ref[...] = jnp.zeros_like(acc_ref)

    def one_head(head, carry):
        for i in range(length // qblk):
            have = (i + 1) * qblk
            rows = pl.ds(i * qblk, qblk)
            mask = head_mask((qblk, cols), head)
            query = jnp.where(mask, q_ref[rows, :], jnp.zeros((), BF))
            scores = mm_t(query, k_ref[:have, :]) * SCALE
            row = lax.broadcasted_iota(jnp.int32, scores.shape, 0) + i * qblk
            col = lax.broadcasted_iota(jnp.int32, scores.shape, 1)
            scores = jnp.where(col <= row, scores, NEG)
            peak = jnp.max(scores, axis=1, keepdims=True)
            weights = jnp.exp(scores - peak)
            total = jnp.sum(weights, axis=1, keepdims=True)
            probs = (weights * (1.0 / total)).astype(BF)
            out = mm(probs, v_ref[:have, :])
            acc_ref[rows, :] = jnp.where(mask, out, acc_ref[rows, :])
        return carry

    lax.fori_loop(0, heads, one_head, 0)
    for slot in range(2 * n_ctx):
        at = pl.multiple_of(slot_block(pair_ref, me_ref, slot, n_ctx) * blk, blk)
        o_ref[pl.ds(slot * blk, blk), :] = acc_ref[pl.ds(at, blk), :].astype(BF)


def attention_forward(pair, me, pieces, weight, cosine, sine):
    length, cols = cosine.shape
    width = weight.shape[0]
    n_ctx = len(pieces)
    return pl.pallas_call(
        functools.partial(forward_kernel, n_ctx, 256),
        out_shape=[jax.ShapeDtypeStruct((length, cols), BF)] * 3
        + [jax.ShapeDtypeStruct((length, 1), F32), jax.ShapeDtypeStruct((length, cols), BF)],
        in_specs=in_smem(2) + in_vmem(n_ctx + 3),
        out_specs=in_vmem(5),
        scratch_shapes=[pltpu.VMEM((length, cols), F32)],
        compiler_params=params(),
        cost_estimate=cost(6 * length * width * cols + 16 * length * length * cols, 12 * width * length),
        name="attention_forward",
    )(pair, me, *pieces, weight, cosine, sine)


def backward_kernel(n_ctx, qblk, pair_ref, me_ref, *refs):
    b_refs = refs[:n_ctx]
    (
        m_ref, q_ref, k_ref, v_ref, r_ref, cos_ref, sin_ref,
        g_ref, gr_ref, go_ref, dq_ref, dk_ref, dv_ref,
    ) = refs[n_ctx:]
    length, cols = q_ref.shape
    blk = length // (2 * n_ctx)
    heads = cols // HEAD_DIM
    for at, b_ref in enumerate(b_refs):
        grad = mm_t(b_ref[...], m_ref[...]).astype(BF)
        for second in range(2):
            to = pl.ds(pl.multiple_of(slot_block(pair_ref, me_ref, 2 * at + second, n_ctx) * blk, blk), blk)
            go_ref[to, :] = grad[second * blk : (second + 1) * blk, :]
    dq_ref[...] = jnp.zeros_like(dq_ref)
    dk_ref[...] = jnp.zeros_like(dk_ref)
    dv_ref[...] = jnp.zeros_like(dv_ref)

    def one_head(head, carry):
        for i in range(length // qblk):
            have = (i + 1) * qblk
            rows = pl.ds(i * qblk, qblk)
            mask = head_mask((qblk, cols), head)
            query = jnp.where(mask, q_ref[rows, :], jnp.zeros((), BF))
            grad = jnp.where(mask, go_ref[rows, :], jnp.zeros((), BF))
            scores = mm_t(k_ref[:have, :], query) * SCALE
            key_at = lax.broadcasted_iota(jnp.int32, scores.shape, 0)
            query_at = lax.broadcasted_iota(jnp.int32, scores.shape, 1) + i * qblk
            scores = jnp.where(key_at <= query_at, scores, NEG)
            peak = jnp.max(scores, axis=0, keepdims=True)
            weights = jnp.exp(scores - peak)
            total = jnp.sum(weights, axis=0, keepdims=True)
            probs = weights * (1.0 / total)
            grad_probs = mm_t(v_ref[:have, :], grad)
            centre = jnp.sum(probs * grad_probs, axis=0, keepdims=True)
            grad_scores = (probs * (grad_probs - centre)).astype(BF)
            dk_ref[:have, :] += mm(grad_scores, query)
            dv_ref[:have, :] += mm(probs.astype(BF), grad)
            out = t_mm(grad_scores, k_ref[:have, :])
            dq_ref[rows, :] = jnp.where(mask, out, dq_ref[rows, :])
        return carry

    lax.fori_loop(0, heads, one_head, 0)
    for slot in range(2 * n_ctx):
        at = pl.multiple_of(slot_block(pair_ref, me_ref, slot, n_ctx) * blk, blk)
        rows = pl.ds(slot * blk, blk)
        to = pl.ds(at, blk)
        cosine, sine = cos_ref[to, :], sin_ref[to, :]
        scale = r_ref[rows, :]
        query = (dq_ref[to, :] * SCALE).astype(BF).astype(F32)
        key = (dk_ref[to, :] * SCALE).astype(BF).astype(F32)
        value = dv_ref[to, :].astype(BF).astype(F32)
        query = query * cosine - swap_halves(query) * sine
        key = key * cosine - swap_halves(key) * sine
        for at_col, part in enumerate((query, key, value)):
            span = pl.ds(at_col * cols, cols)
            g_ref[rows, span] = part.astype(BF)
            gr_ref[rows, span] = (part * scale).astype(BF)


def attention_backward(pair, me, pieces, merge_rows, q, k, v, scale, cosine, sine):
    length, cols = cosine.shape
    width = merge_rows.shape[1]
    n_ctx = len(pieces)
    return pl.pallas_call(
        functools.partial(backward_kernel, n_ctx, 256),
        out_shape=[jax.ShapeDtypeStruct((length, 3 * cols), BF)] * 2,
        in_specs=in_smem(2) + in_vmem(n_ctx + 7),
        out_specs=in_vmem(2),
        scratch_shapes=[pltpu.VMEM((length, cols), BF)] + [pltpu.VMEM((length, cols), F32)] * 3,
        compiler_params=params(),
        cost_estimate=cost(2 * length * width * cols + 40 * length * length * cols, 8 * width * length),
        name="attention_backward",
    )(pair, me, *pieces, merge_rows, q, k, v, scale, cosine, sine)


def fold_heads_kernel(q_ref, k_ref, v_ref, gain_ref, out_ref):
    n_ctx, _, cols = out_ref.shape
    cols //= 3
    gain = gain_ref[...]
    for at, ref in enumerate((q_ref, k_ref, v_ref)):
        for to in range(n_ctx):
            part = ref[:, to * cols : (to + 1) * cols].astype(F32) * gain
            out_ref[to, :, at * cols : (at + 1) * cols] = part.astype(BF)


def fold_heads(weights, gain, n_ctx):
    rows, width = weights[0].shape
    return pl.pallas_call(
        fold_heads_kernel,
        out_shape=jax.ShapeDtypeStruct((n_ctx, rows, 3 * (width // n_ctx)), BF),
        in_specs=in_vmem(4),
        out_specs=pl.BlockSpec(memory_space=pltpu.VMEM),
        compiler_params=params(),
        cost_estimate=cost(3 * rows * width, 12 * rows * width),
        name="fold_heads",
    )(*weights, gain)


def unfold_heads_kernel(s_ref, q_ref, k_ref, v_ref, gain_ref, dq_ref, dk_ref, dv_ref, first_ref):
    n_ctx, rows, cols = s_ref.shape
    cols //= 3
    gain = gain_ref[...]
    total = jnp.zeros((rows, cols), F32)
    for at, (ref, out) in enumerate(((q_ref, dq_ref), (k_ref, dk_ref), (v_ref, dv_ref))):
        for to in range(n_ctx):
            span = slice(to * cols, (to + 1) * cols)
            part = s_ref[to, :, at * cols : (at + 1) * cols].astype(F32)
            total += part * ref[:, span].astype(F32)
            out[:, span] = part * gain
    first_ref[...] = jnp.sum(total, axis=1, keepdims=True)


def unfold_heads(sums, weights, gain):
    rows, width = weights[0].shape
    return pl.pallas_call(
        unfold_heads_kernel,
        out_shape=[jax.ShapeDtypeStruct((rows, width), F32)] * 3 + [jax.ShapeDtypeStruct((rows, 1), F32)],
        in_specs=in_vmem(5),
        out_specs=in_vmem(4),
        compiler_params=params(),
        cost_estimate=cost(12 * rows * width, 24 * rows * width),
        name="unfold_heads",
    )(sums, *weights, gain)


def fold_hidden_kernel(piece, w_ref, gain_ref, out_ref):
    n_core, n_fsdp, _, hid = out_ref.shape
    gain = gain_ref[...]
    for plane in range(hid // piece):
        for core in range(n_core):
            for line in range(n_fsdp):
                at = ((plane * n_core + core) * n_fsdp + line) * piece
                part = w_ref[:, at : at + piece].astype(F32) * gain
                out_ref[core, line, :, plane * piece : (plane + 1) * piece] = part.astype(BF)


def fold_hidden(weight, gain, n_plane, n_core, n_fsdp):
    rows, total = weight.shape
    piece = total // (n_plane * n_core * n_fsdp)
    if piece % 128:
        folded = (weight.astype(F32) * gain).astype(BF).reshape(rows, n_plane, n_core, n_fsdp, piece)
        return folded.transpose(2, 3, 0, 1, 4).reshape(n_core, n_fsdp, rows, n_plane * piece)
    return pl.pallas_call(
        functools.partial(fold_hidden_kernel, piece),
        out_shape=jax.ShapeDtypeStruct((n_core, n_fsdp, rows, n_plane * piece), BF),
        in_specs=in_vmem(2),
        out_specs=pl.BlockSpec(memory_space=pltpu.VMEM),
        compiler_params=params(),
        cost_estimate=cost(rows * total, 4 * rows * total),
        name="fold_hidden",
    )(weight, gain)


def unfold_hidden_kernel(piece, at_ref, *refs):
    *s_refs, w_ref, gain_ref, out_ref, second_ref = refs
    n_fsdp = len(s_refs)
    n_core, rows, hid = s_refs[0].shape
    gain = gain_ref[...]
    total = jnp.zeros((rows, piece), F32)
    for mask, ref in enumerate(s_refs):
        line = jnp.bitwise_xor(at_ref[1], mask)
        for other in range(n_core):
            core = jnp.bitwise_xor(at_ref[0], other)
            for plane in range(hid // piece):
                at = ((plane * n_core + core) * n_fsdp + line) * piece
                span = pl.ds(pl.multiple_of(at, piece), piece)
                part = ref[other, :, plane * piece : (plane + 1) * piece].astype(F32)
                total += part * w_ref[:, span].astype(F32)
                out_ref[:, span] = part * gain
    second_ref[...] = jnp.sum(total, axis=1, keepdims=True)


def unfold_hidden(pieces, weight, gain, n_plane):
    rows, total = weight.shape
    n_core, _, hid = pieces[0].shape
    n_fsdp = len(pieces)
    piece = hid // n_plane
    core, line = lax.axis_index("core"), lax.axis_index("fsdp")
    if piece % 128:
        out = jnp.zeros((rows, n_plane, n_core, n_fsdp, piece), BF)
        for mask, block in enumerate(pieces):
            for other in range(n_core):
                part = block[other].reshape(rows, n_plane, 1, 1, piece)
                out = lax.dynamic_update_slice(out, part, (0, 0, core ^ other, line ^ mask, 0))
        out = out.reshape(rows, total).astype(F32)
        return out * gain, jnp.sum(out * weight.astype(F32), axis=1, keepdims=True)
    return pl.pallas_call(
        functools.partial(unfold_hidden_kernel, piece),
        out_shape=[jax.ShapeDtypeStruct((rows, total), F32), jax.ShapeDtypeStruct((rows, 1), F32)],
        in_specs=in_smem(1) + in_vmem(n_fsdp + 2),
        out_specs=in_vmem(2),
        compiler_params=params(),
        cost_estimate=cost(4 * rows * total, 8 * rows * total),
        name="unfold_hidden",
    )(jnp.stack([core, line]).astype(jnp.int32), *pieces, weight, gain)


def place_kernel(at_ref, *refs):
    *p_refs, out_ref = refs
    for i, ref in enumerate(p_refs):
        out_ref[at_ref[i]] = ref[...]


def place(pieces, index):
    n = len(pieces)
    moved = 2 * n * pieces[0].size * pieces[0].dtype.itemsize
    return pl.pallas_call(
        place_kernel,
        out_shape=jax.ShapeDtypeStruct((n,) + pieces[0].shape, pieces[0].dtype),
        in_specs=in_smem(1) + in_vmem(n),
        out_specs=pl.BlockSpec(memory_space=pltpu.VMEM),
        compiler_params=params(),
        cost_estimate=cost(0, moved),
        name="place",
    )(jnp.stack(index).astype(jnp.int32), *pieces)


def gather(value, axes, axis=0):
    return lax.all_gather(value, axes, axis=axis, tiled=True)


def scatter(value, axes):
    return lax.psum_scatter(value, axes, scatter_dimension=0, tiled=True)


def exchange(value, axes):
    return lax.all_to_all(value, axes, split_axis=0, concat_axis=0, tiled=True)


def after(value, *earlier):
    return lax.optimization_barrier((value, earlier))[0]


def alone(value):
    return lax.optimization_barrier(value)


def core_swap(value):
    n = lax.axis_size("plane") * 2
    return lax.ppermute(value, CTX, [(i, i ^ 1) for i in range(n)])


def plane_step(value, step):
    steps, _ = relative(lax.axis_size("plane"))
    n = lax.axis_size("plane") * 2
    return lax.ppermute(value, CTX, [(i, i ^ (2 * steps[i % 2][step])) for i in range(n)])


def line_swap(value, mask):
    n = lax.axis_size("fsdp")
    return lax.ppermute(value, "fsdp", [(i, i ^ mask) for i in range(n)])


def plane_gather(value):
    pieces = [value]
    for j in range(1, lax.axis_size("plane")):
        step = j.bit_length() - 1
        pieces.append(plane_step(pieces[j - (1 << step)], step))
    return pieces


def plane_scatter(chunks):
    total = list(chunks)
    for j in reversed(range(1, len(total))):
        step = j.bit_length() - 1
        to = j - (1 << step)
        total[to] = total[to].astype(F32) + plane_step(total[j].astype(BF), step).astype(F32)
    return total[0]


def plane_index():
    _, order = relative(lax.axis_size("plane"))
    core = lax.axis_index("core")
    plane = lax.axis_index("plane")
    return [plane ^ jnp.where(core == 0, a, b) for a, b in zip(*order)]


def part(value, at, size, axis):
    return lax.dynamic_slice_in_dim(value, at * size, size, axis)


def ctx_gather(value):
    mine = plane_gather(value)
    return mine + [core_swap(piece) for piece in mine]


def ctx_scatter(theirs, mine, n_plane):
    total = (mine.astype(F32) + core_swap(theirs).astype(F32)).astype(BF)
    rows = total.shape[0] // n_plane
    return plane_scatter([total[i * rows : (i + 1) * rows] for i in range(n_plane)])


def token_scatter(left, product):
    core = lax.axis_index("core")
    rows = left.shape[0] // 2
    theirs = core_swap(alone(product(part(left, 1 - core, rows, 0)).astype(BF)))
    mine = alone(product(part(left, core, rows, 0)).astype(BF))
    return (mine.astype(F32) + theirs.astype(F32)).astype(BF)


def line_exchange(value):
    core, line = lax.axis_index("core"), lax.axis_index("fsdp")
    kept = lax.dynamic_index_in_dim(value, core, 0, keepdims=False)
    came = core_swap(lax.dynamic_index_in_dim(value, 1 - core, 0, keepdims=False))
    pieces = []
    for mask in range(lax.axis_size("fsdp")):
        to = line ^ mask
        pair = jnp.stack(
            [lax.dynamic_index_in_dim(v, to, 0, keepdims=False) for v in (kept, came)]
        )
        pieces.append(pair if mask == 0 else line_swap(pair, mask))
    return pieces


def line_rows(pieces):
    core, line = lax.axis_index("core"), lax.axis_index("fsdp")
    n_fsdp = len(pieces)
    blocks = [(piece[other], (core ^ other) * n_fsdp + (line ^ mask)) for mask, piece in enumerate(pieces) for other in range(2)]
    return place([b for b, _ in blocks], [i for _, i in blocks])


def on_device(
    layer_input, pairing, query_weight, key_weight, value_weight, merge_weight,
    gate_weight, up_weight, down_weight, norm_first, norm_second, output_cotangent,
):
    n_plane = lax.axis_size("plane")
    n_core = lax.axis_size("core")
    n_fsdp = lax.axis_size("fsdp")
    n_ctx = n_plane * n_core
    n_tok = n_core * n_fsdp
    me = jnp.stack([lax.axis_index("plane"), lax.axis_index("core")]).astype(jnp.int32)
    index = plane_index()
    _, rows, width = layer_input.shape
    length = rows * n_ctx
    half = length // 2
    cols = width // n_ctx
    dev_rows = gate_weight.shape[0]
    piece = gate_weight.shape[1] // (n_ctx * n_fsdp)
    hid = piece * n_plane
    d_rows = n_tok * dev_rows
    tokens = layer_input.reshape(rows, width)
    cotangent = output_cotangent.reshape(rows, width)
    gain_first = norm_first.astype(F32)[:, None]
    gain_second = norm_second.astype(F32)[:, None]
    projections = (query_weight, key_weight, value_weight)

    gate_moved = line_exchange(fold_hidden(gate_weight, gain_second, n_plane, n_core, n_fsdp))
    own = exchange(fold_heads(projections, gain_first, n_ctx), CTX)
    own = after(own, gate_moved)
    qkv_weight = gather(own[:, None], "fsdp", axis=1).reshape(width, 3 * cols)
    x_pieces = ctx_gather(tokens)
    gate_pieces = plane_gather(line_rows(gate_moved).reshape(d_rows, hid))
    up_own = after(fold_hidden(up_weight, gain_second, n_plane, n_core, n_fsdp), qkv_weight)
    up_moved = line_exchange(up_own)
    merge_rows = gather(after(merge_weight, qkv_weight), "fsdp")
    cot_all = gather(after(cotangent, merge_rows), TOK)
    down_pieces = plane_gather(after(down_weight, x_pieces, gate_pieces))

    cosine, sine = rope_tables(length, cols)
    x_pieces, gate_pieces = lax.optimization_barrier((x_pieces, gate_pieces))
    q, k, v, scale_all, attended = attention_forward(pairing, me, x_pieces, qkv_weight, cosine, sine)
    x_all = jnp.concatenate(x_pieces, axis=0)
    own_f = tokens.astype(F32)
    theirs = alone(mm(attended[half:], merge_rows).astype(BF))
    mine = alone(mm(attended[:half], merge_rows).astype(BF))
    mixed = own_f + ctx_scatter(theirs, mine, n_plane)
    up_pieces = plane_gather(line_rows(up_moved).reshape(d_rows, hid))

    scale_second = lax.rsqrt(jnp.mean(mixed * mixed, axis=-1, keepdims=True) + EPS)
    unit_second = mixed * scale_second
    normed = after(unit_second.astype(BF), down_pieces)
    normed_all = gather(normed, TOK)
    gate_rows = place(gate_pieces, index).reshape(width, hid)
    up_rows = place(up_pieces, index).reshape(width, hid)
    down_rows = place(down_pieces, index).reshape(hid, width)
    gate = mm(normed_all, gate_rows)
    up = mm(normed_all, up_rows)
    sig = jax.nn.sigmoid(gate)
    active = gate * sig
    hidden = (active * up).astype(BF)
    grad_hidden = mm_t(cot_all, down_rows)
    grad_gate = (grad_hidden * up * sig * (1.0 + gate * (1.0 - sig))).astype(BF)
    grad_up = (grad_hidden * active).astype(BF)
    hidden, grad_gate, grad_up = lax.optimization_barrier((hidden, grad_gate, grad_up))
    grad_gu = jnp.concatenate([grad_gate, grad_up], axis=1)
    e_two = token_scatter(
        grad_gu, lambda v: mm_t(v[:, :hid], gate_rows) + mm_t(v[:, hid:], up_rows)
    )

    hidden_w, gate_w, up_w = after((hidden, grad_gate, grad_up), e_two)
    normed_w = [part(normed_all, at, d_rows, 1) for at in index]
    down_chunks = [t_mm(part(hidden_w, at, piece, 1), cot_all).astype(BF) for at in index]
    gate_chunks = [t_mm(rows_of, gate_w).astype(BF) for rows_of in normed_w]
    up_chunks = [t_mm(rows_of, up_w).astype(BF) for rows_of in normed_w]
    branch = token_scatter(hidden_w, lambda v: mm(v, down_rows))
    down_chunks, gate_chunks, up_chunks, branch = lax.optimization_barrier(
        (down_chunks, gate_chunks, up_chunks, branch)
    )
    e_two = scatter(e_two, "fsdp")
    branch_sum = scatter(after(branch, e_two), "fsdp").astype(F32)
    layer_output = (mixed + branch_sum).astype(BF)
    gate_sum = plane_scatter(gate_chunks).astype(BF).reshape(n_core, n_fsdp, dev_rows, hid)
    gate_back = line_exchange(gate_sum)
    up_sum = plane_scatter(up_chunks).astype(BF).reshape(n_core, n_fsdp, dev_rows, hid)
    up_back = line_exchange(up_sum)
    down_grad = plane_scatter(down_chunks).astype(F32)
    gate_grad, second_gate = unfold_hidden(gate_back, gate_weight, gain_second, n_plane)
    up_grad, second_up = unfold_hidden(up_back, up_weight, gain_second, n_plane)
    second_grad = (second_gate + second_up)[:, 0]

    e_two = after(e_two, gate_chunks, up_chunks, down_chunks, branch).astype(F32)
    grad_mixed = cotangent.astype(F32) + scale_second * (
        e_two - unit_second * jnp.mean(e_two * unit_second, axis=-1, keepdims=True)
    )
    branch_pieces = ctx_gather(grad_mixed.astype(BF))
    grad_qkv, grad_scaled = attention_backward(
        pairing, me, branch_pieces, merge_rows, q, k, v, scale_all, cosine, sine
    )
    sums = t_mm(x_all, grad_scaled).astype(BF).reshape(n_ctx, n_fsdp, dev_rows, 3 * cols)
    sums = scatter(sums.transpose(1, 0, 2, 3).reshape(width, 3 * cols), "fsdp")
    branch_all = jnp.concatenate(branch_pieces, axis=0)
    merge_grad = t_mm(attended, branch_all).astype(BF)
    merge_grad = scatter(after(merge_grad, sums), "fsdp").astype(F32)
    theirs = alone(mm_t(grad_qkv[half:], qkv_weight).astype(BF))
    mine = alone(mm_t(grad_qkv[:half], qkv_weight).astype(BF))
    e_one = ctx_scatter(theirs, mine, n_plane)
    scale_first = lax.rsqrt(jnp.mean(own_f * own_f, axis=-1, keepdims=True) + EPS)
    unit_first = own_f * scale_first
    input_grad = (
        grad_mixed
        + scale_first * (e_one - unit_first * jnp.mean(e_one * unit_first, axis=-1, keepdims=True))
    ).astype(BF)
    sums = exchange(sums.reshape(n_ctx, dev_rows, 3 * cols), CTX)
    query_grad, key_grad, value_grad, first_grad = unfold_heads(sums, projections, gain_first)
    return (
        layer_output.reshape(1, rows, width),
        input_grad.reshape(1, rows, width),
        query_grad,
        key_grad,
        value_grad,
        merge_grad,
        gate_grad,
        up_grad,
        down_grad,
        first_grad[:, 0],
        second_grad,
    )


def solution(mesh):
    n_ctx, n_fsdp = mesh.shape["ctx"], mesh.shape["fsdp"]
    inner = Mesh(mesh.devices.reshape(n_ctx // 2, 2, n_fsdp), ("plane", "core", "fsdp"))
    token = P("fsdp", CTX, None)
    weight = P(("plane", "core", "fsdp"), None)
    gain = P(("plane", "core", "fsdp"))
    return jax.shard_map(
        on_device,
        mesh=inner,
        in_specs=(token, P("fsdp", None)) + (weight,) * 7 + (gain, gain, token),
        out_specs=(token, token) + (weight,) * 7 + (gain, gain),
        check_vma=False,
    )
```

time: 995 us -> 692 us (0.70)
  waiting for transfers between devices: 672 us -> 341 us
  blocking collectives: 72.6 us -> 0 us
  starting transfers between devices: 11.5 us -> 71.5 us
  Pallas kernels: 31.6 us -> 74.8 us
    reduce_scatter x8 -> x4, waiting for transfers between devices: 344 us -> 10.7 us  [scatter(): return lax.psum_scatter(value, axes, scatter_dimension=0, tiled=True)]
    all_gather x8 -> x4, waiting for transfers between devices: 325 us -> 36.6 us  [gather(): return lax.all_gather(value, axes, axis=axis, tiled=True)]
    ppermute x0 -> x58, waiting for transfers between devices: none -> 279 us  [the longest x30 184 us: plane_step(): lax.ppermute(value, CTX, [(i, i ^ 2 * steps[i % 2][step]) for i in range(...]
    all_to_all x2 -> x0, blocking collectives: 72.6 us -> none  [exchange(): return lax.all_to_all(value, axes, split_axis=0, concat_axis=0, tiled=True)]
    ppermute x0 -> x58, starting transfers between devices: none -> 61.6 us  [the longest x30 44.2 us: plane_step(): lax.ppermute(value, CTX, [(i, i ^ 2 * steps[i % 2][step]) for i in range(...]
    pallas_call x0 -> x11, Pallas kernels: none -> 34.9 us  [the longest x5 18.2 us: place(): pl.pallas_call(place_kernel, out_shape=jax.ShapeDtypeStruct((n,) + pieces...]
    convert_element_type x7 -> x0, local copies, waits for them, and re-layouts: 25.4 us -> none  [the longest x3 16.2 us: on_device(): gu_sum = gu_sum.reshape(dev_rows, 2, hidden_total).astype(F32)]
    all_to_all x2, waiting for transfers between devices: 0.01 us -> 13.3 us  [exchange(): return lax.all_to_all(value, axes, split_axis=0, concat_axis=0, tiled=True)]
  transfers between devices with their start and end apart: 18 -> 68, of which waited for: 15 -> 32; matrix products, arithmetic and copies ran while one was open for 14% -> 17% of each run, Pallas kernels for 3% -> 7%
where the time goes in v2:
time: 692 us; the launch traced here: 683 us
  waiting for transfers between devices  341 us (49%)
  matrix products  102 us (15%)
  Pallas kernels  74.8 us (11%)
  starting transfers between devices  71.5 us (10%)
  other arithmetic  39.5 us (6%)
  local copies, waits for them, and re-layouts  39.1 us (6%)
  between operations  15.3 us (2%)
    ppermute x30, waiting for transfers between devices, plane_step(): lax.ppermute(value, CTX, [(i, i ^ 2 * steps[i % 2][step]) for i in range(...  184 us
    ppermute x12, waiting for transfers between devices, line_swap(): return lax.ppermute(value, 'fsdp', [(i, i ^ mask) for i in range(n)])  92.6 us
    ppermute x30, starting transfers between devices, plane_step(): lax.ppermute(value, CTX, [(i, i ^ 2 * steps[i % 2][step]) for i in range(...  44.2 us
    dot_general x14, matrix products, t_mm(): lax.dot_general(left, right, (((0,), (0,)), ((), ())), preferred_element_...  39.5 us
    all_gather x4, waiting for transfers between devices, gather(): return lax.all_gather(value, axes, axis=axis, tiled=True)  36.6 us
    dot_general x7, matrix products, mm_t(): lax.dot_general(left, right, (((1,), (1,)), ((), ())), preferred_element_...  31.8 us
    dot_general x6, matrix products, mm(): return jnp.dot(left, right, preferred_element_type=F32)  30.7 us
    pallas_call x1, Pallas kernels, attention_backward(): pl.pallas_call(functools.partial(backward_kernel, n_ctx, 256), out_shape=...  22 us
  transfers between devices with their start and end apart: 68, of which 32 were waited for; matrix products, arithmetic and copies ran while one was open for 17% of the time, Pallas kernels for 7%

profile of v2, /device:TPU:18, one launch (start us, length us, event | category | flops | bytes accessed | tf_op | source)
XLA Modules:
  0.0 682.7 jit_solution(14024953913394226299)
XLA Ops:
  15.8 4.4 all-to-all-start
  22.1 3.6 collective-permute-start.9
  25.8 5.4 all-to-all-done
  31.3 10.8 %collective-permute-done.10 = bf16[2,64,1024]{2,1,0:T(8,128)(2,1)S(1)} collective-permute-done((bf16[2,64,1024]{2,1,0:T(8,128)(2,1)S(1)}, bf16[2,64,1024]{2,1,0:T(8,128)(2,1)S(1)}, u32[]{:S(2)}, u32[]{:S(2)}) %collective-permute-start.10) | collective-permute-done | bytes 262176 | tf_op jit(solution)/shard_map/ppermute | solution.py:415
  53.6 22.5 %collective-permute-done.refs_1_ = bf16[128,2048]{1,0:T(8,128)(2,1)} collective-permute-done((bf16[128,2048]{1,0:T(8,128)(2,1)S(1)}, bf16[128,2048]{1,0:T(8,128)(2,1)}, u32[]{:S(2)}, u32[]{:S(2)}) %collective-permute-start) | collective-permute-done | bytes 524320 | tf_op jit(solution)/shard_map/ppermute | solution.py:410
  79.6 30.5 %all-gather.12.cloned.1.call-done = bf16[8,256,768]{2,1,0:T(8,128)(2,1)} async-done(((bf16[8,64,768]{2,1,0:T(8,128)(2,1)}), bf16[8,256,768]{2,1,0:T(8,128)(2,1)}) %all-gather.12.cloned.1.call-update) | async-done | bytes 3145744 | tf_op jit(solution)/shard_map/all_gather | solution.py:383
  115.2 17.9 %attention_forward.1 = (bf16[1024,256]{1,0:T(8,128)(2,1)}, bf16[1024,256]{1,0:T(8,128)(2,1)}, bf16[1024,256]{1,0:T(8,128)(2,1)}, f32[1024,1]{1,0:T(8,128)}, bf16[1024,256]{1,0:T(8,128)(2,1)}) custom-call(s32[1,8]{1,0:T(1,128)} %pair_ref.3, s32[2]{0:T(128)} %pad_add_fusion.me_ref, bf16[128,2048]{1,0:T(8,128)(2,1)} %bitcast.153, ...), custom_call_target="tpu_custom_call" | custom-call | flops 7516192768 | bytes 25165824 | tf_op jit(solution)/shard_map/attention_forward/pallas_call | solution.py:151
  133.1 6.0 all-gather.6.cloned.1.call-done.refs_8_
  149.1 12.1 %collective-permute-done.16 = bf16[128,2048]{1,0:T(8,128)(2,1)S(1)} collective-permute-done((bf16[128,2048]{1,0:T(8,128)(2,1)S(1)}, bf16[128,2048]{1,0:T(8,128)(2,1)S(1)}, u32[]{:S(2)}, u32[]{:S(2)}) %collective-permute-start.16) | collective-permute-done | bytes 524320 | tf_op jit(solution)/shard_map/ppermute | solution.py:410
  163.2 10.8 %collective-permute-done.18.refs_1_ = bf16[256,2048]{1,0:T(8,128)(2,1)S(1)} collective-permute-done((bf16[256,2048]{1,0:T(8,128)(2,1)S(1)}, bf16[256,2048]{1,0:T(8,128)(2,1)S(1)}, u32[]{:S(2)}, u32[]{:S(2)}) %collective-permute-start.18) | collective-permute-done | bytes 1048608 | tf_op jit(solution)/shard_map/ppermute | solution.py:410
  174.6 10.7 %collective-permute-done.17 = bf16[128,2048]{1,0:T(8,128)(2,1)S(1)} collective-permute-done((bf16[128,2048]{1,0:T(8,128)(2,1)S(1)}, bf16[128,2048]{1,0:T(8,128)(2,1)S(1)}, u32[]{:S(2)}, u32[]{:S(2)}) %collective-permute-start.17) | collective-permute-done | bytes 524320 | tf_op jit(solution)/shard_map/ppermute | solution.py:410
  188.9 11.2 %collective-permute-done.20.refs_3_ = bf16[256,2048]{1,0:T(8,128)(2,1)} collective-permute-done((bf16[256,2048]{1,0:T(8,128)(2,1)S(1)}, bf16[256,2048]{1,0:T(8,128)(2,1)}, u32[]{:S(2)}, u32[]{:S(2)}) %collective-permute-start.20) | collective-permute-done | bytes 1048608 | tf_op jit(solution)/shard_map/ppermute | solution.py:410
  211.1 29.6 %collective-permute-done.24 = bf16[2,64,1024]{2,1,0:T(8,128)(2,1)S(1)} collective-permute-done((bf16[2,64,1024]{2,1,0:T(8,128)(2,1)S(1)}, bf16[2,64,1024]{2,1,0:T(8,128)(2,1)S(1)}, u32[]{:S(2)}, u32[]{:S(2)}) %collective-permute-start.24) | collective-permute-done | bytes 262176 | tf_op jit(solution)/shard_map/ppermute | solution.py:415
  241.4 16.7 %collective-permute-done.23 = bf16[2,64,1024]{2,1,0:T(8,128)(2,1)S(1)} collective-permute-done((bf16[2,64,1024]{2,1,0:T(8,128)(2,1)S(1)}, bf16[2,64,1024]{2,1,0:T(8,128)(2,1)S(1)}, u32[]{:S(2)}, u32[]{:S(2)}) %collective-permute-start.23) | collective-permute-done | bytes 262176 | tf_op jit(solution)/shard_map/ppermute | solution.py:415
  264.4 23.8 %collective-permute-done.25.refs_1_ = bf16[512,1024]{1,0:T(8,128)(2,1)S(1)} collective-permute-done((bf16[512,1024]{1,0:T(8,128)(2,1)}, bf16[512,1024]{1,0:T(8,128)(2,1)S(1)}, u32[]{:S(2)}, u32[]{:S(2)}) %collective-permute-start.25) | collective-permute-done | bytes 1048608 | tf_op jit(solution)/shard_map/ppermute | solution.py:410
  289.2 4.5 place.6
  293.8 4.5 place.9
  298.3 4.8 collective-permute-done.27.refs_3_
  303.1 4.5 place.8
  307.6 10.2 %fusion.60 = f32[1024,1024]{1,0:T(8,128)} fusion(bf16[1024,2048]{1,0:T(8,128)(2,1)} %all-gather.8.cloned.1.call-done, bf16[2048,1024]{1,0:T(8,128)(2,1)} %bitcast.173), kind=kOutput, calls=%fused_computation.202 | convolution fusion | flops 4294967296 | bytes 12582912 | tf_op jit(solution)/shard_map/dot_general | solution.py:23
  317.8 6.5 fusion.59
  324.3 13.2 %multiply_convert_fusion = (bf16[1024,1024]{1,0:T(8,128)(2,1)S(1)}, bf16[1024,1024]{1,0:T(8,128)(2,1)S(1)}, bf16[1024,1024]{1,0:T(8,128)(2,1)}) fusion(f32[1024,1024]{1,0:T(8,128)} %fusion.59, f32[1024,1024]{1,0:T(8,128)} %fusion.60, bf16[1024,2048]{1,0:T(8,128)(2,1)} %all-gather.10.cloned.1.call-done, bf16[1024,2048]{1,0:T(8,128)(2,1)} %bitcast.167), kind=kOutput, calls=%fused_computation.5 | convolution fusion | flops 4310695936 | bytes 23068672 | tf_op jit(solution)/shard_map/dot_general | solution.py:27
  344.2 3.7 add_convert_fusion.3
  347.9 5.0 fusion.16
  353.0 3.8 add_convert_fusion.4
  356.8 3.7 add_convert_fusion.2
  360.5 6.3 convolution_convert_fusion.2
  366.8 3.7 convolution_convert_fusion.1
  371.1 4.5 convolution_convert_fusion.12
  375.7 3.5 convolution_convert_fusion.13
  404.7 10.7 %reduce-scatter.5.cloned.1.call-done = bf16[128,2048]{1,0:T(8,128)(2,1)} async-done(((bf16[512,2048]{1,0:T(8,128)(2,1)}), bf16[128,2048]{1,0:T(8,128)(2,1)}) %reduce-scatter.5.cloned.1.call-update) | async-done | bytes 524304 | tf_op jit(solution)/shard_map/reduce_scatter | solution.py:387
  422.1 10.2 %collective-permute-done.30.refs_1_ = bf16[128,2048]{1,0:T(8,128)(2,1)S(1)} collective-permute-done((bf16[128,2048]{1,0:T(8,128)(2,1)S(1)}, bf16[128,2048]{1,0:T(8,128)(2,1)S(1)}, u32[]{:S(2)}, u32[]{:S(2)}) %collective-permute-start.30) | collective-permute-done | bytes 524320 | tf_op jit(solution)/shard_map/ppermute | solution.py:410
  437.8 4.3 collective-permute-done.32.refs_3_
  448.4 22.0 %attention_backward.1 = (bf16[1024,768]{1,0:T(8,128)(2,1)}, bf16[1024,768]{1,0:T(8,128)(2,1)}) custom-call(s32[1,8]{1,0:T(1,128)} %pair_ref.3, s32[2]{0:T(128)} %pad_add_fusion.me_ref, bf16[128,2048]{1,0:T(8,128)(2,1)} %copy-done.47, bf16[128,2048]{1,0:T(8,128)(2,1)} %copy-done.33, bf16[128,2048]{1,0:T(8,128)(2,1)} %copy-done.35, ...), custom_call_target="tpu_custom_call" | custom-call | flops 11811160064 | bytes 16777216 | tf_op jit(solution)/shard_map/attention_backward/pallas_call | solution.py:228
  470.3 6.2 convolution_convert_fusion
  483.0 11.0 %collective-permute-done.42 = bf16[512,1024]{1,0:T(8,128)(2,1)S(1)} collective-permute-done((bf16[512,1024]{1,0:T(8,128)(2,1)}, bf16[512,1024]{1,0:T(8,128)(2,1)S(1)}, u32[]{:S(2)}, u32[]{:S(2)}) %collective-permute-start.42) | collective-permute-done | bytes 1048608 | tf_op jit(solution)/shard_map/ppermute | solution.py:410
  497.0 16.4 %collective-permute-done.49 = bf16[512,1024]{1,0:T(8,128)(2,1)S(1)} collective-permute-done((bf16[512,1024]{1,0:T(8,128)(2,1)}, bf16[512,1024]{1,0:T(8,128)(2,1)S(1)}, u32[]{:S(2)}, u32[]{:S(2)}) %collective-permute-start.49) | collective-permute-done | bytes 1048608 | tf_op jit(solution)/shard_map/ppermute | solution.py:410
  517.3 18.6 %collective-permute-done.41 = bf16[512,1024]{1,0:T(8,128)(2,1)S(1)} collective-permute-done((bf16[512,1024]{1,0:T(8,128)(2,1)}, bf16[512,1024]{1,0:T(8,128)(2,1)S(1)}, u32[]{:S(2)}, u32[]{:S(2)}) %collective-permute-start.41) | collective-permute-done | bytes 1048608 | tf_op jit(solution)/shard_map/ppermute | solution.py:410
  539.7 10.4 %collective-permute-done.48 = bf16[512,1024]{1,0:T(8,128)(2,1)S(1)} collective-permute-done((bf16[512,1024]{1,0:T(8,128)(2,1)}, bf16[512,1024]{1,0:T(8,128)(2,1)S(1)}, u32[]{:S(2)}, u32[]{:S(2)}) %collective-permute-start.48) | collective-permute-done | bytes 1048608 | tf_op jit(solution)/shard_map/ppermute | solution.py:410
  551.6 9.7 %collective-permute-done.56 = bf16[256,2048]{1,0:T(8,128)(2,1)S(1)} collective-permute-done((bf16[256,2048]{1,0:T(8,128)(2,1)S(1)}, bf16[256,2048]{1,0:T(8,128)(2,1)S(1)}, u32[]{:S(2)}, u32[]{:S(2)}) %collective-permute-start.56) | collective-permute-done | bytes 1048608 | tf_op jit(solution)/shard_map/ppermute | solution.py:410
  584.2 5.3 collective-permute-done.39
  595.2 4.4 collective-permute-done.54.refs_3_
  599.6 21.6 %collective-permute-done.53.refs_2_ = bf16[2,64,1024]{2,1,0:T(8,128)(2,1)} collective-permute-done((bf16[2,64,1024]{2,1,0:T(8,128)(2,1)}, bf16[2,64,1024]{2,1,0:T(8,128)(2,1)}, u32[]{:S(2)}, u32[]{:S(2)}) %collective-permute-start.53) | collective-permute-done | bytes 262176 | tf_op jit(solution)/shard_map/ppermute | solution.py:415
  621.2 9.2 %collective-permute-start.38 = (bf16[128,2048]{1,0:T(8,128)(2,1)}, bf16[128,2048]{1,0:T(8,128)(2,1)S(1)}, u32[]{:S(2)}, u32[]{:S(2)}) collective-permute-start(bf16[128,2048]{1,0:T(8,128)(2,1)} %get-tuple-element.128), channel_id=1, source_target_pairs={{0,16},{4,12},{8,24},{12,4},{16,0},{20,28},{24,8},{28,20},{1,17},{... | collective-permute-start | bytes 1572872 | tf_op jit(solution)/shard_map/ppermute | solution.py:410
  631.4 3.7 convert_add_fusion
  643.0 3.7 collective-permute-done.46.refs_2_
  653.9 4.6 all-to-all-start.1
  662.0 7.8 %all-to-all-done.1.s_ref = bf16[8,64,768]{2,1,0:T(8,128)(2,1)} async-done(((bf16[8,64,768]{2,1,0:T(8,128)(2,1)}), bf16[8,64,768]{2,1,0:T(8,128)(2,1)}, u32[]{:S(2)}, u32[]{:S(2)}) %all-to-all-start.1) | async-done | bytes 786464 | tf_op jit(solution)/shard_map/all_to_all | solution.py:391
  (352 shorter events, 189.0 us)
Async XLA Ops:
  20.2 89.9 %all-gather.12.cloned.1.call-start = ((), (), s32[]{:S(2)}) async-start(), calls=%async_computation.13 | async-start | bytes 3932160 | tf_op jit(solution)/shard_map/all_gather | solution.py:383
  21.6 20.5 %collective-permute-start.10 = (bf16[2,64,1024]{2,1,0:T(8,128)(2,1)S(1)}, bf16[2,64,1024]{2,1,0:T(8,128)(2,1)S(1)}, u32[]{:S(2)}, u32[]{:S(2)}) collective-permute-start(bf16[2,64,1024]{2,1,0:T(8,128)(2,1)S(1)} %pad_maximum_fusion.2), channel_id=1, source_target_pairs={{0,3},{1,2},{2,1},{3,0},{4,7},{5,6},{6,5},{7,4},{8,11},{9,10},{10,... | collective-permute-start | bytes 786440 | tf_op jit(solution)/shard_map/ppermute | solution.py:415
  22.1 22.7 %collective-permute-start.9 = (bf16[2,64,1024]{2,1,0:T(8,128)(2,1)S(1)}, bf16[2,64,1024]{2,1,0:T(8,128)(2,1)S(1)}, u32[]{:S(2)}, u32[]{:S(2)}) collective-permute-start(bf16[2,64,1024]{2,1,0:T(8,128)(2,1)S(1)} %pad_maximum_fusion.1), channel_id=1, source_target_pairs={{0,2},{1,3},{2,0},{3,1},{4,6},{5,7},{6,4},{7,5},{8,10},{9,11},{10,... | collective-permute-start | bytes 786440 | tf_op jit(solution)/shard_map/ppermute | solution.py:415
  25.7 19.1 %collective-permute-start.8 = (bf16[2,64,1024]{2,1,0:T(8,128)(2,1)S(1)}, bf16[2,64,1024]{2,1,0:T(8,128)(2,1)S(1)}, u32[]{:S(2)}, u32[]{:S(2)}) collective-permute-start(bf16[2,64,1024]{2,1,0:T(8,128)(2,1)S(1)} %pad_maximum_fusion), channel_id=1, source_target_pairs={{0,1},{1,0},{2,3},{3,2},{4,5},{5,4},{6,7},{7,6},{8,9},{9,8},{10,11... | collective-permute-start | bytes 786440 | tf_op jit(solution)/shard_map/ppermute | solution.py:415
  44.9 94.3 %all-gather.6.cloned.1.call-start = ((), (), s32[]{:S(2)}) async-start(), calls=%async_computation.6 | async-start | bytes 1310720 | tf_op jit(solution)/shard_map/all_gather | solution.py:383
  50.1 28.0 %collective-permute-start.11 = (bf16[512,1024]{1,0:T(8,128)(2,1)}, bf16[512,1024]{1,0:T(8,128)(2,1)S(1)}, u32[]{:S(2)}, u32[]{:S(2)}) collective-permute-start(bf16[512,1024]{1,0:T(8,128)(2,1)} %bitcast.159), channel_id=1, source_target_pairs={{0,8},{4,20},{8,0},{12,28},{16,24},{20,4},{24,16},{28,12},{1,9},{5... | collective-permute-start | bytes 3145736 | tf_op jit(solution)/shard_map/ppermute | solution.py:410
  50.5 25.6 %collective-permute-start = (bf16[128,2048]{1,0:T(8,128)(2,1)S(1)}, bf16[128,2048]{1,0:T(8,128)(2,1)}, u32[]{:S(2)}, u32[]{:S(2)}) collective-permute-start(bf16[128,2048]{1,0:T(8,128)(2,1)S(1)} %bitcast.154), channel_id=1, source_target_pairs={{0,8},{4,20},{8,0},{12,28},{16,24},{20,4},{24,16},{28,12},{1,9},{5... | collective-permute-start | bytes 1572872 | tf_op jit(solution)/shard_map/ppermute | solution.py:410
  52.1 58.3 %collective-permute-start.1 = (bf16[128,2048]{1,0:T(8,128)(2,1)S(1)}, bf16[128,2048]{1,0:T(8,128)(2,1)}, u32[]{:S(2)}, u32[]{:S(2)}) collective-permute-start(bf16[128,2048]{1,0:T(8,128)(2,1)S(1)} %bitcast.155), channel_id=1, source_target_pairs={{0,16},{4,12},{8,24},{12,4},{16,0},{20,28},{24,8},{28,20},{1,17},{... | collective-permute-start | bytes 1572872 | tf_op jit(solution)/shard_map/ppermute | solution.py:410
  53.6 56.9 %collective-permute-start.3 = (bf16[128,2048]{1,0:T(8,128)(2,1)S(1)}, bf16[128,2048]{1,0:T(8,128)(2,1)S(1)}, u32[]{:S(2)}, u32[]{:S(2)}) collective-permute-start(bf16[128,2048]{1,0:T(8,128)(2,1)S(1)} %bitcast.156), channel_id=1, source_target_pairs={{0,4},{4,0},{8,12},{12,8},{16,20},{20,16},{24,28},{28,24},{1,5},{5... | collective-permute-start | bytes 1572872 | tf_op jit(solution)/shard_map/ppermute | solution.py:404
  76.1 34.9 %collective-permute-start.2 = (bf16[128,2048]{1,0:T(8,128)(2,1)}, bf16[128,2048]{1,0:T(8,128)(2,1)}, u32[]{:S(2)}, u32[]{:S(2)}) collective-permute-start(bf16[128,2048]{1,0:T(8,128)(2,1)} %collective-permute-done.refs_1_), channel_id=1, source_target_pairs={{0,16},{4,12},{8,24},{12,4},{16,0},{20,28},{24,8},{28,20},{1,17},{... | collective-permute-start | bytes 1572872 | tf_op jit(solution)/shard_map/ppermute | solution.py:410
  77.5 37.6 %collective-permute-start.12 = (bf16[512,1024]{1,0:T(8,128)(2,1)}, bf16[512,1024]{1,0:T(8,128)(2,1)S(1)}, u32[]{:S(2)}, u32[]{:S(2)}) collective-permute-start(bf16[512,1024]{1,0:T(8,128)(2,1)} %bitcast.160), channel_id=1, source_target_pairs={{0,16},{4,12},{8,24},{12,4},{16,0},{20,28},{24,8},{28,20},{1,17},{... | collective-permute-start | bytes 3145736 | tf_op jit(solution)/shard_map/ppermute | solution.py:410
  78.1 37.1 %collective-permute-start.13 = (bf16[512,1024]{1,0:T(8,128)(2,1)S(1)}, bf16[512,1024]{1,0:T(8,128)(2,1)}, u32[]{:S(2)}, u32[]{:S(2)}) collective-permute-start(bf16[512,1024]{1,0:T(8,128)(2,1)S(1)} %collective-permute-done.11.refs_1_), channel_id=1, source_target_pairs={{0,16},{4,12},{8,24},{12,4},{16,0},{20,28},{24,8},{28,20},{1,17},{... | collective-permute-start | bytes 3145736 | tf_op jit(solution)/shard_map/ppermute | solution.py:410
  110.1 197.5 %all-gather.8.cloned.1.call-start = ((), (), s32[]{:S(2)}) async-start(), calls=%async_computation.7 | async-start | bytes 4718592 | tf_op jit(solution)/shard_map/all_gather | solution.py:383
  147.9 26.1 %collective-permute-start.18 = (bf16[256,2048]{1,0:T(8,128)(2,1)S(1)}, bf16[256,2048]{1,0:T(8,128)(2,1)S(1)}, u32[]{:S(2)}, u32[]{:S(2)}) collective-permute-start(bf16[256,2048]{1,0:T(8,128)(2,1)S(1)} %copy-done.23), channel_id=1, source_target_pairs={{0,8},{4,20},{8,0},{12,28},{16,24},{20,4},{24,16},{28,12},{1,9},{5... | collective-permute-start | bytes 3145736 | tf_op jit(solution)/shard_map/ppermute | solution.py:410
  148.5 26.1 %collective-permute-start.15 = (bf16[128,2048]{1,0:T(8,128)(2,1)S(1)}, bf16[128,2048]{1,0:T(8,128)(2,1)S(1)}, u32[]{:S(2)}, u32[]{:S(2)}) collective-permute-start(bf16[128,2048]{1,0:T(8,128)(2,1)S(1)} %get-tuple-element.130), channel_id=1, source_target_pairs={{0,16},{4,12},{8,24},{12,4},{16,0},{20,28},{24,8},{28,20},{1,17},{... | collective-permute-start | bytes 1572872 | tf_op jit(solution)/shard_map/ppermute | solution.py:410
  161.3 23.9 %collective-permute-start.17 = (bf16[128,2048]{1,0:T(8,128)(2,1)S(1)}, bf16[128,2048]{1,0:T(8,128)(2,1)S(1)}, u32[]{:S(2)}, u32[]{:S(2)}) collective-permute-start(bf16[128,2048]{1,0:T(8,128)(2,1)S(1)} %add_convert_fusion.13), channel_id=1, source_target_pairs={{0,8},{4,20},{8,0},{12,28},{16,24},{20,4},{24,16},{28,12},{1,9},{5... | collective-permute-start | bytes 1572872 | tf_op jit(solution)/shard_map/ppermute | solution.py:410
  161.8 27.2 %collective-permute-start.19 = (bf16[256,2048]{1,0:T(8,128)(2,1)S(1)}, bf16[256,2048]{1,0:T(8,128)(2,1)}, u32[]{:S(2)}, u32[]{:S(2)}) collective-permute-start(bf16[256,2048]{1,0:T(8,128)(2,1)S(1)} %copy-done.23), channel_id=1, source_target_pairs={{0,16},{4,12},{8,24},{12,4},{16,0},{20,28},{24,8},{28,20},{1,17},{... | collective-permute-start | bytes 3145736 | tf_op jit(solution)/shard_map/ppermute | solution.py:410
  174.0 26.1 %collective-permute-start.20 = (bf16[256,2048]{1,0:T(8,128)(2,1)S(1)}, bf16[256,2048]{1,0:T(8,128)(2,1)}, u32[]{:S(2)}, u32[]{:S(2)}) collective-permute-start(bf16[256,2048]{1,0:T(8,128)(2,1)S(1)} %collective-permute-done.18.refs_1_), channel_id=1, source_target_pairs={{0,16},{4,12},{8,24},{12,4},{16,0},{20,28},{24,8},{28,20},{1,17},{... | collective-permute-start | bytes 3145736 | tf_op jit(solution)/shard_map/ppermute | solution.py:410
  200.2 124.1 %all-gather.10.cloned.1.call-start = ((), (), s32[]{:S(2)}) async-start(), calls=%async_computation.8 | async-start | bytes 4718592 | tf_op jit(solution)/shard_map/all_gather | solution.py:383
  200.8 214.6 %reduce-scatter.5.cloned.1.call-start = ((), (), s32[]{:S(2)}) async-start(), calls=%async_computation.9 | async-start | bytes 2621440 | tf_op jit(solution)/shard_map/reduce_scatter | solution.py:387
  207.3 33.4 %collective-permute-start.24 = (bf16[2,64,1024]{2,1,0:T(8,128)(2,1)S(1)}, bf16[2,64,1024]{2,1,0:T(8,128)(2,1)S(1)}, u32[]{:S(2)}, u32[]{:S(2)}) collective-permute-start(bf16[2,64,1024]{2,1,0:T(8,128)(2,1)S(1)} %pad_maximum_fusion.7), channel_id=1, source_target_pairs={{0,3},{1,2},{2,1},{3,0},{4,7},{5,6},{6,5},{7,4},{8,11},{9,10},{10,... | collective-permute-start | bytes 786440 | tf_op jit(solution)/shard_map/ppermute | solution.py:415
  208.4 49.7 %collective-permute-start.23 = (bf16[2,64,1024]{2,1,0:T(8,128)(2,1)S(1)}, bf16[2,64,1024]{2,1,0:T(8,128)(2,1)S(1)}, u32[]{:S(2)}, u32[]{:S(2)}) collective-permute-start(bf16[2,64,1024]{2,1,0:T(8,128)(2,1)S(1)} %pad_maximum_fusion.6), channel_id=1, source_target_pairs={{0,2},{1,3},{2,0},{3,1},{4,6},{5,7},{6,4},{7,5},{8,10},{9,11},{10,... | collective-permute-start | bytes 786440 | tf_op jit(solution)/shard_map/ppermute | solution.py:415
  210.4 48.4 %collective-permute-start.22 = (bf16[2,64,1024]{2,1,0:T(8,128)(2,1)S(1)}, bf16[2,64,1024]{2,1,0:T(8,128)(2,1)S(1)}, u32[]{:S(2)}, u32[]{:S(2)}) collective-permute-start(bf16[2,64,1024]{2,1,0:T(8,128)(2,1)S(1)} %pad_maximum_fusion.5), channel_id=1, source_target_pairs={{0,1},{1,0},{2,3},{3,2},{4,5},{5,4},{6,7},{7,6},{8,9},{9,8},{10,11... | collective-permute-start | bytes 786440 | tf_op jit(solution)/shard_map/ppermute | solution.py:415
  261.9 26.2 %collective-permute-start.25 = (bf16[512,1024]{1,0:T(8,128)(2,1)}, bf16[512,1024]{1,0:T(8,128)(2,1)S(1)}, u32[]{:S(2)}, u32[]{:S(2)}) collective-permute-start(bf16[512,1024]{1,0:T(8,128)(2,1)} %bitcast.162), channel_id=1, source_target_pairs={{0,8},{4,20},{8,0},{12,28},{16,24},{20,4},{24,16},{28,12},{1,9},{5... | collective-permute-start | bytes 3145736 | tf_op jit(solution)/shard_map/ppermute | solution.py:410
  263.1 35.2 %collective-permute-start.26 = (bf16[512,1024]{1,0:T(8,128)(2,1)}, bf16[512,1024]{1,0:T(8,128)(2,1)S(1)}, u32[]{:S(2)}, u32[]{:S(2)}) collective-permute-start(bf16[512,1024]{1,0:T(8,128)(2,1)} %bitcast.163), channel_id=1, source_target_pairs={{0,16},{4,12},{8,24},{12,4},{16,0},{20,28},{24,8},{28,20},{1,17},{... | collective-permute-start | bytes 3145736 | tf_op jit(solution)/shard_map/ppermute | solution.py:410
  370.5 213.7 %reduce-scatter.9.cloned.1.call-start = ((), (), s32[]{:S(2)}) async-start(), calls=%async_computation.11 | async-start | bytes 3932160 | tf_op jit(solution)/shard_map/reduce_scatter | solution.py:387
  370.6 31.6 %collective-permute-start.29 = (bf16[512,2048]{1,0:T(8,128)(2,1)}, bf16[512,2048]{1,0:T(8,128)(2,1)S(1)}, u32[]{:S(2)}, u32[]{:S(2)}) collective-permute-start(bf16[512,2048]{1,0:T(8,128)(2,1)} %convolution_convert_fusion.1), channel_id=1, source_target_pairs={{0,4},{4,0},{8,12},{12,8},{16,20},{20,16},{24,28},{28,24},{1,5},{5... | collective-permute-start | bytes 6291464 | tf_op jit(solution)/shard_map/ppermute | solution.py:404
  420.6 17.1 %collective-permute-start.31 = (bf16[128,2048]{1,0:T(8,128)(2,1)S(1)}, bf16[128,2048]{1,0:T(8,128)(2,1)S(1)}, u32[]{:S(2)}, u32[]{:S(2)}) collective-permute-start(bf16[128,2048]{1,0:T(8,128)(2,1)S(1)} %get-tuple-element.122.refs_0_), channel_id=1, source_target_pairs={{0,16},{4,12},{8,24},{12,4},{16,0},{20,28},{24,8},{28,20},{1,17},{... | collective-permute-start | bytes 1572872 | tf_op jit(solution)/shard_map/ppermute | solution.py:410
  478.6 179.9 %reduce-scatter.7.cloned.1.call-start = ((), (), s32[]{:S(2)}) async-start(), calls=%async_computation.10 | async-start | bytes 2621440 | tf_op jit(solution)/shard_map/reduce_scatter | solution.py:387
  481.0 32.5 %collective-permute-start.49 = (bf16[512,1024]{1,0:T(8,128)(2,1)}, bf16[512,1024]{1,0:T(8,128)(2,1)S(1)}, u32[]{:S(2)}, u32[]{:S(2)}) collective-permute-start(bf16[512,1024]{1,0:T(8,128)(2,1)} %convolution_convert_fusion.12), channel_id=1, source_target_pairs={{0,16},{4,12},{8,24},{12,4},{16,0},{20,28},{24,8},{28,20},{1,17},{... | collective-permute-start | bytes 3145736 | tf_op jit(solution)/shard_map/ppermute | solution.py:410
  481.0 54.9 %collective-permute-start.41 = (bf16[512,1024]{1,0:T(8,128)(2,1)}, bf16[512,1024]{1,0:T(8,128)(2,1)S(1)}, u32[]{:S(2)}, u32[]{:S(2)}) collective-permute-start(bf16[512,1024]{1,0:T(8,128)(2,1)} %convolution_convert_fusion.17), channel_id=1, source_target_pairs={{0,16},{4,12},{8,24},{12,4},{16,0},{20,28},{24,8},{28,20},{1,17},{... | collective-permute-start | bytes 3145736 | tf_op jit(solution)/shard_map/ppermute | solution.py:410
  494.4 43.8 %collective-permute-start.43 = (bf16[512,1024]{1,0:T(8,128)(2,1)S(1)}, bf16[512,1024]{1,0:T(8,128)(2,1)S(1)}, u32[]{:S(2)}, u32[]{:S(2)}) collective-permute-start(bf16[512,1024]{1,0:T(8,128)(2,1)S(1)} %add_convert_fusion.10), channel_id=1, source_target_pairs={{0,8},{4,20},{8,0},{12,28},{16,24},{20,4},{24,16},{28,12},{1,9},{5... | collective-permute-start | bytes 3145736 | tf_op jit(solution)/shard_map/ppermute | solution.py:410
  495.0 55.2 %collective-permute-start.48 = (bf16[512,1024]{1,0:T(8,128)(2,1)}, bf16[512,1024]{1,0:T(8,128)(2,1)S(1)}, u32[]{:S(2)}, u32[]{:S(2)}) collective-permute-start(bf16[512,1024]{1,0:T(8,128)(2,1)} %convolution_convert_fusion.13), channel_id=1, source_target_pairs={{0,16},{4,12},{8,24},{12,4},{16,0},{20,28},{24,8},{28,20},{1,17},{... | collective-permute-start | bytes 3145736 | tf_op jit(solution)/shard_map/ppermute | solution.py:410
  513.8 36.3 %collective-permute-start.50 = (bf16[512,1024]{1,0:T(8,128)(2,1)S(1)}, bf16[512,1024]{1,0:T(8,128)(2,1)S(1)}, u32[]{:S(2)}, u32[]{:S(2)}) collective-permute-start(bf16[512,1024]{1,0:T(8,128)(2,1)S(1)} %add_convert_fusion.8), channel_id=1, source_target_pairs={{0,8},{4,20},{8,0},{12,28},{16,24},{20,4},{24,16},{28,12},{1,9},{5... | collective-permute-start | bytes 3145736 | tf_op jit(solution)/shard_map/ppermute | solution.py:410
  515.0 46.3 %collective-permute-start.56 = (bf16[256,2048]{1,0:T(8,128)(2,1)S(1)}, bf16[256,2048]{1,0:T(8,128)(2,1)S(1)}, u32[]{:S(2)}, u32[]{:S(2)}) collective-permute-start(bf16[256,2048]{1,0:T(8,128)(2,1)S(1)} %copy-done.58), channel_id=1, source_target_pairs={{0,16},{4,12},{8,24},{12,4},{16,0},{20,28},{24,8},{28,20},{1,17},{... | collective-permute-start | bytes 3145736 | tf_op jit(solution)/shard_map/ppermute | solution.py:410
  535.9 55.3 %collective-permute-start.55 = (bf16[256,2048]{1,0:T(8,128)(2,1)}, bf16[256,2048]{1,0:T(8,128)(2,1)}, u32[]{:S(2)}, u32[]{:S(2)}) collective-permute-start(bf16[256,2048]{1,0:T(8,128)(2,1)} %convolution_convert_fusion.9), channel_id=1, source_target_pairs={{0,16},{4,12},{8,24},{12,4},{16,0},{20,28},{24,8},{28,20},{1,17},{... | collective-permute-start | bytes 3145736 | tf_op jit(solution)/shard_map/ppermute | solution.py:410
  539.7 24.4 %collective-permute-start.44 = (bf16[4,64,1024]{2,1,0:T(8,128)(2,1)}, bf16[4,64,1024]{2,1,0:T(8,128)(2,1)}, u32[]{:S(2)}, u32[]{:S(2)}) collective-permute-start(bf16[4,64,1024]{2,1,0:T(8,128)(2,1)} %dynamic-slice_bitcast_fusion.1), channel_id=1, source_target_pairs={{0,4},{4,0},{8,12},{12,8},{16,20},{20,16},{24,28},{28,24},{1,5},{5... | collective-permute-start | bytes 1572872 | tf_op jit(solution)/shard_map/ppermute | solution.py:404
  562.7 29.9 %collective-permute-start.57 = (bf16[256,2048]{1,0:T(8,128)(2,1)}, bf16[256,2048]{1,0:T(8,128)(2,1)}, u32[]{:S(2)}, u32[]{:S(2)}) collective-permute-start(bf16[256,2048]{1,0:T(8,128)(2,1)} %add_convert_fusion.6), channel_id=1, source_target_pairs={{0,8},{4,20},{8,0},{12,28},{16,24},{20,4},{24,16},{28,12},{1,9},{5... | collective-permute-start | bytes 3145736 | tf_op jit(solution)/shard_map/ppermute | solution.py:410
  563.3 110.6 %reduce-scatter.11.cloned.1.call-start = ((), (), s32[]{:S(2)}) async-start(), calls=%async_computation.12 | async-start | bytes 1310720 | tf_op jit(solution)/shard_map/reduce_scatter | solution.py:387
  566.7 32.9 %collective-permute-start.54 = (bf16[2,64,1024]{2,1,0:T(8,128)(2,1)}, bf16[2,64,1024]{2,1,0:T(8,128)(2,1)}, u32[]{:S(2)}, u32[]{:S(2)}) collective-permute-start(bf16[2,64,1024]{2,1,0:T(8,128)(2,1)} %pad_maximum_fusion.15), channel_id=1, source_target_pairs={{0,3},{1,2},{2,1},{3,0},{4,7},{5,6},{6,5},{7,4},{8,11},{9,10},{10,... | collective-permute-start | bytes 786440 | tf_op jit(solution)/shard_map/ppermute | solution.py:415
  567.5 53.7 %collective-permute-start.53 = (bf16[2,64,1024]{2,1,0:T(8,128)(2,1)}, bf16[2,64,1024]{2,1,0:T(8,128)(2,1)}, u32[]{:S(2)}, u32[]{:S(2)}) collective-permute-start(bf16[2,64,1024]{2,1,0:T(8,128)(2,1)} %pad_maximum_fusion.14), channel_id=1, source_target_pairs={{0,2},{1,3},{2,0},{3,1},{4,6},{5,7},{6,4},{7,5},{8,10},{9,11},{10,... | collective-permute-start | bytes 786440 | tf_op jit(solution)/shard_map/ppermute | solution.py:415
  589.6 40.8 %collective-permute-start.52 = (bf16[2,64,1024]{2,1,0:T(8,128)(2,1)}, bf16[2,64,1024]{2,1,0:T(8,128)(2,1)S(1)}, u32[]{:S(2)}, u32[]{:S(2)}) collective-permute-start(bf16[2,64,1024]{2,1,0:T(8,128)(2,1)} %pad_maximum_fusion.13), channel_id=1, source_target_pairs={{0,1},{1,0},{2,3},{3,2},{4,5},{5,4},{6,7},{7,6},{8,9},{9,8},{10,11... | collective-permute-start | bytes 786440 | tf_op jit(solution)/shard_map/ppermute | solution.py:415
  591.3 51.8 %collective-permute-start.47 = (bf16[2,64,1024]{2,1,0:T(8,128)(2,1)}, bf16[2,64,1024]{2,1,0:T(8,128)(2,1)S(1)}, u32[]{:S(2)}, u32[]{:S(2)}) collective-permute-start(bf16[2,64,1024]{2,1,0:T(8,128)(2,1)} %pad_maximum_fusion.11), channel_id=1, source_target_pairs={{0,3},{1,2},{2,1},{3,0},{4,7},{5,6},{6,5},{7,4},{8,11},{9,10},{10,... | collective-permute-start | bytes 786440 | tf_op jit(solution)/shard_map/ppermute | solution.py:415
  592.7 54.1 %collective-permute-start.46 = (bf16[2,64,1024]{2,1,0:T(8,128)(2,1)}, bf16[2,64,1024]{2,1,0:T(8,128)(2,1)S(1)}, u32[]{:S(2)}, u32[]{:S(2)}) collective-permute-start(bf16[2,64,1024]{2,1,0:T(8,128)(2,1)} %pad_maximum_fusion.10), channel_id=1, source_target_pairs={{0,2},{1,3},{2,0},{3,1},{4,6},{5,7},{6,4},{7,5},{8,10},{9,11},{10,... | collective-permute-start | bytes 786440 | tf_op jit(solution)/shard_map/ppermute | solution.py:415
  599.6 47.2 %collective-permute-start.45 = (bf16[2,64,1024]{2,1,0:T(8,128)(2,1)}, bf16[2,64,1024]{2,1,0:T(8,128)(2,1)S(1)}, u32[]{:S(2)}, u32[]{:S(2)}) collective-permute-start(bf16[2,64,1024]{2,1,0:T(8,128)(2,1)} %pad_maximum_fusion.9), channel_id=1, source_target_pairs={{0,1},{1,0},{2,3},{3,2},{4,5},{5,4},{6,7},{7,6},{8,9},{9,8},{10,11... | collective-permute-start | bytes 786440 | tf_op jit(solution)/shard_map/ppermute | solution.py:415
  621.2 31.8 %collective-permute-start.38 = (bf16[128,2048]{1,0:T(8,128)(2,1)}, bf16[128,2048]{1,0:T(8,128)(2,1)S(1)}, u32[]{:S(2)}, u32[]{:S(2)}) collective-permute-start(bf16[128,2048]{1,0:T(8,128)(2,1)} %get-tuple-element.128), channel_id=1, source_target_pairs={{0,16},{4,12},{8,24},{12,4},{16,0},{20,28},{24,8},{28,20},{1,17},{... | collective-permute-start | bytes 1572872 | tf_op jit(solution)/shard_map/ppermute | solution.py:410
  630.4 22.6 %collective-permute-start.40 = (bf16[128,2048]{1,0:T(8,128)(2,1)S(1)}, bf16[128,2048]{1,0:T(8,128)(2,1)S(1)}, u32[]{:S(2)}, u32[]{:S(2)}) collective-permute-start(bf16[128,2048]{1,0:T(8,128)(2,1)S(1)} %add_convert_fusion.11), channel_id=1, source_target_pairs={{0,8},{4,20},{8,0},{12,28},{16,24},{20,4},{24,16},{28,12},{1,9},{5... | collective-permute-start | bytes 1572872 | tf_op jit(solution)/shard_map/ppermute | solution.py:410
  653.9 15.8 %all-to-all-start.1 = ((bf16[8,64,768]{2,1,0:T(8,128)(2,1)}), bf16[8,64,768]{2,1,0:T(8,128)(2,1)}, u32[]{:S(2)}, u32[]{:S(2)}) async-start(bf16[8,64,768]{2,1,0:T(8,128)(2,1)} %bitcast.181), calls=%async_computation.4 | async-start | bytes 1572864 | tf_op jit(solution)/shard_map/all_to_all | solution.py:391
  (82 other events, 943.9 us)
Sparse Core Ops, SparseCore 0:
  45.0 65.0 all-gather.11
  111.7 27.4 all-gather.5
  200.3 64.9 all-gather.7
  266.8 48.9 all-gather.9
  370.6 44.7 reduce-scatter.4
  478.8 60.8 reduce-scatter.8
  563.4 81.6 reduce-scatter.6
  647.4 24.9 reduce-scatter.10

commit v3 on v2

--- a/solution.py
+++ b/solution.py
@@ -17,6 +17,7 @@
 CTX = ("plane", "core")
 TOK = ("core", "fsdp")
 VMEM_LIMIT = 56 * 1024 * 1024
+LIGHT = pl.CostEstimate(flops=1024, bytes_accessed=1024, transcendentals=0)
 
 
 def mm(left, right):
@@ -86,10 +87,6 @@
     return pltpu.CompilerParams(vmem_limit_bytes=VMEM_LIMIT)
 
 
-def cost(flops, moved):
-    return pl.CostEstimate(flops=int(flops), bytes_accessed=int(moved), transcendentals=0)
-
-
 def in_vmem(n):
     return [pl.BlockSpec(memory_space=pltpu.VMEM)] * n
 
@@ -98,14 +95,14 @@
     return [pl.BlockSpec(memory_space=pltpu.SMEM)] * n
 
 
-def forward_kernel(n_ctx, qblk, pair_ref, me_ref, *refs):
-    x_refs = refs[:n_ctx]
-    w_ref, cos_ref, sin_ref, q_ref, k_ref, v_ref, r_ref, o_ref, acc_ref = refs[n_ctx:]
+def forward_kernel(
+    n_ctx, qblk, pair_ref, me_ref, x_ref, w_ref, cos_ref, sin_ref, q_ref, k_ref, v_ref, r_ref, o_ref, lse_ref, acc_ref
+):
     length, cols = q_ref.shape
     blk = length // (2 * n_ctx)
     heads = cols // HEAD_DIM
-    for at, x_ref in enumerate(x_refs):
-        x = x_ref[...]
+    for at in range(n_ctx):
+        x = x_ref[pl.ds(at * 2 * blk, 2 * blk), :]
         x_f = x.astype(F32)
         scale = lax.rsqrt(jnp.mean(x_f * x_f, axis=1, keepdims=True) + EPS)
         r_ref[pl.ds(at * 2 * blk, 2 * blk), :] = scale
@@ -119,23 +116,30 @@
             k_ref[to, :] = (key * cosine + swap_halves(key) * sine).astype(BF)
             v_ref[to, :] = qkv[second * blk : (second + 1) * blk, 2 * cols :].astype(BF)
     acc_ref[...] = jnp.zeros_like(acc_ref)
+    lse_ref[...] = jnp.zeros_like(lse_ref)
 
     def one_head(head, carry):
+        mask = head_mask((qblk, cols), head)
+        here = lax.broadcasted_iota(jnp.int32, (qblk, lse_ref.shape[1]), 1) == head
+        below = lax.broadcasted_iota(jnp.int32, (qblk, qblk), 1) <= lax.broadcasted_iota(jnp.int32, (qblk, qblk), 0)
         for i in range(length // qblk):
-            have = (i + 1) * qblk
             rows = pl.ds(i * qblk, qblk)
-            mask = head_mask((qblk, cols), head)
             query = jnp.where(mask, q_ref[rows, :], jnp.zeros((), BF))
-            scores = mm_t(query, k_ref[:have, :]) * SCALE
-            row = lax.broadcasted_iota(jnp.int32, scores.shape, 0) + i * qblk
-            col = lax.broadcasted_iota(jnp.int32, scores.shape, 1)
-            scores = jnp.where(col <= row, scores, NEG)
-            peak = jnp.max(scores, axis=1, keepdims=True)
-            weights = jnp.exp(scores - peak)
-            total = jnp.sum(weights, axis=1, keepdims=True)
-            probs = (weights * (1.0 / total)).astype(BF)
-            out = mm(probs, v_ref[:have, :])
-            acc_ref[rows, :] = jnp.where(mask, out, acc_ref[rows, :])
+            last = jnp.where(below, mm_t(query, k_ref[rows, :]), NEG)
+            peak = jnp.max(last, axis=1, keepdims=True)
+            if i:
+                before = mm_t(query, k_ref[: i * qblk, :])
+                peak = jnp.maximum(peak, jnp.max(before, axis=1, keepdims=True))
+            shift = peak * SCALE
+            last = jnp.exp(last * SCALE - shift)
+            total = jnp.sum(last, axis=1, keepdims=True)
+            out = mm(last.astype(BF), v_ref[rows, :])
+            if i:
+                before = jnp.exp(before * SCALE - shift)
+                total += jnp.sum(before, axis=1, keepdims=True)
+                out += mm(before.astype(BF), v_ref[: i * qblk, :])
+            acc_ref[rows, :] = jnp.where(mask, out * (1.0 / total), acc_ref[rows, :])
+            lse_ref[rows, :] = jnp.where(here, shift + jnp.log(total), lse_ref[rows, :])
         return carry
 
     lax.fori_loop(0, heads, one_head, 0)
@@ -144,28 +148,32 @@
         o_ref[pl.ds(slot * blk, blk), :] = acc_ref[pl.ds(at, blk), :].astype(BF)
 
 
-def attention_forward(pair, me, pieces, weight, cosine, sine):
+def attention_forward(pair, me, tokens, weight, cosine, sine):
     length, cols = cosine.shape
     width = weight.shape[0]
-    n_ctx = len(pieces)
+    n_ctx = width // cols
     return pl.pallas_call(
         functools.partial(forward_kernel, n_ctx, 256),
         out_shape=[jax.ShapeDtypeStruct((length, cols), BF)] * 3
-        + [jax.ShapeDtypeStruct((length, 1), F32), jax.ShapeDtypeStruct((length, cols), BF)],
-        in_specs=in_smem(2) + in_vmem(n_ctx + 3),
-        out_specs=in_vmem(5),
+        + [
+            jax.ShapeDtypeStruct((length, 1), F32),
+            jax.ShapeDtypeStruct((length, cols), BF),
+            jax.ShapeDtypeStruct((length, 128), F32),
+        ],
+        in_specs=in_smem(2) + in_vmem(4),
+        out_specs=in_vmem(6),
         scratch_shapes=[pltpu.VMEM((length, cols), F32)],
         compiler_params=params(),
-        cost_estimate=cost(6 * length * width * cols + 16 * length * length * cols, 12 * width * length),
+        cost_estimate=LIGHT,
         name="attention_forward",
-    )(pair, me, *pieces, weight, cosine, sine)
+    )(pair, me, tokens, weight, cosine, sine)
 
 
 def backward_kernel(n_ctx, qblk, pair_ref, me_ref, *refs):
     b_refs = refs[:n_ctx]
     (
-        m_ref, q_ref, k_ref, v_ref, r_ref, cos_ref, sin_ref,
-        g_ref, gr_ref, go_ref, dq_ref, dk_ref, dv_ref,
+        m_ref, q_ref, k_ref, v_ref, r_ref, o_ref, lse_ref, cos_ref, sin_ref,
+        g_ref, gr_ref, go_ref, dq_ref, dk_ref, dv_ref, do_ref, centre_ref,
     ) = refs[n_ctx:]
     length, cols = q_ref.shape
     blk = length // (2 * n_ctx)
@@ -175,31 +183,43 @@
         for second in range(2):
             to = pl.ds(pl.multiple_of(slot_block(pair_ref, me_ref, 2 * at + second, n_ctx) * blk, blk), blk)
             go_ref[to, :] = grad[second * blk : (second + 1) * blk, :]
+            do_ref[to, :] = o_ref[pl.ds((2 * at + second) * blk, blk), :]
     dq_ref[...] = jnp.zeros_like(dq_ref)
     dk_ref[...] = jnp.zeros_like(dk_ref)
     dv_ref[...] = jnp.zeros_like(dv_ref)
 
+    pick = head_mask((8, cols), lax.broadcasted_iota(jnp.int32, (8, cols), 0)).astype(F32)
+    centre_ref[...] = lax.dot_general(
+        pick,
+        go_ref[...].astype(F32) * do_ref[...].astype(F32),
+        (((1,), (1,)), ((), ())),
+        precision=lax.Precision.HIGHEST,
+        preferred_element_type=F32,
+    )
+
     def one_head(head, carry):
+        mask = head_mask((qblk, cols), head)
+        below = lax.broadcasted_iota(jnp.int32, (qblk, qblk), 0) <= lax.broadcasted_iota(jnp.int32, (qblk, qblk), 1)
         for i in range(length // qblk):
-            have = (i + 1) * qblk
             rows = pl.ds(i * qblk, qblk)
-            mask = head_mask((qblk, cols), head)
             query = jnp.where(mask, q_ref[rows, :], jnp.zeros((), BF))
             grad = jnp.where(mask, go_ref[rows, :], jnp.zeros((), BF))
-            scores = mm_t(k_ref[:have, :], query) * SCALE
-            key_at = lax.broadcasted_iota(jnp.int32, scores.shape, 0)
-            query_at = lax.broadcasted_iota(jnp.int32, scores.shape, 1) + i * qblk
-            scores = jnp.where(key_at <= query_at, scores, NEG)
-            peak = jnp.max(scores, axis=0, keepdims=True)
-            weights = jnp.exp(scores - peak)
-            total = jnp.sum(weights, axis=0, keepdims=True)
-            probs = weights * (1.0 / total)
-            grad_probs = mm_t(v_ref[:have, :], grad)
-            centre = jnp.sum(probs * grad_probs, axis=0, keepdims=True)
-            grad_scores = (probs * (grad_probs - centre)).astype(BF)
-            dk_ref[:have, :] += mm(grad_scores, query)
-            dv_ref[:have, :] += mm(probs.astype(BF), grad)
-            out = t_mm(grad_scores, k_ref[:have, :])
+            lse = lse_ref[pl.ds(head, 1), rows]
+            centre = centre_ref[pl.ds(head, 1), rows]
+            out = None
+            for at, size in ((i * qblk, qblk), (0, i * qblk)):
+                if not size:
+                    continue
+                keys = pl.ds(at, size)
+                probs = jnp.exp(mm_t(k_ref[keys, :], query) * SCALE - lse)
+                if at or not i:
+                    probs = jnp.where(below, probs, 0.0)
+                grad_probs = mm_t(v_ref[keys, :], grad)
+                grad_scores = (probs * (grad_probs - centre)).astype(BF)
+                dk_ref[keys, :] += mm(grad_scores, query)
+                dv_ref[keys, :] += mm(probs.astype(BF), grad)
+                term = t_mm(grad_scores, k_ref[keys, :])
+                out = term if out is None else out + term
             dq_ref[rows, :] = jnp.where(mask, out, dq_ref[rows, :])
         return carry
 
@@ -221,20 +241,204 @@
             gr_ref[rows, span] = (part * scale).astype(BF)
 
 
-def attention_backward(pair, me, pieces, merge_rows, q, k, v, scale, cosine, sine):
+def attention_backward(pair, me, pieces, merge_rows, q, k, v, scale, attended, lse, cosine, sine):
     length, cols = cosine.shape
     width = merge_rows.shape[1]
     n_ctx = len(pieces)
     return pl.pallas_call(
         functools.partial(backward_kernel, n_ctx, 256),
         out_shape=[jax.ShapeDtypeStruct((length, 3 * cols), BF)] * 2,
-        in_specs=in_smem(2) + in_vmem(n_ctx + 7),
+        in_specs=in_smem(2) + in_vmem(n_ctx + 9),
         out_specs=in_vmem(2),
-        scratch_shapes=[pltpu.VMEM((length, cols), BF)] + [pltpu.VMEM((length, cols), F32)] * 3,
-        compiler_params=params(),
-        cost_estimate=cost(2 * length * width * cols + 40 * length * length * cols, 8 * width * length),
+        scratch_shapes=[pltpu.VMEM((length, cols), BF)]
+        + [pltpu.VMEM((length, cols), F32)] * 3
+        + [pltpu.VMEM((length, cols), BF), pltpu.VMEM((8, length), F32)],
+        compiler_params=params(),
+        cost_estimate=LIGHT,
         name="attention_backward",
-    )(pair, me, *pieces, merge_rows, q, k, v, scale, cosine, sine)
+    )(pair, me, *pieces, merge_rows, q, k, v, scale, attended, lse, cosine, sine)
+
+
+def feed_forward_kernel(
+    core_ref, n_ref, c_ref, g_ref, u_ref, d_ref, h_ref, dg_ref, du_ref, theirs_ref, mine_ref
+):
+    rows, cot = n_ref[...], c_ref[...]
+    hid, tile = g_ref.shape[1], 256
+    for at in range(0, hid, tile):
+        span = slice(at, at + tile)
+        gate = mm(rows, g_ref[:, span])
+        up = mm(rows, u_ref[:, span])
+        grad = mm_t(cot, d_ref[span, :])
+        sig = 1.0 / (1.0 + jnp.exp(-gate))
+        active = gate * sig
+        h_ref[:, span] = (active * up).astype(BF)
+        dg_ref[:, span] = (grad * up * sig * (1.0 + gate * (1.0 - sig))).astype(BF)
+        du_ref[:, span] = (grad * active).astype(BF)
+    back = (mm_t(dg_ref[...], g_ref[...]) + mm_t(du_ref[...], u_ref[...])).astype(BF)
+    first = pl.program_id(0) < pl.num_programs(0) // 2
+
+    @pl.when(first)
+    def _():
+        theirs_ref[...] = back
+
+    @pl.when(jnp.logical_not(first))
+    def _():
+        mine_ref[...] = back
+
+
+def feed_forward(normed, cotangent, gate_w, up_w, down_w):
+    count, width = normed.shape
+    hid = gate_w.shape[1]
+    tile = 256
+    half = count // tile // 2
+
+    def rows_of(r, core):
+        return (jnp.where(r < half, (1 - core[0]) * half + r, core[0] * half + r - half), 0)
+
+    def fixed(r, core):
+        return (0, 0)
+
+    once = pl.Buffered(1)
+    return pl.pallas_call(
+        feed_forward_kernel,
+        grid_spec=pltpu.PrefetchScalarGridSpec(
+            num_scalar_prefetch=1,
+            grid=(2 * half,),
+            in_specs=[
+                pl.BlockSpec((tile, width), rows_of),
+                pl.BlockSpec((tile, width), rows_of),
+                pl.BlockSpec((width, hid), fixed, pipeline_mode=once),
+                pl.BlockSpec((width, hid), fixed, pipeline_mode=once),
+                pl.BlockSpec((hid, width), fixed, pipeline_mode=once),
+            ],
+            out_specs=[pl.BlockSpec((tile, hid), rows_of)] * 3
+            + [
+                pl.BlockSpec((tile, width), lambda r, core: (jnp.minimum(r, half - 1), 0)),
+                pl.BlockSpec((tile, width), lambda r, core: (jnp.maximum(r - half, 0), 0)),
+            ],
+        ),
+        out_shape=[jax.ShapeDtypeStruct((count, hid), BF)] * 3
+        + [jax.ShapeDtypeStruct((count // 2, width), BF)] * 2,
+        compiler_params=params(),
+        cost_estimate=LIGHT,
+        name="feed_forward",
+    )(lax.axis_index("core").astype(jnp.int32)[None], normed, cotangent, gate_w, up_w, down_w)
+
+
+def branch_kernel(core_ref, h_ref, d_ref, theirs_ref, mine_ref):
+    out = mm(h_ref[...], d_ref[...]).astype(BF)
+    first = pl.program_id(0) < pl.num_programs(0) // 2
+
+    @pl.when(first)
+    def _():
+        theirs_ref[...] = out
+
+    @pl.when(jnp.logical_not(first))
+    def _():
+        mine_ref[...] = out
+
+
+def branch_rows(hidden, down_w):
+    count, hid = hidden.shape
+    width = down_w.shape[1]
+    tile = 256
+    half = count // tile // 2
+    return pl.pallas_call(
+        branch_kernel,
+        grid_spec=pltpu.PrefetchScalarGridSpec(
+            num_scalar_prefetch=1,
+            grid=(2 * half,),
+            in_specs=[
+                pl.BlockSpec(
+                    (tile, hid),
+                    lambda r, core: (jnp.where(r < half, (1 - core[0]) * half + r, core[0] * half + r - half), 0),
+                ),
+                pl.BlockSpec((hid, width), lambda r, core: (0, 0), pipeline_mode=pl.Buffered(1)),
+            ],
+            out_specs=[
+                pl.BlockSpec((tile, width), lambda r, core: (jnp.minimum(r, half - 1), 0)),
+                pl.BlockSpec((tile, width), lambda r, core: (jnp.maximum(r - half, 0), 0)),
+            ],
+        ),
+        out_shape=[jax.ShapeDtypeStruct((count // 2, width), BF)] * 2,
+        compiler_params=params(),
+        cost_estimate=LIGHT,
+        name="branch_rows",
+    )(lax.axis_index("core").astype(jnp.int32)[None], hidden, down_w)
+
+
+def merge_kernel(a_ref, *refs):
+    *b_refs, out_ref, all_ref = refs
+    rows = b_refs[0].shape[0]
+    for at, ref in enumerate(b_refs):
+        all_ref[pl.ds(at * rows, rows), :] = ref[...]
+    out_ref[...] = t_mm(a_ref[...], all_ref[...]).astype(BF)
+
+
+def merge_term(attended, pieces):
+    cols, width = attended.shape[1], pieces[0].shape[1]
+    return pl.pallas_call(
+        merge_kernel,
+        out_shape=jax.ShapeDtypeStruct((cols, width), BF),
+        in_specs=in_vmem(1 + len(pieces)),
+        out_specs=pl.BlockSpec(memory_space=pltpu.VMEM),
+        scratch_shapes=[pltpu.VMEM((attended.shape[0], width), BF)],
+        compiler_params=params(),
+        cost_estimate=LIGHT,
+        name="merge_term",
+    )(attended, *pieces)
+
+
+def heads_term_kernel(x_ref, g_ref, out_ref):
+    n_fsdp, _, rows, cols = out_ref.shape
+    out_ref[...] = t_mm(x_ref[...], g_ref[...]).astype(BF).reshape(n_fsdp, 1, rows, cols)
+
+
+def heads_term(tokens, grad, n_ctx, n_fsdp):
+    count, width = tokens.shape
+    cols = grad.shape[1]
+    rows = width // (n_ctx * n_fsdp)
+    if n_fsdp * rows % 128:
+        out = t_mm(tokens, grad).astype(BF).reshape(n_ctx, n_fsdp, rows, cols)
+        return out.transpose(1, 0, 2, 3).reshape(width, cols)
+    out = pl.pallas_call(
+        heads_term_kernel,
+        grid=(n_ctx,),
+        in_specs=[
+            pl.BlockSpec((count, n_fsdp * rows), lambda c: (0, c)),
+            pl.BlockSpec((count, cols), lambda c: (0, 0), pipeline_mode=pl.Buffered(1)),
+        ],
+        out_specs=pl.BlockSpec((n_fsdp, 1, rows, cols), lambda c: (0, c, 0, 0)),
+        out_shape=jax.ShapeDtypeStruct((n_fsdp, n_ctx, rows, cols), BF),
+        compiler_params=params(),
+        cost_estimate=LIGHT,
+        name="heads_term",
+    )(tokens, grad)
+    return out.reshape(width, cols)
+
+
+def back_kernel(g_ref, w_ref, out_ref):
+    out_ref[...] = mm_t(g_ref[...], w_ref[...]).astype(BF)
+
+
+def back_rows(grad, weight, half):
+    count, cols = grad.shape
+    width = weight.shape[0]
+    tile = 256
+    steps = count // 2 // tile
+    return pl.pallas_call(
+        back_kernel,
+        grid=(steps,),
+        in_specs=[
+            pl.BlockSpec((tile, cols), lambda r: (half * steps + r, 0)),
+            pl.BlockSpec((width, cols), lambda r: (0, 0), pipeline_mode=pl.Buffered(1)),
+        ],
+        out_specs=pl.BlockSpec((tile, width), lambda r: (r, 0)),
+        out_shape=jax.ShapeDtypeStruct((count // 2, width), BF),
+        compiler_params=params(),
+        cost_estimate=LIGHT,
+        name="back_rows",
+    )(grad, weight)
 
 
 def fold_heads_kernel(q_ref, k_ref, v_ref, gain_ref, out_ref):
@@ -255,7 +459,7 @@
         in_specs=in_vmem(4),
         out_specs=pl.BlockSpec(memory_space=pltpu.VMEM),
         compiler_params=params(),
-        cost_estimate=cost(3 * rows * width, 12 * rows * width),
+        cost_estimate=LIGHT,
         name="fold_heads",
     )(*weights, gain)
 
@@ -282,7 +486,7 @@
         in_specs=in_vmem(5),
         out_specs=in_vmem(4),
         compiler_params=params(),
-        cost_estimate=cost(12 * rows * width, 24 * rows * width),
+        cost_estimate=LIGHT,
         name="unfold_heads",
     )(sums, *weights, gain)
 
@@ -310,7 +514,7 @@
         in_specs=in_vmem(2),
         out_specs=pl.BlockSpec(memory_space=pltpu.VMEM),
         compiler_params=params(),
-        cost_estimate=cost(rows * total, 4 * rows * total),
+        cost_estimate=LIGHT,
         name="fold_hidden",
     )(weight, gain)
 
@@ -354,7 +558,7 @@
         in_specs=in_smem(1) + in_vmem(n_fsdp + 2),
         out_specs=in_vmem(2),
         compiler_params=params(),
-        cost_estimate=cost(4 * rows * total, 8 * rows * total),
+        cost_estimate=LIGHT,
         name="unfold_hidden",
     )(jnp.stack([core, line]).astype(jnp.int32), *pieces, weight, gain)
 
@@ -374,7 +578,7 @@
         in_specs=in_smem(1) + in_vmem(n),
         out_specs=pl.BlockSpec(memory_space=pltpu.VMEM),
         compiler_params=params(),
-        cost_estimate=cost(0, moved),
+        cost_estimate=LIGHT,
         name="place",
     )(jnp.stack(index).astype(jnp.int32), *pieces)
 
@@ -391,12 +595,8 @@
     return lax.all_to_all(value, axes, split_axis=0, concat_axis=0, tiled=True)
 
 
-def after(value, *earlier):
-    return lax.optimization_barrier((value, earlier))[0]
-
-
-def alone(value):
-    return lax.optimization_barrier(value)
+def together(values):
+    return lax.optimization_barrier(values)
 
 
 def core_swap(value):
@@ -415,21 +615,31 @@
     return lax.ppermute(value, "fsdp", [(i, i ^ mask) for i in range(n)])
 
 
+def plane_gather_more(pieces):
+    step = len(pieces).bit_length() - 1
+    return pieces + [plane_step(piece, step) for piece in pieces]
+
+
 def plane_gather(value):
     pieces = [value]
-    for j in range(1, lax.axis_size("plane")):
-        step = j.bit_length() - 1
-        pieces.append(plane_step(pieces[j - (1 << step)], step))
+    while len(pieces) < lax.axis_size("plane"):
+        pieces = plane_gather_more(pieces)
     return pieces
 
 
+def plane_send(chunks):
+    n = len(chunks) // 2
+    return [plane_step(chunk, n.bit_length() - 1) for chunk in chunks[n:]]
+
+
+def plane_add(chunks, came):
+    return [(mine.astype(F32) + chunk.astype(F32)).astype(BF) for mine, chunk in zip(chunks, came)]
+
+
 def plane_scatter(chunks):
-    total = list(chunks)
-    for j in reversed(range(1, len(total))):
-        step = j.bit_length() - 1
-        to = j - (1 << step)
-        total[to] = total[to].astype(F32) + plane_step(total[j].astype(BF), step).astype(F32)
-    return total[0]
+    while len(chunks) > 1:
+        chunks = plane_add(chunks, plane_send(chunks))
+    return chunks[0]
 
 
 def plane_index():
@@ -454,26 +664,26 @@
     return plane_scatter([total[i * rows : (i + 1) * rows] for i in range(n_plane)])
 
 
-def token_scatter(left, product):
+def cores_pair(value):
     core = lax.axis_index("core")
-    rows = left.shape[0] // 2
-    theirs = core_swap(alone(product(part(left, 1 - core, rows, 0)).astype(BF)))
-    mine = alone(product(part(left, core, rows, 0)).astype(BF))
-    return (mine.astype(F32) + theirs.astype(F32)).astype(BF)
-
-
-def line_exchange(value):
-    core, line = lax.axis_index("core"), lax.axis_index("fsdp")
     kept = lax.dynamic_index_in_dim(value, core, 0, keepdims=False)
-    came = core_swap(lax.dynamic_index_in_dim(value, 1 - core, 0, keepdims=False))
-    pieces = []
-    for mask in range(lax.axis_size("fsdp")):
-        to = line ^ mask
-        pair = jnp.stack(
-            [lax.dynamic_index_in_dim(v, to, 0, keepdims=False) for v in (kept, came)]
-        )
-        pieces.append(pair if mask == 0 else line_swap(pair, mask))
-    return pieces
+    return kept, core_swap(lax.dynamic_index_in_dim(value, 1 - core, 0, keepdims=False))
+
+
+def lines_parts(pair):
+    line = lax.axis_index("fsdp")
+    return [
+        jnp.stack([lax.dynamic_index_in_dim(v, line ^ mask, 0, keepdims=False) for v in pair])
+        for mask in range(lax.axis_size("fsdp"))
+    ]
+
+
+def lines_swap(parts):
+    return parts[:1] + [line_swap(parts[mask], mask) for mask in range(1, len(parts))]
+
+
+def lines_pair(pair):
+    return lines_swap(lines_parts(pair))
 
 
 def line_rows(pieces):
@@ -508,93 +718,106 @@
     gain_second = norm_second.astype(F32)[:, None]
     projections = (query_weight, key_weight, value_weight)
 
-    gate_moved = line_exchange(fold_hidden(gate_weight, gain_second, n_plane, n_core, n_fsdp))
+    merge_rows = gather(merge_weight, "fsdp")
+    gate_moved = lines_pair(cores_pair(fold_hidden(gate_weight, gain_second, n_plane, n_core, n_fsdp)))
     own = exchange(fold_heads(projections, gain_first, n_ctx), CTX)
-    own = after(own, gate_moved)
+    x_pieces = ctx_gather(tokens)
+    up_pair = cores_pair(fold_hidden(up_weight, gain_second, n_plane, n_core, n_fsdp))
+    cosine, sine = rope_tables(length, cols)
+    own, gate_moved, x_pieces, up_pair, merge_rows = together(
+        (own, gate_moved, x_pieces, up_pair, merge_rows)
+    )
     qkv_weight = gather(own[:, None], "fsdp", axis=1).reshape(width, 3 * cols)
-    x_pieces = ctx_gather(tokens)
     gate_pieces = plane_gather(line_rows(gate_moved).reshape(d_rows, hid))
-    up_own = after(fold_hidden(up_weight, gain_second, n_plane, n_core, n_fsdp), qkv_weight)
-    up_moved = line_exchange(up_own)
-    merge_rows = gather(after(merge_weight, qkv_weight), "fsdp")
-    cot_all = gather(after(cotangent, merge_rows), TOK)
-    down_pieces = plane_gather(after(down_weight, x_pieces, gate_pieces))
-
-    cosine, sine = rope_tables(length, cols)
-    x_pieces, gate_pieces = lax.optimization_barrier((x_pieces, gate_pieces))
-    q, k, v, scale_all, attended = attention_forward(pairing, me, x_pieces, qkv_weight, cosine, sine)
+    down_pieces = plane_gather_more([down_weight])
     x_all = jnp.concatenate(x_pieces, axis=0)
+    x_all, gate_pieces, down_pieces = together((x_all, gate_pieces, down_pieces))
+    up_moved = lines_pair(up_pair)
+    cot_all = gather(cotangent, TOK)
+
+    q, k, v, scale_all, attended, lse = attention_forward(pairing, me, x_all, qkv_weight, cosine, sine)
+    while len(down_pieces) < n_plane:
+        down_pieces = plane_gather_more(down_pieces)
+    attended, down_pieces = together((attended, down_pieces))
+    gate_rows = place(gate_pieces, index).reshape(width, hid)
+    down_rows = place(down_pieces, index).reshape(hid, width)
     own_f = tokens.astype(F32)
-    theirs = alone(mm(attended[half:], merge_rows).astype(BF))
-    mine = alone(mm(attended[:half], merge_rows).astype(BF))
+    theirs = together(mm(attended[half:], merge_rows).astype(BF))
+    mine = together(mm(attended[:half], merge_rows).astype(BF))
     mixed = own_f + ctx_scatter(theirs, mine, n_plane)
+    mixed, up_moved = together((mixed, up_moved))
     up_pieces = plane_gather(line_rows(up_moved).reshape(d_rows, hid))
 
     scale_second = lax.rsqrt(jnp.mean(mixed * mixed, axis=-1, keepdims=True) + EPS)
     unit_second = mixed * scale_second
-    normed = after(unit_second.astype(BF), down_pieces)
-    normed_all = gather(normed, TOK)
-    gate_rows = place(gate_pieces, index).reshape(width, hid)
+    normed_all = gather(unit_second.astype(BF), TOK)
     up_rows = place(up_pieces, index).reshape(width, hid)
-    down_rows = place(down_pieces, index).reshape(hid, width)
-    gate = mm(normed_all, gate_rows)
-    up = mm(normed_all, up_rows)
-    sig = jax.nn.sigmoid(gate)
-    active = gate * sig
-    hidden = (active * up).astype(BF)
-    grad_hidden = mm_t(cot_all, down_rows)
-    grad_gate = (grad_hidden * up * sig * (1.0 + gate * (1.0 - sig))).astype(BF)
-    grad_up = (grad_hidden * active).astype(BF)
-    hidden, grad_gate, grad_up = lax.optimization_barrier((hidden, grad_gate, grad_up))
-    grad_gu = jnp.concatenate([grad_gate, grad_up], axis=1)
-    e_two = token_scatter(
-        grad_gu, lambda v: mm_t(v[:, :hid], gate_rows) + mm_t(v[:, hid:], up_rows)
-    )
-
-    hidden_w, gate_w, up_w = after((hidden, grad_gate, grad_up), e_two)
+    hidden, grad_gate, grad_up, theirs, mine = feed_forward(
+        normed_all, cot_all, gate_rows, up_rows, down_rows
+    )
+    lse_rows = lse[:, :8].T
+    e_two = (mine.astype(F32) + core_swap(theirs).astype(F32)).astype(BF)
+
     normed_w = [part(normed_all, at, d_rows, 1) for at in index]
-    down_chunks = [t_mm(part(hidden_w, at, piece, 1), cot_all).astype(BF) for at in index]
-    gate_chunks = [t_mm(rows_of, gate_w).astype(BF) for rows_of in normed_w]
-    up_chunks = [t_mm(rows_of, up_w).astype(BF) for rows_of in normed_w]
-    branch = token_scatter(hidden_w, lambda v: mm(v, down_rows))
-    down_chunks, gate_chunks, up_chunks, branch = lax.optimization_barrier(
-        (down_chunks, gate_chunks, up_chunks, branch)
-    )
+    gate_late = [together(t_mm(rows_of, grad_gate).astype(BF)) for rows_of in normed_w[n_plane // 2 :]]
+    hidden, grad_gate, grad_up, e_two = together((hidden, grad_gate, grad_up, e_two))
+    gate_chunks = [together(t_mm(rows_of, grad_gate).astype(BF)) for rows_of in normed_w[: n_plane // 2]]
+    gate_chunks += gate_late
+    gate_came = plane_send(gate_chunks)
+    up_chunks = [together(t_mm(rows_of, grad_up).astype(BF)) for rows_of in normed_w]
+    theirs, mine = branch_rows(hidden, down_rows)
+    gate_chunks, gate_came, up_chunks, theirs, mine, lse_rows = together(
+        (gate_chunks, gate_came, up_chunks, theirs, mine, lse_rows)
+    )
+    gate_sum = plane_scatter(plane_add(gate_chunks, gate_came))
+    branch = (mine.astype(F32) + core_swap(theirs).astype(F32)).astype(BF)
     e_two = scatter(e_two, "fsdp")
-    branch_sum = scatter(after(branch, e_two), "fsdp").astype(F32)
-    layer_output = (mixed + branch_sum).astype(BF)
-    gate_sum = plane_scatter(gate_chunks).astype(BF).reshape(n_core, n_fsdp, dev_rows, hid)
-    gate_back = line_exchange(gate_sum)
-    up_sum = plane_scatter(up_chunks).astype(BF).reshape(n_core, n_fsdp, dev_rows, hid)
-    up_back = line_exchange(up_sum)
-    down_grad = plane_scatter(down_chunks).astype(F32)
-    gate_grad, second_gate = unfold_hidden(gate_back, gate_weight, gain_second, n_plane)
-    up_grad, second_up = unfold_hidden(up_back, up_weight, gain_second, n_plane)
-    second_grad = (second_gate + second_up)[:, 0]
-
-    e_two = after(e_two, gate_chunks, up_chunks, down_chunks, branch).astype(F32)
+    e_two, gate_sum, up_chunks, branch = together((e_two, gate_sum, up_chunks, branch))
+    branch_sum = scatter(branch, "fsdp")
+    gate_parts = lines_parts(cores_pair(gate_sum.reshape(n_core, n_fsdp, dev_rows, hid)))
+    e_two_f = e_two.astype(F32)
     grad_mixed = cotangent.astype(F32) + scale_second * (
-        e_two - unit_second * jnp.mean(e_two * unit_second, axis=-1, keepdims=True)
+        e_two_f - unit_second * jnp.mean(e_two_f * unit_second, axis=-1, keepdims=True)
     )
     branch_pieces = ctx_gather(grad_mixed.astype(BF))
+    gate_back = lines_swap(gate_parts)
+
+    branch_pieces, up_chunks = together((branch_pieces, up_chunks))
+    up_came = plane_send(up_chunks)
     grad_qkv, grad_scaled = attention_backward(
-        pairing, me, branch_pieces, merge_rows, q, k, v, scale_all, cosine, sine
-    )
-    sums = t_mm(x_all, grad_scaled).astype(BF).reshape(n_ctx, n_fsdp, dev_rows, 3 * cols)
-    sums = scatter(sums.transpose(1, 0, 2, 3).reshape(width, 3 * cols), "fsdp")
-    branch_all = jnp.concatenate(branch_pieces, axis=0)
-    merge_grad = t_mm(attended, branch_all).astype(BF)
-    merge_grad = scatter(after(merge_grad, sums), "fsdp").astype(F32)
-    theirs = alone(mm_t(grad_qkv[half:], qkv_weight).astype(BF))
-    mine = alone(mm_t(grad_qkv[:half], qkv_weight).astype(BF))
+        pairing, me, branch_pieces, merge_rows, q, k, v, scale_all, attended, lse_rows, cosine, sine
+    )
+    sums = heads_term(x_all, grad_scaled, n_ctx, n_fsdp)
+    grad_qkv, up_chunks, up_came, gate_back, sums, attended, branch_sum = together(
+        (grad_qkv, up_chunks, up_came, gate_back, sums, attended, branch_sum)
+    )
+    sums = scatter(sums, "fsdp")
+    up_sum = plane_scatter(plane_add(up_chunks, up_came))
+    attended, up_sum = together((attended, up_sum))
+    merge_grad = scatter(merge_term(attended, branch_pieces), "fsdp")
+    layer_output = (mixed + branch_sum.astype(F32)).astype(BF)
+    theirs = back_rows(grad_qkv, qkv_weight, 1)
+    mine = back_rows(grad_qkv, qkv_weight, 0)
     e_one = ctx_scatter(theirs, mine, n_plane)
+    up_parts = lines_parts(cores_pair(up_sum.reshape(n_core, n_fsdp, dev_rows, hid)))
+    hidden, mine = together((hidden, mine))
+    down_chunks = [together(t_mm(part(hidden, at, piece, 1), cot_all).astype(BF)) for at in index]
+    e_one, down_chunks = together((e_one, down_chunks))
+    down_came = plane_send(down_chunks)
+    sums, up_parts = together((sums, up_parts))
+    up_back = lines_swap(up_parts)
+    sums = exchange(sums.reshape(n_ctx, dev_rows, 3 * cols), CTX)
+    sums, up_back, merge_grad = together((sums, up_back, merge_grad))
     scale_first = lax.rsqrt(jnp.mean(own_f * own_f, axis=-1, keepdims=True) + EPS)
     unit_first = own_f * scale_first
     input_grad = (
         grad_mixed
         + scale_first * (e_one - unit_first * jnp.mean(e_one * unit_first, axis=-1, keepdims=True))
     ).astype(BF)
-    sums = exchange(sums.reshape(n_ctx, dev_rows, 3 * cols), CTX)
+    down_grad = plane_scatter(plane_add(down_chunks, down_came)).astype(F32)
+    gate_grad, second_gate = unfold_hidden(gate_back, gate_weight, gain_second, n_plane)
+    up_grad, second_up = unfold_hidden(up_back, up_weight, gain_second, n_plane)
+    second_grad = (second_gate + second_up)[:, 0]
     query_grad, key_grad, value_grad, first_grad = unfold_heads(sums, projections, gain_first)
     return (
         layer_output.reshape(1, rows, width),
@@ -602,7 +825,7 @@
         query_grad,
         key_grad,
         value_grad,
-        merge_grad,
+        merge_grad.astype(F32),
         gate_grad,
         up_grad,
         down_grad,

time: 692 us -> 536 us (0.77)
  waiting for transfers between devices: 341 us -> 199 us
  matrix products: 102 us -> 37.6 us
  Pallas kernels: 74.8 us -> 137 us
  starting transfers between devices: 71.5 us -> 64.2 us
    pallas_call x0 -> x6, Pallas kernels: none -> 64.8 us  [the longest x1 31 us: feed_forward(): pl.pallas_call(feed_forward_kernel, grid_spec=pltpu.PrefetchScalarGridSpe...]
    ppermute x30, waiting for transfers between devices: 184 us -> 132 us  [plane_step(): lax.ppermute(value, CTX, [(i, i ^ 2 * steps[i % 2][step]) for i in range(...]
    ppermute x12, waiting for transfers between devices: 92.6 us -> 52.3 us  [line_swap(): return lax.ppermute(value, 'fsdp', [(i, i ^ mask) for i in range(n)])]
    all_gather x4, waiting for transfers between devices: 36.6 us -> 0.03 us  [gather(): return lax.all_gather(value, axes, axis=axis, tiled=True)]
    dot_general x7 -> x0, matrix products: 31.8 us -> none  [mm_t(): lax.dot_general(left, right, (((1,), (1,)), ((), ())), preferred_element_...]
    dot_general x6 -> x2, matrix products: 30.7 us -> 2.38 us  [mm(): return jnp.dot(left, right, preferred_element_type=F32)]
    all_to_all x2, waiting for transfers between devices: 13.3 us -> 0.01 us  [exchange(): return lax.all_to_all(value, axes, split_axis=0, concat_axis=0, tiled=True)]
    ppermute x30, starting transfers between devices: 44.2 us -> 34.7 us  [plane_step(): lax.ppermute(value, CTX, [(i, i ^ 2 * steps[i % 2][step]) for i in range(...]
  transfers between devices with their start and end apart: 68 -> 68, of which waited for: 32 -> 29; matrix products, arithmetic and copies ran while one was open for 17% -> 20% of each run, Pallas kernels for 7% -> 19%
where the time goes in v3:
time: 536 us; the launch traced here: 530 us
  waiting for transfers between devices  199 us (37%)
  Pallas kernels  137 us (26%)
  starting transfers between devices  64.2 us (12%)
  other arithmetic  38.6 us (7%)
  local copies, waits for them, and re-layouts  38 us (7%)
  matrix products  37.6 us (7%)
  between operations  15.2 us (3%)
    ppermute x30, waiting for transfers between devices, plane_step(): lax.ppermute(value, CTX, [(i, i ^ 2 * steps[i % 2][step]) for i in range(...  132 us
    ppermute x12, waiting for transfers between devices, line_swap(): return lax.ppermute(value, 'fsdp', [(i, i ^ mask) for i in range(n)])  52.3 us
    dot_general x12, matrix products, t_mm(): lax.dot_general(left, right, (((0,), (0,)), ((), ())), preferred_element_...  35.2 us
    ppermute x30, starting transfers between devices, plane_step(): lax.ppermute(value, CTX, [(i, i ^ 2 * steps[i % 2][step]) for i in range(...  34.7 us
    pallas_call x1, Pallas kernels, feed_forward(): pl.pallas_call(feed_forward_kernel, grid_spec=pltpu.PrefetchScalarGridSpe...  31 us
    pallas_call x1, Pallas kernels, attention_backward(): pl.pallas_call(functools.partial(backward_kernel, n_ctx, 256), out_shape=...  20.4 us
    pallas_call x5, Pallas kernels, place(): pl.pallas_call(place_kernel, out_shape=jax.ShapeDtypeStruct((n,) + pieces...  18.1 us
    pallas_call x1, Pallas kernels, attention_forward(): pl.pallas_call(functools.partial(forward_kernel, n_ctx, 256), out_shape=[...  16.6 us
  transfers between devices with their start and end apart: 68, of which 29 were waited for; matrix products, arithmetic and copies ran while one was open for 20% of the time, Pallas kernels for 19%

profile of v3, /device:TPU:18, one launch (start us, length us, event | category | flops | bytes accessed | tf_op | source)
XLA Modules:
  0.0 529.7 jit_solution(14335532381294103160)
XLA Ops:
  21.2 4.0 all-to-all-start
  35.3 9.7 %collective-permute-done.1 = bf16[2,64,1024]{2,1,0:T(8,128)(2,1)S(1)} collective-permute-done((bf16[2,64,1024]{2,1,0:T(8,128)(2,1)S(1)}, bf16[2,64,1024]{2,1,0:T(8,128)(2,1)S(1)}, u32[]{:S(2)}, u32[]{:S(2)}) %collective-permute-start.1) | collective-permute-done | bytes 262176 | tf_op jit(solution)/shard_map/ppermute | solution.py:615
  48.2 13.3 %collective-permute-done.3 = bf16[2,64,1024]{2,1,0:T(8,128)(2,1)} collective-permute-done((bf16[2,64,1024]{2,1,0:T(8,128)(2,1)}, bf16[2,64,1024]{2,1,0:T(8,128)(2,1)}, u32[]{:S(2)}, u32[]{:S(2)}) %collective-permute-start.3) | collective-permute-done | bytes 262176 | tf_op jit(solution)/shard_map/ppermute | solution.py:615
  70.3 2.7 collective-permute-start.13
  77.5 15.7 %collective-permute-done.12.refs_1_ = bf16[512,1024]{1,0:T(8,128)(2,1)S(1)} collective-permute-done((bf16[512,1024]{1,0:T(8,128)(2,1)}, bf16[512,1024]{1,0:T(8,128)(2,1)S(1)}, u32[]{:S(2)}, u32[]{:S(2)}) %collective-permute-start.12) | collective-permute-done | bytes 1048608 | tf_op jit(solution)/shard_map/ppermute | solution.py:610
  93.2 3.7 collective-permute-start.14
  105.4 10.4 %collective-permute-done.15.refs_1_ = bf16[256,2048]{1,0:T(8,128)(2,1)} collective-permute-done((bf16[256,2048]{1,0:T(8,128)(2,1)}, bf16[256,2048]{1,0:T(8,128)(2,1)}, u32[]{:S(2)}, u32[]{:S(2)}) %collective-permute-start.15) | collective-permute-done | bytes 1048608 | tf_op jit(solution)/shard_map/ppermute | solution.py:610
  116.8 3.7 collective-permute-start.16
  125.9 16.6 %attention_forward.1 = (bf16[1024,256]{1,0:T(8,128)(2,1)}, bf16[1024,256]{1,0:T(8,128)(2,1)}, bf16[1024,256]{1,0:T(8,128)(2,1)}, f32[1024,1]{1,0:T(8,128)}, bf16...) custom-call(s32[1,8]{1,0:T(1,128)} %pair_ref.3, s32[2]{0:T(128)} %pad_add_fusion.me_ref, ...), custom_call_target="tpu_custom_call" | custom-call | flops 1024 | bytes 1024 | tf_op jit(solution)/shard_map/attention_forward/pallas_call | solution.py:155
  147.3 3.4 collective-permute-done.18
  153.8 7.1 %collective-permute-done.20 = bf16[128,2048]{1,0:T(8,128)(2,1)S(1)} collective-permute-done((bf16[128,2048]{1,0:T(8,128)(2,1)S(1)}, bf16[128,2048]{1,0:T(8,128)(2,1)S(1)}, u32[]{:S(2)}, u32[]{:S(2)}) %collective-permute-start.20) | collective-permute-done | bytes 524320 | tf_op jit(solution)/shard_map/ppermute | solution.py:610
  165.4 4.2 collective-permute-done.19
  171.7 8.3 %collective-permute-done.22 = bf16[2,64,1024]{2,1,0:T(8,128)(2,1)S(1)} collective-permute-done((bf16[2,64,1024]{2,1,0:T(8,128)(2,1)S(1)}, bf16[2,64,1024]{2,1,0:T(8,128)(2,1)S(1)}, u32[]{:S(2)}, u32[]{:S(2)}) %collective-permute-start.22) | collective-permute-done | bytes 262176 | tf_op jit(solution)/shard_map/ppermute | solution.py:615
  181.3 11.2 %collective-permute-done.24 = bf16[2,64,1024]{2,1,0:T(8,128)(2,1)S(1)} collective-permute-done((bf16[2,64,1024]{2,1,0:T(8,128)(2,1)S(1)}, bf16[2,64,1024]{2,1,0:T(8,128)(2,1)S(1)}, u32[]{:S(2)}, u32[]{:S(2)}) %collective-permute-start.24) | collective-permute-done | bytes 262176 | tf_op jit(solution)/shard_map/ppermute | solution.py:615
  201.2 24.1 %collective-permute-done.25.refs_1_ = bf16[512,1024]{1,0:T(8,128)(2,1)S(1)} collective-permute-done((bf16[512,1024]{1,0:T(8,128)(2,1)}, bf16[512,1024]{1,0:T(8,128)(2,1)S(1)}, u32[]{:S(2)}, u32[]{:S(2)}) %collective-permute-start.25) | collective-permute-done | bytes 1048608 | tf_op jit(solution)/shard_map/ppermute | solution.py:610
  226.8 4.4 place.6
  231.2 4.5 place.9
  235.7 4.5 collective-permute-done.27.refs_3_
  240.2 4.5 place.8
  244.7 31.0 %feed_forward.1 = (bf16[1024,1024]{1,0:T(8,128)(2,1)}, bf16[1024,1024]{1,0:T(8,128)(2,1)}, bf16[1024,1024]{1,0:T(8,128)(2,1)}, bf16[512,2048]{1,0:T(8,128)(2,1)}, bf16[512,2048]{1,0:T(8,128)(2,1)}) custom-call(s32[1]{0:T(128)} %bitcast.2.core_ref, bf16[1024,2048]{1,0:T(8,128)(2,1)} %all-gather.9.cloned.1.call-done.n_ref, bf16[1024,2048]{1,0:T(8,128)(2,1)} %bitcast.155, ...), custom_call_target="tpu_custom_call" | custom-call | flops 1024 | bytes 1024 | tf_op jit(solution)/shard_map/feed_forward/pallas_call | solution.py:302
  279.2 4.4 convolution_convert_fusion.10
  283.5 3.6 convolution_convert_fusion.11
  292.9 3.6 convolution_convert_fusion.6
  301.2 9.2 %branch_rows.1 = (bf16[512,2048]{1,0:T(8,128)(2,1)}, bf16[512,2048]{1,0:T(8,128)(2,1)}) custom-call(s32[1]{0:T(128)} %bitcast.2.core_ref, bf16[1024,1024]{1,0:T(8,128)(2,1)} %get-tuple-element.216.h_ref, bf16[1024,2048]{1,0:T(8,128)(2,1)} %bitcast.136), custom_call_target="tpu_custom_call" | custom-call | flops 1024 | bytes 1024 | tf_op jit(solution)/shard_map/branch_rows/pallas_call | solution.py:346
  310.4 2.9 convolution_convert_fusion.12
  320.1 14.5 %collective-permute-done.31 = bf16[512,1024]{1,0:T(8,128)(2,1)S(1)} collective-permute-done((bf16[512,1024]{1,0:T(8,128)(2,1)S(1)}, bf16[512,1024]{1,0:T(8,128)(2,1)S(1)}, u32[]{:S(2)}, u32[]{:S(2)}) %collective-permute-start.31) | collective-permute-done | bytes 1048608 | tf_op jit(solution)/shard_map/ppermute | solution.py:610
  341.6 12.8 %collective-permute-done.33.refs_1_ = bf16[128,2048]{1,0:T(8,128)(2,1)S(1)} collective-permute-done((bf16[128,2048]{1,0:T(8,128)(2,1)S(1)}, bf16[128,2048]{1,0:T(8,128)(2,1)S(1)}, u32[]{:S(2)}, u32[]{:S(2)}) %collective-permute-start.33) | collective-permute-done | bytes 524320 | tf_op jit(solution)/shard_map/ppermute | solution.py:610
  356.1 7.5 %collective-permute-done.35.refs_3_ = bf16[128,2048]{1,0:T(8,128)(2,1)S(1)} collective-permute-done((bf16[128,2048]{1,0:T(8,128)(2,1)S(1)}, bf16[128,2048]{1,0:T(8,128)(2,1)S(1)}, u32[]{:S(2)}, u32[]{:S(2)}) %collective-permute-start.35) | collective-permute-done | bytes 524320 | tf_op jit(solution)/shard_map/ppermute | solution.py:610
  367.8 3.3 collective-permute-start.44
  372.2 20.4 %attention_backward.1 = (bf16[1024,768]{1,0:T(8,128)(2,1)}, bf16[1024,768]{1,0:T(8,128)(2,1)}) custom-call(s32[1,8]{1,0:T(1,128)} %pair_ref.3, s32[2]{0:T(128)} %pad_add_fusion.me_ref, bf16[128,2048]{1,0:T(8,128)(2,1)} %copy-done.10, bf16[128,2048]{1,0:T(8,128)(2,1)} %copy-done.22, bf16[128,2048]{1,0:T(8,128)(2,1)} %copy-done.23, ...), custom_call_target="tpu_custom_call" | custom-call | flops 1024 | bytes 1024 | tf_op jit(solution)/shard_map/attention_backward/pallas_call | solution.py:248
  392.6 9.2 %heads_term.1 = bf16[4,8,64,768]{3,2,1,0:T(8,128)(2,1)} custom-call(bf16[1024,2048]{1,0:T(8,128)(2,1)} %constant_dynamic-update-slice_fusion.x_ref, bf16[1024,768]{1,0:T(8,128)(2,1)} %get-tuple-element.212.g_ref), custom_call_target="tpu_custom_call" | custom-call | flops 1024 | bytes 1024 | tf_op jit(solution)/shard_map/heads_term/pallas_call | solution.py:404
  402.1 5.1 back_rows.3
  407.3 5.7 %back_rows.2 = bf16[512,2048]{1,0:T(8,128)(2,1)} custom-call(bf16[1024,768]{1,0:T(8,128)(2,1)} %get-tuple-element.215.g_ref, bf16[2048,768]{1,0:T(8,128)(2,1)} %bitcast.139), custom_call_target="tpu_custom_call" | custom-call | flops 1024 | bytes 1024 | tf_op jit(solution)/shard_map/back_rows/pallas_call | solution.py:429
  415.3 4.7 convolution_convert_fusion.2
  429.3 5.5 %collective-permute-done.48 = bf16[128,2048]{1,0:T(8,128)(2,1)S(1)} collective-permute-done((bf16[128,2048]{1,0:T(8,128)(2,1)S(1)}, bf16[128,2048]{1,0:T(8,128)(2,1)S(1)}, u32[]{:S(2)}, u32[]{:S(2)}) %collective-permute-start.48) | collective-permute-done | bytes 524320 | tf_op jit(solution)/shard_map/ppermute | solution.py:610
  439.6 2.8 collective-permute-done.47
  442.4 4.2 collective-permute-done.49
  449.6 3.4 unfold_hidden.2
  453.0 4.6 merge_term.1
  462.0 2.6 add_convert_fusion.5
  466.1 6.1 %all-to-all-start.1 = ((bf16[8,64,768]{2,1,0:T(8,128)(2,1)}), bf16[8,64,768]{2,1,0:T(8,128)(2,1)}, u32[]{:S(2)}, u32[]{:S(2)}) async-start(bf16[8,64,768]{2,1,0:T(8,128)(2,1)} %bitcast.160), calls=%async_computation.4 | async-start | bytes 1572864 | tf_op jit(solution)/shard_map/all_to_all | solution.py:595
  478.2 7.3 %collective-permute-done.55 = bf16[256,2048]{1,0:T(8,128)(2,1)} collective-permute-done((bf16[256,2048]{1,0:T(8,128)(2,1)}, bf16[256,2048]{1,0:T(8,128)(2,1)}, u32[]{:S(2)}, u32[]{:S(2)}) %collective-permute-start.55) | collective-permute-done | bytes 1048608 | tf_op jit(solution)/shard_map/ppermute | solution.py:610
  485.5 5.0 collective-permute-done.57
  490.5 3.4 fusion.9
  493.9 10.0 %reduce-scatter.11.cloned.1.call-done = bf16[64,2048]{1,0:T(8,128)(2,1)} async-done(((bf16[256,2048]{1,0:T(8,128)(2,1)}), bf16[64,2048]{1,0:T(8,128)(2,1)}) %reduce-scatter.11.cloned.1.call-update) | async-done | bytes 262160 | tf_op jit(solution)/shard_map/reduce_scatter | solution.py:591
  503.9 7.9 %collective-permute-done.54.refs_3_ = bf16[2,64,1024]{2,1,0:T(8,128)(2,1)S(1)} collective-permute-done((bf16[2,64,1024]{2,1,0:T(8,128)(2,1)S(1)}, bf16[2,64,1024]{2,1,0:T(8,128)(2,1)S(1)}, u32[]{:S(2)}, u32[]{:S(2)}) %collective-permute-start.54) | collective-permute-done | bytes 262176 | tf_op jit(solution)/shard_map/ppermute | solution.py:615
  513.7 2.7 unfold_heads.1
  517.8 3.4 unfold_hidden.3
  (311 shorter events, 151.8 us)
Async XLA Ops:
  7.2 54.3 %all-gather.7.cloned.1.call-start = ((), (), s32[]{:S(2)}) async-start(), calls=%async_computation.6 | async-start | bytes 1310720 | tf_op jit(solution)/shard_map/all_gather | solution.py:587
  13.6 16.4 %collective-permute-start = (bf16[4,64,1024]{2,1,0:T(8,128)(2,1)}, bf16[4,64,1024]{2,1,0:T(8,128)(2,1)}, u32[]{:S(2)}, u32[]{:S(2)}) collective-permute-start(bf16[4,64,1024]{2,1,0:T(8,128)(2,1)} %dynamic-slice_bitcast_fusion.4), channel_id=1, source_target_pairs={{0,4},{4,0},{8,12},{12,8},{16,20},{20,16},{24,28},{28,24},{1,5},{5... | collective-permute-start | bytes 1572872 | tf_op jit(solution)/shard_map/ppermute | solution.py:604
  14.1 18.8 %collective-permute-start.7 = (bf16[128,2048]{1,0:T(8,128)(2,1)S(1)}, bf16[128,2048]{1,0:T(8,128)(2,1)}, u32[]{:S(2)}, u32[]{:S(2)}) collective-permute-start(bf16[128,2048]{1,0:T(8,128)(2,1)S(1)} %bitcast.144), channel_id=1, source_target_pairs={{0,4},{4,0},{8,12},{12,8},{16,20},{20,16},{24,28},{28,24},{1,5},{5... | collective-permute-start | bytes 1572872 | tf_op jit(solution)/shard_map/ppermute | solution.py:604
  14.2 18.8 %collective-permute-start.5 = (bf16[128,2048]{1,0:T(8,128)(2,1)S(1)}, bf16[128,2048]{1,0:T(8,128)(2,1)}, u32[]{:S(2)}, u32[]{:S(2)}) collective-permute-start(bf16[128,2048]{1,0:T(8,128)(2,1)S(1)} %bitcast.145), channel_id=1, source_target_pairs={{0,16},{4,12},{8,24},{12,4},{16,0},{20,28},{24,8},{28,20},{1,17},{... | collective-permute-start | bytes 1572872 | tf_op jit(solution)/shard_map/ppermute | solution.py:610
  16.8 16.6 %collective-permute-start.6 = (bf16[128,2048]{1,0:T(8,128)(2,1)}, bf16[128,2048]{1,0:T(8,128)(2,1)}, u32[]{:S(2)}, u32[]{:S(2)}) collective-permute-start(bf16[128,2048]{1,0:T(8,128)(2,1)} %collective-permute-done.4), channel_id=1, source_target_pairs={{0,16},{4,12},{8,24},{12,4},{16,0},{20,28},{24,8},{28,20},{1,17},{... | collective-permute-start | bytes 1572872 | tf_op jit(solution)/shard_map/ppermute | solution.py:610
  21.2 26.4 %all-to-all-start = ((bf16[8,64,768]{2,1,0:T(8,128)(2,1)}), bf16[8,64,768]{2,1,0:T(8,128)(2,1)S(1)}, u32[]{:S(2)}, u32[]{:S(2)}) async-start(bf16[8,64,768]{2,1,0:T(8,128)(2,1)} %fold_heads.1), calls=%async_computation | async-start | bytes 1572864 | tf_op jit(solution)/shard_map/all_to_all | solution.py:595
  25.2 100.7 %all-gather.11.cloned.1.call-start = ((), (), s32[]{:S(2)}) async-start(), calls=%async_computation.12 | async-start | bytes 3932160 | tf_op jit(solution)/shard_map/all_gather | solution.py:587
  32.9 28.6 %collective-permute-start.8 = (bf16[128,2048]{1,0:T(8,128)(2,1)}, bf16[128,2048]{1,0:T(8,128)(2,1)S(1)}, u32[]{:S(2)}, u32[]{:S(2)}) collective-permute-start(bf16[128,2048]{1,0:T(8,128)(2,1)} %collective-permute-done.4), channel_id=1, source_target_pairs={{0,4},{4,0},{8,12},{12,8},{16,20},{20,16},{24,28},{28,24},{1,5},{5... | collective-permute-start | bytes 1572872 | tf_op jit(solution)/shard_map/ppermute | solution.py:604
  33.0 28.5 %collective-permute-start.9 = (bf16[128,2048]{1,0:T(8,128)(2,1)}, bf16[128,2048]{1,0:T(8,128)(2,1)}, u32[]{:S(2)}, u32[]{:S(2)}) collective-permute-start(bf16[128,2048]{1,0:T(8,128)(2,1)} %collective-permute-done.5), channel_id=1, source_target_pairs={{0,4},{4,0},{8,12},{12,8},{16,20},{20,16},{24,28},{28,24},{1,5},{5... | collective-permute-start | bytes 1572872 | tf_op jit(solution)/shard_map/ppermute | solution.py:604
  33.4 28.1 %collective-permute-start.10 = (bf16[128,2048]{1,0:T(8,128)(2,1)}, bf16[128,2048]{1,0:T(8,128)(2,1)}, u32[]{:S(2)}, u32[]{:S(2)}) collective-permute-start(bf16[128,2048]{1,0:T(8,128)(2,1)} %collective-permute-done.6), channel_id=1, source_target_pairs={{0,4},{4,0},{8,12},{12,8},{16,20},{20,16},{24,28},{28,24},{1,5},{5... | collective-permute-start | bytes 1572872 | tf_op jit(solution)/shard_map/ppermute | solution.py:604
  45.0 16.5 %collective-permute-start.3 = (bf16[2,64,1024]{2,1,0:T(8,128)(2,1)}, bf16[2,64,1024]{2,1,0:T(8,128)(2,1)}, u32[]{:S(2)}, u32[]{:S(2)}) collective-permute-start(bf16[2,64,1024]{2,1,0:T(8,128)(2,1)} %pad_maximum_fusion.3), channel_id=1, source_target_pairs={{0,3},{1,2},{2,1},{3,0},{4,7},{5,6},{6,5},{7,4},{8,11},{9,10},{10,... | collective-permute-start | bytes 786440 | tf_op jit(solution)/shard_map/ppermute | solution.py:615
  61.5 183.1 %all-gather.13.cloned.1.call-start = ((), (), s32[]{:S(2)}) async-start(), calls=%async_computation.13 | async-start | bytes 4718592 | tf_op jit(solution)/shard_map/all_gather | solution.py:587
  68.2 25.0 %collective-permute-start.12 = (bf16[512,1024]{1,0:T(8,128)(2,1)}, bf16[512,1024]{1,0:T(8,128)(2,1)S(1)}, u32[]{:S(2)}, u32[]{:S(2)}) collective-permute-start(bf16[512,1024]{1,0:T(8,128)(2,1)} %bitcast.147), channel_id=1, source_target_pairs={{0,8},{4,20},{8,0},{12,28},{16,24},{20,4},{24,16},{28,12},{1,9},{5... | collective-permute-start | bytes 3145736 | tf_op jit(solution)/shard_map/ppermute | solution.py:610
  68.9 46.9 %collective-permute-start.15 = (bf16[256,2048]{1,0:T(8,128)(2,1)}, bf16[256,2048]{1,0:T(8,128)(2,1)}, u32[]{:S(2)}, u32[]{:S(2)}) collective-permute-start(bf16[256,2048]{1,0:T(8,128)(2,1)} %refs_0_), channel_id=1, source_target_pairs={{0,8},{4,20},{8,0},{12,28},{16,24},{20,4},{24,16},{28,12},{1,9},{5... | collective-permute-start | bytes 3145736 | tf_op jit(solution)/shard_map/ppermute | solution.py:610
  70.3 45.6 %collective-permute-start.13 = (bf16[512,1024]{1,0:T(8,128)(2,1)}, bf16[512,1024]{1,0:T(8,128)(2,1)S(1)}, u32[]{:S(2)}, u32[]{:S(2)}) collective-permute-start(bf16[512,1024]{1,0:T(8,128)(2,1)} %bitcast.148), channel_id=1, source_target_pairs={{0,16},{4,12},{8,24},{12,4},{16,0},{20,28},{24,8},{28,20},{1,17},{... | collective-permute-start | bytes 3145736 | tf_op jit(solution)/shard_map/ppermute | solution.py:610
  93.2 23.4 %collective-permute-start.14 = (bf16[512,1024]{1,0:T(8,128)(2,1)S(1)}, bf16[512,1024]{1,0:T(8,128)(2,1)S(1)}, u32[]{:S(2)}, u32[]{:S(2)}) collective-permute-start(bf16[512,1024]{1,0:T(8,128)(2,1)S(1)} %collective-permute-done.12.refs_1_), channel_id=1, source_target_pairs={{0,16},{4,12},{8,24},{12,4},{16,0},{20,28},{24,8},{28,20},{1,17},{... | collective-permute-start | bytes 3145736 | tf_op jit(solution)/shard_map/ppermute | solution.py:610
  116.8 25.7 %collective-permute-start.16 = (bf16[256,2048]{1,0:T(8,128)(2,1)}, bf16[256,2048]{1,0:T(8,128)(2,1)}, u32[]{:S(2)}, u32[]{:S(2)}) collective-permute-start(bf16[256,2048]{1,0:T(8,128)(2,1)} %refs_0_), channel_id=1, source_target_pairs={{0,16},{4,12},{8,24},{12,4},{16,0},{20,28},{24,8},{28,20},{1,17},{... | collective-permute-start | bytes 3145736 | tf_op jit(solution)/shard_map/ppermute | solution.py:610
  120.5 24.3 %collective-permute-start.17 = (bf16[256,2048]{1,0:T(8,128)(2,1)}, bf16[256,2048]{1,0:T(8,128)(2,1)}, u32[]{:S(2)}, u32[]{:S(2)}) collective-permute-start(bf16[256,2048]{1,0:T(8,128)(2,1)} %collective-permute-done.15.refs_1_), channel_id=1, source_target_pairs={{0,16},{4,12},{8,24},{12,4},{16,0},{20,28},{24,8},{28,20},{1,17},{... | collective-permute-start | bytes 3145736 | tf_op jit(solution)/shard_map/ppermute | solution.py:610
  121.5 123.2 %all-gather.9.cloned.1.call-start = ((), (), s32[]{:S(2)}) async-start(), calls=%async_computation.7 | async-start | bytes 4718592 | tf_op jit(solution)/shard_map/all_gather | solution.py:587
  153.7 16.0 %collective-permute-start.19 = (bf16[128,2048]{1,0:T(8,128)(2,1)S(1)}, bf16[128,2048]{1,0:T(8,128)(2,1)S(1)}, u32[]{:S(2)}, u32[]{:S(2)}) collective-permute-start(bf16[128,2048]{1,0:T(8,128)(2,1)S(1)} %get-tuple-element.255), channel_id=1, source_target_pairs={{0,16},{4,12},{8,24},{12,4},{16,0},{20,28},{24,8},{28,20},{1,17},{... | collective-permute-start | bytes 1572872 | tf_op jit(solution)/shard_map/ppermute | solution.py:610
  161.7 18.3 %collective-permute-start.22 = (bf16[2,64,1024]{2,1,0:T(8,128)(2,1)S(1)}, bf16[2,64,1024]{2,1,0:T(8,128)(2,1)S(1)}, u32[]{:S(2)}, u32[]{:S(2)}) collective-permute-start(bf16[2,64,1024]{2,1,0:T(8,128)(2,1)S(1)} %pad_maximum_fusion.7), channel_id=1, source_target_pairs={{0,1},{1,0},{2,3},{3,2},{4,5},{5,4},{6,7},{7,6},{8,9},{9,8},{10,11... | collective-permute-start | bytes 786440 | tf_op jit(solution)/shard_map/ppermute | solution.py:615
  161.8 19.6 %collective-permute-start.23 = (bf16[2,64,1024]{2,1,0:T(8,128)(2,1)S(1)}, bf16[2,64,1024]{2,1,0:T(8,128)(2,1)S(1)}, u32[]{:S(2)}, u32[]{:S(2)}) collective-permute-start(bf16[2,64,1024]{2,1,0:T(8,128)(2,1)S(1)} %pad_maximum_fusion.8), channel_id=1, source_target_pairs={{0,2},{1,3},{2,0},{3,1},{4,6},{5,7},{6,4},{7,5},{8,10},{9,11},{10,... | collective-permute-start | bytes 786440 | tf_op jit(solution)/shard_map/ppermute | solution.py:615
  163.2 29.3 %collective-permute-start.24 = (bf16[2,64,1024]{2,1,0:T(8,128)(2,1)S(1)}, bf16[2,64,1024]{2,1,0:T(8,128)(2,1)S(1)}, u32[]{:S(2)}, u32[]{:S(2)}) collective-permute-start(bf16[2,64,1024]{2,1,0:T(8,128)(2,1)S(1)} %pad_maximum_fusion.9), channel_id=1, source_target_pairs={{0,3},{1,2},{2,1},{3,0},{4,7},{5,6},{6,5},{7,4},{8,11},{9,10},{10,... | collective-permute-start | bytes 786440 | tf_op jit(solution)/shard_map/ppermute | solution.py:615
  193.6 144.9 %reduce-scatter.5.cloned.1.call-start = ((), (), s32[]{:S(2)}) async-start(), calls=%async_computation.8 | async-start | bytes 2621440 | tf_op jit(solution)/shard_map/reduce_scatter | solution.py:591
  199.1 26.2 %collective-permute-start.25 = (bf16[512,1024]{1,0:T(8,128)(2,1)}, bf16[512,1024]{1,0:T(8,128)(2,1)S(1)}, u32[]{:S(2)}, u32[]{:S(2)}) collective-permute-start(bf16[512,1024]{1,0:T(8,128)(2,1)} %bitcast.150), channel_id=1, source_target_pairs={{0,8},{4,20},{8,0},{12,28},{16,24},{20,4},{24,16},{28,12},{1,9},{5... | collective-permute-start | bytes 3145736 | tf_op jit(solution)/shard_map/ppermute | solution.py:610
  199.7 36.0 %collective-permute-start.26 = (bf16[512,1024]{1,0:T(8,128)(2,1)}, bf16[512,1024]{1,0:T(8,128)(2,1)S(1)}, u32[]{:S(2)}, u32[]{:S(2)}) collective-permute-start(bf16[512,1024]{1,0:T(8,128)(2,1)} %bitcast.151), channel_id=1, source_target_pairs={{0,16},{4,12},{8,24},{12,4},{16,0},{20,28},{24,8},{28,20},{1,17},{... | collective-permute-start | bytes 3145736 | tf_op jit(solution)/shard_map/ppermute | solution.py:610
  225.3 14.9 %collective-permute-start.27 = (bf16[512,1024]{1,0:T(8,128)(2,1)S(1)}, bf16[512,1024]{1,0:T(8,128)(2,1)}, u32[]{:S(2)}, u32[]{:S(2)}) collective-permute-start(bf16[512,1024]{1,0:T(8,128)(2,1)S(1)} %collective-permute-done.25.refs_1_), channel_id=1, source_target_pairs={{0,16},{4,12},{8,24},{12,4},{16,0},{20,28},{24,8},{28,20},{1,17},{... | collective-permute-start | bytes 3145736 | tf_op jit(solution)/shard_map/ppermute | solution.py:610
  287.2 30.7 %collective-permute-start.29 = (bf16[512,1024]{1,0:T(8,128)(2,1)}, bf16[512,1024]{1,0:T(8,128)(2,1)}, u32[]{:S(2)}, u32[]{:S(2)}) collective-permute-start(bf16[512,1024]{1,0:T(8,128)(2,1)} %convolution_convert_fusion.11), channel_id=1, source_target_pairs={{0,16},{4,12},{8,24},{12,4},{16,0},{20,28},{24,8},{28,20},{1,17},{... | collective-permute-start | bytes 3145736 | tf_op jit(solution)/shard_map/ppermute | solution.py:610
  288.0 29.9 %collective-permute-start.30 = (bf16[512,1024]{1,0:T(8,128)(2,1)}, bf16[512,1024]{1,0:T(8,128)(2,1)}, u32[]{:S(2)}, u32[]{:S(2)}) collective-permute-start(bf16[512,1024]{1,0:T(8,128)(2,1)} %convolution_convert_fusion.10), channel_id=1, source_target_pairs={{0,16},{4,12},{8,24},{12,4},{16,0},{20,28},{24,8},{28,20},{1,17},{... | collective-permute-start | bytes 3145736 | tf_op jit(solution)/shard_map/ppermute | solution.py:610
  291.3 110.5 %reduce-scatter.7.cloned.1.call-start = ((), (), s32[]{:S(2)}) async-start(), calls=%async_computation.9 | async-start | bytes 2621440 | tf_op jit(solution)/shard_map/reduce_scatter | solution.py:591
  317.9 18.5 %collective-permute-start.32 = (bf16[512,2048]{1,0:T(8,128)(2,1)S(1)}, bf16[512,2048]{1,0:T(8,128)(2,1)S(1)}, u32[]{:S(2)}, u32[]{:S(2)}) collective-permute-start(bf16[512,2048]{1,0:T(8,128)(2,1)S(1)} %copy-done.45), channel_id=1, source_target_pairs={{0,4},{4,0},{8,12},{12,8},{16,20},{20,16},{24,28},{28,24},{1,5},{5... | collective-permute-start | bytes 6291464 | tf_op jit(solution)/shard_map/ppermute | solution.py:604
  319.7 14.9 %collective-permute-start.31 = (bf16[512,1024]{1,0:T(8,128)(2,1)S(1)}, bf16[512,1024]{1,0:T(8,128)(2,1)S(1)}, u32[]{:S(2)}, u32[]{:S(2)}) collective-permute-start(bf16[512,1024]{1,0:T(8,128)(2,1)S(1)} %add_convert_fusion.11), channel_id=1, source_target_pairs={{0,8},{4,20},{8,0},{12,28},{16,24},{20,4},{24,16},{28,12},{1,9},{5... | collective-permute-start | bytes 3145736 | tf_op jit(solution)/shard_map/ppermute | solution.py:610
  338.5 127.5 %reduce-scatter.9.cloned.1.call-start = ((), (), s32[]{:S(2)}) async-start(), calls=%async_computation.10 | async-start | bytes 3932160 | tf_op jit(solution)/shard_map/reduce_scatter | solution.py:591
  340.7 15.3 %collective-permute-start.34 = (bf16[128,2048]{1,0:T(8,128)(2,1)S(1)}, bf16[128,2048]{1,0:T(8,128)(2,1)S(1)}, u32[]{:S(2)}, u32[]{:S(2)}) collective-permute-start(bf16[128,2048]{1,0:T(8,128)(2,1)S(1)} %fusion.43.refs_0_), channel_id=1, source_target_pairs={{0,16},{4,12},{8,24},{12,4},{16,0},{20,28},{24,8},{28,20},{1,17},{... | collective-permute-start | bytes 1572872 | tf_op jit(solution)/shard_map/ppermute | solution.py:610
  365.5 36.4 %collective-permute-start.40 = (bf16[512,1024]{1,0:T(8,128)(2,1)}, bf16[512,1024]{1,0:T(8,128)(2,1)}, u32[]{:S(2)}, u32[]{:S(2)}) collective-permute-start(bf16[512,1024]{1,0:T(8,128)(2,1)} %convolution_convert_fusion.7), channel_id=1, source_target_pairs={{0,16},{4,12},{8,24},{12,4},{16,0},{20,28},{24,8},{28,20},{1,17},{... | collective-permute-start | bytes 3145736 | tf_op jit(solution)/shard_map/ppermute | solution.py:610
  366.6 35.2 %collective-permute-start.41 = (bf16[512,1024]{1,0:T(8,128)(2,1)S(1)}, bf16[512,1024]{1,0:T(8,128)(2,1)}, u32[]{:S(2)}, u32[]{:S(2)}) collective-permute-start(bf16[512,1024]{1,0:T(8,128)(2,1)S(1)} %copy-done.32), channel_id=1, source_target_pairs={{0,16},{4,12},{8,24},{12,4},{16,0},{20,28},{24,8},{28,20},{1,17},{... | collective-permute-start | bytes 3145736 | tf_op jit(solution)/shard_map/ppermute | solution.py:610
  367.6 34.1 %collective-permute-start.43 = (bf16[2,64,1024]{2,1,0:T(8,128)(2,1)S(1)}, bf16[2,64,1024]{2,1,0:T(8,128)(2,1)S(1)}, u32[]{:S(2)}, u32[]{:S(2)}) collective-permute-start(bf16[2,64,1024]{2,1,0:T(8,128)(2,1)S(1)} %pad_maximum_fusion.11), channel_id=1, source_target_pairs={{0,1},{1,0},{2,3},{3,2},{4,5},{5,4},{6,7},{7,6},{8,9},{9,8},{10,11... | collective-permute-start | bytes 786440 | tf_op jit(solution)/shard_map/ppermute | solution.py:615
  367.8 34.0 %collective-permute-start.44 = (bf16[2,64,1024]{2,1,0:T(8,128)(2,1)S(1)}, bf16[2,64,1024]{2,1,0:T(8,128)(2,1)S(1)}, u32[]{:S(2)}, u32[]{:S(2)}) collective-permute-start(bf16[2,64,1024]{2,1,0:T(8,128)(2,1)S(1)} %pad_maximum_fusion.12), channel_id=1, source_target_pairs={{0,2},{1,3},{2,0},{3,1},{4,6},{5,7},{6,4},{7,5},{8,10},{9,11},{10,... | collective-permute-start | bytes 786440 | tf_op jit(solution)/shard_map/ppermute | solution.py:615
  371.1 30.7 %collective-permute-start.45 = (bf16[2,64,1024]{2,1,0:T(8,128)(2,1)S(1)}, bf16[2,64,1024]{2,1,0:T(8,128)(2,1)S(1)}, u32[]{:S(2)}, u32[]{:S(2)}) collective-permute-start(bf16[2,64,1024]{2,1,0:T(8,128)(2,1)S(1)} %pad_maximum_fusion.13), channel_id=1, source_target_pairs={{0,3},{1,2},{2,1},{3,0},{4,7},{5,6},{6,5},{7,4},{8,11},{9,10},{10,... | collective-permute-start | bytes 786440 | tf_op jit(solution)/shard_map/ppermute | solution.py:615
  401.9 102.0 %reduce-scatter.11.cloned.1.call-start = ((), (), s32[]{:S(2)}) async-start(), calls=%async_computation.11 | async-start | bytes 1310720 | tf_op jit(solution)/shard_map/reduce_scatter | solution.py:591
  414.8 22.9 %collective-permute-start.50 = (bf16[512,1024]{1,0:T(8,128)(2,1)S(1)}, bf16[512,1024]{1,0:T(8,128)(2,1)S(1)}, u32[]{:S(2)}, u32[]{:S(2)}) collective-permute-start(bf16[512,1024]{1,0:T(8,128)(2,1)S(1)} %add_convert_fusion.8), channel_id=1, source_target_pairs={{0,8},{4,20},{8,0},{12,28},{16,24},{20,4},{24,16},{28,12},{1,9},{5... | collective-permute-start | bytes 3145736 | tf_op jit(solution)/shard_map/ppermute | solution.py:610
  446.8 15.2 %collective-permute-start.56 = (bf16[256,2048]{1,0:T(8,128)(2,1)}, bf16[256,2048]{1,0:T(8,128)(2,1)}, u32[]{:S(2)}, u32[]{:S(2)}) collective-permute-start(bf16[256,2048]{1,0:T(8,128)(2,1)} %convolution_convert_fusion.2), channel_id=1, source_target_pairs={{0,16},{4,12},{8,24},{12,4},{16,0},{20,28},{24,8},{28,20},{1,17},{... | collective-permute-start | bytes 3145736 | tf_op jit(solution)/shard_map/ppermute | solution.py:610
  460.5 25.0 %collective-permute-start.55 = (bf16[256,2048]{1,0:T(8,128)(2,1)}, bf16[256,2048]{1,0:T(8,128)(2,1)}, u32[]{:S(2)}, u32[]{:S(2)}) collective-permute-start(bf16[256,2048]{1,0:T(8,128)(2,1)} %convolution_convert_fusion.3), channel_id=1, source_target_pairs={{0,16},{4,12},{8,24},{12,4},{16,0},{20,28},{24,8},{28,20},{1,17},{... | collective-permute-start | bytes 3145736 | tf_op jit(solution)/shard_map/ppermute | solution.py:610
  464.6 25.9 %collective-permute-start.57 = (bf16[256,2048]{1,0:T(8,128)(2,1)}, bf16[256,2048]{1,0:T(8,128)(2,1)}, u32[]{:S(2)}, u32[]{:S(2)}) collective-permute-start(bf16[256,2048]{1,0:T(8,128)(2,1)} %add_convert_fusion.5), channel_id=1, source_target_pairs={{0,8},{4,20},{8,0},{12,28},{16,24},{20,4},{24,16},{28,12},{1,9},{5... | collective-permute-start | bytes 3145736 | tf_op jit(solution)/shard_map/ppermute | solution.py:610
  466.1 45.8 %all-to-all-start.1 = ((bf16[8,64,768]{2,1,0:T(8,128)(2,1)}), bf16[8,64,768]{2,1,0:T(8,128)(2,1)}, u32[]{:S(2)}, u32[]{:S(2)}) async-start(bf16[8,64,768]{2,1,0:T(8,128)(2,1)} %bitcast.160), calls=%async_computation.4 | async-start | bytes 1572864 | tf_op jit(solution)/shard_map/all_to_all | solution.py:595
  474.7 29.1 %collective-permute-start.52 = (bf16[2,64,1024]{2,1,0:T(8,128)(2,1)}, bf16[2,64,1024]{2,1,0:T(8,128)(2,1)S(1)}, u32[]{:S(2)}, u32[]{:S(2)}) collective-permute-start(bf16[2,64,1024]{2,1,0:T(8,128)(2,1)} %pad_maximum_fusion.15), channel_id=1, source_target_pairs={{0,1},{1,0},{2,3},{3,2},{4,5},{5,4},{6,7},{7,6},{8,9},{9,8},{10,11... | collective-permute-start | bytes 786440 | tf_op jit(solution)/shard_map/ppermute | solution.py:615
  475.9 28.0 %collective-permute-start.53 = (bf16[2,64,1024]{2,1,0:T(8,128)(2,1)}, bf16[2,64,1024]{2,1,0:T(8,128)(2,1)S(1)}, u32[]{:S(2)}, u32[]{:S(2)}) collective-permute-start(bf16[2,64,1024]{2,1,0:T(8,128)(2,1)} %pad_maximum_fusion.16), channel_id=1, source_target_pairs={{0,2},{1,3},{2,0},{3,1},{4,6},{5,7},{6,4},{7,5},{8,10},{9,11},{10,... | collective-permute-start | bytes 786440 | tf_op jit(solution)/shard_map/ppermute | solution.py:615
  477.4 34.4 %collective-permute-start.54 = (bf16[2,64,1024]{2,1,0:T(8,128)(2,1)S(1)}, bf16[2,64,1024]{2,1,0:T(8,128)(2,1)S(1)}, u32[]{:S(2)}, u32[]{:S(2)}) collective-permute-start(bf16[2,64,1024]{2,1,0:T(8,128)(2,1)S(1)} %pad_maximum_fusion.17), channel_id=1, source_target_pairs={{0,3},{1,2},{2,1},{3,0},{4,7},{5,6},{6,5},{7,4},{8,11},{9,10},{10,... | collective-permute-start | bytes 786440 | tf_op jit(solution)/shard_map/ppermute | solution.py:615
  (67 other events, 586.2 us)
Sparse Core Ops, SparseCore 0:
  9.6 31.9 all-gather.6
  61.7 63.3 all-gather.10
  126.7 51.8 all-gather.12
  193.7 46.1 all-gather.8
  291.5 42.8 reduce-scatter.4
  338.7 52.9 reduce-scatter.6
  402.0 60.4 reduce-scatter.8
  465.4 38.3 reduce-scatter.10

commit v4 on v3

--- a/solution.py
+++ b/solution.py
@@ -17,6 +17,7 @@
 CTX = ("plane", "core")
 TOK = ("core", "fsdp")
 VMEM_LIMIT = 56 * 1024 * 1024
+VMEM_SMALL = 30 * 1024 * 1024
 LIGHT = pl.CostEstimate(flops=1024, bytes_accessed=1024, transcendentals=0)
 
 
@@ -83,8 +84,8 @@
     return lane // HEAD_DIM == head
 
 
-def params():
-    return pltpu.CompilerParams(vmem_limit_bytes=VMEM_LIMIT)
+def params(grant=VMEM_SMALL):
+    return pltpu.CompilerParams(vmem_limit_bytes=grant)
 
 
 def in_vmem(n):
@@ -96,8 +97,10 @@
 
 
 def forward_kernel(
-    n_ctx, qblk, pair_ref, me_ref, x_ref, w_ref, cos_ref, sin_ref, q_ref, k_ref, v_ref, r_ref, o_ref, lse_ref, acc_ref
+    n_ctx, qblk, pair_ref, me_ref, x_ref, w_ref, turn_ref, kept_ref, r_ref, o_ref, lse_ref, acc_ref
 ):
+    q_ref, k_ref, v_ref = (kept_ref.at[i] for i in range(3))
+    cos_ref, sin_ref = turn_ref.at[0], turn_ref.at[1]
     length, cols = q_ref.shape
     blk = length // (2 * n_ctx)
     heads = cols // HEAD_DIM
@@ -146,44 +149,42 @@
     for slot in range(2 * n_ctx):
         at = pl.multiple_of(slot_block(pair_ref, me_ref, slot, n_ctx) * blk, blk)
         o_ref[pl.ds(slot * blk, blk), :] = acc_ref[pl.ds(at, blk), :].astype(BF)
-
-
-def attention_forward(pair, me, tokens, weight, cosine, sine):
-    length, cols = cosine.shape
+    kept_ref[3] = acc_ref[...].astype(BF)
+
+
+def attention_forward(pair, me, tokens, weight, turn):
+    _, length, cols = turn.shape
     width = weight.shape[0]
     n_ctx = width // cols
     return pl.pallas_call(
         functools.partial(forward_kernel, n_ctx, 256),
-        out_shape=[jax.ShapeDtypeStruct((length, cols), BF)] * 3
-        + [
+        out_shape=[
+            jax.ShapeDtypeStruct((4, length, cols), BF),
             jax.ShapeDtypeStruct((length, 1), F32),
             jax.ShapeDtypeStruct((length, cols), BF),
             jax.ShapeDtypeStruct((length, 128), F32),
         ],
-        in_specs=in_smem(2) + in_vmem(4),
-        out_specs=in_vmem(6),
+        in_specs=in_smem(2) + in_vmem(3),
+        out_specs=in_vmem(4),
         scratch_shapes=[pltpu.VMEM((length, cols), F32)],
-        compiler_params=params(),
+        compiler_params=params(VMEM_LIMIT),
         cost_estimate=LIGHT,
         name="attention_forward",
-    )(pair, me, tokens, weight, cosine, sine)
-
-
-def backward_kernel(n_ctx, qblk, pair_ref, me_ref, *refs):
-    b_refs = refs[:n_ctx]
-    (
-        m_ref, q_ref, k_ref, v_ref, r_ref, o_ref, lse_ref, cos_ref, sin_ref,
-        g_ref, gr_ref, go_ref, dq_ref, dk_ref, dv_ref, do_ref, centre_ref,
-    ) = refs[n_ctx:]
+    )(pair, me, tokens, weight, turn)
+
+
+def backward_kernel(
+    n_ctx, qblk, pair_ref, me_ref, do_ref, kept_ref, r_ref, lse_ref, turn_ref,
+    g_ref, gr_ref, go_ref, dq_ref, dk_ref, dv_ref, centre_ref,
+):
+    q_ref, k_ref, v_ref, o_ref = (kept_ref.at[i] for i in range(4))
+    cos_ref, sin_ref = turn_ref.at[0], turn_ref.at[1]
     length, cols = q_ref.shape
     blk = length // (2 * n_ctx)
     heads = cols // HEAD_DIM
-    for at, b_ref in enumerate(b_refs):
-        grad = mm_t(b_ref[...], m_ref[...]).astype(BF)
-        for second in range(2):
-            to = pl.ds(pl.multiple_of(slot_block(pair_ref, me_ref, 2 * at + second, n_ctx) * blk, blk), blk)
-            go_ref[to, :] = grad[second * blk : (second + 1) * blk, :]
-            do_ref[to, :] = o_ref[pl.ds((2 * at + second) * blk, blk), :]
+    for slot in range(2 * n_ctx):
+        at = pl.multiple_of(slot_block(pair_ref, me_ref, slot, n_ctx) * blk, blk)
+        go_ref[pl.ds(at, blk), :] = do_ref[pl.ds(slot * blk, blk), :]
     dq_ref[...] = jnp.zeros_like(dq_ref)
     dk_ref[...] = jnp.zeros_like(dk_ref)
     dv_ref[...] = jnp.zeros_like(dv_ref)
@@ -191,7 +192,7 @@
     pick = head_mask((8, cols), lax.broadcasted_iota(jnp.int32, (8, cols), 0)).astype(F32)
     centre_ref[...] = lax.dot_general(
         pick,
-        go_ref[...].astype(F32) * do_ref[...].astype(F32),
+        go_ref[...].astype(F32) * o_ref[...].astype(F32),
         (((1,), (1,)), ((), ())),
         precision=lax.Precision.HIGHEST,
         preferred_element_type=F32,
@@ -241,22 +242,20 @@
             gr_ref[rows, span] = (part * scale).astype(BF)
 
 
-def attention_backward(pair, me, pieces, merge_rows, q, k, v, scale, attended, lse, cosine, sine):
-    length, cols = cosine.shape
-    width = merge_rows.shape[1]
-    n_ctx = len(pieces)
+def attention_backward(pair, me, n_ctx, grad, kept, scale, lse, turn):
+    _, length, cols = turn.shape
     return pl.pallas_call(
         functools.partial(backward_kernel, n_ctx, 256),
         out_shape=[jax.ShapeDtypeStruct((length, 3 * cols), BF)] * 2,
-        in_specs=in_smem(2) + in_vmem(n_ctx + 9),
+        in_specs=in_smem(2) + in_vmem(5),
         out_specs=in_vmem(2),
         scratch_shapes=[pltpu.VMEM((length, cols), BF)]
         + [pltpu.VMEM((length, cols), F32)] * 3
-        + [pltpu.VMEM((length, cols), BF), pltpu.VMEM((8, length), F32)],
+        + [pltpu.VMEM((8, length), F32)],
         compiler_params=params(),
         cost_estimate=LIGHT,
         name="attention_backward",
-    )(pair, me, *pieces, merge_rows, q, k, v, scale, attended, lse, cosine, sine)
+    )(pair, me, grad, kept, scale, lse, turn)
 
 
 def feed_forward_kernel(
@@ -319,7 +318,7 @@
         ),
         out_shape=[jax.ShapeDtypeStruct((count, hid), BF)] * 3
         + [jax.ShapeDtypeStruct((count // 2, width), BF)] * 2,
-        compiler_params=params(),
+        compiler_params=params(VMEM_LIMIT),
         cost_estimate=LIGHT,
         name="feed_forward",
     )(lax.axis_index("core").astype(jnp.int32)[None], normed, cotangent, gate_w, up_w, down_w)
@@ -367,54 +366,81 @@
     )(lax.axis_index("core").astype(jnp.int32)[None], hidden, down_w)
 
 
-def merge_kernel(a_ref, *refs):
-    *b_refs, out_ref, all_ref = refs
+def merge_kernel(a_ref, m_ref, *refs):
+    *b_refs, go_ref, out_ref, all_ref = refs
     rows = b_refs[0].shape[0]
     for at, ref in enumerate(b_refs):
         all_ref[pl.ds(at * rows, rows), :] = ref[...]
+    go_ref[...] = mm_t(all_ref[...], m_ref[...]).astype(BF)
     out_ref[...] = t_mm(a_ref[...], all_ref[...]).astype(BF)
 
 
-def merge_term(attended, pieces):
-    cols, width = attended.shape[1], pieces[0].shape[1]
+def merge_terms(attended, merge_rows, pieces):
+    length, cols = attended.shape
+    width = merge_rows.shape[1]
     return pl.pallas_call(
         merge_kernel,
-        out_shape=jax.ShapeDtypeStruct((cols, width), BF),
-        in_specs=in_vmem(1 + len(pieces)),
-        out_specs=pl.BlockSpec(memory_space=pltpu.VMEM),
-        scratch_shapes=[pltpu.VMEM((attended.shape[0], width), BF)],
+        out_shape=[jax.ShapeDtypeStruct((length, cols), BF), jax.ShapeDtypeStruct((cols, width), BF)],
+        in_specs=in_vmem(2 + len(pieces)),
+        out_specs=in_vmem(2),
+        scratch_shapes=[pltpu.VMEM((length, width), BF)],
         compiler_params=params(),
         cost_estimate=LIGHT,
-        name="merge_term",
-    )(attended, *pieces)
+        name="merge_terms",
+    )(attended, merge_rows, *pieces)
 
 
 def heads_term_kernel(x_ref, g_ref, out_ref):
-    n_fsdp, _, rows, cols = out_ref.shape
-    out_ref[...] = t_mm(x_ref[...], g_ref[...]).astype(BF).reshape(n_fsdp, 1, rows, cols)
-
-
-def heads_term(tokens, grad, n_ctx, n_fsdp):
-    count, width = tokens.shape
+    out_ref[...] = mm(x_ref[...], g_ref[...]).astype(BF)
+
+
+def heads_term(tokens_t, grad):
+    width, count = tokens_t.shape
     cols = grad.shape[1]
-    rows = width // (n_ctx * n_fsdp)
-    if n_fsdp * rows % 128:
-        out = t_mm(tokens, grad).astype(BF).reshape(n_ctx, n_fsdp, rows, cols)
-        return out.transpose(1, 0, 2, 3).reshape(width, cols)
-    out = pl.pallas_call(
+    tile = 512
+    return pl.pallas_call(
         heads_term_kernel,
-        grid=(n_ctx,),
+        grid=(width // tile,),
         in_specs=[
-            pl.BlockSpec((count, n_fsdp * rows), lambda c: (0, c)),
-            pl.BlockSpec((count, cols), lambda c: (0, 0), pipeline_mode=pl.Buffered(1)),
+            pl.BlockSpec((tile, count), lambda i: (i, 0)),
+            pl.BlockSpec((count, cols), lambda i: (0, 0), pipeline_mode=pl.Buffered(1)),
         ],
-        out_specs=pl.BlockSpec((n_fsdp, 1, rows, cols), lambda c: (0, c, 0, 0)),
-        out_shape=jax.ShapeDtypeStruct((n_fsdp, n_ctx, rows, cols), BF),
+        out_specs=pl.BlockSpec((tile, cols), lambda i: (i, 0)),
+        out_shape=jax.ShapeDtypeStruct((width, cols), BF),
         compiler_params=params(),
         cost_estimate=LIGHT,
         name="heads_term",
-    )(tokens, grad)
-    return out.reshape(width, cols)
+    )(tokens_t, grad)
+
+
+def weight_rows_kernel(at_ref, left_ref, right_ref, *out_refs):
+    out = t_mm(left_ref[...], right_ref[...]).astype(BF)
+    for i, ref in enumerate(out_refs):
+
+        @pl.when(pl.program_id(0) == i)
+        def _(ref=ref):
+            ref[...] = out
+
+
+def weight_rows(left, right, index, size):
+    count, n = left.shape[0], len(index)
+    width = right.shape[1]
+    return pl.pallas_call(
+        weight_rows_kernel,
+        grid_spec=pltpu.PrefetchScalarGridSpec(
+            num_scalar_prefetch=1,
+            grid=(n,),
+            in_specs=[
+                pl.BlockSpec((count, size), lambda i, at: (0, at[i])),
+                pl.BlockSpec((count, width), lambda i, at: (0, 0), pipeline_mode=pl.Buffered(1)),
+            ],
+            out_specs=[pl.BlockSpec((size, width), lambda i, at: (0, 0), pipeline_mode=pl.Buffered(1))] * n,
+        ),
+        out_shape=[jax.ShapeDtypeStruct((size, width), BF)] * n,
+        compiler_params=params(),
+        cost_estimate=LIGHT,
+        name="weight_rows",
+    )(jnp.stack(index).astype(jnp.int32), left, right)
 
 
 def back_kernel(g_ref, w_ref, out_ref):
@@ -569,15 +595,15 @@
         out_ref[at_ref[i]] = ref[...]
 
 
-def place(pieces, index):
+def place(pieces, index, room=None):
     n = len(pieces)
     moved = 2 * n * pieces[0].size * pieces[0].dtype.itemsize
     return pl.pallas_call(
         place_kernel,
-        out_shape=jax.ShapeDtypeStruct((n,) + pieces[0].shape, pieces[0].dtype),
+        out_shape=jax.ShapeDtypeStruct((room or n,) + pieces[0].shape, pieces[0].dtype),
         in_specs=in_smem(1) + in_vmem(n),
         out_specs=pl.BlockSpec(memory_space=pltpu.VMEM),
-        compiler_params=params(),
+        compiler_params=params(VMEM_LIMIT),
         cost_estimate=LIGHT,
         name="place",
     )(jnp.stack(index).astype(jnp.int32), *pieces)
@@ -686,11 +712,28 @@
     return lines_swap(lines_parts(pair))
 
 
+def line_rows_kernel(at_ref, *refs):
+    *p_refs, out_ref = refs
+    n_fsdp = len(p_refs)
+    for mask, ref in enumerate(p_refs):
+        line = jnp.bitwise_xor(at_ref[1], mask)
+        for other in range(2):
+            core = jnp.bitwise_xor(at_ref[0], other)
+            out_ref[core * n_fsdp + line] = ref[other]
+
+
 def line_rows(pieces):
-    core, line = lax.axis_index("core"), lax.axis_index("fsdp")
-    n_fsdp = len(pieces)
-    blocks = [(piece[other], (core ^ other) * n_fsdp + (line ^ mask)) for mask, piece in enumerate(pieces) for other in range(2)]
-    return place([b for b, _ in blocks], [i for _, i in blocks])
+    n = 2 * len(pieces)
+    at = jnp.stack([lax.axis_index("core"), lax.axis_index("fsdp")]).astype(jnp.int32)
+    return pl.pallas_call(
+        line_rows_kernel,
+        out_shape=jax.ShapeDtypeStruct((n,) + pieces[0].shape[1:], pieces[0].dtype),
+        in_specs=in_smem(1) + in_vmem(len(pieces)),
+        out_specs=pl.BlockSpec(memory_space=pltpu.VMEM),
+        compiler_params=params(VMEM_LIMIT),
+        cost_estimate=LIGHT,
+        name="line_rows",
+    )(at, *pieces)
 
 
 def on_device(
@@ -723,7 +766,7 @@
     own = exchange(fold_heads(projections, gain_first, n_ctx), CTX)
     x_pieces = ctx_gather(tokens)
     up_pair = cores_pair(fold_hidden(up_weight, gain_second, n_plane, n_core, n_fsdp))
-    cosine, sine = rope_tables(length, cols)
+    turn = jnp.stack(rope_tables(length, cols))
     own, gate_moved, x_pieces, up_pair, merge_rows = together(
         (own, gate_moved, x_pieces, up_pair, merge_rows)
     )
@@ -735,66 +778,75 @@
     up_moved = lines_pair(up_pair)
     cot_all = gather(cotangent, TOK)
 
-    q, k, v, scale_all, attended, lse = attention_forward(pairing, me, x_all, qkv_weight, cosine, sine)
+    kept, scale_all, attended, lse = attention_forward(pairing, me, x_all, qkv_weight, turn)
     while len(down_pieces) < n_plane:
         down_pieces = plane_gather_more(down_pieces)
     attended, down_pieces = together((attended, down_pieces))
-    gate_rows = place(gate_pieces, index).reshape(width, hid)
     down_rows = place(down_pieces, index).reshape(hid, width)
     own_f = tokens.astype(F32)
     theirs = together(mm(attended[half:], merge_rows).astype(BF))
     mine = together(mm(attended[:half], merge_rows).astype(BF))
     mixed = own_f + ctx_scatter(theirs, mine, n_plane)
-    mixed, up_moved = together((mixed, up_moved))
+    lse_rows = lse[:, :8].T
+    x_t = x_all.reshape(length, n_ctx, n_fsdp, dev_rows).transpose(2, 1, 3, 0).reshape(width, length)
+    gate_rows = place(gate_pieces, index).reshape(width, hid)
+    mixed, up_moved, lse_rows, x_t, down_rows, gate_rows = together(
+        (mixed, up_moved, lse_rows, x_t, down_rows, gate_rows)
+    )
     up_pieces = plane_gather(line_rows(up_moved).reshape(d_rows, hid))
+    up_rows = place(up_pieces[:-1], index[:-1], n_plane)
+    up_rows = lax.dynamic_update_slice(up_rows, up_pieces[-1][None], (index[-1], 0, 0)).reshape(width, hid)
 
     scale_second = lax.rsqrt(jnp.mean(mixed * mixed, axis=-1, keepdims=True) + EPS)
     unit_second = mixed * scale_second
     normed_all = gather(unit_second.astype(BF), TOK)
-    up_rows = place(up_pieces, index).reshape(width, hid)
     hidden, grad_gate, grad_up, theirs, mine = feed_forward(
         normed_all, cot_all, gate_rows, up_rows, down_rows
     )
-    lse_rows = lse[:, :8].T
     e_two = (mine.astype(F32) + core_swap(theirs).astype(F32)).astype(BF)
 
-    normed_w = [part(normed_all, at, d_rows, 1) for at in index]
-    gate_late = [together(t_mm(rows_of, grad_gate).astype(BF)) for rows_of in normed_w[n_plane // 2 :]]
     hidden, grad_gate, grad_up, e_two = together((hidden, grad_gate, grad_up, e_two))
-    gate_chunks = [together(t_mm(rows_of, grad_gate).astype(BF)) for rows_of in normed_w[: n_plane // 2]]
-    gate_chunks += gate_late
+    gate_late = weight_rows(normed_all, grad_gate, index[n_plane // 2 :], d_rows)
+    gate_chunks = list(weight_rows(normed_all, grad_gate, index[: n_plane // 2], d_rows)) + list(gate_late)
     gate_came = plane_send(gate_chunks)
-    up_chunks = [together(t_mm(rows_of, grad_up).astype(BF)) for rows_of in normed_w]
+    up_chunks = [together(t_mm(part(normed_all, at, d_rows, 1), grad_up).astype(BF)) for at in index]
     theirs, mine = branch_rows(hidden, down_rows)
-    gate_chunks, gate_came, up_chunks, theirs, mine, lse_rows = together(
-        (gate_chunks, gate_came, up_chunks, theirs, mine, lse_rows)
-    )
-    gate_sum = plane_scatter(plane_add(gate_chunks, gate_came))
+    gate_chunks, gate_came, up_chunks, theirs, mine = together(
+        (gate_chunks, gate_came, up_chunks, theirs, mine)
+    )
+    gate_chunks = plane_add(gate_chunks, gate_came)
     branch = (mine.astype(F32) + core_swap(theirs).astype(F32)).astype(BF)
     e_two = scatter(e_two, "fsdp")
-    e_two, gate_sum, up_chunks, branch = together((e_two, gate_sum, up_chunks, branch))
+    e_two, gate_chunks, up_chunks, branch = together((e_two, gate_chunks, up_chunks, branch))
     branch_sum = scatter(branch, "fsdp")
-    gate_parts = lines_parts(cores_pair(gate_sum.reshape(n_core, n_fsdp, dev_rows, hid)))
+    gate_sum = plane_scatter(gate_chunks)
     e_two_f = e_two.astype(F32)
     grad_mixed = cotangent.astype(F32) + scale_second * (
         e_two_f - unit_second * jnp.mean(e_two_f * unit_second, axis=-1, keepdims=True)
     )
-    branch_pieces = ctx_gather(grad_mixed.astype(BF))
+    branch_pieces = plane_gather_more([grad_mixed.astype(BF)])
+    branch_pieces, gate_sum = together((branch_pieces, gate_sum))
+    gate_parts = lines_parts(cores_pair(gate_sum.reshape(n_core, n_fsdp, dev_rows, hid)))
+    while len(branch_pieces) < n_plane:
+        branch_pieces = plane_gather_more(branch_pieces)
+    branch_pieces = branch_pieces + [core_swap(value) for value in branch_pieces]
     gate_back = lines_swap(gate_parts)
 
     branch_pieces, up_chunks = together((branch_pieces, up_chunks))
     up_came = plane_send(up_chunks)
+    grad_attended, merge_grad = merge_terms(attended, merge_rows, branch_pieces)
+    merge_grad, grad_attended = together((merge_grad, grad_attended))
+    merge_grad = scatter(merge_grad, "fsdp")
     grad_qkv, grad_scaled = attention_backward(
-        pairing, me, branch_pieces, merge_rows, q, k, v, scale_all, attended, lse_rows, cosine, sine
-    )
-    sums = heads_term(x_all, grad_scaled, n_ctx, n_fsdp)
-    grad_qkv, up_chunks, up_came, gate_back, sums, attended, branch_sum = together(
-        (grad_qkv, up_chunks, up_came, gate_back, sums, attended, branch_sum)
+        pairing, me, n_ctx, grad_attended, kept, scale_all, lse_rows, turn
+    )
+    grad_scaled, branch_sum = together((grad_scaled, branch_sum))
+    sums = heads_term(x_t, grad_scaled)
+    grad_qkv, up_chunks, up_came, gate_back, sums, merge_grad, branch_sum = together(
+        (grad_qkv, up_chunks, up_came, gate_back, sums, merge_grad, branch_sum)
     )
     sums = scatter(sums, "fsdp")
     up_sum = plane_scatter(plane_add(up_chunks, up_came))
-    attended, up_sum = together((attended, up_sum))
-    merge_grad = scatter(merge_term(attended, branch_pieces), "fsdp")
     layer_output = (mixed + branch_sum.astype(F32)).astype(BF)
     theirs = back_rows(grad_qkv, qkv_weight, 1)
     mine = back_rows(grad_qkv, qkv_weight, 0)
@@ -807,7 +859,10 @@
     sums, up_parts = together((sums, up_parts))
     up_back = lines_swap(up_parts)
     sums = exchange(sums.reshape(n_ctx, dev_rows, 3 * cols), CTX)
-    sums, up_back, merge_grad = together((sums, up_back, merge_grad))
+    query_grad, key_grad, value_grad, first_grad = unfold_heads(sums, projections, gain_first)
+    query_grad, key_grad, value_grad, first_grad, up_back, merge_grad = together(
+        (query_grad, key_grad, value_grad, first_grad, up_back, merge_grad)
+    )
     scale_first = lax.rsqrt(jnp.mean(own_f * own_f, axis=-1, keepdims=True) + EPS)
     unit_first = own_f * scale_first
     input_grad = (
@@ -818,7 +873,6 @@
     gate_grad, second_gate = unfold_hidden(gate_back, gate_weight, gain_second, n_plane)
     up_grad, second_up = unfold_hidden(up_back, up_weight, gain_second, n_plane)
     second_grad = (second_gate + second_up)[:, 0]
-    query_grad, key_grad, value_grad, first_grad = unfold_heads(sums, projections, gain_first)
     return (
         layer_output.reshape(1, rows, width),
         input_grad.reshape(1, rows, width),

time: 536 us -> 531 us (level)
  Pallas kernels: 137 us -> 113 us
  waiting for transfers between devices: 199 us -> 219 us
  matrix products: 37.6 us -> 18.7 us
  other arithmetic: 38.6 us -> 50.4 us
  local copies, waits for them, and re-layouts: 38 us -> 48.9 us
  starting transfers between devices: 64.2 us -> 57.1 us
    dot_general x12 -> x8, matrix products: 35.2 us -> 16.3 us  [t_mm(): lax.dot_general(left, right, (((0,), (0,)), ((), ())), preferred_element_...]
    unnamed x101 -> x131, local copies, waits for them, and re-layouts: 13.5 us -> 27.4 us
    pallas_call x1, Pallas kernels: 20.4 us -> 12.6 us  [attention_backward(): pl.pallas_call(functools.partial(backward_kernel, n_ctx, 256), out_shape=...]
    all_gather x4, waiting for transfers between devices: 0.03 us -> 7.06 us  [gather(): return lax.all_gather(value, axes, axis=axis, tiled=True)]
    squeeze x6 -> x0, local copies, waits for them, and re-layouts: 6.56 us -> none  [line_rows(): piece[other]]
    optimization_barrier x0 -> x1, local copies, waits for them, and re-layouts: none -> 6.41 us  [together(): return lax.optimization_barrier(values)]
    ppermute x16, waiting for transfers between devices: 4.71 us -> 10.8 us  [core_swap(): return lax.ppermute(value, CTX, [(i, i ^ 1) for i in range(n)])]
    another operation x16, other arithmetic: 4.62 us -> 10.2 us  [lines_parts(): jnp.stack([lax.dynamic_index_in_dim(v, line ^ mask, 0, keepdims=False) fo...]
  transfers between devices with their start and end apart: 68 -> 68, of which waited for: 29 -> 34; matrix products, arithmetic and copies ran while one was open for 20% -> 18% of each run, Pallas kernels for 19% -> 14%
where the time goes in v4:
time: 531 us; the launch traced here: 523 us
  waiting for transfers between devices  219 us (41%)
  Pallas kernels  113 us (21%)
  starting transfers between devices  57.1 us (11%)
  other arithmetic  50.4 us (9%)
  local copies, waits for them, and re-layouts  48.9 us (9%)
  matrix products  18.7 us (4%)
  between operations  15.5 us (3%)
    ppermute x30, waiting for transfers between devices, plane_step(): lax.ppermute(value, CTX, [(i, i ^ 2 * steps[i % 2][step]) for i in range(...  135 us
    ppermute x12, waiting for transfers between devices, line_swap(): return lax.ppermute(value, 'fsdp', [(i, i ^ mask) for i in range(n)])  52.8 us
    pallas_call x1, Pallas kernels, feed_forward(): pl.pallas_call(feed_forward_kernel, grid_spec=pltpu.PrefetchScalarGridSpe...  31.5 us
    ppermute x30, starting transfers between devices, plane_step(): lax.ppermute(value, CTX, [(i, i ^ 2 * steps[i % 2][step]) for i in range(...  31.3 us
    unnamed x131, local copies, waits for them, and re-layouts  27.4 us
    pallas_call x1, Pallas kernels, attention_forward(): pl.pallas_call(functools.partial(forward_kernel, n_ctx, 256), out_shape=[...  17.1 us
    dot_general x8, matrix products, t_mm(): lax.dot_general(left, right, (((0,), (0,)), ((), ())), preferred_element_...  16.3 us
    ppermute x12, starting transfers between devices, line_swap(): return lax.ppermute(value, 'fsdp', [(i, i ^ mask) for i in range(n)])  14.7 us
  transfers between devices with their start and end apart: 68, of which 34 were waited for; matrix products, arithmetic and copies ran while one was open for 18% of the time, Pallas kernels for 14%

profile of v4, /device:TPU:18, one launch (start us, length us, event | category | flops | bytes accessed | tf_op | source)
XLA Modules:
  0.0 522.8 jit_solution(6352452651321648146)
XLA Ops:
  14.4 4.7 collective-permute-done.4
  23.7 3.5 all-to-all-start
  33.7 19.3 %collective-permute-done.2.refs_2_ = bf16[2,64,1024]{2,1,0:T(8,128)(2,1)S(1)} collective-permute-done((bf16[2,64,1024]{2,1,0:T(8,128)(2,1)S(1)}, bf16[2,64,1024]{2,1,0:T(8,128)(2,1)S(1)}, u32[]{:S(2)}, u32[]{:S(2)}) %collective-permute-start.2) | collective-permute-done | bytes 262176 | tf_op jit(solution)/shard_map/ppermute | solution.py:641
  56.0 3.4 collective-permute-done.3.refs_3_
  74.5 16.7 %collective-permute-done.12.refs_1_ = bf16[512,1024]{1,0:T(8,128)(2,1)S(1)} collective-permute-done((bf16[512,1024]{1,0:T(8,128)(2,1)}, bf16[512,1024]{1,0:T(8,128)(2,1)S(1)}, u32[]{:S(2)}, u32[]{:S(2)}) %collective-permute-start.12) | collective-permute-done | bytes 1048608 | tf_op jit(solution)/shard_map/ppermute | solution.py:636
  99.1 14.5 %collective-permute-done.15.refs_1_ = bf16[256,2048]{1,0:T(8,128)(2,1)} collective-permute-done((bf16[256,2048]{1,0:T(8,128)(2,1)}, bf16[256,2048]{1,0:T(8,128)(2,1)}, u32[]{:S(2)}, u32[]{:S(2)}) %collective-permute-start.15) | collective-permute-done | bytes 1048608 | tf_op jit(solution)/shard_map/ppermute | solution.py:636
  120.9 4.6 all-gather.11.cloned.1.call-done
  125.4 17.1 %attention_forward.1 = (bf16[4,1024,256]{2,1,0:T(8,128)(2,1)}, f32[1024,1]{1,0:T(8,128)}, bf16[1024,256]{1,0:T(8,128)(2,1)}, f32[1024,128]{1,0:T(8,128)}) custom-call(s32[1,8]{1,0:T(1,128)} %pair_ref.3, s32[2]{0:T(128)} %pad_add_fusion.me_ref, bf16[1024,2048]{1,0:T(8,128)(2,1)} %constant_dynamic-update-slice_fusion.x_ref, bf16[2048,768]{1,0:T(8,128)(2,1)} %bitcast.98, ...), custom_call_target="tpu_custom_call" | custom-call | flops 1024 | bytes 1024 | tf_op jit(solution)/shard_map/attention_forward/pallas_call | solution.py:159
  145.1 3.4 collective-permute-done.18
  156.0 4.0 collective-permute-done.20
  166.6 4.5 place.4
  171.1 6.4 %copy.37 = bf16[1024,2048]{0,1:T(8,128)(2,1)} copy(bf16[1024,2048]{1,0:T(8,128)(2,1)} %constant_dynamic-update-slice_fusion.x_ref) | data formatting | bytes 8388608 | tf_op jit(solution)/shard_map/optimization_barrier | solution.py:625
  177.5 4.9 copy.38
  182.4 4.5 place.3
  188.9 3.9 collective-permute-done.24.refs_3_
  198.3 23.7 %collective-permute-done.25.refs_1_ = bf16[512,1024]{1,0:T(8,128)(2,1)S(1)} collective-permute-done((bf16[512,1024]{1,0:T(8,128)(2,1)}, bf16[512,1024]{1,0:T(8,128)(2,1)S(1)}, u32[]{:S(2)}, u32[]{:S(2)}) %collective-permute-start.25) | collective-permute-done | bytes 1048608 | tf_op jit(solution)/shard_map/ppermute | solution.py:636
  223.7 4.1 place.5
  227.8 9.0 %collective-permute-done.27 = bf16[512,1024]{1,0:T(8,128)(2,1)S(1)} collective-permute-done((bf16[512,1024]{1,0:T(8,128)(2,1)S(1)}, bf16[512,1024]{1,0:T(8,128)(2,1)S(1)}, u32[]{:S(2)}, u32[]{:S(2)}) %collective-permute-start.27) | collective-permute-done | bytes 1048608 | tf_op jit(solution)/shard_map/ppermute | solution.py:636
  240.4 31.5 %feed_forward.1 = (bf16[1024,1024]{1,0:T(8,128)(2,1)}, bf16[1024,1024]{1,0:T(8,128)(2,1)}, bf16[1024,1024]{1,0:T(8,128)(2,1)}, bf16[512,2048]{1,0:T(8,128)(2,1)}, bf16[512,2048]{1,0:T(8,128)(2,1)}) custom-call(s32[1]{0:T(128)} %bitcast.2.core_ref, bf16[1024,2048]{1,0:T(8,128)(2,1)} %all-gather.9.cloned.1.call-done.n_ref.left_ref, ...), custom_call_target="tpu_custom_call" | custom-call | flops 1024 | bytes 1024 | tf_op jit(solution)/shard_map/feed_forward/pallas_call | solution.py:301
  272.1 4.1 collective-permute-done.28
  276.3 3.7 add_convert_fusion.2
  283.7 3.7 weight_rows.3
  291.8 5.5 %branch_rows.1 = (bf16[512,2048]{1,0:T(8,128)(2,1)S(1)}, bf16[512,2048]{1,0:T(8,128)(2,1)S(1)}) custom-call(s32[1]{0:T(128)} %bitcast.2.core_ref, bf16[1024,1024]{1,0:T(8,128)(2,1)S(1)} %copy-done.16, bf16[1024,2048]{1,0:T(8,128)(2,1)S(1)} %bitcast.97), custom_call_target="tpu_custom_call" | custom-call | flops 1024 | bytes 1024 | tf_op jit(solution)/shard_map/branch_rows/pallas_call | solution.py:345
  297.3 3.5 weight_rows.2
  307.7 5.8 %collective-permute-done.30 = bf16[512,1024]{1,0:T(8,128)(2,1)S(1)} collective-permute-done((bf16[512,1024]{1,0:T(8,128)(2,1)S(1)}, bf16[512,1024]{1,0:T(8,128)(2,1)S(1)}, u32[]{:S(2)}, u32[]{:S(2)}) %collective-permute-start.30) | collective-permute-done | bytes 1048608 | tf_op jit(solution)/shard_map/ppermute | solution.py:636
  319.9 3.4 reduce-scatter.5.cloned.1.call-done
  326.4 12.3 %collective-permute-done.33 = bf16[512,1024]{1,0:T(8,128)(2,1)S(1)} collective-permute-done((bf16[512,1024]{1,0:T(8,128)(2,1)}, bf16[512,1024]{1,0:T(8,128)(2,1)S(1)}, u32[]{:S(2)}, u32[]{:S(2)}) %collective-permute-start.33) | collective-permute-done | bytes 1048608 | tf_op jit(solution)/shard_map/ppermute | solution.py:636
  339.1 5.2 collective-permute-done.32.refs_1_
  346.8 6.6 %collective-permute-done.34.refs_2_ = bf16[128,2048]{1,0:T(8,128)(2,1)S(1)} collective-permute-done((bf16[128,2048]{1,0:T(8,128)(2,1)S(1)}, bf16[128,2048]{1,0:T(8,128)(2,1)S(1)}, u32[]{:S(2)}, u32[]{:S(2)}) %collective-permute-start.34) | collective-permute-done | bytes 524320 | tf_op jit(solution)/shard_map/ppermute | solution.py:636
  353.5 5.6 %collective-permute-done.35.refs_3_ = bf16[128,2048]{1,0:T(8,128)(2,1)S(1)} collective-permute-done((bf16[128,2048]{1,0:T(8,128)(2,1)S(1)}, bf16[128,2048]{1,0:T(8,128)(2,1)S(1)}, u32[]{:S(2)}, u32[]{:S(2)}) %collective-permute-start.35) | collective-permute-done | bytes 524320 | tf_op jit(solution)/shard_map/ppermute | solution.py:636
  361.0 3.3 merge_terms.1
  368.4 2.8 collective-permute-start.44
  373.3 12.6 %attention_backward.1 = (bf16[1024,768]{1,0:T(8,128)(2,1)S(1)}, bf16[1024,768]{1,0:T(8,128)(2,1)S(1)}) custom-call(s32[1,8]{1,0:T(1,128)S(1)} %copy-done.31, s32[2]{0:T(128)S(1)} %copy-done.32, bf16[1024,256]{1,0:T(8,128)(2,1)S(1)} %get-tuple-element.229.do_ref, bf16[4,1024,256]{2,1,0:T(8,128)(2,1)S(1)} %copy-done.18, f32[1024,1]{1,0:T(8,128)S(1)} %copy-done.29, ...), custom_call_target="tpu_custom_call" | custom-call | flops 1024 | bytes 1024 | tf_op jit(solution)/shard_map/attention_backward/pallas_call | solution.py:247
  391.8 4.0 heads_term.1
  399.0 8.4 %collective-permute-done.44.refs_2_ = bf16[2,64,1024]{2,1,0:T(8,128)(2,1)} collective-permute-done((bf16[2,64,1024]{2,1,0:T(8,128)(2,1)}, bf16[2,64,1024]{2,1,0:T(8,128)(2,1)}, u32[]{:S(2)}, u32[]{:S(2)}) %collective-permute-start.44) | collective-permute-done | bytes 262176 | tf_op jit(solution)/shard_map/ppermute | solution.py:641
  410.2 3.0 back_rows.3
  427.7 9.2 %collective-permute-done.48 = bf16[128,2048]{1,0:T(8,128)(2,1)S(1)} collective-permute-done((bf16[128,2048]{1,0:T(8,128)(2,1)S(1)}, bf16[128,2048]{1,0:T(8,128)(2,1)S(1)}, u32[]{:S(2)}, u32[]{:S(2)}) %collective-permute-start.48) | collective-permute-done | bytes 524320 | tf_op jit(solution)/shard_map/ppermute | solution.py:636
  442.4 4.0 collective-permute-done.47
  446.4 3.0 collective-permute-done.49
  451.1 3.0 unfold_hidden.2
  457.2 7.4 %collective-permute-done.56 = bf16[256,2048]{1,0:T(8,128)(2,1)S(1)} collective-permute-done((bf16[256,2048]{1,0:T(8,128)(2,1)S(1)}, bf16[256,2048]{1,0:T(8,128)(2,1)S(1)}, u32[]{:S(2)}, u32[]{:S(2)}) %collective-permute-start.56) | collective-permute-done | bytes 1048608 | tf_op jit(solution)/shard_map/ppermute | solution.py:636
  468.5 7.3 %reduce-scatter.11.cloned.1.call-done = bf16[512,768]{1,0:T(8,128)(2,1)} async-done(((bf16[2048,768]{1,0:T(8,128)(2,1)}), bf16[512,768]{1,0:T(8,128)(2,1)}) %reduce-scatter.11.cloned.1.call-update) | async-done | bytes 786448 | tf_op jit(solution)/shard_map/reduce_scatter | solution.py:617
  475.7 4.2 all-to-all-start.1
  479.9 2.9 fusion.15
  486.4 3.6 collective-permute-done.57
  490.0 3.4 fusion.9
  495.8 6.7 %collective-permute-done.53.refs_2_ = bf16[2,64,1024]{2,1,0:T(8,128)(2,1)S(1)} collective-permute-done((bf16[2,64,1024]{2,1,0:T(8,128)(2,1)}, bf16[2,64,1024]{2,1,0:T(8,128)(2,1)S(1)}, u32[]{:S(2)}, u32[]{:S(2)}) %collective-permute-start.53) | collective-permute-done | bytes 262176 | tf_op jit(solution)/shard_map/ppermute | solution.py:641
  502.5 7.1 %collective-permute-done.54.refs_3_ = bf16[2,64,1024]{2,1,0:T(8,128)(2,1)} collective-permute-done((bf16[2,64,1024]{2,1,0:T(8,128)(2,1)}, bf16[2,64,1024]{2,1,0:T(8,128)(2,1)}, u32[]{:S(2)}, u32[]{:S(2)}) %collective-permute-start.54) | collective-permute-done | bytes 262176 | tf_op jit(solution)/shard_map/ppermute | solution.py:641
  (339 shorter events, 168.2 us)
Async XLA Ops:
  7.2 54.7 %all-gather.7.cloned.1.call-start = ((), (), s32[]{:S(2)}) async-start(), calls=%async_computation.6 | async-start | bytes 1310720 | tf_op jit(solution)/shard_map/all_gather | solution.py:613
  11.0 16.3 %collective-permute-start = (bf16[4,64,1024]{2,1,0:T(8,128)(2,1)}, bf16[4,64,1024]{2,1,0:T(8,128)(2,1)}, u32[]{:S(2)}, u32[]{:S(2)}) collective-permute-start(bf16[4,64,1024]{2,1,0:T(8,128)(2,1)} %dynamic-slice_bitcast_fusion.4), channel_id=1, source_target_pairs={{0,4},{4,0},{8,12},{12,8},{16,20},{20,16},{24,28},{28,24},{1,5},{5... | collective-permute-start | bytes 1572872 | tf_op jit(solution)/shard_map/ppermute | solution.py:630
  11.5 17.5 %collective-permute-start.5 = (bf16[128,2048]{1,0:T(8,128)(2,1)}, bf16[128,2048]{1,0:T(8,128)(2,1)}, u32[]{:S(2)}, u32[]{:S(2)}) collective-permute-start(bf16[128,2048]{1,0:T(8,128)(2,1)} %bitcast), channel_id=1, source_target_pairs={{0,16},{4,12},{8,24},{12,4},{16,0},{20,28},{24,8},{28,20},{1,17},{... | collective-permute-start | bytes 1572872 | tf_op jit(solution)/shard_map/ppermute | solution.py:636
  12.5 18.5 %collective-permute-start.7 = (bf16[128,2048]{1,0:T(8,128)(2,1)}, bf16[128,2048]{1,0:T(8,128)(2,1)}, u32[]{:S(2)}, u32[]{:S(2)}) collective-permute-start(bf16[128,2048]{1,0:T(8,128)(2,1)} %bitcast), channel_id=1, source_target_pairs={{0,4},{4,0},{8,12},{12,8},{16,20},{20,16},{24,28},{28,24},{1,5},{5... | collective-permute-start | bytes 1572872 | tf_op jit(solution)/shard_map/ppermute | solution.py:630
  14.0 14.9 %collective-permute-start.11 = (bf16[4,64,1024]{2,1,0:T(8,128)(2,1)}, bf16[4,64,1024]{2,1,0:T(8,128)(2,1)S(1)}, u32[]{:S(2)}, u32[]{:S(2)}) collective-permute-start(bf16[4,64,1024]{2,1,0:T(8,128)(2,1)} %get-tuple-element.299), channel_id=1, source_target_pairs={{0,4},{4,0},{8,12},{12,8},{16,20},{20,16},{24,28},{28,24},{1,5},{5... | collective-permute-start | bytes 1572872 | tf_op jit(solution)/shard_map/ppermute | solution.py:630
  23.7 32.3 %all-to-all-start = ((bf16[8,64,768]{2,1,0:T(8,128)(2,1)}), bf16[8,64,768]{2,1,0:T(8,128)(2,1)S(1)}, u32[]{:S(2)}, u32[]{:S(2)}) async-start(bf16[8,64,768]{2,1,0:T(8,128)(2,1)} %fold_heads.1), calls=%async_computation | async-start | bytes 1572864 | tf_op jit(solution)/shard_map/all_to_all | solution.py:621
  27.2 98.2 %all-gather.11.cloned.1.call-start = ((), (), s32[]{:S(2)}) async-start(), calls=%async_computation.12 | async-start | bytes 3932160 | tf_op jit(solution)/shard_map/all_gather | solution.py:613
  28.5 24.4 %collective-permute-start.2 = (bf16[2,64,1024]{2,1,0:T(8,128)(2,1)S(1)}, bf16[2,64,1024]{2,1,0:T(8,128)(2,1)S(1)}, u32[]{:S(2)}, u32[]{:S(2)}) collective-permute-start(bf16[2,64,1024]{2,1,0:T(8,128)(2,1)S(1)} %pad_maximum_fusion.3), channel_id=1, source_target_pairs={{0,2},{1,3},{2,0},{3,1},{4,6},{5,7},{6,4},{7,5},{8,10},{9,11},{10,... | collective-permute-start | bytes 786440 | tf_op jit(solution)/shard_map/ppermute | solution.py:641
  28.9 32.9 %collective-permute-start.8 = (bf16[128,2048]{1,0:T(8,128)(2,1)}, bf16[128,2048]{1,0:T(8,128)(2,1)S(1)}, u32[]{:S(2)}, u32[]{:S(2)}) collective-permute-start(bf16[128,2048]{1,0:T(8,128)(2,1)} %collective-permute-done.4), channel_id=1, source_target_pairs={{0,4},{4,0},{8,12},{12,8},{16,20},{20,16},{24,28},{28,24},{1,5},{5... | collective-permute-start | bytes 1572872 | tf_op jit(solution)/shard_map/ppermute | solution.py:630
  29.0 32.9 %collective-permute-start.9 = (bf16[128,2048]{1,0:T(8,128)(2,1)}, bf16[128,2048]{1,0:T(8,128)(2,1)S(1)}, u32[]{:S(2)}, u32[]{:S(2)}) collective-permute-start(bf16[128,2048]{1,0:T(8,128)(2,1)} %collective-permute-done.5), channel_id=1, source_target_pairs={{0,4},{4,0},{8,12},{12,8},{16,20},{20,16},{24,28},{28,24},{1,5},{5... | collective-permute-start | bytes 1572872 | tf_op jit(solution)/shard_map/ppermute | solution.py:630
  29.5 32.4 %collective-permute-start.10 = (bf16[128,2048]{1,0:T(8,128)(2,1)S(1)}, bf16[128,2048]{1,0:T(8,128)(2,1)}, u32[]{:S(2)}, u32[]{:S(2)}) collective-permute-start(bf16[128,2048]{1,0:T(8,128)(2,1)S(1)} %collective-permute-done.6), channel_id=1, source_target_pairs={{0,4},{4,0},{8,12},{12,8},{16,20},{20,16},{24,28},{28,24},{1,5},{5... | collective-permute-start | bytes 1572872 | tf_op jit(solution)/shard_map/ppermute | solution.py:630
  31.0 28.3 %collective-permute-start.3 = (bf16[2,64,1024]{2,1,0:T(8,128)(2,1)}, bf16[2,64,1024]{2,1,0:T(8,128)(2,1)}, u32[]{:S(2)}, u32[]{:S(2)}) collective-permute-start(bf16[2,64,1024]{2,1,0:T(8,128)(2,1)} %pad_maximum_fusion.4), channel_id=1, source_target_pairs={{0,3},{1,2},{2,1},{3,0},{4,7},{5,6},{6,5},{7,4},{8,11},{9,10},{10,... | collective-permute-start | bytes 786440 | tf_op jit(solution)/shard_map/ppermute | solution.py:641
  61.9 176.0 %all-gather.13.cloned.1.call-start = ((), (), s32[]{:S(2)}) async-start(), calls=%async_computation.13 | async-start | bytes 4718592 | tf_op jit(solution)/shard_map/all_gather | solution.py:613
  64.9 26.3 %collective-permute-start.12 = (bf16[512,1024]{1,0:T(8,128)(2,1)}, bf16[512,1024]{1,0:T(8,128)(2,1)S(1)}, u32[]{:S(2)}, u32[]{:S(2)}) collective-permute-start(bf16[512,1024]{1,0:T(8,128)(2,1)} %bitcast.105), channel_id=1, source_target_pairs={{0,8},{4,20},{8,0},{12,28},{16,24},{20,4},{24,16},{28,12},{1,9},{5... | collective-permute-start | bytes 3145736 | tf_op jit(solution)/shard_map/ppermute | solution.py:636
  65.4 48.3 %collective-permute-start.15 = (bf16[256,2048]{1,0:T(8,128)(2,1)}, bf16[256,2048]{1,0:T(8,128)(2,1)}, u32[]{:S(2)}, u32[]{:S(2)}) collective-permute-start(bf16[256,2048]{1,0:T(8,128)(2,1)} %refs_0_), channel_id=1, source_target_pairs={{0,8},{4,20},{8,0},{12,28},{16,24},{20,4},{24,16},{28,12},{1,9},{5... | collective-permute-start | bytes 3145736 | tf_op jit(solution)/shard_map/ppermute | solution.py:636
  67.0 173.4 %all-gather.9.cloned.1.call-start = ((), (), s32[]{:S(2)}) async-start(), calls=%async_computation.7 | async-start | bytes 4718592 | tf_op jit(solution)/shard_map/all_gather | solution.py:613
  67.1 46.6 %collective-permute-start.13 = (bf16[512,1024]{1,0:T(8,128)(2,1)}, bf16[512,1024]{1,0:T(8,128)(2,1)S(1)}, u32[]{:S(2)}, u32[]{:S(2)}) collective-permute-start(bf16[512,1024]{1,0:T(8,128)(2,1)} %bitcast.106), channel_id=1, source_target_pairs={{0,16},{4,12},{8,24},{12,4},{16,0},{20,28},{24,8},{28,20},{1,17},{... | collective-permute-start | bytes 3145736 | tf_op jit(solution)/shard_map/ppermute | solution.py:636
  91.2 22.5 %collective-permute-start.14 = (bf16[512,1024]{1,0:T(8,128)(2,1)S(1)}, bf16[512,1024]{1,0:T(8,128)(2,1)S(1)}, u32[]{:S(2)}, u32[]{:S(2)}) collective-permute-start(bf16[512,1024]{1,0:T(8,128)(2,1)S(1)} %collective-permute-done.12.refs_1_), channel_id=1, source_target_pairs={{0,16},{4,12},{8,24},{12,4},{16,0},{20,28},{24,8},{28,20},{1,17},{... | collective-permute-start | bytes 3145736 | tf_op jit(solution)/shard_map/ppermute | solution.py:636
  114.7 27.9 %collective-permute-start.16 = (bf16[256,2048]{1,0:T(8,128)(2,1)}, bf16[256,2048]{1,0:T(8,128)(2,1)}, u32[]{:S(2)}, u32[]{:S(2)}) collective-permute-start(bf16[256,2048]{1,0:T(8,128)(2,1)} %refs_0_), channel_id=1, source_target_pairs={{0,16},{4,12},{8,24},{12,4},{16,0},{20,28},{24,8},{28,20},{1,17},{... | collective-permute-start | bytes 3145736 | tf_op jit(solution)/shard_map/ppermute | solution.py:636
  116.3 26.3 %collective-permute-start.17 = (bf16[256,2048]{1,0:T(8,128)(2,1)}, bf16[256,2048]{1,0:T(8,128)(2,1)}, u32[]{:S(2)}, u32[]{:S(2)}) collective-permute-start(bf16[256,2048]{1,0:T(8,128)(2,1)} %collective-permute-done.15.refs_1_), channel_id=1, source_target_pairs={{0,16},{4,12},{8,24},{12,4},{16,0},{20,28},{24,8},{28,20},{1,17},{... | collective-permute-start | bytes 3145736 | tf_op jit(solution)/shard_map/ppermute | solution.py:636
  154.7 34.2 %collective-permute-start.22 = (bf16[2,64,1024]{2,1,0:T(8,128)(2,1)}, bf16[2,64,1024]{2,1,0:T(8,128)(2,1)}, u32[]{:S(2)}, u32[]{:S(2)}) collective-permute-start(bf16[2,64,1024]{2,1,0:T(8,128)(2,1)} %pad_maximum_fusion.8), channel_id=1, source_target_pairs={{0,1},{1,0},{2,3},{3,2},{4,5},{5,4},{6,7},{7,6},{8,9},{9,8},{10,11... | collective-permute-start | bytes 786440 | tf_op jit(solution)/shard_map/ppermute | solution.py:641
  155.3 31.8 %collective-permute-start.19 = (bf16[128,2048]{1,0:T(8,128)(2,1)}, bf16[128,2048]{1,0:T(8,128)(2,1)}, u32[]{:S(2)}, u32[]{:S(2)}) collective-permute-start(bf16[128,2048]{1,0:T(8,128)(2,1)} %get-tuple-element.287), channel_id=1, source_target_pairs={{0,16},{4,12},{8,24},{12,4},{16,0},{20,28},{24,8},{28,20},{1,17},{... | collective-permute-start | bytes 1572872 | tf_op jit(solution)/shard_map/ppermute | solution.py:636
  162.0 25.1 %collective-permute-start.21 = (bf16[128,2048]{1,0:T(8,128)(2,1)}, bf16[128,2048]{1,0:T(8,128)(2,1)S(1)}, u32[]{:S(2)}, u32[]{:S(2)}) collective-permute-start(bf16[128,2048]{1,0:T(8,128)(2,1)} %add_convert_fusion.18), channel_id=1, source_target_pairs={{0,8},{4,20},{8,0},{12,28},{16,24},{20,4},{24,16},{28,12},{1,9},{5... | collective-permute-start | bytes 1572872 | tf_op jit(solution)/shard_map/ppermute | solution.py:636
  163.3 25.6 %collective-permute-start.23 = (bf16[2,64,1024]{2,1,0:T(8,128)(2,1)}, bf16[2,64,1024]{2,1,0:T(8,128)(2,1)S(1)}, u32[]{:S(2)}, u32[]{:S(2)}) collective-permute-start(bf16[2,64,1024]{2,1,0:T(8,128)(2,1)} %pad_maximum_fusion.9), channel_id=1, source_target_pairs={{0,2},{1,3},{2,0},{3,1},{4,6},{5,7},{6,4},{7,5},{8,10},{9,11},{10,... | collective-permute-start | bytes 786440 | tf_op jit(solution)/shard_map/ppermute | solution.py:641
  165.8 27.0 %collective-permute-start.24 = (bf16[2,64,1024]{2,1,0:T(8,128)(2,1)}, bf16[2,64,1024]{2,1,0:T(8,128)(2,1)S(1)}, u32[]{:S(2)}, u32[]{:S(2)}) collective-permute-start(bf16[2,64,1024]{2,1,0:T(8,128)(2,1)} %pad_maximum_fusion.10), channel_id=1, source_target_pairs={{0,3},{1,2},{2,1},{3,0},{4,7},{5,6},{6,5},{7,4},{8,11},{9,10},{10,... | collective-permute-start | bytes 786440 | tf_op jit(solution)/shard_map/ppermute | solution.py:641
  193.9 129.4 %reduce-scatter.5.cloned.1.call-start = ((), (), s32[]{:S(2)}) async-start(), calls=%async_computation.8 | async-start | bytes 2621440 | tf_op jit(solution)/shard_map/reduce_scatter | solution.py:617
  196.2 25.8 %collective-permute-start.25 = (bf16[512,1024]{1,0:T(8,128)(2,1)}, bf16[512,1024]{1,0:T(8,128)(2,1)S(1)}, u32[]{:S(2)}, u32[]{:S(2)}) collective-permute-start(bf16[512,1024]{1,0:T(8,128)(2,1)} %bitcast.115), channel_id=1, source_target_pairs={{0,8},{4,20},{8,0},{12,28},{16,24},{20,4},{24,16},{28,12},{1,9},{5... | collective-permute-start | bytes 3145736 | tf_op jit(solution)/shard_map/ppermute | solution.py:636
  196.7 26.9 %collective-permute-start.26 = (bf16[512,1024]{1,0:T(8,128)(2,1)}, bf16[512,1024]{1,0:T(8,128)(2,1)}, u32[]{:S(2)}, u32[]{:S(2)}) collective-permute-start(bf16[512,1024]{1,0:T(8,128)(2,1)} %bitcast.116), channel_id=1, source_target_pairs={{0,16},{4,12},{8,24},{12,4},{16,0},{20,28},{24,8},{28,20},{1,17},{... | collective-permute-start | bytes 3145736 | tf_op jit(solution)/shard_map/ppermute | solution.py:636
  280.0 108.2 %reduce-scatter.7.cloned.1.call-start = ((), (), s32[]{:S(2)}) async-start(), calls=%async_computation.9 | async-start | bytes 2621440 | tf_op jit(solution)/shard_map/reduce_scatter | solution.py:617
  287.4 20.3 %collective-permute-start.29 = (bf16[512,1024]{1,0:T(8,128)(2,1)S(1)}, bf16[512,1024]{1,0:T(8,128)(2,1)S(1)}, u32[]{:S(2)}, u32[]{:S(2)}) collective-permute-start(bf16[512,1024]{1,0:T(8,128)(2,1)S(1)} %get-tuple-element.194), channel_id=1, source_target_pairs={{0,16},{4,12},{8,24},{12,4},{16,0},{20,28},{24,8},{28,20},{1,17},{... | collective-permute-start | bytes 3145736 | tf_op jit(solution)/shard_map/ppermute | solution.py:636
  289.0 24.6 %collective-permute-start.30 = (bf16[512,1024]{1,0:T(8,128)(2,1)S(1)}, bf16[512,1024]{1,0:T(8,128)(2,1)S(1)}, u32[]{:S(2)}, u32[]{:S(2)}) collective-permute-start(bf16[512,1024]{1,0:T(8,128)(2,1)S(1)} %get-tuple-element.195), channel_id=1, source_target_pairs={{0,16},{4,12},{8,24},{12,4},{16,0},{20,28},{24,8},{28,20},{1,17},{... | collective-permute-start | bytes 3145736 | tf_op jit(solution)/shard_map/ppermute | solution.py:636
  323.3 85.4 %reduce-scatter.9.cloned.1.call-start = ((), (), s32[]{:S(2)}) async-start(), calls=%async_computation.10 | async-start | bytes 1310720 | tf_op jit(solution)/shard_map/reduce_scatter | solution.py:617
  323.6 15.1 %collective-permute-start.33 = (bf16[512,1024]{1,0:T(8,128)(2,1)}, bf16[512,1024]{1,0:T(8,128)(2,1)S(1)}, u32[]{:S(2)}, u32[]{:S(2)}) collective-permute-start(bf16[512,1024]{1,0:T(8,128)(2,1)} %add_convert_fusion.11), channel_id=1, source_target_pairs={{0,8},{4,20},{8,0},{12,28},{16,24},{20,4},{24,16},{28,12},{1,9},{5... | collective-permute-start | bytes 3145736 | tf_op jit(solution)/shard_map/ppermute | solution.py:636
  325.0 19.3 %collective-permute-start.32 = (bf16[128,2048]{1,0:T(8,128)(2,1)S(1)}, bf16[128,2048]{1,0:T(8,128)(2,1)S(1)}, u32[]{:S(2)}, u32[]{:S(2)}) collective-permute-start(bf16[128,2048]{1,0:T(8,128)(2,1)S(1)} %fusion.35.refs_0_), channel_id=1, source_target_pairs={{0,8},{4,20},{8,0},{12,28},{16,24},{20,4},{24,16},{28,12},{1,9},{5... | collective-permute-start | bytes 1572872 | tf_op jit(solution)/shard_map/ppermute | solution.py:636
  364.4 111.3 %reduce-scatter.11.cloned.1.call-start = ((), (), s32[]{:S(2)}) async-start(), calls=%async_computation.11 | async-start | bytes 3932160 | tf_op jit(solution)/shard_map/reduce_scatter | solution.py:617
  364.7 42.7 %collective-permute-start.40 = (bf16[512,1024]{1,0:T(8,128)(2,1)}, bf16[512,1024]{1,0:T(8,128)(2,1)}, u32[]{:S(2)}, u32[]{:S(2)}) collective-permute-start(bf16[512,1024]{1,0:T(8,128)(2,1)} %convolution_convert_fusion.7), channel_id=1, source_target_pairs={{0,16},{4,12},{8,24},{12,4},{16,0},{20,28},{24,8},{28,20},{1,17},{... | collective-permute-start | bytes 3145736 | tf_op jit(solution)/shard_map/ppermute | solution.py:636
  366.3 41.2 %collective-permute-start.41 = (bf16[512,1024]{1,0:T(8,128)(2,1)}, bf16[512,1024]{1,0:T(8,128)(2,1)}, u32[]{:S(2)}, u32[]{:S(2)}) collective-permute-start(bf16[512,1024]{1,0:T(8,128)(2,1)} %convolution_convert_fusion.6), channel_id=1, source_target_pairs={{0,16},{4,12},{8,24},{12,4},{16,0},{20,28},{24,8},{28,20},{1,17},{... | collective-permute-start | bytes 3145736 | tf_op jit(solution)/shard_map/ppermute | solution.py:636
  367.6 31.4 %collective-permute-start.45 = (bf16[2,64,1024]{2,1,0:T(8,128)(2,1)}, bf16[2,64,1024]{2,1,0:T(8,128)(2,1)}, u32[]{:S(2)}, u32[]{:S(2)}) collective-permute-start(bf16[2,64,1024]{2,1,0:T(8,128)(2,1)} %pad_maximum_fusion.14), channel_id=1, source_target_pairs={{0,3},{1,2},{2,1},{3,0},{4,7},{5,6},{6,5},{7,4},{8,11},{9,10},{10,... | collective-permute-start | bytes 786440 | tf_op jit(solution)/shard_map/ppermute | solution.py:641
  368.4 39.0 %collective-permute-start.44 = (bf16[2,64,1024]{2,1,0:T(8,128)(2,1)}, bf16[2,64,1024]{2,1,0:T(8,128)(2,1)}, u32[]{:S(2)}, u32[]{:S(2)}) collective-permute-start(bf16[2,64,1024]{2,1,0:T(8,128)(2,1)} %pad_maximum_fusion.13), channel_id=1, source_target_pairs={{0,2},{1,3},{2,0},{3,1},{4,6},{5,7},{6,4},{7,5},{8,10},{9,11},{10,... | collective-permute-start | bytes 786440 | tf_op jit(solution)/shard_map/ppermute | solution.py:641
  372.0 35.5 %collective-permute-start.43 = (bf16[2,64,1024]{2,1,0:T(8,128)(2,1)}, bf16[2,64,1024]{2,1,0:T(8,128)(2,1)}, u32[]{:S(2)}, u32[]{:S(2)}) collective-permute-start(bf16[2,64,1024]{2,1,0:T(8,128)(2,1)} %pad_maximum_fusion.12), channel_id=1, source_target_pairs={{0,1},{1,0},{2,3},{3,2},{4,5},{5,4},{6,7},{7,6},{8,9},{9,8},{10,11... | collective-permute-start | bytes 786440 | tf_op jit(solution)/shard_map/ppermute | solution.py:641
  417.7 22.8 %collective-permute-start.50 = (bf16[512,1024]{1,0:T(8,128)(2,1)S(1)}, bf16[512,1024]{1,0:T(8,128)(2,1)S(1)}, u32[]{:S(2)}, u32[]{:S(2)}) collective-permute-start(bf16[512,1024]{1,0:T(8,128)(2,1)S(1)} %add_convert_fusion.8), channel_id=1, source_target_pairs={{0,8},{4,20},{8,0},{12,28},{16,24},{20,4},{24,16},{28,12},{1,9},{5... | collective-permute-start | bytes 3145736 | tf_op jit(solution)/shard_map/ppermute | solution.py:636
  422.0 14.9 %collective-permute-start.48 = (bf16[128,2048]{1,0:T(8,128)(2,1)S(1)}, bf16[128,2048]{1,0:T(8,128)(2,1)S(1)}, u32[]{:S(2)}, u32[]{:S(2)}) collective-permute-start(bf16[128,2048]{1,0:T(8,128)(2,1)S(1)} %get-tuple-element.286), channel_id=1, source_target_pairs={{0,16},{4,12},{8,24},{12,4},{16,0},{20,28},{24,8},{28,20},{1,17},{... | collective-permute-start | bytes 1572872 | tf_op jit(solution)/shard_map/ppermute | solution.py:636
  427.2 19.2 %collective-permute-start.47 = (bf16[128,2048]{1,0:T(8,128)(2,1)S(1)}, bf16[128,2048]{1,0:T(8,128)(2,1)S(1)}, u32[]{:S(2)}, u32[]{:S(2)}) collective-permute-start(bf16[128,2048]{1,0:T(8,128)(2,1)S(1)} %get-tuple-element.285), channel_id=1, source_target_pairs={{0,16},{4,12},{8,24},{12,4},{16,0},{20,28},{24,8},{28,20},{1,17},{... | collective-permute-start | bytes 1572872 | tf_op jit(solution)/shard_map/ppermute | solution.py:636
  456.4 30.0 %collective-permute-start.55 = (bf16[256,2048]{1,0:T(8,128)(2,1)}, bf16[256,2048]{1,0:T(8,128)(2,1)}, u32[]{:S(2)}, u32[]{:S(2)}) collective-permute-start(bf16[256,2048]{1,0:T(8,128)(2,1)} %convolution_convert_fusion.3), channel_id=1, source_target_pairs={{0,16},{4,12},{8,24},{12,4},{16,0},{20,28},{24,8},{28,20},{1,17},{... | collective-permute-start | bytes 3145736 | tf_op jit(solution)/shard_map/ppermute | solution.py:636
  465.9 24.0 %collective-permute-start.57 = (bf16[256,2048]{1,0:T(8,128)(2,1)}, bf16[256,2048]{1,0:T(8,128)(2,1)}, u32[]{:S(2)}, u32[]{:S(2)}) collective-permute-start(bf16[256,2048]{1,0:T(8,128)(2,1)} %add_convert_fusion.5), channel_id=1, source_target_pairs={{0,8},{4,20},{8,0},{12,28},{16,24},{20,4},{24,16},{28,12},{1,9},{5... | collective-permute-start | bytes 3145736 | tf_op jit(solution)/shard_map/ppermute | solution.py:636
  475.7 18.7 %all-to-all-start.1 = ((bf16[8,64,768]{2,1,0:T(8,128)(2,1)}), bf16[8,64,768]{2,1,0:T(8,128)(2,1)S(1)}, u32[]{:S(2)}, u32[]{:S(2)}) async-start(bf16[8,64,768]{2,1,0:T(8,128)(2,1)} %bitcast.118), calls=%async_computation.5 | async-start | bytes 1572864 | tf_op jit(solution)/shard_map/all_to_all | solution.py:621
  483.3 19.1 %collective-permute-start.53 = (bf16[2,64,1024]{2,1,0:T(8,128)(2,1)}, bf16[2,64,1024]{2,1,0:T(8,128)(2,1)S(1)}, u32[]{:S(2)}, u32[]{:S(2)}) collective-permute-start(bf16[2,64,1024]{2,1,0:T(8,128)(2,1)} %pad_maximum_fusion.17), channel_id=1, source_target_pairs={{0,2},{1,3},{2,0},{3,1},{4,6},{5,7},{6,4},{7,5},{8,10},{9,11},{10,... | collective-permute-start | bytes 786440 | tf_op jit(solution)/shard_map/ppermute | solution.py:641
  484.4 25.3 %collective-permute-start.54 = (bf16[2,64,1024]{2,1,0:T(8,128)(2,1)}, bf16[2,64,1024]{2,1,0:T(8,128)(2,1)}, u32[]{:S(2)}, u32[]{:S(2)}) collective-permute-start(bf16[2,64,1024]{2,1,0:T(8,128)(2,1)} %pad_maximum_fusion.18), channel_id=1, source_target_pairs={{0,3},{1,2},{2,1},{3,0},{4,7},{5,6},{6,5},{7,4},{8,11},{9,10},{10,... | collective-permute-start | bytes 786440 | tf_op jit(solution)/shard_map/ppermute | solution.py:641
  (82 other events, 679.1 us)
Sparse Core Ops, SparseCore 0:
  9.6 41.0 all-gather.6
  62.0 63.3 all-gather.10
  127.0 60.0 all-gather.12
  194.0 46.3 all-gather.8
  280.1 43.1 reduce-scatter.4
  325.6 43.2 reduce-scatter.6
  371.2 37.5 reduce-scatter.8
  413.4 62.2 reduce-scatter.10

commit v5 on v4

--- a/solution.py
+++ b/solution.py
@@ -856,12 +856,12 @@
     down_chunks = [together(t_mm(part(hidden, at, piece, 1), cot_all).astype(BF)) for at in index]
     e_one, down_chunks = together((e_one, down_chunks))
     down_came = plane_send(down_chunks)
-    sums, up_parts = together((sums, up_parts))
+    sums, up_parts, merge_grad = together((sums, up_parts, merge_grad.astype(F32)))
     up_back = lines_swap(up_parts)
     sums = exchange(sums.reshape(n_ctx, dev_rows, 3 * cols), CTX)
     query_grad, key_grad, value_grad, first_grad = unfold_heads(sums, projections, gain_first)
-    query_grad, key_grad, value_grad, first_grad, up_back, merge_grad = together(
-        (query_grad, key_grad, value_grad, first_grad, up_back, merge_grad)
+    query_grad, key_grad, value_grad, first_grad, up_back = together(
+        (query_grad, key_grad, value_grad, first_grad, up_back)
     )
     scale_first = lax.rsqrt(jnp.mean(own_f * own_f, axis=-1, keepdims=True) + EPS)
     unit_first = own_f * scale_first
@@ -879,7 +879,7 @@
         query_grad,
         key_grad,
         value_grad,
-        merge_grad.astype(F32),
+        merge_grad,
         gate_grad,
         up_grad,
         down_grad,

time: 531 us -> 529 us (level)
    unnamed x131 -> x133, local copies, waits for them, and re-layouts: 27.4 us -> 27.5 us
where the time goes in v5:
time: 529 us; the launch traced here: 521 us
  waiting for transfers between devices  218 us (41%)
  Pallas kernels  113 us (21%)
  starting transfers between devices  57 us (11%)
  other arithmetic  49.7 us (9%)
  local copies, waits for them, and re-layouts  49 us (9%)
  matrix products  18.7 us (4%)
  between operations  15.5 us (3%)
    ppermute x30, waiting for transfers between devices, plane_step(): lax.ppermute(value, CTX, [(i, i ^ 2 * steps[i % 2][step]) for i in range(...  134 us
    ppermute x12, waiting for transfers between devices, line_swap(): return lax.ppermute(value, 'fsdp', [(i, i ^ mask) for i in range(n)])  52.8 us
    pallas_call x1, Pallas kernels, feed_forward(): pl.pallas_call(feed_forward_kernel, grid_spec=pltpu.PrefetchScalarGridSpe...  31.5 us
    ppermute x30, starting transfers between devices, plane_step(): lax.ppermute(value, CTX, [(i, i ^ 2 * steps[i % 2][step]) for i in range(...  31.2 us
    unnamed x133, local copies, waits for them, and re-layouts  27.5 us
    pallas_call x1, Pallas kernels, attention_forward(): pl.pallas_call(functools.partial(forward_kernel, n_ctx, 256), out_shape=[...  17.1 us
    dot_general x8, matrix products, t_mm(): lax.dot_general(left, right, (((0,), (0,)), ((), ())), preferred_element_...  16.3 us
    ppermute x12, starting transfers between devices, line_swap(): return lax.ppermute(value, 'fsdp', [(i, i ^ mask) for i in range(n)])  14.7 us
  transfers between devices with their start and end apart: 68, of which 34 were waited for; matrix products, arithmetic and copies ran while one was open for 18% of the time, Pallas kernels for 14%

profile of v5, /device:TPU:18, one launch (start us, length us, event | category | flops | bytes accessed | tf_op | source)
XLA Modules:
  0.0 520.9 jit_solution(8933163010157774608)
XLA Ops:
  14.4 4.7 collective-permute-done.4
  23.7 3.5 all-to-all-start
  33.7 19.3 %collective-permute-done.2.refs_2_ = bf16[2,64,1024]{2,1,0:T(8,128)(2,1)S(1)} collective-permute-done((bf16[2,64,1024]{2,1,0:T(8,128)(2,1)S(1)}, bf16[2,64,1024]{2,1,0:T(8,128)(2,1)S(1)}, u32[]{:S(2)}, u32[]{:S(2)}) %collective-permute-start.2) | collective-permute-done | bytes 262176 | tf_op jit(solution)/shard_map/ppermute | solution.py:641
  56.0 3.4 collective-permute-done.3.refs_3_
  74.6 16.7 %collective-permute-done.12.refs_1_ = bf16[512,1024]{1,0:T(8,128)(2,1)S(1)} collective-permute-done((bf16[512,1024]{1,0:T(8,128)(2,1)}, bf16[512,1024]{1,0:T(8,128)(2,1)S(1)}, u32[]{:S(2)}, u32[]{:S(2)}) %collective-permute-start.12) | collective-permute-done | bytes 1048608 | tf_op jit(solution)/shard_map/ppermute | solution.py:636
  99.3 14.5 %collective-permute-done.15.refs_1_ = bf16[256,2048]{1,0:T(8,128)(2,1)} collective-permute-done((bf16[256,2048]{1,0:T(8,128)(2,1)}, bf16[256,2048]{1,0:T(8,128)(2,1)}, u32[]{:S(2)}, u32[]{:S(2)}) %collective-permute-start.15) | collective-permute-done | bytes 1048608 | tf_op jit(solution)/shard_map/ppermute | solution.py:636
  120.9 4.5 all-gather.11.cloned.1.call-done
  125.4 17.1 %attention_forward.1 = (bf16[4,1024,256]{2,1,0:T(8,128)(2,1)}, f32[1024,1]{1,0:T(8,128)}, bf16[1024,256]{1,0:T(8,128)(2,1)}, f32[1024,128]{1,0:T(8,128)}) custom-call(s32[1,8]{1,0:T(1,128)} %pair_ref.3, s32[2]{0:T(128)} %pad_add_fusion.me_ref, bf16[1024,2048]{1,0:T(8,128)(2,1)} %constant_dynamic-update-slice_fusion.x_ref, bf16[2048,768]{1,0:T(8,128)(2,1)} %bitcast.98, ...), custom_call_target="tpu_custom_call" | custom-call | flops 1024 | bytes 1024 | tf_op jit(solution)/shard_map/attention_forward/pallas_call | solution.py:159
  145.1 3.4 collective-permute-done.18
  156.1 3.9 collective-permute-done.20
  166.6 4.5 place.4
  171.1 6.4 %copy.37 = bf16[1024,2048]{0,1:T(8,128)(2,1)} copy(bf16[1024,2048]{1,0:T(8,128)(2,1)} %constant_dynamic-update-slice_fusion.x_ref) | data formatting | bytes 8388608 | tf_op jit(solution)/shard_map/optimization_barrier | solution.py:625
  177.5 4.9 copy.38
  182.4 4.5 place.3
  189.0 3.8 collective-permute-done.24.refs_3_
  198.3 23.7 %collective-permute-done.25.refs_1_ = bf16[512,1024]{1,0:T(8,128)(2,1)S(1)} collective-permute-done((bf16[512,1024]{1,0:T(8,128)(2,1)}, bf16[512,1024]{1,0:T(8,128)(2,1)S(1)}, u32[]{:S(2)}, u32[]{:S(2)}) %collective-permute-start.25) | collective-permute-done | bytes 1048608 | tf_op jit(solution)/shard_map/ppermute | solution.py:636
  223.7 4.1 place.5
  227.8 9.0 %collective-permute-done.27 = bf16[512,1024]{1,0:T(8,128)(2,1)S(1)} collective-permute-done((bf16[512,1024]{1,0:T(8,128)(2,1)S(1)}, bf16[512,1024]{1,0:T(8,128)(2,1)S(1)}, u32[]{:S(2)}, u32[]{:S(2)}) %collective-permute-start.27) | collective-permute-done | bytes 1048608 | tf_op jit(solution)/shard_map/ppermute | solution.py:636
  240.3 31.5 %feed_forward.1 = (bf16[1024,1024]{1,0:T(8,128)(2,1)}, bf16[1024,1024]{1,0:T(8,128)(2,1)}, bf16[1024,1024]{1,0:T(8,128)(2,1)}, bf16[512,2048]{1,0:T(8,128)(2,1)}, bf16[512,2048]{1,0:T(8,128)(2,1)}) custom-call(s32[1]{0:T(128)} %bitcast.2.core_ref, bf16[1024,2048]{1,0:T(8,128)(2,1)} %all-gather.9.cloned.1.call-done.n_ref.left_ref, ...), custom_call_target="tpu_custom_call" | custom-call | flops 1024 | bytes 1024 | tf_op jit(solution)/shard_map/feed_forward/pallas_call | solution.py:301
  272.1 4.1 collective-permute-done.28
  276.2 3.7 add_convert_fusion.2
  283.7 3.7 weight_rows.3
  291.8 5.5 %branch_rows.1 = (bf16[512,2048]{1,0:T(8,128)(2,1)S(1)}, bf16[512,2048]{1,0:T(8,128)(2,1)S(1)}) custom-call(s32[1]{0:T(128)} %bitcast.2.core_ref, bf16[1024,1024]{1,0:T(8,128)(2,1)S(1)} %copy-done.16, bf16[1024,2048]{1,0:T(8,128)(2,1)S(1)} %bitcast.97), custom_call_target="tpu_custom_call" | custom-call | flops 1024 | bytes 1024 | tf_op jit(solution)/shard_map/branch_rows/pallas_call | solution.py:345
  297.3 3.5 weight_rows.2
  307.7 5.8 %collective-permute-done.30 = bf16[512,1024]{1,0:T(8,128)(2,1)S(1)} collective-permute-done((bf16[512,1024]{1,0:T(8,128)(2,1)S(1)}, bf16[512,1024]{1,0:T(8,128)(2,1)S(1)}, u32[]{:S(2)}, u32[]{:S(2)}) %collective-permute-start.30) | collective-permute-done | bytes 1048608 | tf_op jit(solution)/shard_map/ppermute | solution.py:636
  319.9 3.4 reduce-scatter.5.cloned.1.call-done
  326.5 12.3 %collective-permute-done.33 = bf16[512,1024]{1,0:T(8,128)(2,1)S(1)} collective-permute-done((bf16[512,1024]{1,0:T(8,128)(2,1)}, bf16[512,1024]{1,0:T(8,128)(2,1)S(1)}, u32[]{:S(2)}, u32[]{:S(2)}) %collective-permute-start.33) | collective-permute-done | bytes 1048608 | tf_op jit(solution)/shard_map/ppermute | solution.py:636
  339.1 5.2 collective-permute-done.32.refs_1_
  346.9 6.6 %collective-permute-done.34.refs_2_ = bf16[128,2048]{1,0:T(8,128)(2,1)S(1)} collective-permute-done((bf16[128,2048]{1,0:T(8,128)(2,1)S(1)}, bf16[128,2048]{1,0:T(8,128)(2,1)S(1)}, u32[]{:S(2)}, u32[]{:S(2)}) %collective-permute-start.34) | collective-permute-done | bytes 524320 | tf_op jit(solution)/shard_map/ppermute | solution.py:636
  353.5 5.6 %collective-permute-done.35.refs_3_ = bf16[128,2048]{1,0:T(8,128)(2,1)S(1)} collective-permute-done((bf16[128,2048]{1,0:T(8,128)(2,1)S(1)}, bf16[128,2048]{1,0:T(8,128)(2,1)S(1)}, u32[]{:S(2)}, u32[]{:S(2)}) %collective-permute-start.35) | collective-permute-done | bytes 524320 | tf_op jit(solution)/shard_map/ppermute | solution.py:636
  361.1 3.3 merge_terms.1
  368.4 2.8 collective-permute-start.44
  373.3 12.6 %attention_backward.1 = (bf16[1024,768]{1,0:T(8,128)(2,1)S(1)}, bf16[1024,768]{1,0:T(8,128)(2,1)S(1)}) custom-call(s32[1,8]{1,0:T(1,128)S(1)} %copy-done.31, s32[2]{0:T(128)S(1)} %copy-done.32, bf16[1024,256]{1,0:T(8,128)(2,1)S(1)} %get-tuple-element.229.do_ref, bf16[4,1024,256]{2,1,0:T(8,128)(2,1)S(1)} %copy-done.18, f32[1024,1]{1,0:T(8,128)S(1)} %copy-done.29, ...), custom_call_target="tpu_custom_call" | custom-call | flops 1024 | bytes 1024 | tf_op jit(solution)/shard_map/attention_backward/pallas_call | solution.py:247
  391.8 4.0 heads_term.1
  398.9 8.5 %collective-permute-done.44.refs_2_ = bf16[2,64,1024]{2,1,0:T(8,128)(2,1)} collective-permute-done((bf16[2,64,1024]{2,1,0:T(8,128)(2,1)}, bf16[2,64,1024]{2,1,0:T(8,128)(2,1)}, u32[]{:S(2)}, u32[]{:S(2)}) %collective-permute-start.44) | collective-permute-done | bytes 262176 | tf_op jit(solution)/shard_map/ppermute | solution.py:641
  410.1 3.0 back_rows.3
  427.6 9.2 %collective-permute-done.48 = bf16[128,2048]{1,0:T(8,128)(2,1)S(1)} collective-permute-done((bf16[128,2048]{1,0:T(8,128)(2,1)S(1)}, bf16[128,2048]{1,0:T(8,128)(2,1)S(1)}, u32[]{:S(2)}, u32[]{:S(2)}) %collective-permute-start.48) | collective-permute-done | bytes 524320 | tf_op jit(solution)/shard_map/ppermute | solution.py:636
  442.3 4.0 collective-permute-done.47
  446.3 3.1 collective-permute-done.49
  451.1 3.0 unfold_hidden.2
  458.0 6.5 %collective-permute-done.56 = bf16[256,2048]{1,0:T(8,128)(2,1)S(1)} collective-permute-done((bf16[256,2048]{1,0:T(8,128)(2,1)S(1)}, bf16[256,2048]{1,0:T(8,128)(2,1)S(1)}, u32[]{:S(2)}, u32[]{:S(2)}) %collective-permute-start.56) | collective-permute-done | bytes 1048608 | tf_op jit(solution)/shard_map/ppermute | solution.py:636
  468.4 7.3 %reduce-scatter.11.cloned.1.call-done = bf16[512,768]{1,0:T(8,128)(2,1)} async-done(((bf16[2048,768]{1,0:T(8,128)(2,1)}), bf16[512,768]{1,0:T(8,128)(2,1)}) %reduce-scatter.11.cloned.1.call-update) | async-done | bytes 786448 | tf_op jit(solution)/shard_map/reduce_scatter | solution.py:617
  475.7 4.2 all-to-all-start.1
  479.9 2.9 fusion.15
  486.3 3.6 collective-permute-done.57
  489.9 3.4 fusion.9
  495.7 6.7 %collective-permute-done.53.refs_2_ = bf16[2,64,1024]{2,1,0:T(8,128)(2,1)S(1)} collective-permute-done((bf16[2,64,1024]{2,1,0:T(8,128)(2,1)}, bf16[2,64,1024]{2,1,0:T(8,128)(2,1)S(1)}, u32[]{:S(2)}, u32[]{:S(2)}) %collective-permute-start.53) | collective-permute-done | bytes 262176 | tf_op jit(solution)/shard_map/ppermute | solution.py:641
  502.4 7.2 %collective-permute-done.54.refs_3_ = bf16[2,64,1024]{2,1,0:T(8,128)(2,1)} collective-permute-done((bf16[2,64,1024]{2,1,0:T(8,128)(2,1)}, bf16[2,64,1024]{2,1,0:T(8,128)(2,1)}, u32[]{:S(2)}, u32[]{:S(2)}) %collective-permute-start.54) | collective-permute-done | bytes 262176 | tf_op jit(solution)/shard_map/ppermute | solution.py:641
  (341 shorter events, 167.2 us)
Async XLA Ops:
  7.2 54.7 %all-gather.7.cloned.1.call-start = ((), (), s32[]{:S(2)}) async-start(), calls=%async_computation.6 | async-start | bytes 1310720 | tf_op jit(solution)/shard_map/all_gather | solution.py:613
  11.0 16.3 %collective-permute-start = (bf16[4,64,1024]{2,1,0:T(8,128)(2,1)}, bf16[4,64,1024]{2,1,0:T(8,128)(2,1)}, u32[]{:S(2)}, u32[]{:S(2)}) collective-permute-start(bf16[4,64,1024]{2,1,0:T(8,128)(2,1)} %dynamic-slice_bitcast_fusion.4), channel_id=1, source_target_pairs={{0,4},{4,0},{8,12},{12,8},{16,20},{20,16},{24,28},{28,24},{1,5},{5... | collective-permute-start | bytes 1572872 | tf_op jit(solution)/shard_map/ppermute | solution.py:630
  11.5 17.5 %collective-permute-start.5 = (bf16[128,2048]{1,0:T(8,128)(2,1)}, bf16[128,2048]{1,0:T(8,128)(2,1)}, u32[]{:S(2)}, u32[]{:S(2)}) collective-permute-start(bf16[128,2048]{1,0:T(8,128)(2,1)} %bitcast), channel_id=1, source_target_pairs={{0,16},{4,12},{8,24},{12,4},{16,0},{20,28},{24,8},{28,20},{1,17},{... | collective-permute-start | bytes 1572872 | tf_op jit(solution)/shard_map/ppermute | solution.py:636
  12.5 18.5 %collective-permute-start.7 = (bf16[128,2048]{1,0:T(8,128)(2,1)}, bf16[128,2048]{1,0:T(8,128)(2,1)}, u32[]{:S(2)}, u32[]{:S(2)}) collective-permute-start(bf16[128,2048]{1,0:T(8,128)(2,1)} %bitcast), channel_id=1, source_target_pairs={{0,4},{4,0},{8,12},{12,8},{16,20},{20,16},{24,28},{28,24},{1,5},{5... | collective-permute-start | bytes 1572872 | tf_op jit(solution)/shard_map/ppermute | solution.py:630
  14.0 14.9 %collective-permute-start.11 = (bf16[4,64,1024]{2,1,0:T(8,128)(2,1)}, bf16[4,64,1024]{2,1,0:T(8,128)(2,1)S(1)}, u32[]{:S(2)}, u32[]{:S(2)}) collective-permute-start(bf16[4,64,1024]{2,1,0:T(8,128)(2,1)} %get-tuple-element.299), channel_id=1, source_target_pairs={{0,4},{4,0},{8,12},{12,8},{16,20},{20,16},{24,28},{28,24},{1,5},{5... | collective-permute-start | bytes 1572872 | tf_op jit(solution)/shard_map/ppermute | solution.py:630
  23.7 32.3 %all-to-all-start = ((bf16[8,64,768]{2,1,0:T(8,128)(2,1)}), bf16[8,64,768]{2,1,0:T(8,128)(2,1)S(1)}, u32[]{:S(2)}, u32[]{:S(2)}) async-start(bf16[8,64,768]{2,1,0:T(8,128)(2,1)} %fold_heads.1), calls=%async_computation | async-start | bytes 1572864 | tf_op jit(solution)/shard_map/all_to_all | solution.py:621
  27.2 98.2 %all-gather.11.cloned.1.call-start = ((), (), s32[]{:S(2)}) async-start(), calls=%async_computation.12 | async-start | bytes 3932160 | tf_op jit(solution)/shard_map/all_gather | solution.py:613
  28.5 24.4 %collective-permute-start.2 = (bf16[2,64,1024]{2,1,0:T(8,128)(2,1)S(1)}, bf16[2,64,1024]{2,1,0:T(8,128)(2,1)S(1)}, u32[]{:S(2)}, u32[]{:S(2)}) collective-permute-start(bf16[2,64,1024]{2,1,0:T(8,128)(2,1)S(1)} %pad_maximum_fusion.3), channel_id=1, source_target_pairs={{0,2},{1,3},{2,0},{3,1},{4,6},{5,7},{6,4},{7,5},{8,10},{9,11},{10,... | collective-permute-start | bytes 786440 | tf_op jit(solution)/shard_map/ppermute | solution.py:641
  28.9 32.9 %collective-permute-start.8 = (bf16[128,2048]{1,0:T(8,128)(2,1)}, bf16[128,2048]{1,0:T(8,128)(2,1)S(1)}, u32[]{:S(2)}, u32[]{:S(2)}) collective-permute-start(bf16[128,2048]{1,0:T(8,128)(2,1)} %collective-permute-done.4), channel_id=1, source_target_pairs={{0,4},{4,0},{8,12},{12,8},{16,20},{20,16},{24,28},{28,24},{1,5},{5... | collective-permute-start | bytes 1572872 | tf_op jit(solution)/shard_map/ppermute | solution.py:630
  29.0 32.9 %collective-permute-start.9 = (bf16[128,2048]{1,0:T(8,128)(2,1)}, bf16[128,2048]{1,0:T(8,128)(2,1)S(1)}, u32[]{:S(2)}, u32[]{:S(2)}) collective-permute-start(bf16[128,2048]{1,0:T(8,128)(2,1)} %collective-permute-done.5), channel_id=1, source_target_pairs={{0,4},{4,0},{8,12},{12,8},{16,20},{20,16},{24,28},{28,24},{1,5},{5... | collective-permute-start | bytes 1572872 | tf_op jit(solution)/shard_map/ppermute | solution.py:630
  29.5 32.4 %collective-permute-start.10 = (bf16[128,2048]{1,0:T(8,128)(2,1)S(1)}, bf16[128,2048]{1,0:T(8,128)(2,1)}, u32[]{:S(2)}, u32[]{:S(2)}) collective-permute-start(bf16[128,2048]{1,0:T(8,128)(2,1)S(1)} %collective-permute-done.6), channel_id=1, source_target_pairs={{0,4},{4,0},{8,12},{12,8},{16,20},{20,16},{24,28},{28,24},{1,5},{5... | collective-permute-start | bytes 1572872 | tf_op jit(solution)/shard_map/ppermute | solution.py:630
  31.0 28.3 %collective-permute-start.3 = (bf16[2,64,1024]{2,1,0:T(8,128)(2,1)}, bf16[2,64,1024]{2,1,0:T(8,128)(2,1)}, u32[]{:S(2)}, u32[]{:S(2)}) collective-permute-start(bf16[2,64,1024]{2,1,0:T(8,128)(2,1)} %pad_maximum_fusion.4), channel_id=1, source_target_pairs={{0,3},{1,2},{2,1},{3,0},{4,7},{5,6},{6,5},{7,4},{8,11},{9,10},{10,... | collective-permute-start | bytes 786440 | tf_op jit(solution)/shard_map/ppermute | solution.py:641
  61.9 176.0 %all-gather.13.cloned.1.call-start = ((), (), s32[]{:S(2)}) async-start(), calls=%async_computation.13 | async-start | bytes 4718592 | tf_op jit(solution)/shard_map/all_gather | solution.py:613
  65.0 26.3 %collective-permute-start.12 = (bf16[512,1024]{1,0:T(8,128)(2,1)}, bf16[512,1024]{1,0:T(8,128)(2,1)S(1)}, u32[]{:S(2)}, u32[]{:S(2)}) collective-permute-start(bf16[512,1024]{1,0:T(8,128)(2,1)} %bitcast.105), channel_id=1, source_target_pairs={{0,8},{4,20},{8,0},{12,28},{16,24},{20,4},{24,16},{28,12},{1,9},{5... | collective-permute-start | bytes 3145736 | tf_op jit(solution)/shard_map/ppermute | solution.py:636
  65.4 48.3 %collective-permute-start.15 = (bf16[256,2048]{1,0:T(8,128)(2,1)}, bf16[256,2048]{1,0:T(8,128)(2,1)}, u32[]{:S(2)}, u32[]{:S(2)}) collective-permute-start(bf16[256,2048]{1,0:T(8,128)(2,1)} %refs_0_), channel_id=1, source_target_pairs={{0,8},{4,20},{8,0},{12,28},{16,24},{20,4},{24,16},{28,12},{1,9},{5... | collective-permute-start | bytes 3145736 | tf_op jit(solution)/shard_map/ppermute | solution.py:636
  67.1 173.2 %all-gather.9.cloned.1.call-start = ((), (), s32[]{:S(2)}) async-start(), calls=%async_computation.7 | async-start | bytes 4718592 | tf_op jit(solution)/shard_map/all_gather | solution.py:613
  67.2 46.6 %collective-permute-start.13 = (bf16[512,1024]{1,0:T(8,128)(2,1)}, bf16[512,1024]{1,0:T(8,128)(2,1)S(1)}, u32[]{:S(2)}, u32[]{:S(2)}) collective-permute-start(bf16[512,1024]{1,0:T(8,128)(2,1)} %bitcast.106), channel_id=1, source_target_pairs={{0,16},{4,12},{8,24},{12,4},{16,0},{20,28},{24,8},{28,20},{1,17},{... | collective-permute-start | bytes 3145736 | tf_op jit(solution)/shard_map/ppermute | solution.py:636
  91.3 22.5 %collective-permute-start.14 = (bf16[512,1024]{1,0:T(8,128)(2,1)S(1)}, bf16[512,1024]{1,0:T(8,128)(2,1)S(1)}, u32[]{:S(2)}, u32[]{:S(2)}) collective-permute-start(bf16[512,1024]{1,0:T(8,128)(2,1)S(1)} %collective-permute-done.12.refs_1_), channel_id=1, source_target_pairs={{0,16},{4,12},{8,24},{12,4},{16,0},{20,28},{24,8},{28,20},{1,17},{... | collective-permute-start | bytes 3145736 | tf_op jit(solution)/shard_map/ppermute | solution.py:636
  114.8 27.8 %collective-permute-start.16 = (bf16[256,2048]{1,0:T(8,128)(2,1)}, bf16[256,2048]{1,0:T(8,128)(2,1)}, u32[]{:S(2)}, u32[]{:S(2)}) collective-permute-start(bf16[256,2048]{1,0:T(8,128)(2,1)} %refs_0_), channel_id=1, source_target_pairs={{0,16},{4,12},{8,24},{12,4},{16,0},{20,28},{24,8},{28,20},{1,17},{... | collective-permute-start | bytes 3145736 | tf_op jit(solution)/shard_map/ppermute | solution.py:636
  116.3 26.2 %collective-permute-start.17 = (bf16[256,2048]{1,0:T(8,128)(2,1)}, bf16[256,2048]{1,0:T(8,128)(2,1)}, u32[]{:S(2)}, u32[]{:S(2)}) collective-permute-start(bf16[256,2048]{1,0:T(8,128)(2,1)} %collective-permute-done.15.refs_1_), channel_id=1, source_target_pairs={{0,16},{4,12},{8,24},{12,4},{16,0},{20,28},{24,8},{28,20},{1,17},{... | collective-permute-start | bytes 3145736 | tf_op jit(solution)/shard_map/ppermute | solution.py:636
  154.8 34.1 %collective-permute-start.22 = (bf16[2,64,1024]{2,1,0:T(8,128)(2,1)}, bf16[2,64,1024]{2,1,0:T(8,128)(2,1)}, u32[]{:S(2)}, u32[]{:S(2)}) collective-permute-start(bf16[2,64,1024]{2,1,0:T(8,128)(2,1)} %pad_maximum_fusion.8), channel_id=1, source_target_pairs={{0,1},{1,0},{2,3},{3,2},{4,5},{5,4},{6,7},{7,6},{8,9},{9,8},{10,11... | collective-permute-start | bytes 786440 | tf_op jit(solution)/shard_map/ppermute | solution.py:641
  155.4 31.8 %collective-permute-start.19 = (bf16[128,2048]{1,0:T(8,128)(2,1)}, bf16[128,2048]{1,0:T(8,128)(2,1)}, u32[]{:S(2)}, u32[]{:S(2)}) collective-permute-start(bf16[128,2048]{1,0:T(8,128)(2,1)} %get-tuple-element.287), channel_id=1, source_target_pairs={{0,16},{4,12},{8,24},{12,4},{16,0},{20,28},{24,8},{28,20},{1,17},{... | collective-permute-start | bytes 1572872 | tf_op jit(solution)/shard_map/ppermute | solution.py:636
  162.0 25.1 %collective-permute-start.21 = (bf16[128,2048]{1,0:T(8,128)(2,1)}, bf16[128,2048]{1,0:T(8,128)(2,1)S(1)}, u32[]{:S(2)}, u32[]{:S(2)}) collective-permute-start(bf16[128,2048]{1,0:T(8,128)(2,1)} %add_convert_fusion.18), channel_id=1, source_target_pairs={{0,8},{4,20},{8,0},{12,28},{16,24},{20,4},{24,16},{28,12},{1,9},{5... | collective-permute-start | bytes 1572872 | tf_op jit(solution)/shard_map/ppermute | solution.py:636
  163.3 25.7 %collective-permute-start.23 = (bf16[2,64,1024]{2,1,0:T(8,128)(2,1)}, bf16[2,64,1024]{2,1,0:T(8,128)(2,1)S(1)}, u32[]{:S(2)}, u32[]{:S(2)}) collective-permute-start(bf16[2,64,1024]{2,1,0:T(8,128)(2,1)} %pad_maximum_fusion.9), channel_id=1, source_target_pairs={{0,2},{1,3},{2,0},{3,1},{4,6},{5,7},{6,4},{7,5},{8,10},{9,11},{10,... | collective-permute-start | bytes 786440 | tf_op jit(solution)/shard_map/ppermute | solution.py:641
  165.8 26.9 %collective-permute-start.24 = (bf16[2,64,1024]{2,1,0:T(8,128)(2,1)}, bf16[2,64,1024]{2,1,0:T(8,128)(2,1)S(1)}, u32[]{:S(2)}, u32[]{:S(2)}) collective-permute-start(bf16[2,64,1024]{2,1,0:T(8,128)(2,1)} %pad_maximum_fusion.10), channel_id=1, source_target_pairs={{0,3},{1,2},{2,1},{3,0},{4,7},{5,6},{6,5},{7,4},{8,11},{9,10},{10,... | collective-permute-start | bytes 786440 | tf_op jit(solution)/shard_map/ppermute | solution.py:641
  193.9 129.5 %reduce-scatter.5.cloned.1.call-start = ((), (), s32[]{:S(2)}) async-start(), calls=%async_computation.8 | async-start | bytes 2621440 | tf_op jit(solution)/shard_map/reduce_scatter | solution.py:617
  196.2 25.8 %collective-permute-start.25 = (bf16[512,1024]{1,0:T(8,128)(2,1)}, bf16[512,1024]{1,0:T(8,128)(2,1)S(1)}, u32[]{:S(2)}, u32[]{:S(2)}) collective-permute-start(bf16[512,1024]{1,0:T(8,128)(2,1)} %bitcast.115), channel_id=1, source_target_pairs={{0,8},{4,20},{8,0},{12,28},{16,24},{20,4},{24,16},{28,12},{1,9},{5... | collective-permute-start | bytes 3145736 | tf_op jit(solution)/shard_map/ppermute | solution.py:636
  196.8 26.9 %collective-permute-start.26 = (bf16[512,1024]{1,0:T(8,128)(2,1)}, bf16[512,1024]{1,0:T(8,128)(2,1)}, u32[]{:S(2)}, u32[]{:S(2)}) collective-permute-start(bf16[512,1024]{1,0:T(8,128)(2,1)} %bitcast.116), channel_id=1, source_target_pairs={{0,16},{4,12},{8,24},{12,4},{16,0},{20,28},{24,8},{28,20},{1,17},{... | collective-permute-start | bytes 3145736 | tf_op jit(solution)/shard_map/ppermute | solution.py:636
  279.9 108.3 %reduce-scatter.7.cloned.1.call-start = ((), (), s32[]{:S(2)}) async-start(), calls=%async_computation.9 | async-start | bytes 2621440 | tf_op jit(solution)/shard_map/reduce_scatter | solution.py:617
  287.4 20.3 %collective-permute-start.29 = (bf16[512,1024]{1,0:T(8,128)(2,1)S(1)}, bf16[512,1024]{1,0:T(8,128)(2,1)S(1)}, u32[]{:S(2)}, u32[]{:S(2)}) collective-permute-start(bf16[512,1024]{1,0:T(8,128)(2,1)S(1)} %get-tuple-element.194), channel_id=1, source_target_pairs={{0,16},{4,12},{8,24},{12,4},{16,0},{20,28},{24,8},{28,20},{1,17},{... | collective-permute-start | bytes 3145736 | tf_op jit(solution)/shard_map/ppermute | solution.py:636
  288.9 24.6 %collective-permute-start.30 = (bf16[512,1024]{1,0:T(8,128)(2,1)S(1)}, bf16[512,1024]{1,0:T(8,128)(2,1)S(1)}, u32[]{:S(2)}, u32[]{:S(2)}) collective-permute-start(bf16[512,1024]{1,0:T(8,128)(2,1)S(1)} %get-tuple-element.195), channel_id=1, source_target_pairs={{0,16},{4,12},{8,24},{12,4},{16,0},{20,28},{24,8},{28,20},{1,17},{... | collective-permute-start | bytes 3145736 | tf_op jit(solution)/shard_map/ppermute | solution.py:636
  323.4 85.3 %reduce-scatter.9.cloned.1.call-start = ((), (), s32[]{:S(2)}) async-start(), calls=%async_computation.10 | async-start | bytes 1310720 | tf_op jit(solution)/shard_map/reduce_scatter | solution.py:617
  323.7 15.1 %collective-permute-start.33 = (bf16[512,1024]{1,0:T(8,128)(2,1)}, bf16[512,1024]{1,0:T(8,128)(2,1)S(1)}, u32[]{:S(2)}, u32[]{:S(2)}) collective-permute-start(bf16[512,1024]{1,0:T(8,128)(2,1)} %add_convert_fusion.11), channel_id=1, source_target_pairs={{0,8},{4,20},{8,0},{12,28},{16,24},{20,4},{24,16},{28,12},{1,9},{5... | collective-permute-start | bytes 3145736 | tf_op jit(solution)/shard_map/ppermute | solution.py:636
  325.1 19.3 %collective-permute-start.32 = (bf16[128,2048]{1,0:T(8,128)(2,1)S(1)}, bf16[128,2048]{1,0:T(8,128)(2,1)S(1)}, u32[]{:S(2)}, u32[]{:S(2)}) collective-permute-start(bf16[128,2048]{1,0:T(8,128)(2,1)S(1)} %fusion.35.refs_0_), channel_id=1, source_target_pairs={{0,8},{4,20},{8,0},{12,28},{16,24},{20,4},{24,16},{28,12},{1,9},{5... | collective-permute-start | bytes 1572872 | tf_op jit(solution)/shard_map/ppermute | solution.py:636
  364.4 111.3 %reduce-scatter.11.cloned.1.call-start = ((), (), s32[]{:S(2)}) async-start(), calls=%async_computation.11 | async-start | bytes 3932160 | tf_op jit(solution)/shard_map/reduce_scatter | solution.py:617
  364.8 42.7 %collective-permute-start.40 = (bf16[512,1024]{1,0:T(8,128)(2,1)}, bf16[512,1024]{1,0:T(8,128)(2,1)}, u32[]{:S(2)}, u32[]{:S(2)}) collective-permute-start(bf16[512,1024]{1,0:T(8,128)(2,1)} %convolution_convert_fusion.7), channel_id=1, source_target_pairs={{0,16},{4,12},{8,24},{12,4},{16,0},{20,28},{24,8},{28,20},{1,17},{... | collective-permute-start | bytes 3145736 | tf_op jit(solution)/shard_map/ppermute | solution.py:636
  366.2 41.3 %collective-permute-start.41 = (bf16[512,1024]{1,0:T(8,128)(2,1)}, bf16[512,1024]{1,0:T(8,128)(2,1)}, u32[]{:S(2)}, u32[]{:S(2)}) collective-permute-start(bf16[512,1024]{1,0:T(8,128)(2,1)} %convolution_convert_fusion.6), channel_id=1, source_target_pairs={{0,16},{4,12},{8,24},{12,4},{16,0},{20,28},{24,8},{28,20},{1,17},{... | collective-permute-start | bytes 3145736 | tf_op jit(solution)/shard_map/ppermute | solution.py:636
  367.6 31.3 %collective-permute-start.45 = (bf16[2,64,1024]{2,1,0:T(8,128)(2,1)}, bf16[2,64,1024]{2,1,0:T(8,128)(2,1)}, u32[]{:S(2)}, u32[]{:S(2)}) collective-permute-start(bf16[2,64,1024]{2,1,0:T(8,128)(2,1)} %pad_maximum_fusion.14), channel_id=1, source_target_pairs={{0,3},{1,2},{2,1},{3,0},{4,7},{5,6},{6,5},{7,4},{8,11},{9,10},{10,... | collective-permute-start | bytes 786440 | tf_op jit(solution)/shard_map/ppermute | solution.py:641
  368.4 39.1 %collective-permute-start.44 = (bf16[2,64,1024]{2,1,0:T(8,128)(2,1)}, bf16[2,64,1024]{2,1,0:T(8,128)(2,1)}, u32[]{:S(2)}, u32[]{:S(2)}) collective-permute-start(bf16[2,64,1024]{2,1,0:T(8,128)(2,1)} %pad_maximum_fusion.13), channel_id=1, source_target_pairs={{0,2},{1,3},{2,0},{3,1},{4,6},{5,7},{6,4},{7,5},{8,10},{9,11},{10,... | collective-permute-start | bytes 786440 | tf_op jit(solution)/shard_map/ppermute | solution.py:641
  371.9 35.6 %collective-permute-start.43 = (bf16[2,64,1024]{2,1,0:T(8,128)(2,1)}, bf16[2,64,1024]{2,1,0:T(8,128)(2,1)}, u32[]{:S(2)}, u32[]{:S(2)}) collective-permute-start(bf16[2,64,1024]{2,1,0:T(8,128)(2,1)} %pad_maximum_fusion.12), channel_id=1, source_target_pairs={{0,1},{1,0},{2,3},{3,2},{4,5},{5,4},{6,7},{7,6},{8,9},{9,8},{10,11... | collective-permute-start | bytes 786440 | tf_op jit(solution)/shard_map/ppermute | solution.py:641
  417.6 22.8 %collective-permute-start.50 = (bf16[512,1024]{1,0:T(8,128)(2,1)S(1)}, bf16[512,1024]{1,0:T(8,128)(2,1)S(1)}, u32[]{:S(2)}, u32[]{:S(2)}) collective-permute-start(bf16[512,1024]{1,0:T(8,128)(2,1)S(1)} %add_convert_fusion.8), channel_id=1, source_target_pairs={{0,8},{4,20},{8,0},{12,28},{16,24},{20,4},{24,16},{28,12},{1,9},{5... | collective-permute-start | bytes 3145736 | tf_op jit(solution)/shard_map/ppermute | solution.py:636
  421.9 14.9 %collective-permute-start.48 = (bf16[128,2048]{1,0:T(8,128)(2,1)S(1)}, bf16[128,2048]{1,0:T(8,128)(2,1)S(1)}, u32[]{:S(2)}, u32[]{:S(2)}) collective-permute-start(bf16[128,2048]{1,0:T(8,128)(2,1)S(1)} %get-tuple-element.286), channel_id=1, source_target_pairs={{0,16},{4,12},{8,24},{12,4},{16,0},{20,28},{24,8},{28,20},{1,17},{... | collective-permute-start | bytes 1572872 | tf_op jit(solution)/shard_map/ppermute | solution.py:636
  427.0 19.3 %collective-permute-start.47 = (bf16[128,2048]{1,0:T(8,128)(2,1)S(1)}, bf16[128,2048]{1,0:T(8,128)(2,1)S(1)}, u32[]{:S(2)}, u32[]{:S(2)}) collective-permute-start(bf16[128,2048]{1,0:T(8,128)(2,1)S(1)} %get-tuple-element.285), channel_id=1, source_target_pairs={{0,16},{4,12},{8,24},{12,4},{16,0},{20,28},{24,8},{28,20},{1,17},{... | collective-permute-start | bytes 1572872 | tf_op jit(solution)/shard_map/ppermute | solution.py:636
  457.2 29.1 %collective-permute-start.55 = (bf16[256,2048]{1,0:T(8,128)(2,1)}, bf16[256,2048]{1,0:T(8,128)(2,1)}, u32[]{:S(2)}, u32[]{:S(2)}) collective-permute-start(bf16[256,2048]{1,0:T(8,128)(2,1)} %convolution_convert_fusion.3), channel_id=1, source_target_pairs={{0,16},{4,12},{8,24},{12,4},{16,0},{20,28},{24,8},{28,20},{1,17},{... | collective-permute-start | bytes 3145736 | tf_op jit(solution)/shard_map/ppermute | solution.py:636
  465.9 24.0 %collective-permute-start.57 = (bf16[256,2048]{1,0:T(8,128)(2,1)}, bf16[256,2048]{1,0:T(8,128)(2,1)}, u32[]{:S(2)}, u32[]{:S(2)}) collective-permute-start(bf16[256,2048]{1,0:T(8,128)(2,1)} %add_convert_fusion.5), channel_id=1, source_target_pairs={{0,8},{4,20},{8,0},{12,28},{16,24},{20,4},{24,16},{28,12},{1,9},{5... | collective-permute-start | bytes 3145736 | tf_op jit(solution)/shard_map/ppermute | solution.py:636
  475.7 18.7 %all-to-all-start.1 = ((bf16[8,64,768]{2,1,0:T(8,128)(2,1)}), bf16[8,64,768]{2,1,0:T(8,128)(2,1)S(1)}, u32[]{:S(2)}, u32[]{:S(2)}) async-start(bf16[8,64,768]{2,1,0:T(8,128)(2,1)} %bitcast.118), calls=%async_computation.5 | async-start | bytes 1572864 | tf_op jit(solution)/shard_map/all_to_all | solution.py:621
  483.3 19.1 %collective-permute-start.53 = (bf16[2,64,1024]{2,1,0:T(8,128)(2,1)}, bf16[2,64,1024]{2,1,0:T(8,128)(2,1)S(1)}, u32[]{:S(2)}, u32[]{:S(2)}) collective-permute-start(bf16[2,64,1024]{2,1,0:T(8,128)(2,1)} %pad_maximum_fusion.17), channel_id=1, source_target_pairs={{0,2},{1,3},{2,0},{3,1},{4,6},{5,7},{6,4},{7,5},{8,10},{9,11},{10,... | collective-permute-start | bytes 786440 | tf_op jit(solution)/shard_map/ppermute | solution.py:641
  484.3 25.3 %collective-permute-start.54 = (bf16[2,64,1024]{2,1,0:T(8,128)(2,1)}, bf16[2,64,1024]{2,1,0:T(8,128)(2,1)}, u32[]{:S(2)}, u32[]{:S(2)}) collective-permute-start(bf16[2,64,1024]{2,1,0:T(8,128)(2,1)} %pad_maximum_fusion.18), channel_id=1, source_target_pairs={{0,3},{1,2},{2,1},{3,0},{4,7},{5,6},{6,5},{7,4},{8,11},{9,10},{10,... | collective-permute-start | bytes 786440 | tf_op jit(solution)/shard_map/ppermute | solution.py:641
  (83 other events, 683.0 us)
Sparse Core Ops, SparseCore 0:
  9.6 41.0 all-gather.6
  62.0 63.3 all-gather.10
  127.0 59.9 all-gather.12
  194.0 46.2 all-gather.8
  280.1 43.2 reduce-scatter.4
  325.6 43.1 reduce-scatter.6
  371.1 37.5 reduce-scatter.8
  413.3 62.2 reduce-scatter.10

commit v6 on v5

--- a/solution.py
+++ b/solution.py
@@ -767,14 +767,14 @@
     x_pieces = ctx_gather(tokens)
     up_pair = cores_pair(fold_hidden(up_weight, gain_second, n_plane, n_core, n_fsdp))
     turn = jnp.stack(rope_tables(length, cols))
-    own, gate_moved, x_pieces, up_pair, merge_rows = together(
-        (own, gate_moved, x_pieces, up_pair, merge_rows)
+    own, gate_moved[3:], x_pieces, up_pair, merge_rows = together(
+        (own, gate_moved[3:], x_pieces, up_pair, merge_rows)
     )
     qkv_weight = gather(own[:, None], "fsdp", axis=1).reshape(width, 3 * cols)
     gate_pieces = plane_gather(line_rows(gate_moved).reshape(d_rows, hid))
     down_pieces = plane_gather_more([down_weight])
     x_all = jnp.concatenate(x_pieces, axis=0)
-    x_all, gate_pieces, down_pieces = together((x_all, gate_pieces, down_pieces))
+    x_all, gate_pieces = together((x_all, gate_pieces))
     up_moved = lines_pair(up_pair)
     cot_all = gather(cotangent, TOK)
 
@@ -788,12 +788,12 @@
     mine = together(mm(attended[:half], merge_rows).astype(BF))
     mixed = own_f + ctx_scatter(theirs, mine, n_plane)
     lse_rows = lse[:, :8].T
-    x_t = x_all.reshape(length, n_ctx, n_fsdp, dev_rows).transpose(2, 1, 3, 0).reshape(width, length)
     gate_rows = place(gate_pieces, index).reshape(width, hid)
-    mixed, up_moved, lse_rows, x_t, down_rows, gate_rows = together(
-        (mixed, up_moved, lse_rows, x_t, down_rows, gate_rows)
-    )
-    up_pieces = plane_gather(line_rows(up_moved).reshape(d_rows, hid))
+    mixed, up_moved, lse_rows = together((mixed, up_moved, lse_rows))
+    up_pieces = plane_gather_more([line_rows(up_moved).reshape(d_rows, hid)])
+    gate_rows, down_rows, up_pieces = together((gate_rows, down_rows, up_pieces))
+    while len(up_pieces) < n_plane:
+        up_pieces = plane_gather_more(up_pieces)
     up_rows = place(up_pieces[:-1], index[:-1], n_plane)
     up_rows = lax.dynamic_update_slice(up_rows, up_pieces[-1][None], (index[-1], 0, 0)).reshape(width, hid)
 
@@ -803,10 +803,12 @@
     hidden, grad_gate, grad_up, theirs, mine = feed_forward(
         normed_all, cot_all, gate_rows, up_rows, down_rows
     )
-    e_two = (mine.astype(F32) + core_swap(theirs).astype(F32)).astype(BF)
+    theirs = core_swap(theirs)
+    gate_late = weight_rows(normed_all, grad_gate, index[n_plane // 2 :], d_rows)
+    theirs, gate_late = together((theirs, gate_late))
+    e_two = (mine.astype(F32) + theirs.astype(F32)).astype(BF)
 
     hidden, grad_gate, grad_up, e_two = together((hidden, grad_gate, grad_up, e_two))
-    gate_late = weight_rows(normed_all, grad_gate, index[n_plane // 2 :], d_rows)
     gate_chunks = list(weight_rows(normed_all, grad_gate, index[: n_plane // 2], d_rows)) + list(gate_late)
     gate_came = plane_send(gate_chunks)
     up_chunks = [together(t_mm(part(normed_all, at, d_rows, 1), grad_up).astype(BF)) for at in index]
@@ -817,15 +819,16 @@
     gate_chunks = plane_add(gate_chunks, gate_came)
     branch = (mine.astype(F32) + core_swap(theirs).astype(F32)).astype(BF)
     e_two = scatter(e_two, "fsdp")
-    e_two, gate_chunks, up_chunks, branch = together((e_two, gate_chunks, up_chunks, branch))
+    gate_sum = plane_scatter(gate_chunks)
+    e_two, gate_sum, up_chunks, branch = together((e_two, gate_sum, up_chunks, branch))
     branch_sum = scatter(branch, "fsdp")
-    gate_sum = plane_scatter(gate_chunks)
     e_two_f = e_two.astype(F32)
     grad_mixed = cotangent.astype(F32) + scale_second * (
         e_two_f - unit_second * jnp.mean(e_two_f * unit_second, axis=-1, keepdims=True)
     )
     branch_pieces = plane_gather_more([grad_mixed.astype(BF)])
-    branch_pieces, gate_sum = together((branch_pieces, gate_sum))
+    x_t = x_all.reshape(length, n_ctx, n_fsdp, dev_rows).transpose(2, 1, 3, 0).reshape(width, length)
+    branch_pieces, gate_sum, x_t = together((branch_pieces, gate_sum, x_t))
     gate_parts = lines_parts(cores_pair(gate_sum.reshape(n_core, n_fsdp, dev_rows, hid)))
     while len(branch_pieces) < n_plane:
         branch_pieces = plane_gather_more(branch_pieces)

time: 529 us -> 521 us (0.985)
  waiting for transfers between devices: 218 us -> 204 us
  local copies, waits for them, and re-layouts: 49 us -> 56.5 us
    ppermute x30, waiting for transfers between devices: 134 us -> 117 us  [plane_step(): lax.ppermute(value, CTX, [(i, i ^ 2 * steps[i % 2][step]) for i in range(...]
    ppermute x12, waiting for transfers between devices: 52.8 us -> 66.7 us  [line_swap(): return lax.ppermute(value, 'fsdp', [(i, i ^ mask) for i in range(n)])]
    all_to_all x2, waiting for transfers between devices: 1.07 us -> 8.15 us  [exchange(): return lax.all_to_all(value, axes, split_axis=0, concat_axis=0, tiled=True)]
    all_gather x4, waiting for transfers between devices: 6.91 us -> 0.86 us  [gather(): return lax.all_gather(value, axes, axis=axis, tiled=True)]
    ppermute x16, waiting for transfers between devices: 10.8 us -> 5.03 us  [core_swap(): return lax.ppermute(value, CTX, [(i, i ^ 1) for i in range(n)])]
    unnamed x133 -> x141, local copies, waits for them, and re-layouts: 27.5 us -> 32.1 us
    convert_element_type x9 -> x8, other arithmetic: 10.8 us -> 8.56 us  [plane_add(): (mine.astype(F32) + chunk.astype(F32)).astype(BF)]
  transfers between devices with their start and end apart: 68 -> 68, of which waited for: 34 -> 33; matrix products, arithmetic and copies ran while one was open for 18% -> 19% of each run, Pallas kernels for 14% -> 15%
where the time goes in v6:
time: 521 us; the launch traced here: 512 us
  waiting for transfers between devices  204 us (39%)
  Pallas kernels  113 us (22%)
  starting transfers between devices  56.9 us (11%)
  local copies, waits for them, and re-layouts  56.5 us (11%)
  other arithmetic  45.1 us (9%)
  matrix products  20.8 us (4%)
  between operations  15.5 us (3%)
    ppermute x30, waiting for transfers between devices, plane_step(): lax.ppermute(value, CTX, [(i, i ^ 2 * steps[i % 2][step]) for i in range(...  117 us
    ppermute x12, waiting for transfers between devices, line_swap(): return lax.ppermute(value, 'fsdp', [(i, i ^ mask) for i in range(n)])  66.7 us
    unnamed x141, local copies, waits for them, and re-layouts  32.1 us
    pallas_call x1, Pallas kernels, feed_forward(): pl.pallas_call(feed_forward_kernel, grid_spec=pltpu.PrefetchScalarGridSpe...  31.8 us
    ppermute x30, starting transfers between devices, plane_step(): lax.ppermute(value, CTX, [(i, i ^ 2 * steps[i % 2][step]) for i in range(...  31 us
    dot_general x8, matrix products, t_mm(): lax.dot_general(left, right, (((0,), (0,)), ((), ())), preferred_element_...  18.2 us
    pallas_call x1, Pallas kernels, attention_forward(): pl.pallas_call(functools.partial(forward_kernel, n_ctx, 256), out_shape=[...  17.1 us
    pallas_call x3, Pallas kernels, place(): pl.pallas_call(place_kernel, out_shape=jax.ShapeDtypeStruct((room or n,)...  13.3 us
  transfers between devices with their start and end apart: 68, of which 33 were waited for; matrix products, arithmetic and copies ran while one was open for 19% of the time, Pallas kernels for 15%

profile of v6, /device:TPU:18, one launch (start us, length us, event | category | flops | bytes accessed | tf_op | source)
XLA Modules:
  0.0 512.4 jit_solution(13977206152762465580)
XLA Ops:
  12.5 6.6 %collective-permute-done.2 = bf16[128,2048]{1,0:T(8,128)(2,1)} collective-permute-done((bf16[128,2048]{1,0:T(8,128)(2,1)}, bf16[128,2048]{1,0:T(8,128)(2,1)}, u32[]{:S(2)}, u32[]{:S(2)}) %collective-permute-start.2) | collective-permute-done | bytes 524320 | tf_op jit(solution)/shard_map/ppermute | solution.py:636
  25.0 3.5 all-to-all-start
  32.3 7.3 %all-to-all-done = bf16[8,64,768]{2,1,0:T(8,128)(2,1)S(1)} async-done(((bf16[8,64,768]{2,1,0:T(8,128)(2,1)}), bf16[8,64,768]{2,1,0:T(8,128)(2,1)S(1)}, u32[]{:S(2)}, u32[]{:S(2)}) %all-to-all-start) | async-done | bytes 786464 | tf_op jit(solution)/shard_map/all_to_all | solution.py:621
  39.5 8.4 %collective-permute-done.1.refs_3_ = bf16[2,64,1024]{2,1,0:T(8,128)(2,1)S(1)} collective-permute-done((bf16[2,64,1024]{2,1,0:T(8,128)(2,1)S(1)}, bf16[2,64,1024]{2,1,0:T(8,128)(2,1)S(1)}, u32[]{:S(2)}, u32[]{:S(2)}) %collective-permute-start.1) | collective-permute-done | bytes 262176 | tf_op jit(solution)/shard_map/ppermute | solution.py:641
  50.5 3.2 collective-permute-start.11
  55.5 11.9 %collective-permute-done.10.refs_1_ = bf16[2,64,1024]{2,1,0:T(8,128)(2,1)S(1)} collective-permute-done((bf16[2,64,1024]{2,1,0:T(8,128)(2,1)S(1)}, bf16[2,64,1024]{2,1,0:T(8,128)(2,1)S(1)}, u32[]{:S(2)}, u32[]{:S(2)}) %collective-permute-start.10) | collective-permute-done | bytes 262176 | tf_op jit(solution)/shard_map/ppermute | solution.py:641
  67.4 6.9 %collective-permute-done.11.refs_2_ = bf16[2,64,1024]{2,1,0:T(8,128)(2,1)S(1)} collective-permute-done((bf16[2,64,1024]{2,1,0:T(8,128)(2,1)S(1)}, bf16[2,64,1024]{2,1,0:T(8,128)(2,1)S(1)}, u32[]{:S(2)}, u32[]{:S(2)}) %collective-permute-start.11) | collective-permute-done | bytes 262176 | tf_op jit(solution)/shard_map/ppermute | solution.py:641
  90.0 13.6 %collective-permute-done.12.refs_1_ = bf16[512,1024]{1,0:T(8,128)(2,1)} collective-permute-done((bf16[512,1024]{1,0:T(8,128)(2,1)}, bf16[512,1024]{1,0:T(8,128)(2,1)}, u32[]{:S(2)}, u32[]{:S(2)}) %collective-permute-start.12) | collective-permute-done | bytes 1048608 | tf_op jit(solution)/shard_map/ppermute | solution.py:636
  113.2 6.6 %collective-permute-done.14.refs_3_ = bf16[512,1024]{1,0:T(8,128)(2,1)} collective-permute-done((bf16[512,1024]{1,0:T(8,128)(2,1)}, bf16[512,1024]{1,0:T(8,128)(2,1)}, u32[]{:S(2)}, u32[]{:S(2)}) %collective-permute-start.14) | collective-permute-done | bytes 1048608 | tf_op jit(solution)/shard_map/ppermute | solution.py:636
  119.9 17.1 %attention_forward.1 = (bf16[4,1024,256]{2,1,0:T(8,128)(2,1)}, f32[1024,1]{1,0:T(8,128)}, bf16[1024,256]{1,0:T(8,128)(2,1)}, f32[1024,128]{1,0:T(8,128)}) custom-call(s32[1,8]{1,0:T(1,128)} %pair_ref.3, s32[2]{0:T(128)} %pad_add_fusion.me_ref, bf16[1024,2048]{1,0:T(8,128)(2,1)} %constant_dynamic-update-slice_fusion.x_ref, bf16[2048,768]{1,0:T(8,128)(2,1)} %bitcast.98, ...), custom_call_target="tpu_custom_call" | custom-call | flops 1024 | bytes 1024 | tf_op jit(solution)/shard_map/attention_forward/pallas_call | solution.py:159
  139.0 3.5 collective-permute-start.18
  143.3 3.1 collective-permute-done.18
  151.5 5.8 %collective-permute-done.20 = bf16[128,2048]{1,0:T(8,128)(2,1)S(1)} collective-permute-done((bf16[128,2048]{1,0:T(8,128)(2,1)S(1)}, bf16[128,2048]{1,0:T(8,128)(2,1)S(1)}, u32[]{:S(2)}, u32[]{:S(2)}) %collective-permute-start.20) | collective-permute-done | bytes 524320 | tf_op jit(solution)/shard_map/ppermute | solution.py:636
  165.3 3.1 collective-permute-done.21
  170.8 9.9 %collective-permute-done.23.refs_2_ = bf16[2,64,1024]{2,1,0:T(8,128)(2,1)} collective-permute-done((bf16[2,64,1024]{2,1,0:T(8,128)(2,1)}, bf16[2,64,1024]{2,1,0:T(8,128)(2,1)}, u32[]{:S(2)}, u32[]{:S(2)}) %collective-permute-start.23) | collective-permute-done | bytes 262176 | tf_op jit(solution)/shard_map/ppermute | solution.py:641
  180.7 4.3 collective-permute-done.24.refs_3_
  190.7 4.4 place.3
  195.1 4.7 place.4
  199.8 3.7 collective-permute-done.25.refs_1_
  207.1 12.3 %collective-permute-done.26.refs_2_ = bf16[512,1024]{1,0:T(8,128)(2,1)} collective-permute-done((bf16[512,1024]{1,0:T(8,128)(2,1)S(1)}, bf16[512,1024]{1,0:T(8,128)(2,1)}, u32[]{:S(2)}, u32[]{:S(2)}) %collective-permute-start.26) | collective-permute-done | bytes 1048608 | tf_op jit(solution)/shard_map/ppermute | solution.py:636
  219.4 4.1 place.5
  223.5 7.0 %collective-permute-done.27 = bf16[512,1024]{1,0:T(8,128)(2,1)S(1)} collective-permute-done((bf16[512,1024]{1,0:T(8,128)(2,1)}, bf16[512,1024]{1,0:T(8,128)(2,1)S(1)}, u32[]{:S(2)}, u32[]{:S(2)}) %collective-permute-start.27) | collective-permute-done | bytes 1048608 | tf_op jit(solution)/shard_map/ppermute | solution.py:636
  232.4 31.8 %feed_forward.1 = (bf16[1024,1024]{1,0:T(8,128)(2,1)}, bf16[1024,1024]{1,0:T(8,128)(2,1)}, bf16[1024,1024]{1,0:T(8,128)(2,1)}, bf16[512,2048]{1,0:T(8,128)(2,1)}, bf16[512,2048]{1,0:T(8,128)(2,1)}) custom-call(s32[1]{0:T(128)} %bitcast.2.core_ref, bf16[1024,2048]{1,0:T(8,128)(2,1)} %all-gather.9.cloned.1.call-done.n_ref.left_ref, ...), custom_call_target="tpu_custom_call" | custom-call | flops 1024 | bytes 1024 | tf_op jit(solution)/shard_map/feed_forward/pallas_call | solution.py:301
  266.1 3.5 weight_rows.2
  276.0 4.2 convolution_convert_fusion.6
  280.2 5.6 %branch_rows.1 = (bf16[512,2048]{1,0:T(8,128)(2,1)S(1)}, bf16[512,2048]{1,0:T(8,128)(2,1)S(1)}) custom-call(s32[1]{0:T(128)} %bitcast.2.core_ref, bf16[1024,1024]{1,0:T(8,128)(2,1)S(1)} %copy-done.17, bf16[1024,2048]{1,0:T(8,128)(2,1)S(1)} %bitcast.97), custom_call_target="tpu_custom_call" | custom-call | flops 1024 | bytes 1024 | tf_op jit(solution)/shard_map/branch_rows/pallas_call | solution.py:345
  285.9 3.5 weight_rows.3
  296.3 4.0 collective-permute-done.30
  301.3 14.2 %collective-permute-done.31 = bf16[512,1024]{1,0:T(8,128)(2,1)S(1)} collective-permute-done((bf16[512,1024]{1,0:T(8,128)(2,1)S(1)}, bf16[512,1024]{1,0:T(8,128)(2,1)S(1)}, u32[]{:S(2)}, u32[]{:S(2)}) %collective-permute-start.31) | collective-permute-done | bytes 1048608 | tf_op jit(solution)/shard_map/ppermute | solution.py:636
  323.0 6.3 %copy.37 = bf16[1024,2048]{0,1:T(8,128)(2,1)} copy(bf16[1024,2048]{1,0:T(8,128)(2,1)} %constant_dynamic-update-slice_fusion.x_ref) | data formatting | bytes 8388608 | tf_op jit(solution)/shard_map/optimization_barrier | solution.py:625
  329.3 5.0 copy.38
  336.8 6.6 %collective-permute-done.34.refs_2_ = bf16[128,2048]{1,0:T(8,128)(2,1)S(1)} collective-permute-done((bf16[128,2048]{1,0:T(8,128)(2,1)S(1)}, bf16[128,2048]{1,0:T(8,128)(2,1)S(1)}, u32[]{:S(2)}, u32[]{:S(2)}) %collective-permute-start.34) | collective-permute-done | bytes 524320 | tf_op jit(solution)/shard_map/ppermute | solution.py:636
  343.5 5.6 %collective-permute-done.35.refs_3_ = bf16[128,2048]{1,0:T(8,128)(2,1)S(1)} collective-permute-done((bf16[128,2048]{1,0:T(8,128)(2,1)S(1)}, bf16[128,2048]{1,0:T(8,128)(2,1)S(1)}, u32[]{:S(2)}, u32[]{:S(2)}) %collective-permute-start.35) | collective-permute-done | bytes 524320 | tf_op jit(solution)/shard_map/ppermute | solution.py:636
  351.0 3.3 merge_terms.1
  365.3 12.6 %attention_backward.1 = (bf16[1024,768]{1,0:T(8,128)(2,1)S(1)}, bf16[1024,768]{1,0:T(8,128)(2,1)S(1)}) custom-call(s32[1,8]{1,0:T(1,128)S(1)} %copy-done.32, s32[2]{0:T(128)S(1)} %copy-done.33, bf16[1024,256]{1,0:T(8,128)(2,1)S(1)} %get-tuple-element.227.do_ref, bf16[4,1024,256]{2,1,0:T(8,128)(2,1)S(1)} %copy-done.19, f32[1024,1]{1,0:T(8,128)S(1)} %copy-done.30, ...), custom_call_target="tpu_custom_call" | custom-call | flops 1024 | bytes 1024 | tf_op jit(solution)/shard_map/attention_backward/pallas_call | solution.py:247
  383.8 4.0 heads_term.1
  390.2 11.0 %collective-permute-done.44.refs_2_ = bf16[2,64,1024]{2,1,0:T(8,128)(2,1)} collective-permute-done((bf16[2,64,1024]{2,1,0:T(8,128)(2,1)}, bf16[2,64,1024]{2,1,0:T(8,128)(2,1)}, u32[]{:S(2)}, u32[]{:S(2)}) %collective-permute-start.44) | collective-permute-done | bytes 262176 | tf_op jit(solution)/shard_map/ppermute | solution.py:641
  402.7 3.0 back_rows.3
  420.6 9.2 %collective-permute-done.48 = bf16[128,2048]{1,0:T(8,128)(2,1)S(1)} collective-permute-done((bf16[128,2048]{1,0:T(8,128)(2,1)S(1)}, bf16[128,2048]{1,0:T(8,128)(2,1)S(1)}, u32[]{:S(2)}, u32[]{:S(2)}) %collective-permute-start.48) | collective-permute-done | bytes 524320 | tf_op jit(solution)/shard_map/ppermute | solution.py:636
  434.9 4.1 collective-permute-done.47
  442.9 3.0 unfold_hidden.2
  450.5 6.4 %collective-permute-done.56 = bf16[256,2048]{1,0:T(8,128)(2,1)S(1)} collective-permute-done((bf16[256,2048]{1,0:T(8,128)(2,1)S(1)}, bf16[256,2048]{1,0:T(8,128)(2,1)S(1)}, u32[]{:S(2)}, u32[]{:S(2)}) %collective-permute-start.56) | collective-permute-done | bytes 1048608 | tf_op jit(solution)/shard_map/ppermute | solution.py:636
  460.4 6.7 %reduce-scatter.11.cloned.1.call-done = bf16[512,768]{1,0:T(8,128)(2,1)} async-done(((bf16[2048,768]{1,0:T(8,128)(2,1)}), bf16[512,768]{1,0:T(8,128)(2,1)}) %reduce-scatter.11.cloned.1.call-update) | async-done | bytes 786448 | tf_op jit(solution)/shard_map/reduce_scatter | solution.py:617
  467.1 4.2 all-to-all-start.1
  477.7 4.8 collective-permute-done.57
  482.5 3.4 fusion.9
  488.2 5.6 %collective-permute-done.53.refs_2_ = bf16[2,64,1024]{2,1,0:T(8,128)(2,1)S(1)} collective-permute-done((bf16[2,64,1024]{2,1,0:T(8,128)(2,1)}, bf16[2,64,1024]{2,1,0:T(8,128)(2,1)S(1)}, u32[]{:S(2)}, u32[]{:S(2)}) %collective-permute-start.53) | collective-permute-done | bytes 262176 | tf_op jit(solution)/shard_map/ppermute | solution.py:641
  493.8 7.2 %collective-permute-done.54.refs_3_ = bf16[2,64,1024]{2,1,0:T(8,128)(2,1)} collective-permute-done((bf16[2,64,1024]{2,1,0:T(8,128)(2,1)}, bf16[2,64,1024]{2,1,0:T(8,128)(2,1)}, u32[]{:S(2)}, u32[]{:S(2)}) %collective-permute-start.54) | collective-permute-done | bytes 262176 | tf_op jit(solution)/shard_map/ppermute | solution.py:641
  (348 shorter events, 166.8 us)
Async XLA Ops:
  7.2 40.9 %all-gather.7.cloned.1.call-start = ((), (), s32[]{:S(2)}) async-start(), calls=%async_computation.6 | async-start | bytes 1310720 | tf_op jit(solution)/shard_map/all_gather | solution.py:613
  11.0 18.2 %collective-permute-start = (bf16[4,64,1024]{2,1,0:T(8,128)(2,1)}, bf16[4,64,1024]{2,1,0:T(8,128)(2,1)}, u32[]{:S(2)}, u32[]{:S(2)}) collective-permute-start(bf16[4,64,1024]{2,1,0:T(8,128)(2,1)} %dynamic-slice_bitcast_fusion.4), channel_id=1, source_target_pairs={{0,4},{4,0},{8,12},{12,8},{16,20},{20,16},{24,28},{28,24},{1,5},{5... | collective-permute-start | bytes 1572872 | tf_op jit(solution)/shard_map/ppermute | solution.py:630
  11.5 17.8 %collective-permute-start.3 = (bf16[128,2048]{1,0:T(8,128)(2,1)}, bf16[128,2048]{1,0:T(8,128)(2,1)}, u32[]{:S(2)}, u32[]{:S(2)}) collective-permute-start(bf16[128,2048]{1,0:T(8,128)(2,1)} %bitcast), channel_id=1, source_target_pairs={{0,16},{4,12},{8,24},{12,4},{16,0},{20,28},{24,8},{28,20},{1,17},{... | collective-permute-start | bytes 1572872 | tf_op jit(solution)/shard_map/ppermute | solution.py:636
  25.0 14.5 %all-to-all-start = ((bf16[8,64,768]{2,1,0:T(8,128)(2,1)}), bf16[8,64,768]{2,1,0:T(8,128)(2,1)S(1)}, u32[]{:S(2)}, u32[]{:S(2)}) async-start(bf16[8,64,768]{2,1,0:T(8,128)(2,1)} %fold_heads.1), calls=%async_computation | async-start | bytes 1572864 | tf_op jit(solution)/shard_map/all_to_all | solution.py:621
  28.5 91.3 %all-gather.11.cloned.1.call-start = ((), (), s32[]{:S(2)}) async-start(), calls=%async_computation.12 | async-start | bytes 3932160 | tf_op jit(solution)/shard_map/all_gather | solution.py:613
  29.2 18.8 %collective-permute-start.6 = (bf16[128,2048]{1,0:T(8,128)(2,1)}, bf16[128,2048]{1,0:T(8,128)(2,1)}, u32[]{:S(2)}, u32[]{:S(2)}) collective-permute-start(bf16[128,2048]{1,0:T(8,128)(2,1)} %collective-permute-done.2), channel_id=1, source_target_pairs={{0,4},{4,0},{8,12},{12,8},{16,20},{20,16},{24,28},{28,24},{1,5},{5... | collective-permute-start | bytes 1572872 | tf_op jit(solution)/shard_map/ppermute | solution.py:630
  29.3 18.7 %collective-permute-start.7 = (bf16[128,2048]{1,0:T(8,128)(2,1)}, bf16[128,2048]{1,0:T(8,128)(2,1)}, u32[]{:S(2)}, u32[]{:S(2)}) collective-permute-start(bf16[128,2048]{1,0:T(8,128)(2,1)} %collective-permute-done.3), channel_id=1, source_target_pairs={{0,4},{4,0},{8,12},{12,8},{16,20},{20,16},{24,28},{28,24},{1,5},{5... | collective-permute-start | bytes 1572872 | tf_op jit(solution)/shard_map/ppermute | solution.py:630
  29.7 18.3 %collective-permute-start.8 = (bf16[128,2048]{1,0:T(8,128)(2,1)}, bf16[128,2048]{1,0:T(8,128)(2,1)}, u32[]{:S(2)}, u32[]{:S(2)}) collective-permute-start(bf16[128,2048]{1,0:T(8,128)(2,1)} %collective-permute-done.4), channel_id=1, source_target_pairs={{0,4},{4,0},{8,12},{12,8},{16,20},{20,16},{24,28},{28,24},{1,5},{5... | collective-permute-start | bytes 1572872 | tf_op jit(solution)/shard_map/ppermute | solution.py:630
  31.7 16.2 %collective-permute-start.1 = (bf16[2,64,1024]{2,1,0:T(8,128)(2,1)S(1)}, bf16[2,64,1024]{2,1,0:T(8,128)(2,1)S(1)}, u32[]{:S(2)}, u32[]{:S(2)}) collective-permute-start(bf16[2,64,1024]{2,1,0:T(8,128)(2,1)S(1)} %pad_maximum_fusion.1), channel_id=1, source_target_pairs={{0,3},{1,2},{2,1},{3,0},{4,7},{5,6},{6,5},{7,4},{8,11},{9,10},{10,... | collective-permute-start | bytes 786440 | tf_op jit(solution)/shard_map/ppermute | solution.py:641
  48.1 183.5 %all-gather.13.cloned.1.call-start = ((), (), s32[]{:S(2)}) async-start(), calls=%async_computation.13 | async-start | bytes 4718592 | tf_op jit(solution)/shard_map/all_gather | solution.py:613
  48.1 34.2 %collective-permute-start.15 = (bf16[256,2048]{1,0:T(8,128)(2,1)}, bf16[256,2048]{1,0:T(8,128)(2,1)}, u32[]{:S(2)}, u32[]{:S(2)}) collective-permute-start(bf16[256,2048]{1,0:T(8,128)(2,1)} %refs_0_), channel_id=1, source_target_pairs={{0,8},{4,20},{8,0},{12,28},{16,24},{20,4},{24,16},{28,12},{1,9},{5... | collective-permute-start | bytes 3145736 | tf_op jit(solution)/shard_map/ppermute | solution.py:636
  48.5 88.5 %collective-permute-start.16 = (bf16[256,2048]{1,0:T(8,128)(2,1)}, bf16[256,2048]{1,0:T(8,128)(2,1)}, u32[]{:S(2)}, u32[]{:S(2)}) collective-permute-start(bf16[256,2048]{1,0:T(8,128)(2,1)} %refs_0_), channel_id=1, source_target_pairs={{0,16},{4,12},{8,24},{12,4},{16,0},{20,28},{24,8},{28,20},{1,17},{... | collective-permute-start | bytes 3145736 | tf_op jit(solution)/shard_map/ppermute | solution.py:636
  50.2 182.1 %all-gather.9.cloned.1.call-start = ((), (), s32[]{:S(2)}) async-start(), calls=%async_computation.7 | async-start | bytes 4718592 | tf_op jit(solution)/shard_map/all_gather | solution.py:613
  50.4 17.0 %collective-permute-start.10 = (bf16[2,64,1024]{2,1,0:T(8,128)(2,1)S(1)}, bf16[2,64,1024]{2,1,0:T(8,128)(2,1)S(1)}, u32[]{:S(2)}, u32[]{:S(2)}) collective-permute-start(bf16[2,64,1024]{2,1,0:T(8,128)(2,1)S(1)} %pad_maximum_fusion.3), channel_id=1, source_target_pairs={{0,1},{1,0},{2,3},{3,2},{4,5},{5,4},{6,7},{7,6},{8,9},{9,8},{10,11... | collective-permute-start | bytes 786440 | tf_op jit(solution)/shard_map/ppermute | solution.py:641
  50.5 23.8 %collective-permute-start.11 = (bf16[2,64,1024]{2,1,0:T(8,128)(2,1)S(1)}, bf16[2,64,1024]{2,1,0:T(8,128)(2,1)S(1)}, u32[]{:S(2)}, u32[]{:S(2)}) collective-permute-start(bf16[2,64,1024]{2,1,0:T(8,128)(2,1)S(1)} %pad_maximum_fusion.4), channel_id=1, source_target_pairs={{0,2},{1,3},{2,0},{3,1},{4,6},{5,7},{6,4},{7,5},{8,10},{9,11},{10,... | collective-permute-start | bytes 786440 | tf_op jit(solution)/shard_map/ppermute | solution.py:641
  77.2 26.4 %collective-permute-start.12 = (bf16[512,1024]{1,0:T(8,128)(2,1)}, bf16[512,1024]{1,0:T(8,128)(2,1)}, u32[]{:S(2)}, u32[]{:S(2)}) collective-permute-start(bf16[512,1024]{1,0:T(8,128)(2,1)} %bitcast.105), channel_id=1, source_target_pairs={{0,8},{4,20},{8,0},{12,28},{16,24},{20,4},{24,16},{28,12},{1,9},{5... | collective-permute-start | bytes 3145736 | tf_op jit(solution)/shard_map/ppermute | solution.py:636
  82.3 54.7 %collective-permute-start.17 = (bf16[256,2048]{1,0:T(8,128)(2,1)}, bf16[256,2048]{1,0:T(8,128)(2,1)S(1)}, u32[]{:S(2)}, u32[]{:S(2)}) collective-permute-start(bf16[256,2048]{1,0:T(8,128)(2,1)} %collective-permute-done.15.refs_1_), channel_id=1, source_target_pairs={{0,16},{4,12},{8,24},{12,4},{16,0},{20,28},{24,8},{28,20},{1,17},{... | collective-permute-start | bytes 3145736 | tf_op jit(solution)/shard_map/ppermute | solution.py:636
  82.5 29.8 %collective-permute-start.13 = (bf16[512,1024]{1,0:T(8,128)(2,1)S(1)}, bf16[512,1024]{1,0:T(8,128)(2,1)S(1)}, u32[]{:S(2)}, u32[]{:S(2)}) collective-permute-start(bf16[512,1024]{1,0:T(8,128)(2,1)S(1)} %bitcast.107), channel_id=1, source_target_pairs={{0,16},{4,12},{8,24},{12,4},{16,0},{20,28},{24,8},{28,20},{1,17},{... | collective-permute-start | bytes 3145736 | tf_op jit(solution)/shard_map/ppermute | solution.py:636
  103.6 16.2 %collective-permute-start.14 = (bf16[512,1024]{1,0:T(8,128)(2,1)}, bf16[512,1024]{1,0:T(8,128)(2,1)}, u32[]{:S(2)}, u32[]{:S(2)}) collective-permute-start(bf16[512,1024]{1,0:T(8,128)(2,1)} %collective-permute-done.12.refs_1_), channel_id=1, source_target_pairs={{0,16},{4,12},{8,24},{12,4},{16,0},{20,28},{24,8},{28,20},{1,17},{... | collective-permute-start | bytes 3145736 | tf_op jit(solution)/shard_map/ppermute | solution.py:636
  151.1 19.7 %collective-permute-start.22 = (bf16[2,64,1024]{2,1,0:T(8,128)(2,1)}, bf16[2,64,1024]{2,1,0:T(8,128)(2,1)}, u32[]{:S(2)}, u32[]{:S(2)}) collective-permute-start(bf16[2,64,1024]{2,1,0:T(8,128)(2,1)} %pad_maximum_fusion.8), channel_id=1, source_target_pairs={{0,1},{1,0},{2,3},{3,2},{4,5},{5,4},{6,7},{7,6},{8,9},{9,8},{10,11... | collective-permute-start | bytes 786440 | tf_op jit(solution)/shard_map/ppermute | solution.py:641
  151.1 14.2 %collective-permute-start.19 = (bf16[128,2048]{1,0:T(8,128)(2,1)}, bf16[128,2048]{1,0:T(8,128)(2,1)}, u32[]{:S(2)}, u32[]{:S(2)}) collective-permute-start(bf16[128,2048]{1,0:T(8,128)(2,1)} %get-tuple-element.285), channel_id=1, source_target_pairs={{0,16},{4,12},{8,24},{12,4},{16,0},{20,28},{24,8},{28,20},{1,17},{... | collective-permute-start | bytes 1572872 | tf_op jit(solution)/shard_map/ppermute | solution.py:636
  161.0 19.7 %collective-permute-start.23 = (bf16[2,64,1024]{2,1,0:T(8,128)(2,1)}, bf16[2,64,1024]{2,1,0:T(8,128)(2,1)}, u32[]{:S(2)}, u32[]{:S(2)}) collective-permute-start(bf16[2,64,1024]{2,1,0:T(8,128)(2,1)} %pad_maximum_fusion.9), channel_id=1, source_target_pairs={{0,2},{1,3},{2,0},{3,1},{4,6},{5,7},{6,4},{7,5},{8,10},{9,11},{10,... | collective-permute-start | bytes 786440 | tf_op jit(solution)/shard_map/ppermute | solution.py:641
  161.8 23.3 %collective-permute-start.24 = (bf16[2,64,1024]{2,1,0:T(8,128)(2,1)}, bf16[2,64,1024]{2,1,0:T(8,128)(2,1)}, u32[]{:S(2)}, u32[]{:S(2)}) collective-permute-start(bf16[2,64,1024]{2,1,0:T(8,128)(2,1)} %pad_maximum_fusion.10), channel_id=1, source_target_pairs={{0,3},{1,2},{2,1},{3,0},{4,7},{5,6},{6,5},{7,4},{8,11},{9,10},{10,... | collective-permute-start | bytes 786440 | tf_op jit(solution)/shard_map/ppermute | solution.py:641
  186.1 133.1 %reduce-scatter.5.cloned.1.call-start = ((), (), s32[]{:S(2)}) async-start(), calls=%async_computation.8 | async-start | bytes 2621440 | tf_op jit(solution)/shard_map/reduce_scatter | solution.py:617
  188.5 15.0 %collective-permute-start.25 = (bf16[512,1024]{1,0:T(8,128)(2,1)}, bf16[512,1024]{1,0:T(8,128)(2,1)S(1)}, u32[]{:S(2)}, u32[]{:S(2)}) collective-permute-start(bf16[512,1024]{1,0:T(8,128)(2,1)} %bitcast.115), channel_id=1, source_target_pairs={{0,8},{4,20},{8,0},{12,28},{16,24},{20,4},{24,16},{28,12},{1,9},{5... | collective-permute-start | bytes 3145736 | tf_op jit(solution)/shard_map/ppermute | solution.py:636
  204.4 14.9 %collective-permute-start.26 = (bf16[512,1024]{1,0:T(8,128)(2,1)S(1)}, bf16[512,1024]{1,0:T(8,128)(2,1)}, u32[]{:S(2)}, u32[]{:S(2)}) collective-permute-start(bf16[512,1024]{1,0:T(8,128)(2,1)S(1)} %bitcast.117), channel_id=1, source_target_pairs={{0,16},{4,12},{8,24},{12,4},{16,0},{20,28},{24,8},{28,20},{1,17},{... | collective-permute-start | bytes 3145736 | tf_op jit(solution)/shard_map/ppermute | solution.py:636
  205.2 25.3 %collective-permute-start.27 = (bf16[512,1024]{1,0:T(8,128)(2,1)}, bf16[512,1024]{1,0:T(8,128)(2,1)S(1)}, u32[]{:S(2)}, u32[]{:S(2)}) collective-permute-start(bf16[512,1024]{1,0:T(8,128)(2,1)} %copy-done.56), channel_id=1, source_target_pairs={{0,16},{4,12},{8,24},{12,4},{16,0},{20,28},{24,8},{28,20},{1,17},{... | collective-permute-start | bytes 3145736 | tf_op jit(solution)/shard_map/ppermute | solution.py:636
  273.9 106.3 %reduce-scatter.7.cloned.1.call-start = ((), (), s32[]{:S(2)}) async-start(), calls=%async_computation.9 | async-start | bytes 2621440 | tf_op jit(solution)/shard_map/reduce_scatter | solution.py:617
  273.9 22.3 %collective-permute-start.29 = (bf16[512,1024]{1,0:T(8,128)(2,1)}, bf16[512,1024]{1,0:T(8,128)(2,1)S(1)}, u32[]{:S(2)}, u32[]{:S(2)}) collective-permute-start(bf16[512,1024]{1,0:T(8,128)(2,1)} %copy-done.35), channel_id=1, source_target_pairs={{0,16},{4,12},{8,24},{12,4},{16,0},{20,28},{24,8},{28,20},{1,17},{... | collective-permute-start | bytes 3145736 | tf_op jit(solution)/shard_map/ppermute | solution.py:636
  275.5 24.8 %collective-permute-start.30 = (bf16[512,1024]{1,0:T(8,128)(2,1)}, bf16[512,1024]{1,0:T(8,128)(2,1)S(1)}, u32[]{:S(2)}, u32[]{:S(2)}) collective-permute-start(bf16[512,1024]{1,0:T(8,128)(2,1)} %copy-done.34), channel_id=1, source_target_pairs={{0,16},{4,12},{8,24},{12,4},{16,0},{20,28},{24,8},{28,20},{1,17},{... | collective-permute-start | bytes 3145736 | tf_op jit(solution)/shard_map/ppermute | solution.py:636
  300.3 16.9 %collective-permute-start.32 = (bf16[512,2048]{1,0:T(8,128)(2,1)S(1)}, bf16[512,2048]{1,0:T(8,128)(2,1)S(1)}, u32[]{:S(2)}, u32[]{:S(2)}) collective-permute-start(bf16[512,2048]{1,0:T(8,128)(2,1)S(1)} %get-tuple-element.208), channel_id=1, source_target_pairs={{0,4},{4,0},{8,12},{12,8},{16,20},{20,16},{24,28},{28,24},{1,5},{5... | collective-permute-start | bytes 6291464 | tf_op jit(solution)/shard_map/ppermute | solution.py:630
  300.7 14.9 %collective-permute-start.31 = (bf16[512,1024]{1,0:T(8,128)(2,1)S(1)}, bf16[512,1024]{1,0:T(8,128)(2,1)S(1)}, u32[]{:S(2)}, u32[]{:S(2)}) collective-permute-start(bf16[512,1024]{1,0:T(8,128)(2,1)S(1)} %add_convert_fusion.11), channel_id=1, source_target_pairs={{0,8},{4,20},{8,0},{12,28},{16,24},{20,4},{24,16},{28,12},{1,9},{5... | collective-permute-start | bytes 3145736 | tf_op jit(solution)/shard_map/ppermute | solution.py:636
  319.3 81.9 %reduce-scatter.9.cloned.1.call-start = ((), (), s32[]{:S(2)}) async-start(), calls=%async_computation.10 | async-start | bytes 1310720 | tf_op jit(solution)/shard_map/reduce_scatter | solution.py:617
  354.4 112.7 %reduce-scatter.11.cloned.1.call-start = ((), (), s32[]{:S(2)}) async-start(), calls=%async_computation.11 | async-start | bytes 3932160 | tf_op jit(solution)/shard_map/reduce_scatter | solution.py:617
  356.1 45.1 %collective-permute-start.40 = (bf16[512,1024]{1,0:T(8,128)(2,1)}, bf16[512,1024]{1,0:T(8,128)(2,1)}, u32[]{:S(2)}, u32[]{:S(2)}) collective-permute-start(bf16[512,1024]{1,0:T(8,128)(2,1)} %convolution_convert_fusion.7), channel_id=1, source_target_pairs={{0,16},{4,12},{8,24},{12,4},{16,0},{20,28},{24,8},{28,20},{1,17},{... | collective-permute-start | bytes 3145736 | tf_op jit(solution)/shard_map/ppermute | solution.py:636
  357.5 43.7 %collective-permute-start.41 = (bf16[512,1024]{1,0:T(8,128)(2,1)}, bf16[512,1024]{1,0:T(8,128)(2,1)}, u32[]{:S(2)}, u32[]{:S(2)}) collective-permute-start(bf16[512,1024]{1,0:T(8,128)(2,1)} %convolution_convert_fusion.6), channel_id=1, source_target_pairs={{0,16},{4,12},{8,24},{12,4},{16,0},{20,28},{24,8},{28,20},{1,17},{... | collective-permute-start | bytes 3145736 | tf_op jit(solution)/shard_map/ppermute | solution.py:636
  358.9 31.2 %collective-permute-start.45 = (bf16[2,64,1024]{2,1,0:T(8,128)(2,1)}, bf16[2,64,1024]{2,1,0:T(8,128)(2,1)}, u32[]{:S(2)}, u32[]{:S(2)}) collective-permute-start(bf16[2,64,1024]{2,1,0:T(8,128)(2,1)} %pad_maximum_fusion.14), channel_id=1, source_target_pairs={{0,3},{1,2},{2,1},{3,0},{4,7},{5,6},{6,5},{7,4},{8,11},{9,10},{10,... | collective-permute-start | bytes 786440 | tf_op jit(solution)/shard_map/ppermute | solution.py:641
  362.3 38.8 %collective-permute-start.44 = (bf16[2,64,1024]{2,1,0:T(8,128)(2,1)}, bf16[2,64,1024]{2,1,0:T(8,128)(2,1)}, u32[]{:S(2)}, u32[]{:S(2)}) collective-permute-start(bf16[2,64,1024]{2,1,0:T(8,128)(2,1)} %pad_maximum_fusion.13), channel_id=1, source_target_pairs={{0,2},{1,3},{2,0},{3,1},{4,6},{5,7},{6,4},{7,5},{8,10},{9,11},{10,... | collective-permute-start | bytes 786440 | tf_op jit(solution)/shard_map/ppermute | solution.py:641
  363.5 37.7 %collective-permute-start.43 = (bf16[2,64,1024]{2,1,0:T(8,128)(2,1)}, bf16[2,64,1024]{2,1,0:T(8,128)(2,1)}, u32[]{:S(2)}, u32[]{:S(2)}) collective-permute-start(bf16[2,64,1024]{2,1,0:T(8,128)(2,1)} %pad_maximum_fusion.12), channel_id=1, source_target_pairs={{0,1},{1,0},{2,3},{3,2},{4,5},{5,4},{6,7},{7,6},{8,9},{9,8},{10,11... | collective-permute-start | bytes 786440 | tf_op jit(solution)/shard_map/ppermute | solution.py:641
  410.1 22.9 %collective-permute-start.50 = (bf16[512,1024]{1,0:T(8,128)(2,1)S(1)}, bf16[512,1024]{1,0:T(8,128)(2,1)S(1)}, u32[]{:S(2)}, u32[]{:S(2)}) collective-permute-start(bf16[512,1024]{1,0:T(8,128)(2,1)S(1)} %add_convert_fusion.8), channel_id=1, source_target_pairs={{0,8},{4,20},{8,0},{12,28},{16,24},{20,4},{24,16},{28,12},{1,9},{5... | collective-permute-start | bytes 3145736 | tf_op jit(solution)/shard_map/ppermute | solution.py:636
  414.9 14.9 %collective-permute-start.48 = (bf16[128,2048]{1,0:T(8,128)(2,1)S(1)}, bf16[128,2048]{1,0:T(8,128)(2,1)S(1)}, u32[]{:S(2)}, u32[]{:S(2)}) collective-permute-start(bf16[128,2048]{1,0:T(8,128)(2,1)S(1)} %get-tuple-element.284), channel_id=1, source_target_pairs={{0,16},{4,12},{8,24},{12,4},{16,0},{20,28},{24,8},{28,20},{1,17},{... | collective-permute-start | bytes 1572872 | tf_op jit(solution)/shard_map/ppermute | solution.py:636
  420.0 19.1 %collective-permute-start.47 = (bf16[128,2048]{1,0:T(8,128)(2,1)S(1)}, bf16[128,2048]{1,0:T(8,128)(2,1)S(1)}, u32[]{:S(2)}, u32[]{:S(2)}) collective-permute-start(bf16[128,2048]{1,0:T(8,128)(2,1)S(1)} %get-tuple-element.283), channel_id=1, source_target_pairs={{0,16},{4,12},{8,24},{12,4},{16,0},{20,28},{24,8},{28,20},{1,17},{... | collective-permute-start | bytes 1572872 | tf_op jit(solution)/shard_map/ppermute | solution.py:636
  442.1 14.9 %collective-permute-start.56 = (bf16[256,2048]{1,0:T(8,128)(2,1)S(1)}, bf16[256,2048]{1,0:T(8,128)(2,1)S(1)}, u32[]{:S(2)}, u32[]{:S(2)}) collective-permute-start(bf16[256,2048]{1,0:T(8,128)(2,1)S(1)} %convolution_convert_fusion.2), channel_id=1, source_target_pairs={{0,16},{4,12},{8,24},{12,4},{16,0},{20,28},{24,8},{28,20},{1,17},{... | collective-permute-start | bytes 3145736 | tf_op jit(solution)/shard_map/ppermute | solution.py:636
  449.1 28.7 %collective-permute-start.55 = (bf16[256,2048]{1,0:T(8,128)(2,1)}, bf16[256,2048]{1,0:T(8,128)(2,1)}, u32[]{:S(2)}, u32[]{:S(2)}) collective-permute-start(bf16[256,2048]{1,0:T(8,128)(2,1)} %convolution_convert_fusion.3), channel_id=1, source_target_pairs={{0,16},{4,12},{8,24},{12,4},{16,0},{20,28},{24,8},{28,20},{1,17},{... | collective-permute-start | bytes 3145736 | tf_op jit(solution)/shard_map/ppermute | solution.py:636
  458.3 24.2 %collective-permute-start.57 = (bf16[256,2048]{1,0:T(8,128)(2,1)}, bf16[256,2048]{1,0:T(8,128)(2,1)}, u32[]{:S(2)}, u32[]{:S(2)}) collective-permute-start(bf16[256,2048]{1,0:T(8,128)(2,1)} %add_convert_fusion.5), channel_id=1, source_target_pairs={{0,8},{4,20},{8,0},{12,28},{16,24},{20,4},{24,16},{28,12},{1,9},{5... | collective-permute-start | bytes 3145736 | tf_op jit(solution)/shard_map/ppermute | solution.py:636
  467.1 19.7 %all-to-all-start.1 = ((bf16[8,64,768]{2,1,0:T(8,128)(2,1)}), bf16[8,64,768]{2,1,0:T(8,128)(2,1)S(1)}, u32[]{:S(2)}, u32[]{:S(2)}) async-start(bf16[8,64,768]{2,1,0:T(8,128)(2,1)} %bitcast.118), calls=%async_computation.5 | async-start | bytes 1572864 | tf_op jit(solution)/shard_map/all_to_all | solution.py:621
  474.7 19.1 %collective-permute-start.53 = (bf16[2,64,1024]{2,1,0:T(8,128)(2,1)}, bf16[2,64,1024]{2,1,0:T(8,128)(2,1)S(1)}, u32[]{:S(2)}, u32[]{:S(2)}) collective-permute-start(bf16[2,64,1024]{2,1,0:T(8,128)(2,1)} %pad_maximum_fusion.17), channel_id=1, source_target_pairs={{0,2},{1,3},{2,0},{3,1},{4,6},{5,7},{6,4},{7,5},{8,10},{9,11},{10,... | collective-permute-start | bytes 786440 | tf_op jit(solution)/shard_map/ppermute | solution.py:641
  475.7 25.3 %collective-permute-start.54 = (bf16[2,64,1024]{2,1,0:T(8,128)(2,1)}, bf16[2,64,1024]{2,1,0:T(8,128)(2,1)}, u32[]{:S(2)}, u32[]{:S(2)}) collective-permute-start(bf16[2,64,1024]{2,1,0:T(8,128)(2,1)} %pad_maximum_fusion.18), channel_id=1, source_target_pairs={{0,3},{1,2},{2,1},{3,0},{4,7},{5,6},{6,5},{7,4},{8,11},{9,10},{10,... | collective-permute-start | bytes 786440 | tf_op jit(solution)/shard_map/ppermute | solution.py:641
  (87 other events, 774.6 us)
Sparse Core Ops, SparseCore 0:
  9.6 33.2 all-gather.6
  48.2 67.0 all-gather.10
  116.9 54.8 all-gather.12
  186.3 46.0 all-gather.8
  274.0 43.2 reduce-scatter.4
  319.5 43.1 reduce-scatter.6
  365.0 35.1 reduce-scatter.8
  405.8 61.2 reduce-scatter.10

commit v7 on v6

--- a/solution.py
+++ b/solution.py
@@ -774,14 +774,14 @@
     gate_pieces = plane_gather(line_rows(gate_moved).reshape(d_rows, hid))
     down_pieces = plane_gather_more([down_weight])
     x_all = jnp.concatenate(x_pieces, axis=0)
-    x_all, gate_pieces = together((x_all, gate_pieces))
+    x_all, gate_pieces[:3] = together((x_all, gate_pieces[:3]))
     up_moved = lines_pair(up_pair)
     cot_all = gather(cotangent, TOK)
 
     kept, scale_all, attended, lse = attention_forward(pairing, me, x_all, qkv_weight, turn)
     while len(down_pieces) < n_plane:
         down_pieces = plane_gather_more(down_pieces)
-    attended, down_pieces = together((attended, down_pieces))
+    attended, down_pieces, gate_pieces = together((attended, down_pieces, gate_pieces))
     down_rows = place(down_pieces, index).reshape(hid, width)
     own_f = tokens.astype(F32)
     theirs = together(mm(attended[half:], merge_rows).astype(BF))

time: 521 us -> 521 us (level)
    ppermute x30, waiting for transfers between devices: 117 us -> 103 us  [plane_step(): lax.ppermute(value, CTX, [(i, i ^ 2 * steps[i % 2][step]) for i in range(...]
    ppermute x12, waiting for transfers between devices: 66.7 us -> 72.6 us  [line_swap(): return lax.ppermute(value, 'fsdp', [(i, i ^ mask) for i in range(n)])]
    ppermute x12, starting transfers between devices: 11.4 us -> 17.1 us  [line_swap(): return lax.ppermute(value, 'fsdp', [(i, i ^ mask) for i in range(n)])]
where the time goes in v7:
time: 521 us; the launch traced here: 513 us
  waiting for transfers between devices  202 us (39%)
  Pallas kernels  113 us (22%)
  starting transfers between devices  60 us (12%)
  local copies, waits for them, and re-layouts  55.6 us (11%)
  other arithmetic  44.9 us (9%)
  matrix products  20.9 us (4%)
  between operations  15.5 us (3%)
    ppermute x30, waiting for transfers between devices, plane_step(): lax.ppermute(value, CTX, [(i, i ^ 2 * steps[i % 2][step]) for i in range(...  103 us
    ppermute x12, waiting for transfers between devices, line_swap(): return lax.ppermute(value, 'fsdp', [(i, i ^ mask) for i in range(n)])  72.6 us
    pallas_call x1, Pallas kernels, feed_forward(): pl.pallas_call(feed_forward_kernel, grid_spec=pltpu.PrefetchScalarGridSpe...  31.8 us
    ppermute x30, starting transfers between devices, plane_step(): lax.ppermute(value, CTX, [(i, i ^ 2 * steps[i % 2][step]) for i in range(...  31.7 us
    unnamed x141, local copies, waits for them, and re-layouts  31.2 us
    dot_general x8, matrix products, t_mm(): lax.dot_general(left, right, (((0,), (0,)), ((), ())), preferred_element_...  18.1 us
    pallas_call x1, Pallas kernels, attention_forward(): pl.pallas_call(functools.partial(forward_kernel, n_ctx, 256), out_shape=[...  17.1 us
    ppermute x12, starting transfers between devices, line_swap(): return lax.ppermute(value, 'fsdp', [(i, i ^ mask) for i in range(n)])  17.1 us
  transfers between devices with their start and end apart: 68, of which 33 were waited for; matrix products, arithmetic and copies ran while one was open for 19% of the time, Pallas kernels for 15%

profile of v7, /device:TPU:18, one launch (start us, length us, event | category | flops | bytes accessed | tf_op | source)
XLA Modules:
  0.0 512.7 jit_solution(5520551923352269121)
XLA Ops:
  12.5 6.6 %collective-permute-done.2 = bf16[128,2048]{1,0:T(8,128)(2,1)} collective-permute-done((bf16[128,2048]{1,0:T(8,128)(2,1)}, bf16[128,2048]{1,0:T(8,128)(2,1)}, u32[]{:S(2)}, u32[]{:S(2)}) %collective-permute-start.2) | collective-permute-done | bytes 524320 | tf_op jit(solution)/shard_map/ppermute | solution.py:636
  25.0 3.5 all-to-all-start
  32.3 7.3 %all-to-all-done = bf16[8,64,768]{2,1,0:T(8,128)(2,1)S(1)} async-done(((bf16[8,64,768]{2,1,0:T(8,128)(2,1)}), bf16[8,64,768]{2,1,0:T(8,128)(2,1)S(1)}, u32[]{:S(2)}, u32[]{:S(2)}) %all-to-all-start) | async-done | bytes 786464 | tf_op jit(solution)/shard_map/all_to_all | solution.py:621
  39.5 8.4 %collective-permute-done.1.refs_3_ = bf16[2,64,1024]{2,1,0:T(8,128)(2,1)S(1)} collective-permute-done((bf16[2,64,1024]{2,1,0:T(8,128)(2,1)S(1)}, bf16[2,64,1024]{2,1,0:T(8,128)(2,1)S(1)}, u32[]{:S(2)}, u32[]{:S(2)}) %collective-permute-start.1) | collective-permute-done | bytes 262176 | tf_op jit(solution)/shard_map/ppermute | solution.py:641
  50.5 3.2 collective-permute-start.11
  55.5 11.9 %collective-permute-done.10.refs_1_ = bf16[2,64,1024]{2,1,0:T(8,128)(2,1)S(1)} collective-permute-done((bf16[2,64,1024]{2,1,0:T(8,128)(2,1)S(1)}, bf16[2,64,1024]{2,1,0:T(8,128)(2,1)S(1)}, u32[]{:S(2)}, u32[]{:S(2)}) %collective-permute-start.10) | collective-permute-done | bytes 262176 | tf_op jit(solution)/shard_map/ppermute | solution.py:641
  67.4 6.9 %collective-permute-done.11.refs_2_ = bf16[2,64,1024]{2,1,0:T(8,128)(2,1)S(1)} collective-permute-done((bf16[2,64,1024]{2,1,0:T(8,128)(2,1)S(1)}, bf16[2,64,1024]{2,1,0:T(8,128)(2,1)S(1)}, u32[]{:S(2)}, u32[]{:S(2)}) %collective-permute-start.11) | collective-permute-done | bytes 262176 | tf_op jit(solution)/shard_map/ppermute | solution.py:641
  90.0 13.6 %collective-permute-done.12.refs_1_ = bf16[512,1024]{1,0:T(8,128)(2,1)} collective-permute-done((bf16[512,1024]{1,0:T(8,128)(2,1)}, bf16[512,1024]{1,0:T(8,128)(2,1)}, u32[]{:S(2)}, u32[]{:S(2)}) %collective-permute-start.12) | collective-permute-done | bytes 1048608 | tf_op jit(solution)/shard_map/ppermute | solution.py:636
  112.2 3.0 all-gather.11.cloned.1.call-done
  115.3 17.1 %attention_forward.1 = (bf16[4,1024,256]{2,1,0:T(8,128)(2,1)}, f32[1024,1]{1,0:T(8,128)}, bf16[1024,256]{1,0:T(8,128)(2,1)}, f32[1024,128]{1,0:T(8,128)}) custom-call(s32[1,8]{1,0:T(1,128)} %pair_ref.3, s32[2]{0:T(128)} %pad_add_fusion.me_ref, bf16[1024,2048]{1,0:T(8,128)(2,1)} %constant_dynamic-update-slice_fusion.x_ref, bf16[2048,768]{1,0:T(8,128)(2,1)} %bitcast.98, ...), custom_call_target="tpu_custom_call" | custom-call | flops 1024 | bytes 1024 | tf_op jit(solution)/shard_map/attention_forward/pallas_call | solution.py:159
  135.4 3.3 collective-permute-done.18
  145.9 3.8 collective-permute-done.20
  152.8 3.6 collective-permute-start.23
  162.8 5.1 collective-permute-done.22.refs_1_
  167.9 11.4 %collective-permute-done.23.refs_2_ = bf16[2,64,1024]{2,1,0:T(8,128)(2,1)} collective-permute-done((bf16[2,64,1024]{2,1,0:T(8,128)(2,1)}, bf16[2,64,1024]{2,1,0:T(8,128)(2,1)}, u32[]{:S(2)}, u32[]{:S(2)}) %collective-permute-start.23) | collective-permute-done | bytes 262176 | tf_op jit(solution)/shard_map/ppermute | solution.py:641
  179.3 5.0 collective-permute-done.24.refs_3_
  188.9 4.5 place.4
  193.4 4.8 place.3
  198.2 4.6 collective-permute-done.25.refs_1_
  206.4 12.3 %collective-permute-done.26.refs_2_ = bf16[512,1024]{1,0:T(8,128)(2,1)} collective-permute-done((bf16[512,1024]{1,0:T(8,128)(2,1)S(1)}, bf16[512,1024]{1,0:T(8,128)(2,1)}, u32[]{:S(2)}, u32[]{:S(2)}) %collective-permute-start.26) | collective-permute-done | bytes 1048608 | tf_op jit(solution)/shard_map/ppermute | solution.py:636
  218.7 4.1 place.5
  222.8 7.0 %collective-permute-done.27 = bf16[512,1024]{1,0:T(8,128)(2,1)S(1)} collective-permute-done((bf16[512,1024]{1,0:T(8,128)(2,1)}, bf16[512,1024]{1,0:T(8,128)(2,1)S(1)}, u32[]{:S(2)}, u32[]{:S(2)}) %collective-permute-start.27) | collective-permute-done | bytes 1048608 | tf_op jit(solution)/shard_map/ppermute | solution.py:636
  232.7 31.8 %feed_forward.1 = (bf16[1024,1024]{1,0:T(8,128)(2,1)}, bf16[1024,1024]{1,0:T(8,128)(2,1)}, bf16[1024,1024]{1,0:T(8,128)(2,1)}, bf16[512,2048]{1,0:T(8,128)(2,1)}, bf16[512,2048]{1,0:T(8,128)(2,1)}) custom-call(s32[1]{0:T(128)} %bitcast.2.core_ref, bf16[1024,2048]{1,0:T(8,128)(2,1)} %all-gather.9.cloned.1.call-done.n_ref.left_ref, ...), custom_call_target="tpu_custom_call" | custom-call | flops 1024 | bytes 1024 | tf_op jit(solution)/shard_map/feed_forward/pallas_call | solution.py:301
  266.4 3.5 weight_rows.2
  276.4 4.2 convolution_convert_fusion.6
  280.6 5.6 %branch_rows.1 = (bf16[512,2048]{1,0:T(8,128)(2,1)S(1)}, bf16[512,2048]{1,0:T(8,128)(2,1)S(1)}) custom-call(s32[1]{0:T(128)} %bitcast.2.core_ref, bf16[1024,1024]{1,0:T(8,128)(2,1)S(1)} %copy-done.17, bf16[1024,2048]{1,0:T(8,128)(2,1)S(1)} %bitcast.97), custom_call_target="tpu_custom_call" | custom-call | flops 1024 | bytes 1024 | tf_op jit(solution)/shard_map/branch_rows/pallas_call | solution.py:345
  286.2 3.5 weight_rows.3
  296.6 4.0 collective-permute-done.30
  301.6 14.3 %collective-permute-done.31 = bf16[512,1024]{1,0:T(8,128)(2,1)S(1)} collective-permute-done((bf16[512,1024]{1,0:T(8,128)(2,1)S(1)}, bf16[512,1024]{1,0:T(8,128)(2,1)S(1)}, u32[]{:S(2)}, u32[]{:S(2)}) %collective-permute-start.31) | collective-permute-done | bytes 1048608 | tf_op jit(solution)/shard_map/ppermute | solution.py:636
  323.3 6.3 %copy.37 = bf16[1024,2048]{0,1:T(8,128)(2,1)} copy(bf16[1024,2048]{1,0:T(8,128)(2,1)} %constant_dynamic-update-slice_fusion.x_ref) | data formatting | bytes 8388608 | tf_op jit(solution)/shard_map/optimization_barrier | solution.py:625
  329.6 5.0 copy.38
  337.2 6.6 %collective-permute-done.34.refs_2_ = bf16[128,2048]{1,0:T(8,128)(2,1)S(1)} collective-permute-done((bf16[128,2048]{1,0:T(8,128)(2,1)S(1)}, bf16[128,2048]{1,0:T(8,128)(2,1)S(1)}, u32[]{:S(2)}, u32[]{:S(2)}) %collective-permute-start.34) | collective-permute-done | bytes 524320 | tf_op jit(solution)/shard_map/ppermute | solution.py:636
  343.8 5.6 %collective-permute-done.35.refs_3_ = bf16[128,2048]{1,0:T(8,128)(2,1)S(1)} collective-permute-done((bf16[128,2048]{1,0:T(8,128)(2,1)S(1)}, bf16[128,2048]{1,0:T(8,128)(2,1)S(1)}, u32[]{:S(2)}, u32[]{:S(2)}) %collective-permute-start.35) | collective-permute-done | bytes 524320 | tf_op jit(solution)/shard_map/ppermute | solution.py:636
  351.3 3.3 merge_terms.1
  364.9 12.6 %attention_backward.1 = (bf16[1024,768]{1,0:T(8,128)(2,1)S(1)}, bf16[1024,768]{1,0:T(8,128)(2,1)S(1)}) custom-call(s32[1,8]{1,0:T(1,128)S(1)} %copy-done.32, s32[2]{0:T(128)S(1)} %copy-done.33, bf16[1024,256]{1,0:T(8,128)(2,1)S(1)} %get-tuple-element.233.do_ref, bf16[4,1024,256]{2,1,0:T(8,128)(2,1)S(1)} %copy-done.19, f32[1024,1]{1,0:T(8,128)S(1)} %copy-done.30, ...), custom_call_target="tpu_custom_call" | custom-call | flops 1024 | bytes 1024 | tf_op jit(solution)/shard_map/attention_backward/pallas_call | solution.py:247
  383.4 4.0 heads_term.1
  390.4 8.8 %collective-permute-done.44.refs_2_ = bf16[2,64,1024]{2,1,0:T(8,128)(2,1)} collective-permute-done((bf16[2,64,1024]{2,1,0:T(8,128)(2,1)}, bf16[2,64,1024]{2,1,0:T(8,128)(2,1)}, u32[]{:S(2)}, u32[]{:S(2)}) %collective-permute-start.44) | collective-permute-done | bytes 262176 | tf_op jit(solution)/shard_map/ppermute | solution.py:641
  402.0 3.0 back_rows.3
  421.0 8.5 %collective-permute-done.48 = bf16[128,2048]{1,0:T(8,128)(2,1)S(1)} collective-permute-done((bf16[128,2048]{1,0:T(8,128)(2,1)S(1)}, bf16[128,2048]{1,0:T(8,128)(2,1)S(1)}, u32[]{:S(2)}, u32[]{:S(2)}) %collective-permute-start.48) | collective-permute-done | bytes 524320 | tf_op jit(solution)/shard_map/ppermute | solution.py:636
  437.7 3.5 collective-permute-done.49
  443.2 3.0 unfold_hidden.2
  450.2 6.2 %collective-permute-done.56 = bf16[256,2048]{1,0:T(8,128)(2,1)S(1)} collective-permute-done((bf16[256,2048]{1,0:T(8,128)(2,1)S(1)}, bf16[256,2048]{1,0:T(8,128)(2,1)S(1)}, u32[]{:S(2)}, u32[]{:S(2)}) %collective-permute-start.56) | collective-permute-done | bytes 1048608 | tf_op jit(solution)/shard_map/ppermute | solution.py:636
  460.6 6.8 %reduce-scatter.11.cloned.1.call-done = bf16[512,768]{1,0:T(8,128)(2,1)} async-done(((bf16[2048,768]{1,0:T(8,128)(2,1)}), bf16[512,768]{1,0:T(8,128)(2,1)}) %reduce-scatter.11.cloned.1.call-update) | async-done | bytes 786448 | tf_op jit(solution)/shard_map/reduce_scatter | solution.py:617
  467.4 4.2 all-to-all-start.1
  478.1 3.8 collective-permute-done.57
  481.9 3.4 fusion.9
  487.6 6.6 %collective-permute-done.53.refs_2_ = bf16[2,64,1024]{2,1,0:T(8,128)(2,1)S(1)} collective-permute-done((bf16[2,64,1024]{2,1,0:T(8,128)(2,1)}, bf16[2,64,1024]{2,1,0:T(8,128)(2,1)S(1)}, u32[]{:S(2)}, u32[]{:S(2)}) %collective-permute-start.53) | collective-permute-done | bytes 262176 | tf_op jit(solution)/shard_map/ppermute | solution.py:641
  494.2 7.2 %collective-permute-done.54.refs_3_ = bf16[2,64,1024]{2,1,0:T(8,128)(2,1)} collective-permute-done((bf16[2,64,1024]{2,1,0:T(8,128)(2,1)}, bf16[2,64,1024]{2,1,0:T(8,128)(2,1)}, u32[]{:S(2)}, u32[]{:S(2)}) %collective-permute-start.54) | collective-permute-done | bytes 262176 | tf_op jit(solution)/shard_map/ppermute | solution.py:641
  (348 shorter events, 170.8 us)
Async XLA Ops:
  7.2 40.9 %all-gather.7.cloned.1.call-start = ((), (), s32[]{:S(2)}) async-start(), calls=%async_computation.6 | async-start | bytes 1310720 | tf_op jit(solution)/shard_map/all_gather | solution.py:613
  11.0 18.2 %collective-permute-start = (bf16[4,64,1024]{2,1,0:T(8,128)(2,1)}, bf16[4,64,1024]{2,1,0:T(8,128)(2,1)}, u32[]{:S(2)}, u32[]{:S(2)}) collective-permute-start(bf16[4,64,1024]{2,1,0:T(8,128)(2,1)} %dynamic-slice_bitcast_fusion.4), channel_id=1, source_target_pairs={{0,4},{4,0},{8,12},{12,8},{16,20},{20,16},{24,28},{28,24},{1,5},{5... | collective-permute-start | bytes 1572872 | tf_op jit(solution)/shard_map/ppermute | solution.py:630
  11.5 17.8 %collective-permute-start.3 = (bf16[128,2048]{1,0:T(8,128)(2,1)}, bf16[128,2048]{1,0:T(8,128)(2,1)}, u32[]{:S(2)}, u32[]{:S(2)}) collective-permute-start(bf16[128,2048]{1,0:T(8,128)(2,1)} %bitcast), channel_id=1, source_target_pairs={{0,16},{4,12},{8,24},{12,4},{16,0},{20,28},{24,8},{28,20},{1,17},{... | collective-permute-start | bytes 1572872 | tf_op jit(solution)/shard_map/ppermute | solution.py:636
  25.0 14.5 %all-to-all-start = ((bf16[8,64,768]{2,1,0:T(8,128)(2,1)}), bf16[8,64,768]{2,1,0:T(8,128)(2,1)S(1)}, u32[]{:S(2)}, u32[]{:S(2)}) async-start(bf16[8,64,768]{2,1,0:T(8,128)(2,1)} %fold_heads.1), calls=%async_computation | async-start | bytes 1572864 | tf_op jit(solution)/shard_map/all_to_all | solution.py:621
  28.5 86.7 %all-gather.11.cloned.1.call-start = ((), (), s32[]{:S(2)}) async-start(), calls=%async_computation.12 | async-start | bytes 3932160 | tf_op jit(solution)/shard_map/all_gather | solution.py:613
  29.2 18.8 %collective-permute-start.6 = (bf16[128,2048]{1,0:T(8,128)(2,1)}, bf16[128,2048]{1,0:T(8,128)(2,1)}, u32[]{:S(2)}, u32[]{:S(2)}) collective-permute-start(bf16[128,2048]{1,0:T(8,128)(2,1)} %collective-permute-done.2), channel_id=1, source_target_pairs={{0,4},{4,0},{8,12},{12,8},{16,20},{20,16},{24,28},{28,24},{1,5},{5... | collective-permute-start | bytes 1572872 | tf_op jit(solution)/shard_map/ppermute | solution.py:630
  29.3 18.7 %collective-permute-start.7 = (bf16[128,2048]{1,0:T(8,128)(2,1)}, bf16[128,2048]{1,0:T(8,128)(2,1)}, u32[]{:S(2)}, u32[]{:S(2)}) collective-permute-start(bf16[128,2048]{1,0:T(8,128)(2,1)} %collective-permute-done.3), channel_id=1, source_target_pairs={{0,4},{4,0},{8,12},{12,8},{16,20},{20,16},{24,28},{28,24},{1,5},{5... | collective-permute-start | bytes 1572872 | tf_op jit(solution)/shard_map/ppermute | solution.py:630
  29.7 18.3 %collective-permute-start.8 = (bf16[128,2048]{1,0:T(8,128)(2,1)}, bf16[128,2048]{1,0:T(8,128)(2,1)}, u32[]{:S(2)}, u32[]{:S(2)}) collective-permute-start(bf16[128,2048]{1,0:T(8,128)(2,1)} %collective-permute-done.4), channel_id=1, source_target_pairs={{0,4},{4,0},{8,12},{12,8},{16,20},{20,16},{24,28},{28,24},{1,5},{5... | collective-permute-start | bytes 1572872 | tf_op jit(solution)/shard_map/ppermute | solution.py:630
  31.7 16.2 %collective-permute-start.1 = (bf16[2,64,1024]{2,1,0:T(8,128)(2,1)S(1)}, bf16[2,64,1024]{2,1,0:T(8,128)(2,1)S(1)}, u32[]{:S(2)}, u32[]{:S(2)}) collective-permute-start(bf16[2,64,1024]{2,1,0:T(8,128)(2,1)S(1)} %pad_maximum_fusion.1), channel_id=1, source_target_pairs={{0,3},{1,2},{2,1},{3,0},{4,7},{5,6},{6,5},{7,4},{8,11},{9,10},{10,... | collective-permute-start | bytes 786440 | tf_op jit(solution)/shard_map/ppermute | solution.py:641
  48.1 182.8 %all-gather.13.cloned.1.call-start = ((), (), s32[]{:S(2)}) async-start(), calls=%async_computation.13 | async-start | bytes 4718592 | tf_op jit(solution)/shard_map/all_gather | solution.py:613
  48.1 34.2 %collective-permute-start.14 = (bf16[256,2048]{1,0:T(8,128)(2,1)}, bf16[256,2048]{1,0:T(8,128)(2,1)}, u32[]{:S(2)}, u32[]{:S(2)}) collective-permute-start(bf16[256,2048]{1,0:T(8,128)(2,1)} %refs_0_), channel_id=1, source_target_pairs={{0,8},{4,20},{8,0},{12,28},{16,24},{20,4},{24,16},{28,12},{1,9},{5... | collective-permute-start | bytes 3145736 | tf_op jit(solution)/shard_map/ppermute | solution.py:636
  48.5 83.9 %collective-permute-start.15 = (bf16[256,2048]{1,0:T(8,128)(2,1)}, bf16[256,2048]{1,0:T(8,128)(2,1)}, u32[]{:S(2)}, u32[]{:S(2)}) collective-permute-start(bf16[256,2048]{1,0:T(8,128)(2,1)} %refs_0_), channel_id=1, source_target_pairs={{0,16},{4,12},{8,24},{12,4},{16,0},{20,28},{24,8},{28,20},{1,17},{... | collective-permute-start | bytes 3145736 | tf_op jit(solution)/shard_map/ppermute | solution.py:636
  50.2 182.5 %all-gather.9.cloned.1.call-start = ((), (), s32[]{:S(2)}) async-start(), calls=%async_computation.7 | async-start | bytes 4718592 | tf_op jit(solution)/shard_map/all_gather | solution.py:613
  50.4 17.0 %collective-permute-start.10 = (bf16[2,64,1024]{2,1,0:T(8,128)(2,1)S(1)}, bf16[2,64,1024]{2,1,0:T(8,128)(2,1)S(1)}, u32[]{:S(2)}, u32[]{:S(2)}) collective-permute-start(bf16[2,64,1024]{2,1,0:T(8,128)(2,1)S(1)} %pad_maximum_fusion.3), channel_id=1, source_target_pairs={{0,1},{1,0},{2,3},{3,2},{4,5},{5,4},{6,7},{7,6},{8,9},{9,8},{10,11... | collective-permute-start | bytes 786440 | tf_op jit(solution)/shard_map/ppermute | solution.py:641
  50.5 23.8 %collective-permute-start.11 = (bf16[2,64,1024]{2,1,0:T(8,128)(2,1)S(1)}, bf16[2,64,1024]{2,1,0:T(8,128)(2,1)S(1)}, u32[]{:S(2)}, u32[]{:S(2)}) collective-permute-start(bf16[2,64,1024]{2,1,0:T(8,128)(2,1)S(1)} %pad_maximum_fusion.4), channel_id=1, source_target_pairs={{0,2},{1,3},{2,0},{3,1},{4,6},{5,7},{6,4},{7,5},{8,10},{9,11},{10,... | collective-permute-start | bytes 786440 | tf_op jit(solution)/shard_map/ppermute | solution.py:641
  77.2 26.4 %collective-permute-start.12 = (bf16[512,1024]{1,0:T(8,128)(2,1)}, bf16[512,1024]{1,0:T(8,128)(2,1)}, u32[]{:S(2)}, u32[]{:S(2)}) collective-permute-start(bf16[512,1024]{1,0:T(8,128)(2,1)} %bitcast.105), channel_id=1, source_target_pairs={{0,8},{4,20},{8,0},{12,28},{16,24},{20,4},{24,16},{28,12},{1,9},{5... | collective-permute-start | bytes 3145736 | tf_op jit(solution)/shard_map/ppermute | solution.py:636
  82.3 50.1 %collective-permute-start.16 = (bf16[256,2048]{1,0:T(8,128)(2,1)}, bf16[256,2048]{1,0:T(8,128)(2,1)S(1)}, u32[]{:S(2)}, u32[]{:S(2)}) collective-permute-start(bf16[256,2048]{1,0:T(8,128)(2,1)} %collective-permute-done.14.refs_1_), channel_id=1, source_target_pairs={{0,16},{4,12},{8,24},{12,4},{16,0},{20,28},{24,8},{28,20},{1,17},{... | collective-permute-start | bytes 3145736 | tf_op jit(solution)/shard_map/ppermute | solution.py:636
  82.5 29.8 %collective-permute-start.13 = (bf16[512,1024]{1,0:T(8,128)(2,1)S(1)}, bf16[512,1024]{1,0:T(8,128)(2,1)}, u32[]{:S(2)}, u32[]{:S(2)}) collective-permute-start(bf16[512,1024]{1,0:T(8,128)(2,1)S(1)} %bitcast.107), channel_id=1, source_target_pairs={{0,16},{4,12},{8,24},{12,4},{16,0},{20,28},{24,8},{28,20},{1,17},{... | collective-permute-start | bytes 3145736 | tf_op jit(solution)/shard_map/ppermute | solution.py:636
  103.6 28.8 %collective-permute-start.17 = (bf16[512,1024]{1,0:T(8,128)(2,1)}, bf16[512,1024]{1,0:T(8,128)(2,1)S(1)}, u32[]{:S(2)}, u32[]{:S(2)}) collective-permute-start(bf16[512,1024]{1,0:T(8,128)(2,1)} %collective-permute-done.12.refs_1_), channel_id=1, source_target_pairs={{0,16},{4,12},{8,24},{12,4},{16,0},{20,28},{24,8},{28,20},{1,17},{... | collective-permute-start | bytes 3145736 | tf_op jit(solution)/shard_map/ppermute | solution.py:636
  142.1 25.8 %collective-permute-start.22 = (bf16[2,64,1024]{2,1,0:T(8,128)(2,1)}, bf16[2,64,1024]{2,1,0:T(8,128)(2,1)}, u32[]{:S(2)}, u32[]{:S(2)}) collective-permute-start(bf16[2,64,1024]{2,1,0:T(8,128)(2,1)} %pad_maximum_fusion.8), channel_id=1, source_target_pairs={{0,1},{1,0},{2,3},{3,2},{4,5},{5,4},{6,7},{7,6},{8,9},{9,8},{10,11... | collective-permute-start | bytes 786440 | tf_op jit(solution)/shard_map/ppermute | solution.py:641
  144.5 16.6 %collective-permute-start.19 = (bf16[128,2048]{1,0:T(8,128)(2,1)}, bf16[128,2048]{1,0:T(8,128)(2,1)}, u32[]{:S(2)}, u32[]{:S(2)}) collective-permute-start(bf16[128,2048]{1,0:T(8,128)(2,1)} %get-tuple-element.291), channel_id=1, source_target_pairs={{0,16},{4,12},{8,24},{12,4},{16,0},{20,28},{24,8},{28,20},{1,17},{... | collective-permute-start | bytes 1572872 | tf_op jit(solution)/shard_map/ppermute | solution.py:636
  152.8 26.5 %collective-permute-start.23 = (bf16[2,64,1024]{2,1,0:T(8,128)(2,1)}, bf16[2,64,1024]{2,1,0:T(8,128)(2,1)}, u32[]{:S(2)}, u32[]{:S(2)}) collective-permute-start(bf16[2,64,1024]{2,1,0:T(8,128)(2,1)} %pad_maximum_fusion.9), channel_id=1, source_target_pairs={{0,2},{1,3},{2,0},{3,1},{4,6},{5,7},{6,4},{7,5},{8,10},{9,11},{10,... | collective-permute-start | bytes 786440 | tf_op jit(solution)/shard_map/ppermute | solution.py:641
  157.2 27.1 %collective-permute-start.24 = (bf16[2,64,1024]{2,1,0:T(8,128)(2,1)}, bf16[2,64,1024]{2,1,0:T(8,128)(2,1)}, u32[]{:S(2)}, u32[]{:S(2)}) collective-permute-start(bf16[2,64,1024]{2,1,0:T(8,128)(2,1)} %pad_maximum_fusion.10), channel_id=1, source_target_pairs={{0,3},{1,2},{2,1},{3,0},{4,7},{5,6},{6,5},{7,4},{8,11},{9,10},{10,... | collective-permute-start | bytes 786440 | tf_op jit(solution)/shard_map/ppermute | solution.py:641
  185.5 134.1 %reduce-scatter.5.cloned.1.call-start = ((), (), s32[]{:S(2)}) async-start(), calls=%async_computation.8 | async-start | bytes 2621440 | tf_op jit(solution)/shard_map/reduce_scatter | solution.py:617
  187.8 15.0 %collective-permute-start.25 = (bf16[512,1024]{1,0:T(8,128)(2,1)}, bf16[512,1024]{1,0:T(8,128)(2,1)S(1)}, u32[]{:S(2)}, u32[]{:S(2)}) collective-permute-start(bf16[512,1024]{1,0:T(8,128)(2,1)} %bitcast.115), channel_id=1, source_target_pairs={{0,8},{4,20},{8,0},{12,28},{16,24},{20,4},{24,16},{28,12},{1,9},{5... | collective-permute-start | bytes 3145736 | tf_op jit(solution)/shard_map/ppermute | solution.py:636
  203.8 14.9 %collective-permute-start.26 = (bf16[512,1024]{1,0:T(8,128)(2,1)S(1)}, bf16[512,1024]{1,0:T(8,128)(2,1)}, u32[]{:S(2)}, u32[]{:S(2)}) collective-permute-start(bf16[512,1024]{1,0:T(8,128)(2,1)S(1)} %bitcast.117), channel_id=1, source_target_pairs={{0,16},{4,12},{8,24},{12,4},{16,0},{20,28},{24,8},{28,20},{1,17},{... | collective-permute-start | bytes 3145736 | tf_op jit(solution)/shard_map/ppermute | solution.py:636
  205.6 24.3 %collective-permute-start.27 = (bf16[512,1024]{1,0:T(8,128)(2,1)}, bf16[512,1024]{1,0:T(8,128)(2,1)S(1)}, u32[]{:S(2)}, u32[]{:S(2)}) collective-permute-start(bf16[512,1024]{1,0:T(8,128)(2,1)} %copy-done.56), channel_id=1, source_target_pairs={{0,16},{4,12},{8,24},{12,4},{16,0},{20,28},{24,8},{28,20},{1,17},{... | collective-permute-start | bytes 3145736 | tf_op jit(solution)/shard_map/ppermute | solution.py:636
  274.2 105.6 %reduce-scatter.7.cloned.1.call-start = ((), (), s32[]{:S(2)}) async-start(), calls=%async_computation.9 | async-start | bytes 2621440 | tf_op jit(solution)/shard_map/reduce_scatter | solution.py:617
  274.3 22.3 %collective-permute-start.29 = (bf16[512,1024]{1,0:T(8,128)(2,1)}, bf16[512,1024]{1,0:T(8,128)(2,1)S(1)}, u32[]{:S(2)}, u32[]{:S(2)}) collective-permute-start(bf16[512,1024]{1,0:T(8,128)(2,1)} %copy-done.35), channel_id=1, source_target_pairs={{0,16},{4,12},{8,24},{12,4},{16,0},{20,28},{24,8},{28,20},{1,17},{... | collective-permute-start | bytes 3145736 | tf_op jit(solution)/shard_map/ppermute | solution.py:636
  275.8 24.8 %collective-permute-start.30 = (bf16[512,1024]{1,0:T(8,128)(2,1)}, bf16[512,1024]{1,0:T(8,128)(2,1)S(1)}, u32[]{:S(2)}, u32[]{:S(2)}) collective-permute-start(bf16[512,1024]{1,0:T(8,128)(2,1)} %copy-done.34), channel_id=1, source_target_pairs={{0,16},{4,12},{8,24},{12,4},{16,0},{20,28},{24,8},{28,20},{1,17},{... | collective-permute-start | bytes 3145736 | tf_op jit(solution)/shard_map/ppermute | solution.py:636
  300.6 16.9 %collective-permute-start.32 = (bf16[512,2048]{1,0:T(8,128)(2,1)S(1)}, bf16[512,2048]{1,0:T(8,128)(2,1)S(1)}, u32[]{:S(2)}, u32[]{:S(2)}) collective-permute-start(bf16[512,2048]{1,0:T(8,128)(2,1)S(1)} %get-tuple-element.214), channel_id=1, source_target_pairs={{0,4},{4,0},{8,12},{12,8},{16,20},{20,16},{24,28},{28,24},{1,5},{5... | collective-permute-start | bytes 6291464 | tf_op jit(solution)/shard_map/ppermute | solution.py:630
  301.0 14.9 %collective-permute-start.31 = (bf16[512,1024]{1,0:T(8,128)(2,1)S(1)}, bf16[512,1024]{1,0:T(8,128)(2,1)S(1)}, u32[]{:S(2)}, u32[]{:S(2)}) collective-permute-start(bf16[512,1024]{1,0:T(8,128)(2,1)S(1)} %add_convert_fusion.11), channel_id=1, source_target_pairs={{0,8},{4,20},{8,0},{12,28},{16,24},{20,4},{24,16},{28,12},{1,9},{5... | collective-permute-start | bytes 3145736 | tf_op jit(solution)/shard_map/ppermute | solution.py:636
  319.6 80.9 %reduce-scatter.9.cloned.1.call-start = ((), (), s32[]{:S(2)}) async-start(), calls=%async_computation.10 | async-start | bytes 1310720 | tf_op jit(solution)/shard_map/reduce_scatter | solution.py:617
  354.7 112.7 %reduce-scatter.11.cloned.1.call-start = ((), (), s32[]{:S(2)}) async-start(), calls=%async_computation.11 | async-start | bytes 3932160 | tf_op jit(solution)/shard_map/reduce_scatter | solution.py:617
  356.4 42.8 %collective-permute-start.40 = (bf16[512,1024]{1,0:T(8,128)(2,1)}, bf16[512,1024]{1,0:T(8,128)(2,1)}, u32[]{:S(2)}, u32[]{:S(2)}) collective-permute-start(bf16[512,1024]{1,0:T(8,128)(2,1)} %convolution_convert_fusion.7), channel_id=1, source_target_pairs={{0,16},{4,12},{8,24},{12,4},{16,0},{20,28},{24,8},{28,20},{1,17},{... | collective-permute-start | bytes 3145736 | tf_op jit(solution)/shard_map/ppermute | solution.py:636
  357.9 41.4 %collective-permute-start.41 = (bf16[512,1024]{1,0:T(8,128)(2,1)}, bf16[512,1024]{1,0:T(8,128)(2,1)}, u32[]{:S(2)}, u32[]{:S(2)}) collective-permute-start(bf16[512,1024]{1,0:T(8,128)(2,1)} %convolution_convert_fusion.6), channel_id=1, source_target_pairs={{0,16},{4,12},{8,24},{12,4},{16,0},{20,28},{24,8},{28,20},{1,17},{... | collective-permute-start | bytes 3145736 | tf_op jit(solution)/shard_map/ppermute | solution.py:636
  359.2 31.2 %collective-permute-start.45 = (bf16[2,64,1024]{2,1,0:T(8,128)(2,1)}, bf16[2,64,1024]{2,1,0:T(8,128)(2,1)}, u32[]{:S(2)}, u32[]{:S(2)}) collective-permute-start(bf16[2,64,1024]{2,1,0:T(8,128)(2,1)} %pad_maximum_fusion.14), channel_id=1, source_target_pairs={{0,3},{1,2},{2,1},{3,0},{4,7},{5,6},{6,5},{7,4},{8,11},{9,10},{10,... | collective-permute-start | bytes 786440 | tf_op jit(solution)/shard_map/ppermute | solution.py:641
  360.4 38.9 %collective-permute-start.44 = (bf16[2,64,1024]{2,1,0:T(8,128)(2,1)}, bf16[2,64,1024]{2,1,0:T(8,128)(2,1)}, u32[]{:S(2)}, u32[]{:S(2)}) collective-permute-start(bf16[2,64,1024]{2,1,0:T(8,128)(2,1)} %pad_maximum_fusion.13), channel_id=1, source_target_pairs={{0,2},{1,3},{2,0},{3,1},{4,6},{5,7},{6,4},{7,5},{8,10},{9,11},{10,... | collective-permute-start | bytes 786440 | tf_op jit(solution)/shard_map/ppermute | solution.py:641
  363.8 35.4 %collective-permute-start.43 = (bf16[2,64,1024]{2,1,0:T(8,128)(2,1)}, bf16[2,64,1024]{2,1,0:T(8,128)(2,1)}, u32[]{:S(2)}, u32[]{:S(2)}) collective-permute-start(bf16[2,64,1024]{2,1,0:T(8,128)(2,1)} %pad_maximum_fusion.12), channel_id=1, source_target_pairs={{0,1},{1,0},{2,3},{3,2},{4,5},{5,4},{6,7},{7,6},{8,9},{9,8},{10,11... | collective-permute-start | bytes 786440 | tf_op jit(solution)/shard_map/ppermute | solution.py:641
  409.5 23.8 %collective-permute-start.50 = (bf16[512,1024]{1,0:T(8,128)(2,1)S(1)}, bf16[512,1024]{1,0:T(8,128)(2,1)S(1)}, u32[]{:S(2)}, u32[]{:S(2)}) collective-permute-start(bf16[512,1024]{1,0:T(8,128)(2,1)S(1)} %add_convert_fusion.8), channel_id=1, source_target_pairs={{0,8},{4,20},{8,0},{12,28},{16,24},{20,4},{24,16},{28,12},{1,9},{5... | collective-permute-start | bytes 3145736 | tf_op jit(solution)/shard_map/ppermute | solution.py:636
  415.2 14.2 %collective-permute-start.48 = (bf16[128,2048]{1,0:T(8,128)(2,1)S(1)}, bf16[128,2048]{1,0:T(8,128)(2,1)S(1)}, u32[]{:S(2)}, u32[]{:S(2)}) collective-permute-start(bf16[128,2048]{1,0:T(8,128)(2,1)S(1)} %get-tuple-element.290), channel_id=1, source_target_pairs={{0,16},{4,12},{8,24},{12,4},{16,0},{20,28},{24,8},{28,20},{1,17},{... | collective-permute-start | bytes 1572872 | tf_op jit(solution)/shard_map/ppermute | solution.py:636
  420.3 17.4 %collective-permute-start.47 = (bf16[128,2048]{1,0:T(8,128)(2,1)S(1)}, bf16[128,2048]{1,0:T(8,128)(2,1)S(1)}, u32[]{:S(2)}, u32[]{:S(2)}) collective-permute-start(bf16[128,2048]{1,0:T(8,128)(2,1)S(1)} %get-tuple-element.289), channel_id=1, source_target_pairs={{0,16},{4,12},{8,24},{12,4},{16,0},{20,28},{24,8},{28,20},{1,17},{... | collective-permute-start | bytes 1572872 | tf_op jit(solution)/shard_map/ppermute | solution.py:636
  441.5 14.9 %collective-permute-start.56 = (bf16[256,2048]{1,0:T(8,128)(2,1)S(1)}, bf16[256,2048]{1,0:T(8,128)(2,1)S(1)}, u32[]{:S(2)}, u32[]{:S(2)}) collective-permute-start(bf16[256,2048]{1,0:T(8,128)(2,1)S(1)} %convolution_convert_fusion.2), channel_id=1, source_target_pairs={{0,16},{4,12},{8,24},{12,4},{16,0},{20,28},{24,8},{28,20},{1,17},{... | collective-permute-start | bytes 3145736 | tf_op jit(solution)/shard_map/ppermute | solution.py:636
  449.4 28.7 %collective-permute-start.55 = (bf16[256,2048]{1,0:T(8,128)(2,1)}, bf16[256,2048]{1,0:T(8,128)(2,1)}, u32[]{:S(2)}, u32[]{:S(2)}) collective-permute-start(bf16[256,2048]{1,0:T(8,128)(2,1)} %convolution_convert_fusion.3), channel_id=1, source_target_pairs={{0,16},{4,12},{8,24},{12,4},{16,0},{20,28},{24,8},{28,20},{1,17},{... | collective-permute-start | bytes 3145736 | tf_op jit(solution)/shard_map/ppermute | solution.py:636
  457.8 24.1 %collective-permute-start.57 = (bf16[256,2048]{1,0:T(8,128)(2,1)}, bf16[256,2048]{1,0:T(8,128)(2,1)}, u32[]{:S(2)}, u32[]{:S(2)}) collective-permute-start(bf16[256,2048]{1,0:T(8,128)(2,1)} %add_convert_fusion.5), channel_id=1, source_target_pairs={{0,8},{4,20},{8,0},{12,28},{16,24},{20,4},{24,16},{28,12},{1,9},{5... | collective-permute-start | bytes 3145736 | tf_op jit(solution)/shard_map/ppermute | solution.py:636
  467.4 18.8 %all-to-all-start.1 = ((bf16[8,64,768]{2,1,0:T(8,128)(2,1)}), bf16[8,64,768]{2,1,0:T(8,128)(2,1)S(1)}, u32[]{:S(2)}, u32[]{:S(2)}) async-start(bf16[8,64,768]{2,1,0:T(8,128)(2,1)} %bitcast.118), calls=%async_computation.5 | async-start | bytes 1572864 | tf_op jit(solution)/shard_map/all_to_all | solution.py:621
  475.0 19.1 %collective-permute-start.53 = (bf16[2,64,1024]{2,1,0:T(8,128)(2,1)}, bf16[2,64,1024]{2,1,0:T(8,128)(2,1)S(1)}, u32[]{:S(2)}, u32[]{:S(2)}) collective-permute-start(bf16[2,64,1024]{2,1,0:T(8,128)(2,1)} %pad_maximum_fusion.17), channel_id=1, source_target_pairs={{0,2},{1,3},{2,0},{3,1},{4,6},{5,7},{6,4},{7,5},{8,10},{9,11},{10,... | collective-permute-start | bytes 786440 | tf_op jit(solution)/shard_map/ppermute | solution.py:641
  476.1 25.3 %collective-permute-start.54 = (bf16[2,64,1024]{2,1,0:T(8,128)(2,1)}, bf16[2,64,1024]{2,1,0:T(8,128)(2,1)}, u32[]{:S(2)}, u32[]{:S(2)}) collective-permute-start(bf16[2,64,1024]{2,1,0:T(8,128)(2,1)} %pad_maximum_fusion.18), channel_id=1, source_target_pairs={{0,3},{1,2},{2,1},{3,0},{4,7},{5,6},{6,5},{7,4},{8,11},{9,10},{10,... | collective-permute-start | bytes 786440 | tf_op jit(solution)/shard_map/ppermute | solution.py:641
  (87 other events, 773.9 us)
Sparse Core Ops, SparseCore 0:
  9.6 33.2 all-gather.6
  48.2 67.0 all-gather.10
  116.9 62.8 all-gather.12
  185.6 47.0 all-gather.8
  274.3 43.2 reduce-scatter.4
  319.9 43.1 reduce-scatter.6
  365.4 35.1 reduce-scatter.8
  405.2 62.1 reduce-scatter.10
